TPU v7x, 32 devices: a whole 2x2x4 slice. The times are simulated.
32 devices in a mesh: src: 8 (over z, y), tgt: 4 (over x, core).
Axes of the slice: x: 2, y: 2, z: 4, core: 2. Of those that a mesh axis runs over, the one named last changes fastest.
Arguments:
- edge_state: bfloat16 [8, 4, 1024, 512], P('src', 'tgt'), may hold values from -6 to 6
- edge_source: int32 [8, 4, 1024], P('src', 'tgt'), may hold values from 0 to 255
- edge_target: int32 [8, 4, 1024], P('src', 'tgt'), may hold values from 0 to 511
- live_edges: int32 [8, 4], P('src', 'tgt'), may hold values from 64 to 1024, as said below
- inner_one: bfloat16 [512, 512], replicated, may hold values from -0.25 to 0.25
- outer_one: bfloat16 [512, 512], replicated, may hold values from -0.25 to 0.25
- inner_two: bfloat16 [512, 512], replicated, may hold values from -0.25 to 0.25
- outer_two: bfloat16 [512, 512], replicated, may hold values from -0.25 to 0.25
- gain_one: float32 [512], replicated, may hold values from 0.1 to 1.9
- gain_two: float32 [512], replicated, may hold values from 0.1 to 1.9
Outputs:
- final_state: bfloat16 [8, 4, 1024, 512], P('src', 'tgt')
Inputs may be any that keep to these rules, and one draw needn't show every extreme that they name: `edge_source`: source atoms within a block. `edge_target`: target atoms within a block. `live_edges`: a multiple of 64; some block pair is full in every draw.
All inputs are finite; a program needn't handle non-finite values.
Results may differ from a plain program's by a relative error of at most 0.013.
Values sent between devices are 32-bit elements; how exact they have to be, the bound alone decides.
No kernel may reach another device: no remote copies, remote signals or barrier semaphores. Data moves between devices by JAX's collectives and lax.ppermute only.
A program may use at most 64 MiB of HBM per device.

v0:
```python
import jax
import jax.numpy as jnp
from jax import lax
from jax.sharding import PartitionSpec as P

ATOM_DEV = 64


def update_edges(message, inner, outer, gain):
    mean_square = jnp.mean(message * message, axis=-1, keepdims=True)
    normed = message * lax.rsqrt(mean_square + 1e-05) * gain
    normed_low = normed.astype(jnp.bfloat16)
    activated = jax.nn.relu(jnp.dot(normed_low, inner, preferred_element_type=jnp.float32)).astype(
        jnp.bfloat16
    )
    return normed + jnp.dot(activated, outer, preferred_element_type=jnp.float32)


def apply_layer(message, alive, inner, outer, gain):
    result = update_edges(message, inner, outer, gain)
    return jnp.where(alive[:, None], result, jnp.float32(0.0)).astype(jnp.bfloat16)


def target_totals(partial_value):
    return lax.psum(partial_value, "src")


def source_totals(partial_value):
    return lax.psum(partial_value, "tgt")


def body(
    edge_state,
    edge_source,
    edge_target,
    live_edges,
    inner_one,
    outer_one,
    inner_two,
    outer_two,
    gain_one,
    gain_two,
):
    edge_rows = edge_state.shape[2]
    channels = edge_state.shape[3]
    states = edge_state.reshape(edge_rows, channels)
    sources = edge_source.reshape(edge_rows)
    targets = edge_target.reshape(edge_rows)
    live_count = live_edges.reshape(())
    alive = lax.iota(jnp.int32, edge_rows) < live_count
    target_group = ATOM_DEV * lax.axis_size("src")
    source_group = ATOM_DEV * lax.axis_size("tgt")
    partial_value = jax.ops.segment_sum(
        jnp.where(alive[:, None], states.astype(jnp.float32), jnp.float32(0.0)),
        targets,
        num_segments=target_group,
    )
    incoming = target_totals(partial_value)
    message = jnp.take(incoming, targets, axis=0) - states.astype(jnp.float32)
    reverse_state = apply_layer(message, alive, inner_one, outer_one, gain_one)
    reverse_wide = reverse_state.astype(jnp.float32)
    partial_two = jax.ops.segment_sum(reverse_wide, sources, num_segments=source_group)
    outgoing = source_totals(partial_two)
    message_two = jnp.take(outgoing, sources, axis=0) - reverse_wide
    final_state = apply_layer(message_two, alive, inner_two, outer_two, gain_two)
    return final_state.reshape(1, 1, edge_rows, channels)


def solution(mesh):
    placed = (
        P("src", "tgt", None, None),
        P("src", "tgt", None),
        P("src", "tgt", None),
        P("src", "tgt"),
        P(),
        P(),
        P(),
        P(),
        P(),
        P(),
    )
    return jax.shard_map(
        body, mesh=mesh, in_specs=placed, out_specs=P("src", "tgt", None, None), check_vma=False
    )
```

profile of v0, /device:TPU:0, one launch (start us, length us, event | category | flops | bytes accessed | tf_op | source)
XLA Modules:
  0.0 185.1 jit_solution(14529367584375206832)
XLA Ops:
  6.5 0.0 copy-start
  6.5 0.0 all-reduce.3.cloned.1.call-start
  6.5 1.5 copy.16
  8.7 1.6 convert_select_fusion
  10.4 0.0 copy-start.2
  10.4 2.9 %copy.17 = f32[1024,512]{1,0:T(8,128)} copy(f32[1024,512]{0,1:T(8,128)} %convert_select_fusion) | data formatting | bytes 4194304 | tf_op jit(solution)/shard_map/jit(_where)/select_n | solution.py:54
  13.3 0.0 copy-start.3
  13.3 0.0 copy-done.2
  13.3 8.2 %scatter_custom_fusion = f32[512,512]{1,0:T(8,128)} fusion(s32[1024]{0:T(1024)S(1)} %bitcast.25, f32[1024,512]{1,0:T(8,128)} %copy.17, f32[]{:T(128)} %constant.37.clone.1), kind=kCustom, calls=%fused_computation.28 | custom fusion | flops 524288 | bytes 1049088 | tf_op jit(solution)/shard_map/scatter-add | solution.py:53
  21.5 0.0 all-reduce.3.cloned.1.call-update
  21.5 0.0 all-reduce.5.cloned.1.call-start
  21.6 0.0 copy-done.3
  21.7 80.7 %all-reduce.3.cloned.1.call-done = f32[512,512]{1,0:T(8,128)} async-done(((f32[512,512]{1,0:T(8,128)}), f32[512,512]{1,0:T(8,128)}) %all-reduce.3.cloned.1.call-update) | async-done | bytes 1048592 | tf_op jit(solution)/shard_map/psum | solution.py:25
  102.4 6.5 %gather_fusion = f32[1024,512]{1,0:T(8,128)} fusion(f32[512,512]{1,0:T(8,128)} %all-reduce.3.cloned.1.call-done, s32[1024]{0:T(1024)S(1)} %broadcast_clamp_fusion.1), kind=kCustom, calls=%fused_computation | custom fusion | bytes 4198400 | tf_op jit(solution)/shard_map/jit(_take)/gather | solution.py:59
  108.9 2.9 %copy.18 = f32[1024,512]{0,1:T(8,128)} copy(f32[1024,512]{1,0:T(8,128)} %gather_fusion) | data formatting | bytes 4194304 | tf_op jit(solution)/shard_map/jit(_take)/gather | solution.py:59
  111.8 0.0 copy-start.4
  111.8 0.0 copy-start.6
  111.8 2.0 %multiply_reduce_fusion.1 = f32[1024]{0:T(1024)S(1)} fusion(f32[1024,512]{0,1:T(8,128)} %copy.18, bf16[1,1,1024,512]{2,3,1,0:T(8,128)(2,1)S(1)} %copy.16, pred[1024]{0:T(1024)(128)(4,1)S(1)} %compare_and_fusion), kind=kLoop, calls=%fused_computation.14 | loop fusion | flops 2620416 | bytes 3150848 | tf_op jit(solution)/shard_map/reduce_sum | solution.py:10
  113.8 0.0 copy-done
  113.9 0.0 copy-done.4
  113.9 0.0 copy-done.6
  113.9 5.2 %fusion.2 = f32[1024,512]{0,1:T(8,128)} fusion(bf16[512,512]{1,0:T(8,128)(2,1)S(1)} %copy-done, bf16[512,512]{1,0:T(8,128)(2,1)S(1)} %copy-done.4, f32[1024,512]{0,1:T(8,128)} %copy.18, bf16[1,1,1024,512]{2,3,1,0:T(8,128)(2,1)S(1)} %copy.16, f32[512]{0:T(512)S(1)} %copy-done.6, f32[1024]{0:T(1024)S(1)} %add_rsqrt_fusion.1, ...), kind=kOutput, calls=%fused_computation.17 | convolution fusion | flops 1082654720 | bytes 6299648 | tf_op jit(solution)/shard_map/dot_general | solution.py:16
  119.0 1.9 %copy.19 = f32[1024,512]{1,0:T(8,128)S(1)} copy(f32[1024,512]{0,1:T(8,128)} %fusion.2) | data formatting | bytes 4194304 | tf_op jit(solution)/shard_map/convert_element_type | solution.py:61
  121.0 7.4 %scatter_custom_fusion.1 = f32[256,512]{1,0:T(8,128)} fusion(s32[1024]{0:T(1024)S(1)} %bitcast.27, f32[1024,512]{1,0:T(8,128)S(1)} %copy.19, f32[]{:T(128)} %constant.37.clone.1), kind=kCustom, calls=%fused_computation.30 | custom fusion | flops 524288 | bytes 524292 | tf_op jit(solution)/shard_map/scatter-add | solution.py:62
  128.3 0.0 all-reduce.5.cloned.1.call-update
  128.4 32.9 %all-reduce.5.cloned.1.call-done = f32[256,512]{1,0:T(8,128)} async-done(((f32[256,512]{1,0:T(8,128)}), f32[256,512]{1,0:T(8,128)}) %all-reduce.5.cloned.1.call-update) | async-done | bytes 524304 | tf_op jit(solution)/shard_map/psum | solution.py:29
  161.3 5.1 %gather_fusion.1 = f32[1024,512]{1,0:T(8,128)S(1)} fusion(f32[256,512]{1,0:T(8,128)} %all-reduce.5.cloned.1.call-done, s32[1024]{0:T(1024)S(1)} %broadcast_clamp_fusion), kind=kCustom, calls=%fused_computation.1 | custom fusion | bytes 4198400 | tf_op jit(solution)/shard_map/jit(_take)/gather | solution.py:64
  166.3 1.8 copy.20
  168.2 0.0 copy-start.1
  168.2 0.0 copy-start.5
  168.2 0.0 copy-start.7
  168.2 2.7 %multiply_reduce_fusion = f32[1024]{0:T(1024)S(1)} fusion(f32[1024,512]{0,1:T(8,128)} %fusion.2, f32[1024,512]{0,1:T(8,128)} %copy.20, pred[1024]{0:T(1024)(128)(4,1)S(1)} %compare_and_fusion.1), kind=kLoop, calls=%fused_computation.9 | loop fusion | flops 2096128 | bytes 4199424 | tf_op jit(solution)/shard_map/reduce_sum | solution.py:10
  170.9 0.1 copy-done.1
  171.0 0.1 copy-done.5
  171.1 0.0 copy-done.7
  171.1 4.9 %fusion.3 = bf16[1,1,1024,512]{2,3,1,0:T(8,128)(2,1)} fusion(bf16[512,512]{1,0:T(8,128)(2,1)S(1)} %copy-done.5, bf16[512,512]{1,0:T(8,128)(2,1)} %param.16, f32[512]{0:T(512)S(1)} %copy-done.7, f32[1024]{0:T(1024)S(1)} %add_rsqrt_fusion, pred[1024]{0:T(1024)(128)(4,1)S(1)} %iota_compare_fusion, f32[1024,512]{0,1:T(8,128)S(1)} %copy-done.1, ...), kind=kOutput, calls=%fused_computation.18 | convolution fusion | flops 1081081856 | bytes 6299648 | tf_op jit(solution)/shard_map/dot_general | solution.py:16
  176.0 2.3 %copy.22 = bf16[1,1,1024,512]{3,2,1,0:T(8,128)(2,1)} copy(bf16[1,1,1024,512]{2,3,1,0:T(8,128)(2,1)} %fusion.3) | data formatting | bytes 2097152 | tf_op jit(solution)/shard_map/reshape | solution.py:66
  (9 shorter events, 0.1 us)
Async XLA Ops:
  6.5 107.3 %copy-start = (bf16[512,512]{1,0:T(8,128)(2,1)S(1)}, bf16[512,512]{1,0:T(8,128)(2,1)}, u32[]{:S(2)}) copy-start(bf16[512,512]{1,0:T(8,128)(2,1)} %param.15) | copy-start | bytes 1572868
  6.5 95.9 %all-reduce.3.cloned.1.call-start = ((), (), s32[]{:S(2)}) async-start(), calls=%async_computation | async-start | bytes 2097152 | tf_op jit(solution)/shard_map/psum | solution.py:25
  10.4 2.9 %copy-start.2 = (s32[1,1,1024]{2,1,0:T(1,128)S(1)}, s32[1,1,1024]{2,1,0:T(1,128)}, u32[]{:S(2)}) copy-start(s32[1,1,1024]{2,1,0:T(1,128)} %param.12) | copy-start | bytes 12292
  13.3 8.4 %copy-start.3 = (s32[1,1,1024]{2,1,0:T(1,128)S(1)}, s32[1,1,1024]{2,1,0:T(1,128)}, u32[]{:S(2)}) copy-start(s32[1,1,1024]{2,1,0:T(1,128)} %param.11) | copy-start | bytes 12292
  21.5 139.7 %all-reduce.5.cloned.1.call-start = ((), (), s32[]{:S(2)}) async-start(), calls=%async_computation.1 | async-start | bytes 1048576 | tf_op jit(solution)/shard_map/psum | solution.py:29
  111.8 2.1 %copy-start.4 = (bf16[512,512]{1,0:T(8,128)(2,1)S(1)}, bf16[512,512]{1,0:T(8,128)(2,1)}, u32[]{:S(2)}) copy-start(bf16[512,512]{1,0:T(8,128)(2,1)} %param.14) | copy-start | bytes 1572868
  111.8 2.1 %copy-start.6 = (f32[512]{0:T(512)S(1)}, f32[512]{0:T(512)}, u32[]{:S(2)}) copy-start(f32[512]{0:T(512)} %param.18) | copy-start | bytes 6148
  168.2 2.9 %copy-start.1 = (f32[1024,512]{0,1:T(8,128)S(1)}, f32[1024,512]{0,1:T(8,128)}, u32[]{:S(2)}) copy-start(f32[1024,512]{0,1:T(8,128)} %fusion.2) | copy-start | bytes 6291460
  168.2 2.9 %copy-start.5 = (bf16[512,512]{1,0:T(8,128)(2,1)S(1)}, bf16[512,512]{1,0:T(8,128)(2,1)}, u32[]{:S(2)}) copy-start(bf16[512,512]{1,0:T(8,128)(2,1)} %param.17) | copy-start | bytes 1572868
  168.2 2.9 %copy-start.7 = (f32[512]{0:T(512)S(1)}, f32[512]{0:T(512)}, u32[]{:S(2)}) copy-start(f32[512]{0:T(512)} %param.19) | copy-start | bytes 6148
Sparse Core Ops, SparseCore 0:
  21.7 80.6 all-reduce.2
  128.5 32.7 all-reduce.4
where the time goes:
time: 185 us
  waiting for transfers between devices  114 us (62%)
  local copies, waits for them, and re-layouts  25.1 us (14%)
  other arithmetic  22 us (12%)
  between operations  14.2 us (8%)
  matrix products  10.1 us (5%)
    psum x1, waiting for transfers between devices, target_totals(): return lax.psum(partial_value, 'src')  80.7 us
    psum x1, waiting for transfers between devices, source_totals(): return lax.psum(partial_value, 'tgt')  32.9 us
    dot_general x2, matrix products, update_edges(): jnp.dot(activated, outer, preferred_element_type=jnp.float32)  10.1 us
    gather x2, local copies, waits for them, and re-layouts, body(): message = jnp.take(incoming, targets, axis=0) - states.astype(jnp.float32)  9.4 us
    scatter-add x1, other arithmetic, body(): jax.ops.segment_sum(jnp.where(alive[:, None], states.astype(jnp.float32),...  8.24 us
    scatter-add x1, other arithmetic, body(): jax.ops.segment_sum(reverse_wide, sources, num_segments=source_group)  7.36 us
    gather x2, local copies, waits for them, and re-layouts, body(): message_two = jnp.take(outgoing, sources, axis=0) - reverse_wide  6.88 us
    reduce_sum x2, other arithmetic, update_edges(): mean_square = jnp.mean(message * message, axis=-1, keepdims=True)  4.76 us
  transfers between devices with their start and end apart: 2, of which 2 were waited for; matrix products, arithmetic and copies ran while one was open for 0% of the time, Pallas kernels for 0%

commit v1 on v0

v1 whole, which is shorter than its diff:
```python
import functools

import jax
import jax.numpy as jnp
from jax import lax
from jax.experimental import pallas as pl
from jax.experimental.pallas import tpu as pltpu
from jax.sharding import PartitionSpec as P

ATOM_DEV = 64
GROUP = 4
WAVES = 2
ROW_BLOCK = 256
VMEM_LIMIT = 40 * 1024 * 1024

VMEM = pl.BlockSpec(memory_space=pltpu.VMEM)
SMEM = pl.BlockSpec(memory_space=pltpu.SMEM)


def call(kernel, out_shape, n_smem, n_vmem, flops, bytes_accessed, scratch=()):
    return pl.pallas_call(
        kernel,
        out_shape=out_shape,
        in_specs=[SMEM] * n_smem + [VMEM] * n_vmem,
        out_specs=jax.tree.map(lambda _: VMEM, out_shape),
        scratch_shapes=list(scratch),
        compiler_params=pltpu.CompilerParams(vmem_limit_bytes=VMEM_LIMIT),
        cost_estimate=pl.CostEstimate(flops=flops, bytes_accessed=bytes_accessed, transcendentals=0),
    )


def target_sum_kernel(first, flip_ref, live_ref, target_ref, state_ref, *chunk_refs):
    rows = target_ref.shape[1]
    size = chunk_refs[0].shape[0]
    count = size * len(chunk_refs)
    place = jnp.bitwise_xor(target_ref[...], flip_ref[0])
    place = jnp.where(lax.broadcasted_iota(jnp.int32, (1, rows), 1) < live_ref[0], place, -1)
    slot = lax.broadcasted_iota(jnp.int32, (count, rows), 0) + first
    chosen = jnp.where(place == slot, jnp.float32(1.0), jnp.float32(0.0)).astype(jnp.bfloat16)
    for index, chunk_ref in enumerate(chunk_refs):
        chunk_ref[...] = jnp.dot(
            chosen[index * size : (index + 1) * size], state_ref[...], preferred_element_type=jnp.float32
        )


def target_sums(states, targets, flip, live, wave, size):
    rows, channels = states.shape
    out = [jax.ShapeDtypeStruct((size, channels), jnp.float32)] * GROUP
    return call(
        functools.partial(target_sum_kernel, wave * size * GROUP),
        out, 2, 2,
        2 * size * GROUP * rows * channels, 2 * rows * channels + 4 * size * GROUP * channels,
    )(flip, live, targets, states)


def split_sums(sum_refs, parts_ref):
    total = parts_ref.shape[0] // 3
    at = 0
    for sum_ref in sum_refs:
        size = sum_ref.shape[0]
        value = sum_ref[...]
        for part in range(3):
            low = value.astype(jnp.bfloat16)
            parts_ref[part * total + at : part * total + at + size, :] = low
            value = value - low.astype(jnp.float32)
        at += size


def update_block(chosen, parts_ref, state, live, first_row, inner_ref, outer_ref, gain_ref):
    gathered = jnp.dot(
        jnp.concatenate([chosen, chosen, chosen], axis=1), parts_ref[...], preferred_element_type=jnp.float32
    )
    message = gathered - state.astype(jnp.float32)
    mean_square = jnp.mean(message * message, axis=-1, keepdims=True)
    normed = message * lax.rsqrt(mean_square + 1e-05) * gain_ref[...]
    activated = jax.nn.relu(
        jnp.dot(normed.astype(jnp.bfloat16), inner_ref[...], preferred_element_type=jnp.float32)
    ).astype(jnp.bfloat16)
    result = normed + jnp.dot(activated, outer_ref[...], preferred_element_type=jnp.float32)
    row = lax.broadcasted_iota(jnp.int32, (state.shape[0], 1), 0) + first_row
    return jnp.where(row < live, result, jnp.float32(0.0)).astype(jnp.bfloat16)


def layer_one_kernel(n_sums, live_ref, *refs):
    sum_refs = refs[:n_sums]
    chosen_ref, source_ref, state_ref, inner_ref, outer_ref, gain_ref, reverse_ref, own_ref, other_ref, parts_ref = refs[n_sums:]
    split_sums(sum_refs, parts_ref)
    rows = state_ref.shape[0]
    half = own_ref.shape[0]
    live = live_ref[0]
    total = None
    for first_row in range(0, rows, ROW_BLOCK):
        block = slice(first_row, first_row + ROW_BLOCK)
        low = update_block(
            chosen_ref[block, :], parts_ref, state_ref[block, :], live, first_row, inner_ref, outer_ref, gain_ref
        )
        reverse_ref[block, :] = low
        term = jnp.dot(source_ref[:, block], low, preferred_element_type=jnp.float32)
        total = term if total is None else total + term
    own_ref[...] = total[:half]
    other_ref[...] = total[half:]


def layer_two_kernel(live_ref, own_ref, other_ref, chosen_ref, state_ref, inner_ref, outer_ref, gain_ref, final_ref, parts_ref):
    split_sums((own_ref, other_ref), parts_ref)
    rows = state_ref.shape[0]
    live = live_ref[0]
    for first_row in range(0, rows, ROW_BLOCK):
        block = slice(first_row, first_row + ROW_BLOCK)
        final_ref[block, :] = update_block(
            chosen_ref[block, :], parts_ref, state_ref[block, :], live, first_row, inner_ref, outer_ref, gain_ref
        )


def swap(value, axis, mask):
    return lax.ppermute(value, axis, [(i, i ^ mask) for i in range(lax.axis_size(axis))])


def higher_masks(axis, low):
    masks = []
    while low < lax.axis_size(axis):
        masks.append(low)
        low *= 2
    return masks


def spread(total, axis):
    return [total] + [swap(total, axis, mask) for mask in range(1, GROUP)]


def target_totals(waves):
    received = [[swap(chunks[mask], "src", mask) for mask in range(1, GROUP)] for chunks in waves]
    sums = []
    for chunks, parts in zip(waves, received):
        if sums:
            parts, _ = lax.optimization_barrier((parts, sums[-1]))
        sums.append(chunks[0] + parts[0] + parts[1] + parts[2])
    for mask in higher_masks("src", GROUP):
        sums = [value + swap(value, "src", mask) for value in sums]
    return [chunk for value in sums for chunk in spread(value, "src")]


def source_totals(own, other):
    own = own + swap(other, "tgt", 1)
    for mask in higher_masks("tgt", 2):
        own = own + swap(own, "tgt", mask)
    return own, swap(own, "tgt", 1)


def body(
    edge_state,
    edge_source,
    edge_target,
    live_edges,
    inner_one,
    outer_one,
    inner_two,
    outer_two,
    gain_one,
    gain_two,
):
    rows, channels = edge_state.shape[2:]
    states = edge_state.reshape(rows, channels)
    sources = edge_source.reshape(1, rows)
    targets = edge_target.reshape(1, rows)
    live = live_edges.reshape(1)
    target_atoms = ATOM_DEV * lax.axis_size("src")
    source_atoms = ATOM_DEV * lax.axis_size("tgt")
    size = target_atoms // (GROUP * WAVES)
    half = source_atoms // 2
    target_flip = lax.bitwise_and(lax.axis_index("src"), GROUP - 1) * size
    source_flip = lax.bitwise_and(lax.axis_index("tgt"), 1) * half

    waves = [target_sums(states, targets, target_flip.reshape(1), live, wave, size) for wave in range(WAVES)]

    def chosen(values, flip, count):
        place = jnp.bitwise_xor(values.reshape(rows, 1), flip)
        return (place == lax.broadcasted_iota(jnp.int32, (rows, count), 1)).astype(jnp.bfloat16)

    target_chosen = chosen(targets, target_flip, target_atoms)
    source_chosen = chosen(sources, source_flip, source_atoms)
    source_place = jnp.bitwise_xor(sources, source_flip)
    source_pick = (source_place == lax.broadcasted_iota(jnp.int32, (source_atoms, rows), 0)).astype(jnp.bfloat16)

    totals = target_totals(waves)
    reverse_state, own, other = call(
        functools.partial(layer_one_kernel, len(totals)),
        [
            jax.ShapeDtypeStruct((rows, channels), jnp.bfloat16),
            jax.ShapeDtypeStruct((half, channels), jnp.float32),
            jax.ShapeDtypeStruct((half, channels), jnp.float32),
        ],
        1, len(totals) + 6,
        2 * rows * channels * (3 * target_atoms + 2 * channels + source_atoms), 8 * rows * channels,
        [pltpu.VMEM((3 * target_atoms, channels), jnp.bfloat16)],
    )(live, *totals, target_chosen, source_pick, states, inner_one, outer_one, gain_one.reshape(1, channels))
    own, other = source_totals(own, other)
    final_state = call(
        layer_two_kernel,
        jax.ShapeDtypeStruct((rows, channels), jnp.bfloat16),
        1, 7,
        2 * rows * channels * (3 * source_atoms + 2 * channels), 8 * rows * channels,
        [pltpu.VMEM((3 * source_atoms, channels), jnp.bfloat16)],
    )(live, own, other, source_chosen, reverse_state, inner_two, outer_two, gain_two.reshape(1, channels))
    return final_state.reshape(1, 1, rows, channels)


def solution(mesh):
    placed = (
        P("src", "tgt", None, None),
        P("src", "tgt", None),
        P("src", "tgt", None),
        P("src", "tgt"),
        P(),
        P(),
        P(),
        P(),
        P(),
        P(),
    )
    return jax.shard_map(
        body, mesh=mesh, in_specs=placed, out_specs=P("src", "tgt", None, None), check_vma=False
    )
```

time: 185 us -> 66.1 us (0.36)
  waiting for transfers between devices: 114 us -> 33.3 us
  local copies, waits for them, and re-layouts: 25.1 us -> 1.94 us
  other arithmetic: 22 us -> 0.74 us
  starting transfers between devices: 0.04 us -> 18.7 us
  between operations: 14.2 us -> 0.8 us
  Pallas kernels: 0 us -> 10.3 us
  matrix products: 10.1 us -> 0 us
    psum x2 -> x0, waiting for transfers between devices: 114 us -> none  [the longest x1 80.7 us: target_totals(): return lax.psum(partial_value, 'src')]
    ppermute x0 -> x17, waiting for transfers between devices: none -> 33.3 us  [swap(): lax.ppermute(value, axis, [(i, i ^ mask) for i in range(lax.axis_size(axi...]
    ppermute x0 -> x17, starting transfers between devices: none -> 18.7 us  [swap(): lax.ppermute(value, axis, [(i, i ^ mask) for i in range(lax.axis_size(axi...]
    gather x4 -> x0, local copies, waits for them, and re-layouts: 16.3 us -> none  [the longest x2 9.4 us: body(): message = jnp.take(incoming, targets, axis=0) - states.astype(jnp.float32)]
    scatter-add x2 -> x0, other arithmetic: 15.6 us -> none  [the longest x1 8.24 us: body(): jax.ops.segment_sum(jnp.where(alive[:, None], states.astype(jnp.float32),...]
    pallas_call x0 -> x4, Pallas kernels: none -> 10.3 us  [the longest x1 4.59 us: body(): call(functools.partial(layer_one_kernel, len(totals)), [jax.ShapeDtypeStr...]
    dot_general x2 -> x0, matrix products: 10.1 us -> none  [update_edges(): jnp.dot(activated, outer, preferred_element_type=jnp.float32)]
    reduce_sum x2 -> x0, other arithmetic: 4.76 us -> none  [update_edges(): mean_square = jnp.mean(message * message, axis=-1, keepdims=True)]
  transfers between devices with their start and end apart: 2 -> 17, of which waited for: 2 -> 13; matrix products, arithmetic and copies ran while one was open for 0% -> 1% of each run, Pallas kernels for 0% -> 1%
where the time goes in v1:
time: 66.1 us; the launch traced here: 65.9 us
  waiting for transfers between devices  33.3 us (50%)
  starting transfers between devices  18.7 us (28%)
  Pallas kernels  10.3 us (16%)
  local copies, waits for them, and re-layouts  1.94 us (3%)
  between operations  0.8 us (1%)
  other arithmetic  0.74 us (1%)
    ppermute x17, waiting for transfers between devices, swap(): lax.ppermute(value, axis, [(i, i ^ mask) for i in range(lax.axis_size(axi...  33.3 us
    ppermute x17, starting transfers between devices, swap(): lax.ppermute(value, axis, [(i, i ^ mask) for i in range(lax.axis_size(axi...  18.7 us
    pallas_call x1, Pallas kernels, body(): call(functools.partial(layer_one_kernel, len(totals)), [jax.ShapeDtypeStr...  4.59 us
    pallas_call x1, Pallas kernels, body(): call(layer_two_kernel, jax.ShapeDtypeStruct((rows, channels), jnp.bfloat1...  4.1 us
    unnamed x22, local copies, waits for them, and re-layouts  1.94 us
    pallas_call x2, Pallas kernels, target_sums(): call(functools.partial(target_sum_kernel, wave * size * GROUP), out, 2, 2...  1.65 us
  transfers between devices with their start and end apart: 17, of which 13 were waited for; matrix products, arithmetic and copies ran while one was open for 1% of the time, Pallas kernels for 1%

profile of v1, /device:TPU:0, one launch (start us, length us, event | category | flops | bytes accessed | tf_op | source)
XLA Modules:
  0.0 65.9 jit_solution(2253079769884888491)
XLA Ops:
  0.7 0.0 copy-start
  0.7 1.2 %copy-done = bf16[1,1,1024,512]{3,2,1,0:T(8,128)(2,1)S(1)} copy-done((bf16[1,1,1024,512]{3,2,1,0:T(8,128)(2,1)S(1)}, bf16[1,1,1024,512]{3,2,1,0:T(8,128)(2,1)}, u32[]{:S(2)}) %copy-start) | copy-done | bytes 1048600
  1.9 0.7 %copy-done.2 = s32[1,1,1024]{2,1,0:T(1,128)S(1)} copy-done((s32[1,1,1024]{2,1,0:T(1,128)S(1)}, s32[1,1,1024]{2,1,0:T(1,128)}, u32[]{:S(2)}) %copy-start.2) | copy-done | bytes 4120
  2.6 0.8 %shard_map.100 = (f32[64,512]{1,0:T(8,128)S(1)}, f32[64,512]{1,0:T(8,128)S(1)}, f32[64,512]{1,0:T(8,128)S(1)}, f32[64,512]{1,0:T(8,128)S(1)}) custom-call(s32[1]{0:T(128)} %bitcast.1.flip_ref, s32[1]{0:T(128)} %bitcast.9.live_ref, s32[1,1024]{1,0:T(1,128)S(1)} %bitcast.16, bf16[1024,512]{1,0:T(8,128)(2,1)S(1)} %bitcast.13), custom_call_target="tpu_custom_call" | custom-call | flops 268435456 | bytes 1572864 | tf_op jit(solution)/shard_map/pallas_call | solution.py:49
  3.4 3.0 %collective-permute-start = (f32[64,512]{1,0:T(8,128)S(1)}, f32[64,512]{1,0:T(8,128)S(1)}, u32[]{:S(2)}, u32[]{:S(2)}) collective-permute-start(f32[64,512]{1,0:T(8,128)S(1)} %get-tuple-element.20), channel_id=1, source_target_pairs={{0,4},{4,0},{8,12},{12,8},{16,20},{20,16},{24,28},{28,24},{1,5},{5... | collective-permute-start | bytes 393224 | tf_op jit(solution)/shard_map/ppermute | solution.py:116
  6.4 1.6 %collective-permute-start.1 = (f32[64,512]{1,0:T(8,128)S(1)}, f32[64,512]{1,0:T(8,128)S(1)}, u32[]{:S(2)}, u32[]{:S(2)}) collective-permute-start(f32[64,512]{1,0:T(8,128)S(1)} %get-tuple-element.21), channel_id=1, source_target_pairs={{0,8},{4,12},{8,0},{12,4},{16,24},{20,28},{24,16},{28,20},{1,9},{5... | collective-permute-start | bytes 393224 | tf_op jit(solution)/shard_map/ppermute | solution.py:116
  8.0 0.0 collective-permute-start.2
  8.0 0.8 %shard_map.101 = (f32[64,512]{1,0:T(8,128)S(1)}, f32[64,512]{1,0:T(8,128)S(1)}, f32[64,512]{1,0:T(8,128)S(1)}, f32[64,512]{1,0:T(8,128)S(1)}) custom-call(s32[1]{0:T(128)} %bitcast.1.flip_ref, s32[1]{0:T(128)} %bitcast.10.live_ref, s32[1,1024]{1,0:T(1,128)S(1)} %bitcast.17, bf16[1024,512]{1,0:T(8,128)(2,1)S(1)} %bitcast.14), custom_call_target="tpu_custom_call" | custom-call | flops 268435456 | bytes 1572864 | tf_op jit(solution)/shard_map/pallas_call | solution.py:49
  8.9 2.0 %collective-permute-start.7 = (f32[64,512]{1,0:T(8,128)S(1)}, f32[64,512]{1,0:T(8,128)S(1)}, u32[]{:S(2)}, u32[]{:S(2)}) collective-permute-start(f32[64,512]{1,0:T(8,128)S(1)} %get-tuple-element.24), channel_id=1, source_target_pairs={{0,4},{4,0},{8,12},{12,8},{16,20},{20,16},{24,28},{28,24},{1,5},{5... | collective-permute-start | bytes 393224 | tf_op jit(solution)/shard_map/ppermute | solution.py:116
  10.8 1.6 %collective-permute-start.8 = (f32[64,512]{1,0:T(8,128)S(1)}, f32[64,512]{1,0:T(8,128)S(1)}, u32[]{:S(2)}, u32[]{:S(2)}) collective-permute-start(f32[64,512]{1,0:T(8,128)S(1)} %get-tuple-element.25), channel_id=1, source_target_pairs={{0,8},{4,12},{8,0},{12,4},{16,24},{20,28},{24,16},{28,20},{1,9},{5... | collective-permute-start | bytes 393224 | tf_op jit(solution)/shard_map/ppermute | solution.py:116
  12.4 0.0 copy-done.3
  12.4 0.0 collective-permute-done
  12.4 0.6 collective-permute-start.9
  13.0 0.0 collective-permute-done.1
  13.0 2.4 %collective-permute-done.2 = f32[64,512]{1,0:T(8,128)S(1)} collective-permute-done((f32[64,512]{1,0:T(8,128)S(1)}, f32[64,512]{1,0:T(8,128)S(1)}, u32[]{:S(2)}, u32[]{:S(2)}) %collective-permute-start.2) | collective-permute-done | bytes 131104 | tf_op jit(solution)/shard_map/ppermute | solution.py:116
  15.4 1.9 %collective-permute-done.7 = f32[64,512]{1,0:T(8,128)S(1)} collective-permute-done((f32[64,512]{1,0:T(8,128)S(1)}, f32[64,512]{1,0:T(8,128)S(1)}, u32[]{:S(2)}, u32[]{:S(2)}) %collective-permute-start.7) | collective-permute-done | bytes 131104 | tf_op jit(solution)/shard_map/ppermute | solution.py:116
  17.3 1.1 %collective-permute-done.8 = f32[64,512]{1,0:T(8,128)S(1)} collective-permute-done((f32[64,512]{1,0:T(8,128)S(1)}, f32[64,512]{1,0:T(8,128)S(1)}, u32[]{:S(2)}, u32[]{:S(2)}) %collective-permute-start.8) | collective-permute-done | bytes 131104 | tf_op jit(solution)/shard_map/ppermute | solution.py:116
  18.4 1.2 %collective-permute-done.9 = f32[64,512]{1,0:T(8,128)S(1)} collective-permute-done((f32[64,512]{1,0:T(8,128)S(1)}, f32[64,512]{1,0:T(8,128)S(1)}, u32[]{:S(2)}, u32[]{:S(2)}) %collective-permute-start.9) | collective-permute-done | bytes 131104 | tf_op jit(solution)/shard_map/ppermute | solution.py:116
  19.7 2.8 %collective-permute-start.10 = (f32[64,512]{1,0:T(8,128)S(1)}, f32[64,512]{1,0:T(8,128)S(1)}, u32[]{:S(2)}, u32[]{:S(2)}) collective-permute-start(f32[64,512]{1,0:T(8,128)S(1)} %add_add_fusion), channel_id=1, source_target_pairs={{0,16},{4,20},{8,24},{12,28},{16,0},{20,4},{24,8},{28,12},{1,17},{... | collective-permute-start | bytes 393224 | tf_op jit(solution)/shard_map/ppermute | solution.py:116
  22.5 0.2 fusion.refs_8_
  22.8 0.2 collective-permute-start.3
  23.0 8.3 %collective-permute-done.10 = f32[64,512]{1,0:T(8,128)S(1)} collective-permute-done((f32[64,512]{1,0:T(8,128)S(1)}, f32[64,512]{1,0:T(8,128)S(1)}, u32[]{:S(2)}, u32[]{:S(2)}) %collective-permute-start.10) | collective-permute-done | bytes 131104 | tf_op jit(solution)/shard_map/ppermute | solution.py:116
  31.3 1.7 %collective-permute-start.11 = (f32[64,512]{1,0:T(8,128)S(1)}, f32[64,512]{1,0:T(8,128)S(1)}, u32[]{:S(2)}, u32[]{:S(2)}) collective-permute-start(f32[64,512]{1,0:T(8,128)S(1)} %add.37.refs_4_), channel_id=1, source_target_pairs={{0,4},{4,0},{8,12},{12,8},{16,20},{20,16},{24,28},{28,24},{1,5},{5... | collective-permute-start | bytes 393224 | tf_op jit(solution)/shard_map/ppermute | solution.py:116
  33.0 0.0 copy-done.10
  33.0 0.0 collective-permute-start.12
  33.0 1.9 %collective-permute-start.13 = (f32[64,512]{1,0:T(8,128)S(1)}, f32[64,512]{1,0:T(8,128)S(1)}, u32[]{:S(2)}, u32[]{:S(2)}) collective-permute-start(f32[64,512]{1,0:T(8,128)S(1)} %add.37.refs_4_), channel_id=1, source_target_pairs={{0,12},{4,8},{8,4},{12,0},{16,28},{20,24},{24,20},{28,16},{1,13},{... | collective-permute-start | bytes 393224 | tf_op jit(solution)/shard_map/ppermute | solution.py:116
  34.9 0.0 collective-permute-done.3
  34.9 1.7 %collective-permute-start.4 = (f32[64,512]{1,0:T(8,128)S(1)}, f32[64,512]{1,0:T(8,128)S(1)}, u32[]{:S(2)}, u32[]{:S(2)}) collective-permute-start(f32[64,512]{1,0:T(8,128)S(1)} %add.33.refs_0_), channel_id=1, source_target_pairs={{0,4},{4,0},{8,12},{12,8},{16,20},{20,16},{24,28},{28,24},{1,5},{5... | collective-permute-start | bytes 393224 | tf_op jit(solution)/shard_map/ppermute | solution.py:116
  36.6 0.1 collective-permute-start.5
  36.7 1.9 %collective-permute-done.11.refs_5_ = f32[64,512]{1,0:T(8,128)S(1)} collective-permute-done((f32[64,512]{1,0:T(8,128)S(1)}, f32[64,512]{1,0:T(8,128)S(1)}, u32[]{:S(2)}, u32[]{:S(2)}) %collective-permute-start.11) | collective-permute-done | bytes 131104 | tf_op jit(solution)/shard_map/ppermute | solution.py:116
  38.6 0.0 collective-permute-start.6
  38.6 0.1 fusion.1.refs_9_
  38.7 0.8 %collective-permute-done.12.refs_6_ = f32[64,512]{1,0:T(8,128)S(1)} collective-permute-done((f32[64,512]{1,0:T(8,128)S(1)}, f32[64,512]{1,0:T(8,128)S(1)}, u32[]{:S(2)}, u32[]{:S(2)}) %collective-permute-start.12) | collective-permute-done | bytes 131104 | tf_op jit(solution)/shard_map/ppermute | solution.py:116
  39.5 2.8 %collective-permute-done.13.refs_7_ = f32[64,512]{1,0:T(8,128)S(1)} collective-permute-done((f32[64,512]{1,0:T(8,128)S(1)}, f32[64,512]{1,0:T(8,128)S(1)}, u32[]{:S(2)}, u32[]{:S(2)}) %collective-permute-start.13) | collective-permute-done | bytes 131104 | tf_op jit(solution)/shard_map/ppermute | solution.py:116
  42.3 1.1 %collective-permute-done.4.refs_1_ = f32[64,512]{1,0:T(8,128)S(1)} collective-permute-done((f32[64,512]{1,0:T(8,128)S(1)}, f32[64,512]{1,0:T(8,128)S(1)}, u32[]{:S(2)}, u32[]{:S(2)}) %collective-permute-start.4) | collective-permute-done | bytes 131104 | tf_op jit(solution)/shard_map/ppermute | solution.py:116
  43.4 0.0 collective-permute-done.5.refs_2_
  43.4 2.0 %collective-permute-done.6.refs_3_ = f32[64,512]{1,0:T(8,128)S(1)} collective-permute-done((f32[64,512]{1,0:T(8,128)S(1)}, f32[64,512]{1,0:T(8,128)S(1)}, u32[]{:S(2)}, u32[]{:S(2)}) %collective-permute-start.6) | collective-permute-done | bytes 131104 | tf_op jit(solution)/shard_map/ppermute | solution.py:116
  45.4 0.0 copy-done.1
  45.4 0.0 copy-done.5
  45.4 4.6 %shard_map.102 = (bf16[1024,512]{1,0:T(8,128)(2,1)S(1)}, f32[128,512]{1,0:T(8,128)S(1)}, f32[128,512]{1,0:T(8,128)S(1)}) custom-call(s32[1]{0:T(128)} %bitcast.11.live_ref, f32[64,512]{1,0:T(8,128)S(1)} %add.33.refs_0_, f32[64,512]{1,0:T(8,128)S(1)} %collective-permute-done.4.refs_1_, f32[64,512]{1,0:T(8,128)S(1)} %collective-permute-done.5.refs_2_, ...), custom_call_target="tpu_custom_call" | custom-call | flops 2952790016 | bytes 4194304 | tf_op jit(solution)/shard_map/pallas_call | solution.py:186
  50.0 0.1 collective-permute-start.14
  50.1 1.5 %collective-permute-done.14 = f32[128,512]{1,0:T(8,128)S(1)} collective-permute-done((f32[128,512]{1,0:T(8,128)S(1)}, f32[128,512]{1,0:T(8,128)S(1)}, u32[]{:S(2)}, u32[]{:S(2)}) %collective-permute-start.14) | collective-permute-done | bytes 262176 | tf_op jit(solution)/shard_map/ppermute | solution.py:116
  51.7 1.5 %collective-permute-start.15 = (f32[128,512]{1,0:T(8,128)S(1)}, f32[128,512]{1,0:T(8,128)S(1)}, u32[]{:S(2)}, u32[]{:S(2)}) collective-permute-start(f32[128,512]{1,0:T(8,128)S(1)} %add.38), channel_id=1, source_target_pairs={{0,2},{1,3},{2,0},{3,1},{4,6},{5,7},{6,4},{7,5},{8,10},{9,11},{10,... | collective-permute-start | bytes 786440 | tf_op jit(solution)/shard_map/ppermute | solution.py:116
  53.2 6.9 %collective-permute-done.15 = f32[128,512]{1,0:T(8,128)S(1)} collective-permute-done((f32[128,512]{1,0:T(8,128)S(1)}, f32[128,512]{1,0:T(8,128)S(1)}, u32[]{:S(2)}, u32[]{:S(2)}) %collective-permute-start.15) | collective-permute-done | bytes 262176 | tf_op jit(solution)/shard_map/ppermute | solution.py:116
  60.1 0.1 collective-permute-start.16
  60.2 0.2 fusion.2.chosen_ref
  60.4 1.3 %collective-permute-done.16.other_ref = f32[128,512]{1,0:T(8,128)S(1)} collective-permute-done((f32[128,512]{1,0:T(8,128)S(1)}, f32[128,512]{1,0:T(8,128)S(1)}, u32[]{:S(2)}, u32[]{:S(2)}) %collective-permute-start.16) | collective-permute-done | bytes 262176 | tf_op jit(solution)/shard_map/ppermute | solution.py:116
  61.8 4.1 %shard_map.103 = bf16[1024,512]{1,0:T(8,128)(2,1)} custom-call(s32[1]{0:T(128)} %bitcast.12.live_ref, f32[128,512]{1,0:T(8,128)S(1)} %add.39.own_ref, f32[128,512]{1,0:T(8,128)S(1)} %collective-permute-done.16.other_ref, bf16[1024,256]{1,0:T(8,128)(2,1)S(1)} %fusion.2.chosen_ref, bf16[1024,512]{1,0:T(8,128)(2,1)S(1)} %get-tuple-element.32.state_ref, ...), custom_call_target="tpu_custom_call" | custom-call | flops 1879048192 | bytes 4194304 | tf_op jit(solution)/shard_map/pallas_call | solution.py:198
  (23 shorter events, 0.2 us)
Async XLA Ops:
  0.7 1.2 %copy-start = (bf16[1,1,1024,512]{3,2,1,0:T(8,128)(2,1)S(1)}, bf16[1,1,1024,512]{3,2,1,0:T(8,128)(2,1)}, u32[]{:S(2)}) copy-start(bf16[1,1,1024,512]{3,2,1,0:T(8,128)(2,1)} %param.10) | copy-start | bytes 3145732
  1.9 0.7 %copy-start.2 = (s32[1,1,1024]{2,1,0:T(1,128)S(1)}, s32[1,1,1024]{2,1,0:T(1,128)}, u32[]{:S(2)}) copy-start(s32[1,1,1024]{2,1,0:T(1,128)} %param.12) | copy-start | bytes 12292
  2.6 9.8 %copy-start.3 = (s32[1,1,1024]{2,1,0:T(1,128)S(1)}, s32[1,1,1024]{2,1,0:T(1,128)}, u32[]{:S(2)}) copy-start(s32[1,1,1024]{2,1,0:T(1,128)} %param.12) | copy-start | bytes 12292
  3.4 9.0 %collective-permute-start = (f32[64,512]{1,0:T(8,128)S(1)}, f32[64,512]{1,0:T(8,128)S(1)}, u32[]{:S(2)}, u32[]{:S(2)}) collective-permute-start(f32[64,512]{1,0:T(8,128)S(1)} %get-tuple-element.20), channel_id=1, source_target_pairs={{0,4},{4,0},{8,12},{12,8},{16,20},{20,16},{24,28},{28,24},{1,5},{5... | collective-permute-start | bytes 393224 | tf_op jit(solution)/shard_map/ppermute | solution.py:116
  6.4 6.5 %collective-permute-start.1 = (f32[64,512]{1,0:T(8,128)S(1)}, f32[64,512]{1,0:T(8,128)S(1)}, u32[]{:S(2)}, u32[]{:S(2)}) collective-permute-start(f32[64,512]{1,0:T(8,128)S(1)} %get-tuple-element.21), channel_id=1, source_target_pairs={{0,8},{4,12},{8,0},{12,4},{16,24},{20,28},{24,16},{28,20},{1,9},{5... | collective-permute-start | bytes 393224 | tf_op jit(solution)/shard_map/ppermute | solution.py:116
  8.0 7.4 %collective-permute-start.2 = (f32[64,512]{1,0:T(8,128)S(1)}, f32[64,512]{1,0:T(8,128)S(1)}, u32[]{:S(2)}, u32[]{:S(2)}) collective-permute-start(f32[64,512]{1,0:T(8,128)S(1)} %get-tuple-element.22), channel_id=1, source_target_pairs={{0,12},{4,8},{8,4},{12,0},{16,28},{20,24},{24,20},{28,16},{1,13},{... | collective-permute-start | bytes 393224 | tf_op jit(solution)/shard_map/ppermute | solution.py:116
  8.9 8.4 %collective-permute-start.7 = (f32[64,512]{1,0:T(8,128)S(1)}, f32[64,512]{1,0:T(8,128)S(1)}, u32[]{:S(2)}, u32[]{:S(2)}) collective-permute-start(f32[64,512]{1,0:T(8,128)S(1)} %get-tuple-element.24), channel_id=1, source_target_pairs={{0,4},{4,0},{8,12},{12,8},{16,20},{20,16},{24,28},{28,24},{1,5},{5... | collective-permute-start | bytes 393224 | tf_op jit(solution)/shard_map/ppermute | solution.py:116
  10.8 7.6 %collective-permute-start.8 = (f32[64,512]{1,0:T(8,128)S(1)}, f32[64,512]{1,0:T(8,128)S(1)}, u32[]{:S(2)}, u32[]{:S(2)}) collective-permute-start(f32[64,512]{1,0:T(8,128)S(1)} %get-tuple-element.25), channel_id=1, source_target_pairs={{0,8},{4,12},{8,0},{12,4},{16,24},{20,28},{24,16},{28,20},{1,9},{5... | collective-permute-start | bytes 393224 | tf_op jit(solution)/shard_map/ppermute | solution.py:116
  12.4 7.2 %collective-permute-start.9 = (f32[64,512]{1,0:T(8,128)S(1)}, f32[64,512]{1,0:T(8,128)S(1)}, u32[]{:S(2)}, u32[]{:S(2)}) collective-permute-start(f32[64,512]{1,0:T(8,128)S(1)} %get-tuple-element.26), channel_id=1, source_target_pairs={{0,12},{4,8},{8,4},{12,0},{16,28},{20,24},{24,20},{28,16},{1,13},{... | collective-permute-start | bytes 393224 | tf_op jit(solution)/shard_map/ppermute | solution.py:116
  19.7 13.4 %copy-start.10 = (s32[1,1,1024]{2,1,0:T(1,128)S(1)}, s32[1,1,1024]{2,1,0:T(1,128)}, u32[]{:S(2)}) copy-start(s32[1,1,1024]{2,1,0:T(1,128)} %param.11) | copy-start | bytes 12292
  19.7 11.6 %collective-permute-start.10 = (f32[64,512]{1,0:T(8,128)S(1)}, f32[64,512]{1,0:T(8,128)S(1)}, u32[]{:S(2)}, u32[]{:S(2)}) collective-permute-start(f32[64,512]{1,0:T(8,128)S(1)} %add_add_fusion), channel_id=1, source_target_pairs={{0,16},{4,20},{8,24},{12,28},{16,0},{20,4},{24,8},{28,12},{1,17},{... | collective-permute-start | bytes 393224 | tf_op jit(solution)/shard_map/ppermute | solution.py:116
  22.5 22.9 %copy-start.1 = (bf16[1,1,1024,512]{3,2,1,0:T(8,128)(2,1)S(1)}, bf16[1,1,1024,512]{3,2,1,0:T(8,128)(2,1)}, u32[]{:S(2)}) copy-start(bf16[1,1,1024,512]{3,2,1,0:T(8,128)(2,1)} %param.10) | copy-start | bytes 3145732
  22.5 22.9 %copy-start.4 = (bf16[512,512]{1,0:T(8,128)(2,1)S(1)}, bf16[512,512]{1,0:T(8,128)(2,1)}, u32[]{:S(2)}) copy-start(bf16[512,512]{1,0:T(8,128)(2,1)} %refs_11_.1) | copy-start | bytes 1572868
  22.5 22.9 %copy-start.5 = (bf16[512,512]{1,0:T(8,128)(2,1)S(1)}, bf16[512,512]{1,0:T(8,128)(2,1)}, u32[]{:S(2)}) copy-start(bf16[512,512]{1,0:T(8,128)(2,1)} %refs_12_.1) | copy-start | bytes 1572868
  22.5 22.9 %copy-start.8 = (f32[512]{0:T(512)S(1)}, f32[512]{0:T(512)}, u32[]{:S(2)}) copy-start(f32[512]{0:T(512)} %param.18) | copy-start | bytes 6148
  22.8 12.1 %collective-permute-start.3 = (f32[64,512]{1,0:T(8,128)S(1)}, f32[64,512]{1,0:T(8,128)S(1)}, u32[]{:S(2)}, u32[]{:S(2)}) collective-permute-start(f32[64,512]{1,0:T(8,128)S(1)} %add_add_fusion.1), channel_id=1, source_target_pairs={{0,16},{4,20},{8,24},{12,28},{16,0},{20,4},{24,8},{28,12},{1,17},{... | collective-permute-start | bytes 393224 | tf_op jit(solution)/shard_map/ppermute | solution.py:116
  31.3 7.2 %collective-permute-start.11 = (f32[64,512]{1,0:T(8,128)S(1)}, f32[64,512]{1,0:T(8,128)S(1)}, u32[]{:S(2)}, u32[]{:S(2)}) collective-permute-start(f32[64,512]{1,0:T(8,128)S(1)} %add.37.refs_4_), channel_id=1, source_target_pairs={{0,4},{4,0},{8,12},{12,8},{16,20},{20,16},{24,28},{28,24},{1,5},{5... | collective-permute-start | bytes 393224 | tf_op jit(solution)/shard_map/ppermute | solution.py:116
  33.0 6.4 %collective-permute-start.12 = (f32[64,512]{1,0:T(8,128)S(1)}, f32[64,512]{1,0:T(8,128)S(1)}, u32[]{:S(2)}, u32[]{:S(2)}) collective-permute-start(f32[64,512]{1,0:T(8,128)S(1)} %add.37.refs_4_), channel_id=1, source_target_pairs={{0,8},{4,12},{8,0},{12,4},{16,24},{20,28},{24,16},{28,20},{1,9},{5... | collective-permute-start | bytes 393224 | tf_op jit(solution)/shard_map/ppermute | solution.py:116
  33.0 9.2 %collective-permute-start.13 = (f32[64,512]{1,0:T(8,128)S(1)}, f32[64,512]{1,0:T(8,128)S(1)}, u32[]{:S(2)}, u32[]{:S(2)}) collective-permute-start(f32[64,512]{1,0:T(8,128)S(1)} %add.37.refs_4_), channel_id=1, source_target_pairs={{0,12},{4,8},{8,4},{12,0},{16,28},{20,24},{24,20},{28,16},{1,13},{... | collective-permute-start | bytes 393224 | tf_op jit(solution)/shard_map/ppermute | solution.py:116
  34.9 8.5 %collective-permute-start.4 = (f32[64,512]{1,0:T(8,128)S(1)}, f32[64,512]{1,0:T(8,128)S(1)}, u32[]{:S(2)}, u32[]{:S(2)}) collective-permute-start(f32[64,512]{1,0:T(8,128)S(1)} %add.33.refs_0_), channel_id=1, source_target_pairs={{0,4},{4,0},{8,12},{12,8},{16,20},{20,16},{24,28},{28,24},{1,5},{5... | collective-permute-start | bytes 393224 | tf_op jit(solution)/shard_map/ppermute | solution.py:116
  36.6 6.8 %collective-permute-start.5 = (f32[64,512]{1,0:T(8,128)S(1)}, f32[64,512]{1,0:T(8,128)S(1)}, u32[]{:S(2)}, u32[]{:S(2)}) collective-permute-start(f32[64,512]{1,0:T(8,128)S(1)} %add.33.refs_0_), channel_id=1, source_target_pairs={{0,8},{4,12},{8,0},{12,4},{16,24},{20,28},{24,16},{28,20},{1,9},{5... | collective-permute-start | bytes 393224 | tf_op jit(solution)/shard_map/ppermute | solution.py:116
  38.6 6.8 %collective-permute-start.6 = (f32[64,512]{1,0:T(8,128)S(1)}, f32[64,512]{1,0:T(8,128)S(1)}, u32[]{:S(2)}, u32[]{:S(2)}) collective-permute-start(f32[64,512]{1,0:T(8,128)S(1)} %add.33.refs_0_), channel_id=1, source_target_pairs={{0,12},{4,8},{8,4},{12,0},{16,28},{20,24},{24,20},{28,16},{1,13},{... | collective-permute-start | bytes 393224 | tf_op jit(solution)/shard_map/ppermute | solution.py:116
  50.0 1.6 %collective-permute-start.14 = (f32[128,512]{1,0:T(8,128)S(1)}, f32[128,512]{1,0:T(8,128)S(1)}, u32[]{:S(2)}, u32[]{:S(2)}) collective-permute-start(f32[128,512]{1,0:T(8,128)S(1)} %get-tuple-element.31), channel_id=1, source_target_pairs={{0,1},{1,0},{2,3},{3,2},{4,5},{5,4},{6,7},{7,6},{8,9},{9,8},{10,11... | collective-permute-start | bytes 786440 | tf_op jit(solution)/shard_map/ppermute | solution.py:116
  51.6 10.1 %copy-start.6 = (bf16[512,512]{1,0:T(8,128)(2,1)S(1)}, bf16[512,512]{1,0:T(8,128)(2,1)}, u32[]{:S(2)}) copy-start(bf16[512,512]{1,0:T(8,128)(2,1)} %inner_ref.1) | copy-start | bytes 1572868
  51.6 10.1 %copy-start.7 = (bf16[512,512]{1,0:T(8,128)(2,1)S(1)}, bf16[512,512]{1,0:T(8,128)(2,1)}, u32[]{:S(2)}) copy-start(bf16[512,512]{1,0:T(8,128)(2,1)} %outer_ref.1) | copy-start | bytes 1572868
  51.6 10.1 %copy-start.9 = (f32[512]{0:T(512)S(1)}, f32[512]{0:T(512)}, u32[]{:S(2)}) copy-start(f32[512]{0:T(512)} %param.19) | copy-start | bytes 6148
  51.7 8.4 %collective-permute-start.15 = (f32[128,512]{1,0:T(8,128)S(1)}, f32[128,512]{1,0:T(8,128)S(1)}, u32[]{:S(2)}, u32[]{:S(2)}) collective-permute-start(f32[128,512]{1,0:T(8,128)S(1)} %add.38), channel_id=1, source_target_pairs={{0,2},{1,3},{2,0},{3,1},{4,6},{5,7},{6,4},{7,5},{8,10},{9,11},{10,... | collective-permute-start | bytes 786440 | tf_op jit(solution)/shard_map/ppermute | solution.py:116
  60.1 1.6 %collective-permute-start.16 = (f32[128,512]{1,0:T(8,128)S(1)}, f32[128,512]{1,0:T(8,128)S(1)}, u32[]{:S(2)}, u32[]{:S(2)}) collective-permute-start(f32[128,512]{1,0:T(8,128)S(1)} %add.39.own_ref), channel_id=1, source_target_pairs={{0,1},{1,0},{2,3},{3,2},{4,5},{5,4},{6,7},{7,6},{8,9},{9,8},{10,11... | collective-permute-start | bytes 786440 | tf_op jit(solution)/shard_map/ppermute | solution.py:116

commit v2 on v0

v2 whole, which is shorter than its diff:
```python
import functools

import jax
import jax.numpy as jnp
from jax import lax
from jax.experimental import pallas as pl
from jax.experimental.pallas import tpu as pltpu
from jax.sharding import PartitionSpec as P

ATOM_DEV = 64
GROUP = 4
MASKS = (0, 2, 1, 3)
SHARES = (4, 4)
REDUCE_STEPWISE = (False, False)
SPREAD_STEPWISE = (True, False)
PIECES = 2
LANES = 128
HIDE_FLOPS = 8 * 10**9
VMEM_LIMIT = 40 * 1024 * 1024
FIRST_VMEM_LIMIT = 52 * 1024 * 1024

VMEM = pl.BlockSpec(memory_space=pltpu.VMEM)
HBM = pl.BlockSpec(memory_space=pltpu.HBM)


def call(kernel, out_shape, in_specs, flops, scratch=(), out_specs=None, limit=VMEM_LIMIT):
    return pl.pallas_call(
        kernel,
        out_shape=out_shape,
        in_specs=in_specs,
        out_specs=jax.tree.map(lambda _: VMEM, out_shape) if out_specs is None else out_specs,
        scratch_shapes=list(scratch),
        compiler_params=pltpu.CompilerParams(vmem_limit_bytes=limit),
        cost_estimate=pl.CostEstimate(flops=flops, bytes_accessed=0, transcendentals=0),
    )


def wave_sizes(atoms):
    return [atoms // (GROUP * sum(SHARES)) * share for share in SHARES]


def target_place(atoms, sizes):
    device = lax.axis_index("src")
    own = (device // 2) % 2 + (device % 2) * 2
    place = atoms
    base = 0
    for size in sizes:
        inside = atoms - base
        chunk = sum((inside >= k * size).astype(jnp.int32) for k in range(1, GROUP))
        spot = base + jnp.bitwise_xor(chunk, own) * size + inside - chunk * size
        place = jnp.where(inside >= 0, spot, place)
        base += GROUP * size
    return place


def source_place(atoms, half):
    return jnp.bitwise_xor(atoms, (lax.axis_index("tgt") % 2) * half)


def one_hot(place, slot):
    return jnp.where(place == slot, jnp.float32(1.0), jnp.float32(0.0)).astype(jnp.bfloat16)


def store_sums(wave, sizes, live, targets, fetch, chunk_refs):
    rows = targets.shape[1]
    size = sizes[wave]
    place = target_place(targets, sizes)
    place = jnp.where(lax.broadcasted_iota(jnp.int32, (1, rows), 1) < live, place, -1)
    slot = lax.broadcasted_iota(jnp.int32, (size * GROUP, rows), 0) + sum(sizes[:wave]) * GROUP
    chosen = one_hot(place, slot)
    states = fetch()
    at = 0
    for chunk_ref in chunk_refs:
        count = chunk_ref.shape[0]
        chunk_ref[...] = jnp.dot(chosen[at : at + count], states, preferred_element_type=jnp.float32)
        at += count


def first_sum_kernel(sizes, live_hbm, target_hbm, state_hbm, *refs):
    *chunk_refs, live_out, target_ref, state_ref, live_ref, sems = refs
    copies = [
        pltpu.make_async_copy(source, place, sems.at[index])
        for index, (source, place) in enumerate(((live_hbm, live_ref), (target_hbm, target_ref), (state_hbm, state_ref)))
    ]
    for copy in copies:
        copy.start()
    copies[0].wait()
    live = live_ref[0, 0]
    live_out[...] = jnp.full(live_out.shape, live, jnp.int32)
    copies[1].wait()

    def fetch():
        copies[2].wait()
        return state_ref[...]

    store_sums(0, sizes, live, target_ref[...], fetch, chunk_refs)


def later_sum_kernel(wave, sizes, live_ref, target_ref, state_ref, *chunk_refs):
    store_sums(wave, sizes, live_ref[:, :1], target_ref[...], lambda: state_ref[...], chunk_refs)


def chunk_shapes(wave, size, channels):
    counts = [size, size, 2 * size] if REDUCE_STEPWISE[wave] else [size] * GROUP
    return [jax.ShapeDtypeStruct((count, channels), jnp.float32) for count in counts]


def first_sums(states, targets, live, sizes):
    rows, channels = states.shape
    handed_on = [
        jax.ShapeDtypeStruct((1, LANES), jnp.int32),
        jax.ShapeDtypeStruct(targets.shape, targets.dtype),
        jax.ShapeDtypeStruct(states.shape, states.dtype),
    ]
    out = call(
        functools.partial(first_sum_kernel, sizes), chunk_shapes(0, sizes[0], channels) + handed_on, [HBM] * 3,
        2 * sizes[0] * GROUP * rows * channels,
        [pltpu.SMEM((1, 1), jnp.int32), pltpu.SemaphoreType.DMA((3,))],
        limit=FIRST_VMEM_LIMIT,
    )(live, targets, states)
    return out[:-3], *out[-3:]


def later_sums(states, targets, live, wave, sizes):
    rows, channels = states.shape
    return call(
        functools.partial(later_sum_kernel, wave, sizes), chunk_shapes(wave, sizes[wave], channels), [VMEM] * 3,
        2 * sizes[wave] * GROUP * rows * channels,
    )(live, targets, states)


def choose_kernel(sizes, half, target_ref, source_ref, tie_ref, target_chosen_ref, source_chosen_ref, source_pick_ref):
    del tie_ref
    rows = target_ref.shape[1]
    sources = source_place(source_ref[...], half)
    for values, chosen_ref in ((target_place(target_ref[...], sizes), target_chosen_ref), (sources, source_chosen_ref)):
        place = jnp.transpose(jnp.broadcast_to(values, (LANES, rows)))
        lane = lax.broadcasted_iota(jnp.int32, (rows, LANES), 1)
        for first in range(0, chosen_ref.shape[1], LANES):
            chosen_ref[:, first : first + LANES] = one_hot(place, lane + first)
    source_pick_ref[...] = one_hot(sources, lax.broadcasted_iota(jnp.int32, source_pick_ref.shape, 0))


def split_sums(sum_refs, parts_ref):
    total = parts_ref.shape[0] // 3
    at = 0
    for sum_ref in sum_refs:
        size = sum_ref.shape[0]
        value = sum_ref[...]
        for part in range(3):
            low = value.astype(jnp.bfloat16)
            parts_ref[part * total + at : part * total + at + size, :] = low
            value = value - low.astype(jnp.float32)
        at += size


def normed_activated(chosen_ref, parts_ref, state_ref, inner_ref, gain_ref):
    chosen = chosen_ref[...]
    gathered = jnp.dot(
        jnp.concatenate([chosen, chosen, chosen], axis=1), parts_ref[...], preferred_element_type=jnp.float32
    )
    message = gathered - state_ref[...].astype(jnp.float32)
    mean_square = jnp.mean(message * message, axis=-1, keepdims=True)
    normed = message * lax.rsqrt(mean_square + 1e-05) * gain_ref[...]
    activated = jax.nn.relu(
        jnp.dot(normed.astype(jnp.bfloat16), inner_ref[...], preferred_element_type=jnp.float32)
    ).astype(jnp.bfloat16)
    return normed, activated


def finish(normed, activated, outer_ref, live_ref, first_row):
    result = normed + jnp.dot(activated, outer_ref[...], preferred_element_type=jnp.float32)
    row = lax.broadcasted_iota(jnp.int32, (result.shape[0], 1), 0) + first_row
    return jnp.where(row < live_ref[:, :1], result, jnp.float32(0.0)).astype(jnp.bfloat16)


def layer_one_kernel(n_sums, live_ref, *refs):
    sum_refs = refs[:n_sums]
    chosen_ref, pick_ref, state_ref, inner_ref, outer_ref, gain_ref, reverse_ref, *piece_refs, parts_ref = refs[n_sums:]
    split_sums(sum_refs, parts_ref)
    normed, activated = normed_activated(chosen_ref, parts_ref, state_ref, inner_ref, gain_ref)
    reverse_ref[...] = finish(normed, activated, outer_ref, live_ref, 0)
    total = jnp.dot(pick_ref[...], reverse_ref[...], preferred_element_type=jnp.float32)
    size = piece_refs[0].shape[0]
    for index, piece_ref in enumerate(piece_refs):
        piece_ref[...] = total[index * size : (index + 1) * size]


def layer_two_kernel(n_sums, live_ref, *refs):
    sum_refs = refs[:n_sums]
    chosen_ref, state_ref, inner_ref, outer_ref, gain_ref, final_hbm, parts_ref, final_ref, sems = refs[n_sums:]
    split_sums(sum_refs, parts_ref)
    normed, activated = normed_activated(chosen_ref, parts_ref, state_ref, inner_ref, gain_ref)
    block = final_ref.shape[0] // 2
    copies = []
    for index in range(2):
        rows = pl.ds(index * block, block)
        part = slice(index * block, (index + 1) * block)
        final_ref[rows, :] = finish(normed[part], activated[part], outer_ref, live_ref, index * block)
        copies.append(pltpu.make_async_copy(final_ref.at[rows], final_hbm.at[rows], sems.at[index]))
        copies[-1].start()
    for copy in copies:
        copy.wait()


def swap(value, axis, mask):
    return lax.ppermute(value, axis, [(i, i ^ mask) for i in range(lax.axis_size(axis))])


def higher_masks(axis, low):
    masks = []
    while low < lax.axis_size(axis):
        masks.append(low)
        low *= 2
    return masks


def tie(value, other):
    return lax.optimization_barrier((value, other))[0]


def spread(total, stepwise):
    if not stepwise:
        return [total] + [swap(total, "src", mask) for mask in MASKS[1:]]
    second = swap(total, "src", MASKS[1])
    return [total, second, swap(jnp.concatenate([total, second]), "src", MASKS[2])]


def reduce(chunks, stepwise, ready):
    if not stepwise:
        parts = ready([swap(chunk, "src", mask) for chunk, mask in zip(chunks[1:], MASKS[1:])])
        return chunks[0] + parts[0] + parts[1] + parts[2]
    size = chunks[0].shape[0]
    part = swap(chunks[2], "src", MASKS[2])
    return chunks[0] + part[:size] + ready(swap(chunks[1] + part[size:], "src", MASKS[1]))


def target_totals(waves, between):
    first = reduce(waves[0], REDUCE_STEPWISE[0], lambda parts: parts)
    made = between(first)
    second = reduce(waves[1], REDUCE_STEPWISE[1], lambda parts: tie(parts, made))
    sums = [first, second]
    for mask in higher_masks("src", GROUP):
        parts = [swap(value, "src", mask) for value in sums]
        parts[0] = tie(parts[0], sums[1])
        sums = [value + part for value, part in zip(sums, parts)]
    return [chunk for value, stepwise in zip(sums, SPREAD_STEPWISE) for chunk in spread(value, stepwise)], made


def source_totals(pieces):
    own = [mine + swap(theirs, "tgt", 1) for mine, theirs in zip(pieces[:PIECES], pieces[PIECES:])]
    for mask in higher_masks("tgt", 2):
        own = [value + swap(value, "tgt", mask) for value in own]
    return own + [swap(value, "tgt", 1) for value in own]


def body(
    edge_state,
    edge_source,
    edge_target,
    live_edges,
    inner_one,
    outer_one,
    inner_two,
    outer_two,
    gain_one,
    gain_two,
):
    rows, channels = edge_state.shape[2:]
    states = edge_state.reshape(rows, channels)
    sources = edge_source.reshape(1, rows)
    targets = edge_target.reshape(1, rows)
    target_atoms = ATOM_DEV * lax.axis_size("src")
    source_atoms = ATOM_DEV * lax.axis_size("tgt")
    sizes = wave_sizes(target_atoms)
    half = source_atoms // 2
    first, live, targets, states = first_sums(states, targets, live_edges, sizes)
    waves = [first] + [later_sums(states, targets, live, wave, sizes) for wave in range(1, len(sizes))]

    def choose(first):
        return call(
            functools.partial(choose_kernel, sizes, half),
            [
                jax.ShapeDtypeStruct((rows, target_atoms), jnp.bfloat16),
                jax.ShapeDtypeStruct((rows, source_atoms), jnp.bfloat16),
                jax.ShapeDtypeStruct((source_atoms, rows), jnp.bfloat16),
            ],
            [VMEM] * 3, HIDE_FLOPS,
        )(targets, sources, first)

    totals, (target_chosen, source_chosen, source_pick) = target_totals(waves, choose)
    reverse_state, *pieces = call(
        functools.partial(layer_one_kernel, len(totals)),
        [jax.ShapeDtypeStruct((rows, channels), jnp.bfloat16)]
        + [jax.ShapeDtypeStruct((half // PIECES, channels), jnp.float32)] * (2 * PIECES),
        [VMEM] * (len(totals) + 7),
        2 * rows * channels * (3 * target_atoms + 2 * channels + source_atoms),
        [pltpu.VMEM((3 * target_atoms, channels), jnp.bfloat16)],
    )(live, *totals, target_chosen, source_pick, states, inner_one, outer_one, gain_one.reshape(1, channels))
    totals = source_totals(pieces)
    final_state = call(
        functools.partial(layer_two_kernel, len(totals)),
        jax.ShapeDtypeStruct((rows, channels), jnp.bfloat16),
        [VMEM] * (len(totals) + 6),
        2 * rows * channels * (3 * source_atoms + 2 * channels),
        [
            pltpu.VMEM((3 * source_atoms, channels), jnp.bfloat16),
            pltpu.VMEM((rows, channels), jnp.bfloat16),
            pltpu.SemaphoreType.DMA((2,)),
        ],
        HBM,
    )(live, *totals, source_chosen, reverse_state, inner_two, outer_two, gain_two.reshape(1, channels))
    return final_state.reshape(1, 1, rows, channels)


def solution(mesh):
    placed = (
        P("src", "tgt", None, None),
        P("src", "tgt", None),
        P("src", "tgt", None),
        P("src", "tgt"),
        P(),
        P(),
        P(),
        P(),
        P(),
        P(),
    )
    return jax.shard_map(
        body, mesh=mesh, in_specs=placed, out_specs=P("src", "tgt", None, None), check_vma=False
    )
```

time: 185 us -> 57.7 us (0.31)
  waiting for transfers between devices: 114 us -> 22.8 us
  local copies, waits for them, and re-layouts: 25.1 us -> 0.05 us
  starting transfers between devices: 0.04 us -> 23.7 us
  other arithmetic: 22 us -> 0.21 us
  between operations: 14.2 us -> 0.84 us
  matrix products: 10.1 us -> 0 us
  Pallas kernels: 0 us -> 9.93 us
    psum x2 -> x0, waiting for transfers between devices: 114 us -> none  [the longest x1 80.7 us: target_totals(): return lax.psum(partial_value, 'src')]
    ppermute x0 -> x19, starting transfers between devices: none -> 23.7 us  [swap(): lax.ppermute(value, axis, [(i, i ^ mask) for i in range(lax.axis_size(axi...]
    ppermute x0 -> x19, waiting for transfers between devices: none -> 22.8 us  [swap(): lax.ppermute(value, axis, [(i, i ^ mask) for i in range(lax.axis_size(axi...]
    gather x4 -> x0, local copies, waits for them, and re-layouts: 16.3 us -> none  [the longest x2 9.4 us: body(): message = jnp.take(incoming, targets, axis=0) - states.astype(jnp.float32)]
    scatter-add x2 -> x0, other arithmetic: 15.6 us -> none  [the longest x1 8.24 us: body(): jax.ops.segment_sum(jnp.where(alive[:, None], states.astype(jnp.float32),...]
    dot_general x2 -> x0, matrix products: 10.1 us -> none  [update_edges(): jnp.dot(activated, outer, preferred_element_type=jnp.float32)]
    pallas_call x0 -> x5, Pallas kernels: none -> 9.93 us  [the longest x1 3.3 us: body(): call(functools.partial(layer_one_kernel, len(totals)), [jax.ShapeDtypeStr...]
    reduce_sum x2 -> x0, other arithmetic: 4.76 us -> none  [update_edges(): mean_square = jnp.mean(message * message, axis=-1, keepdims=True)]
  transfers between devices with their start and end apart: 2 -> 19, of which waited for: 2 -> 11; matrix products, arithmetic and copies ran while one was open for 0% -> 0% of each run, Pallas kernels for 0% -> 3%
where the time goes in v2:
time: 57.7 us; the launch traced here: 57.6 us
  starting transfers between devices  23.7 us (41%)
  waiting for transfers between devices  22.8 us (40%)
  Pallas kernels  9.93 us (17%)
  between operations  0.84 us (1%)
    ppermute x19, starting transfers between devices, swap(): lax.ppermute(value, axis, [(i, i ^ mask) for i in range(lax.axis_size(axi...  23.7 us
    ppermute x19, waiting for transfers between devices, swap(): lax.ppermute(value, axis, [(i, i ^ mask) for i in range(lax.axis_size(axi...  22.8 us
    pallas_call x1, Pallas kernels, body(): call(functools.partial(layer_one_kernel, len(totals)), [jax.ShapeDtypeStr...  3.3 us
    pallas_call x1, Pallas kernels, body(): call(functools.partial(layer_two_kernel, len(totals)), jax.ShapeDtypeStru...  3.03 us
    pallas_call x1, Pallas kernels, first_sums(): call(functools.partial(first_sum_kernel, sizes), chunk_shapes(0, sizes[0]...  2.11 us
  transfers between devices with their start and end apart: 19, of which 11 were waited for; matrix products, arithmetic and copies ran while one was open for 0% of the time, Pallas kernels for 3%

profile of v2, /device:TPU:0, one launch (start us, length us, event | category | flops | bytes accessed | tf_op | source)
XLA Modules:
  0.0 57.6 jit_solution(15127189794827501201)
XLA Ops:
  0.7 0.0 copy-done
  0.7 2.1 %shard_map.100 = (f32[64,512]{1,0:T(8,128)S(1)}, f32[64,512]{1,0:T(8,128)S(1)}, f32[64,512]{1,0:T(8,128)S(1)}, f32[64,512]{1,0:T(8,128)S(1)}, s32[1,128]{1,0:T(1...) custom-call(s32[1,1]{1,0:T(1,128)S(6)} %copy.11.live_hbm, s32[1,1024]{1,0:T(1,128)S(1)} %bitcast.6, ...), custom_call_target="tpu_custom_call" | custom-call | flops 268435456 | tf_op jit(solution)/shard_map/pallas_call | solution.py:115
  2.8 3.1 %collective-permute-start = (f32[64,512]{1,0:T(8,128)S(1)}, f32[64,512]{1,0:T(8,128)S(1)}, u32[]{:S(2)}, u32[]{:S(2)}) collective-permute-start(f32[64,512]{1,0:T(8,128)S(1)} %get-tuple-element.30), channel_id=1, source_target_pairs={{0,8},{4,12},{8,0},{12,4},{16,24},{20,28},{24,16},{28,20},{1,9},{5... | collective-permute-start | bytes 393224 | tf_op jit(solution)/shard_map/ppermute | solution.py:207
  5.9 1.5 %collective-permute-start.1 = (f32[64,512]{1,0:T(8,128)S(1)}, f32[64,512]{1,0:T(8,128)S(1)}, u32[]{:S(2)}, u32[]{:S(2)}) collective-permute-start(f32[64,512]{1,0:T(8,128)S(1)} %get-tuple-element.31), channel_id=1, source_target_pairs={{0,4},{4,0},{8,12},{12,8},{16,20},{20,16},{24,28},{28,24},{1,5},{5... | collective-permute-start | bytes 393224 | tf_op jit(solution)/shard_map/ppermute | solution.py:207
  7.4 0.0 collective-permute-start.2
  7.4 0.9 %shard_map.101 = (f32[64,512]{1,0:T(8,128)S(1)}, f32[64,512]{1,0:T(8,128)S(1)}, f32[64,512]{1,0:T(8,128)S(1)}, f32[64,512]{1,0:T(8,128)S(1)}) custom-call(s32[1,128]{1,0:T(1,128)S(1)} %get-tuple-element.28.live_ref, s32[1,1024]{1,0:T(1,128)S(1)} %get-tuple-element.33.target_ref, bf16[1024,512]{1,0:T(8,128)(2,1)S(1)} %get-tuple-element.34.state_ref.refs_9_), custom_call_target="tpu_custom_call" | custom-call | flops 268435456 | tf_op jit(solution)/shard_map/pallas_call | solution.py:126
  8.3 2.0 %collective-permute-start.4 = (f32[64,512]{1,0:T(8,128)S(1)}, f32[64,512]{1,0:T(8,128)S(1)}, u32[]{:S(2)}, u32[]{:S(2)}) collective-permute-start(f32[64,512]{1,0:T(8,128)S(1)} %get-tuple-element.36), channel_id=1, source_target_pairs={{0,8},{4,12},{8,0},{12,4},{16,24},{20,28},{24,16},{28,20},{1,9},{5... | collective-permute-start | bytes 393224 | tf_op jit(solution)/shard_map/ppermute | solution.py:207
  10.3 1.5 %collective-permute-start.5 = (f32[64,512]{1,0:T(8,128)S(1)}, f32[64,512]{1,0:T(8,128)S(1)}, u32[]{:S(2)}, u32[]{:S(2)}) collective-permute-start(f32[64,512]{1,0:T(8,128)S(1)} %get-tuple-element.37), channel_id=1, source_target_pairs={{0,4},{4,0},{8,12},{12,8},{16,20},{20,16},{24,28},{28,24},{1,5},{5... | collective-permute-start | bytes 393224 | tf_op jit(solution)/shard_map/ppermute | solution.py:207
  11.9 0.0 collective-permute-done
  11.9 1.4 %collective-permute-start.6 = (f32[64,512]{1,0:T(8,128)S(1)}, f32[64,512]{1,0:T(8,128)S(1)}, u32[]{:S(2)}, u32[]{:S(2)}) collective-permute-start(f32[64,512]{1,0:T(8,128)S(1)} %get-tuple-element.38), channel_id=1, source_target_pairs={{0,12},{4,8},{8,4},{12,0},{16,28},{20,24},{24,20},{28,16},{1,13},{... | collective-permute-start | bytes 393224 | tf_op jit(solution)/shard_map/ppermute | solution.py:207
  13.2 1.0 %collective-permute-done.1 = f32[64,512]{1,0:T(8,128)S(1)} collective-permute-done((f32[64,512]{1,0:T(8,128)S(1)}, f32[64,512]{1,0:T(8,128)S(1)}, u32[]{:S(2)}, u32[]{:S(2)}) %collective-permute-start.1) | collective-permute-done | bytes 131104 | tf_op jit(solution)/shard_map/ppermute | solution.py:207
  14.2 0.6 collective-permute-done.2
  14.8 2.6 %collective-permute-start.3 = (f32[64,512]{1,0:T(8,128)S(1)}, f32[64,512]{1,0:T(8,128)S(1)}, u32[]{:S(2)}, u32[]{:S(2)}) collective-permute-start(f32[64,512]{1,0:T(8,128)S(1)} %add_add_fusion.1.tie_ref), channel_id=1, source_target_pairs={{0,16},{4,20},{8,24},{12,28},{16,0},{20,4},{24,8},{28,12},{1,17},{... | collective-permute-start | bytes 393224 | tf_op jit(solution)/shard_map/ppermute | solution.py:207
  17.4 0.6 %shard_map.102 = (bf16[1024,512]{1,0:T(8,128)(2,1)S(1)}, bf16[1024,256]{1,0:T(8,128)(2,1)S(1)}, bf16[256,1024]{1,0:T(8,128)(2,1)S(1)}) custom-call(s32[1,1024]{1,0:T(1,128)S(1)} %get-tuple-element.33.target_ref, s32[1,1024]{1,0:T(1,128)S(1)} %bitcast.7, f32[64,512]{1,0:T(8,128)S(1)} %add_add_fusion.1.tie_ref), custom_call_target="tpu_custom_call" | custom-call | flops 8000000000 | tf_op jit(solution)/shard_map/pallas_call | solution.py:281
  18.0 0.0 collective-permute-done.4
  18.1 0.0 collective-permute-done.5
  18.1 2.3 %collective-permute-done.6 = f32[64,512]{1,0:T(8,128)S(1)} collective-permute-done((f32[64,512]{1,0:T(8,128)S(1)}, f32[64,512]{1,0:T(8,128)S(1)}, u32[]{:S(2)}, u32[]{:S(2)}) %collective-permute-start.6) | collective-permute-done | bytes 131104 | tf_op jit(solution)/shard_map/ppermute | solution.py:207
  20.4 2.8 %collective-permute-done.3 = f32[64,512]{1,0:T(8,128)S(1)} collective-permute-done((f32[64,512]{1,0:T(8,128)S(1)}, f32[64,512]{1,0:T(8,128)S(1)}, u32[]{:S(2)}, u32[]{:S(2)}) %collective-permute-start.3) | collective-permute-done | bytes 131104 | tf_op jit(solution)/shard_map/ppermute | solution.py:207
  23.2 0.0 copy-start.1
  23.3 0.4 collective-permute-start.7
  23.6 2.6 %collective-permute-start.9 = (f32[64,512]{1,0:T(8,128)S(1)}, f32[64,512]{1,0:T(8,128)S(1)}, u32[]{:S(2)}, u32[]{:S(2)}) collective-permute-start(f32[64,512]{1,0:T(8,128)S(1)} %add_add_fusion), channel_id=1, source_target_pairs={{0,16},{4,20},{8,24},{12,28},{16,0},{20,4},{24,8},{28,12},{1,17},{... | collective-permute-start | bytes 393224 | tf_op jit(solution)/shard_map/ppermute | solution.py:207
  26.2 4.3 %collective-permute-done.7.refs_1_ = f32[64,512]{1,0:T(8,128)S(1)} collective-permute-done((f32[64,512]{1,0:T(8,128)S(1)}, f32[64,512]{1,0:T(8,128)S(1)}, u32[]{:S(2)}, u32[]{:S(2)}) %collective-permute-start.7) | collective-permute-done | bytes 131104 | tf_op jit(solution)/shard_map/ppermute | solution.py:207
  30.6 0.0 copy-start.6
  30.6 2.1 %collective-permute-start.8 = (f32[128,512]{1,0:T(8,128)S(1)}, f32[128,512]{1,0:T(8,128)S(1)}, u32[]{:S(2)}, u32[]{:S(2)}) collective-permute-start(f32[128,512]{1,0:T(8,128)S(1)} %pad_maximum_fusion), channel_id=1, source_target_pairs={{0,4},{4,0},{8,12},{12,8},{16,20},{20,16},{24,28},{28,24},{1,5},{5... | collective-permute-start | bytes 786440 | tf_op jit(solution)/shard_map/ppermute | solution.py:207
  32.7 0.0 collective-permute-done.9
  32.7 0.3 collective-permute-start.12
  33.0 0.8 %collective-permute-start.11 = (f32[64,512]{1,0:T(8,128)S(1)}, f32[64,512]{1,0:T(8,128)S(1)}, u32[]{:S(2)}, u32[]{:S(2)}) collective-permute-start(f32[64,512]{1,0:T(8,128)S(1)} %add.43.refs_3_), channel_id=1, source_target_pairs={{0,4},{4,0},{8,12},{12,8},{16,20},{20,16},{24,28},{28,24},{1,5},{5... | collective-permute-start | bytes 393224 | tf_op jit(solution)/shard_map/ppermute | solution.py:207
  33.8 2.5 %collective-permute-start.10 = (f32[64,512]{1,0:T(8,128)S(1)}, f32[64,512]{1,0:T(8,128)S(1)}, u32[]{:S(2)}, u32[]{:S(2)}) collective-permute-start(f32[64,512]{1,0:T(8,128)S(1)} %add.43.refs_3_), channel_id=1, source_target_pairs={{0,8},{4,12},{8,0},{12,4},{16,24},{20,28},{24,16},{28,20},{1,9},{5... | collective-permute-start | bytes 393224 | tf_op jit(solution)/shard_map/ppermute | solution.py:207
  36.3 2.5 %collective-permute-done.12.refs_6_ = f32[64,512]{1,0:T(8,128)S(1)} collective-permute-done((f32[64,512]{1,0:T(8,128)S(1)}, f32[64,512]{1,0:T(8,128)S(1)}, u32[]{:S(2)}, u32[]{:S(2)}) %collective-permute-start.12) | collective-permute-done | bytes 131104 | tf_op jit(solution)/shard_map/ppermute | solution.py:207
  38.8 1.1 %collective-permute-done.11.refs_5_ = f32[64,512]{1,0:T(8,128)S(1)} collective-permute-done((f32[64,512]{1,0:T(8,128)S(1)}, f32[64,512]{1,0:T(8,128)S(1)}, u32[]{:S(2)}, u32[]{:S(2)}) %collective-permute-start.11) | collective-permute-done | bytes 131104 | tf_op jit(solution)/shard_map/ppermute | solution.py:207
  39.9 0.0 collective-permute-done.10.refs_4_
  39.9 0.0 collective-permute-done.8.refs_2_
  39.9 0.0 copy-done.2
  39.9 3.3 %shard_map.103 = (bf16[1024,512]{1,0:T(8,128)(2,1)S(1)}, f32[64,512]{1,0:T(8,128)S(1)}, f32[64,512]{1,0:T(8,128)S(1)}, f32[64,512]{1,0:T(8,128)S(1)}, f32[64,512]{1,0:T(8,128)S(1)}) custom-call(s32[1,128]{1,0:T(1,128)S(1)} %get-tuple-element.28.live_ref, f32[64,512]{1,0:T(8,128)S(1)} %add.42.refs_0_, f32[64,512]{1,0:T(8,128)S(1)} %collective-permute-done.7.refs_1_, ...), custom_call_target="tpu_custom_call" | custom-call | flops 2952790016 | tf_op jit(solution)/shard_map/pallas_call | solution.py:292
  43.2 0.1 collective-permute-start.13
  43.3 0.5 collective-permute-start.15
  43.8 0.8 %collective-permute-done.13 = f32[64,512]{1,0:T(8,128)S(1)} collective-permute-done((f32[64,512]{1,0:T(8,128)S(1)}, f32[64,512]{1,0:T(8,128)S(1)}, u32[]{:S(2)}, u32[]{:S(2)}) %collective-permute-start.13) | collective-permute-done | bytes 131104 | tf_op jit(solution)/shard_map/ppermute | solution.py:207
  44.6 1.5 %collective-permute-start.14 = (f32[64,512]{1,0:T(8,128)S(1)}, f32[64,512]{1,0:T(8,128)S(1)}, u32[]{:S(2)}, u32[]{:S(2)}) collective-permute-start(f32[64,512]{1,0:T(8,128)S(1)} %add.44), channel_id=1, source_target_pairs={{0,2},{1,3},{2,0},{3,1},{4,6},{5,7},{6,4},{7,5},{8,10},{9,11},{10,... | collective-permute-start | bytes 393224 | tf_op jit(solution)/shard_map/ppermute | solution.py:207
  46.2 0.0 collective-permute-done.15
  46.2 0.6 %collective-permute-start.16 = (f32[64,512]{1,0:T(8,128)S(1)}, f32[64,512]{1,0:T(8,128)S(1)}, u32[]{:S(2)}, u32[]{:S(2)}) collective-permute-start(f32[64,512]{1,0:T(8,128)S(1)} %add.46), channel_id=1, source_target_pairs={{0,2},{1,3},{2,0},{3,1},{4,6},{5,7},{6,4},{7,5},{8,10},{9,11},{10,... | collective-permute-start | bytes 393224 | tf_op jit(solution)/shard_map/ppermute | solution.py:207
  46.8 4.2 %collective-permute-done.14 = f32[64,512]{1,0:T(8,128)S(1)} collective-permute-done((f32[64,512]{1,0:T(8,128)S(1)}, f32[64,512]{1,0:T(8,128)S(1)}, u32[]{:S(2)}, u32[]{:S(2)}) %collective-permute-start.14) | collective-permute-done | bytes 131104 | tf_op jit(solution)/shard_map/ppermute | solution.py:207
  51.1 0.1 collective-permute-start.17
  51.1 1.9 %collective-permute-done.16 = f32[64,512]{1,0:T(8,128)S(1)} collective-permute-done((f32[64,512]{1,0:T(8,128)S(1)}, f32[64,512]{1,0:T(8,128)S(1)}, u32[]{:S(2)}, u32[]{:S(2)}) %collective-permute-start.16) | collective-permute-done | bytes 131104 | tf_op jit(solution)/shard_map/ppermute | solution.py:207
  53.1 0.0 copy-start.7
  53.1 0.1 collective-permute-start.18
  53.2 0.0 collective-permute-done.17.refs_2_
  53.2 1.3 %collective-permute-done.18.refs_3_ = f32[64,512]{1,0:T(8,128)S(1)} collective-permute-done((f32[64,512]{1,0:T(8,128)S(1)}, f32[64,512]{1,0:T(8,128)S(1)}, u32[]{:S(2)}, u32[]{:S(2)}) %collective-permute-start.18) | collective-permute-done | bytes 131104 | tf_op jit(solution)/shard_map/ppermute | solution.py:207
  54.5 3.0 %shard_map.104 = bf16[1024,512]{1,0:T(8,128)(2,1)} custom-call(s32[1,128]{1,0:T(1,128)S(1)} %get-tuple-element.28.live_ref, f32[64,512]{1,0:T(8,128)S(1)} %add.45.refs_0_, f32[64,512]{1,0:T(8,128)S(1)} %add.47.refs_1_, f32[64,512]{1,0:T(8,128)S(1)} %collective-permute-done.17.refs_2_, f32[64,512]{1,0:T(8,128)S(1)} %collective-permute-done.18.refs_3_, ...), custom_call_target="tpu_custom_call" | custom-call | flops 1879048192 | tf_op jit(solution)/shard_map/pallas_call | solution.py:301
  (20 shorter events, 0.2 us)
Async XLA Ops:
  0.0 0.7 %copy-start = (s32[1,1,1024]{2,1,0:T(1,128)S(1)}, s32[1,1,1024]{2,1,0:T(1,128)}, u32[]{:S(2)}) copy-start(s32[1,1,1024]{2,1,0:T(1,128)} %param.12) | copy-start | bytes 12292
  2.8 9.1 %collective-permute-start = (f32[64,512]{1,0:T(8,128)S(1)}, f32[64,512]{1,0:T(8,128)S(1)}, u32[]{:S(2)}, u32[]{:S(2)}) collective-permute-start(f32[64,512]{1,0:T(8,128)S(1)} %get-tuple-element.30), channel_id=1, source_target_pairs={{0,8},{4,12},{8,0},{12,4},{16,24},{20,28},{24,16},{28,20},{1,9},{5... | collective-permute-start | bytes 393224 | tf_op jit(solution)/shard_map/ppermute | solution.py:207
  5.9 8.3 %collective-permute-start.1 = (f32[64,512]{1,0:T(8,128)S(1)}, f32[64,512]{1,0:T(8,128)S(1)}, u32[]{:S(2)}, u32[]{:S(2)}) collective-permute-start(f32[64,512]{1,0:T(8,128)S(1)} %get-tuple-element.31), channel_id=1, source_target_pairs={{0,4},{4,0},{8,12},{12,8},{16,20},{20,16},{24,28},{28,24},{1,5},{5... | collective-permute-start | bytes 393224 | tf_op jit(solution)/shard_map/ppermute | solution.py:207
  7.4 7.3 %collective-permute-start.2 = (f32[64,512]{1,0:T(8,128)S(1)}, f32[64,512]{1,0:T(8,128)S(1)}, u32[]{:S(2)}, u32[]{:S(2)}) collective-permute-start(f32[64,512]{1,0:T(8,128)S(1)} %get-tuple-element.32), channel_id=1, source_target_pairs={{0,12},{4,8},{8,4},{12,0},{16,28},{20,24},{24,20},{28,16},{1,13},{... | collective-permute-start | bytes 393224 | tf_op jit(solution)/shard_map/ppermute | solution.py:207
  8.3 9.7 %collective-permute-start.4 = (f32[64,512]{1,0:T(8,128)S(1)}, f32[64,512]{1,0:T(8,128)S(1)}, u32[]{:S(2)}, u32[]{:S(2)}) collective-permute-start(f32[64,512]{1,0:T(8,128)S(1)} %get-tuple-element.36), channel_id=1, source_target_pairs={{0,8},{4,12},{8,0},{12,4},{16,24},{20,28},{24,16},{28,20},{1,9},{5... | collective-permute-start | bytes 393224 | tf_op jit(solution)/shard_map/ppermute | solution.py:207
  10.3 7.7 %collective-permute-start.5 = (f32[64,512]{1,0:T(8,128)S(1)}, f32[64,512]{1,0:T(8,128)S(1)}, u32[]{:S(2)}, u32[]{:S(2)}) collective-permute-start(f32[64,512]{1,0:T(8,128)S(1)} %get-tuple-element.37), channel_id=1, source_target_pairs={{0,4},{4,0},{8,12},{12,8},{16,20},{20,16},{24,28},{28,24},{1,5},{5... | collective-permute-start | bytes 393224 | tf_op jit(solution)/shard_map/ppermute | solution.py:207
  11.9 8.5 %collective-permute-start.6 = (f32[64,512]{1,0:T(8,128)S(1)}, f32[64,512]{1,0:T(8,128)S(1)}, u32[]{:S(2)}, u32[]{:S(2)}) collective-permute-start(f32[64,512]{1,0:T(8,128)S(1)} %get-tuple-element.38), channel_id=1, source_target_pairs={{0,12},{4,8},{8,4},{12,0},{16,28},{20,24},{24,20},{28,16},{1,13},{... | collective-permute-start | bytes 393224 | tf_op jit(solution)/shard_map/ppermute | solution.py:207
  14.8 2.7 %copy-start.5 = (s32[1,1,1024]{2,1,0:T(1,128)S(1)}, s32[1,1,1024]{2,1,0:T(1,128)}, u32[]{:S(2)}) copy-start(s32[1,1,1024]{2,1,0:T(1,128)} %param.11) | copy-start | bytes 12292
  14.8 8.4 %collective-permute-start.3 = (f32[64,512]{1,0:T(8,128)S(1)}, f32[64,512]{1,0:T(8,128)S(1)}, u32[]{:S(2)}, u32[]{:S(2)}) collective-permute-start(f32[64,512]{1,0:T(8,128)S(1)} %add_add_fusion.1.tie_ref), channel_id=1, source_target_pairs={{0,16},{4,20},{8,24},{12,28},{16,0},{20,4},{24,8},{28,12},{1,17},{... | collective-permute-start | bytes 393224 | tf_op jit(solution)/shard_map/ppermute | solution.py:207
  23.2 16.7 %copy-start.2 = (bf16[512,512]{1,0:T(8,128)(2,1)S(1)}, bf16[512,512]{1,0:T(8,128)(2,1)}, u32[]{:S(2)}) copy-start(bf16[512,512]{1,0:T(8,128)(2,1)} %refs_11_.1) | copy-start | bytes 1572868
  23.2 16.6 %copy-start.1 = (bf16[512,512]{1,0:T(8,128)(2,1)S(1)}, bf16[512,512]{1,0:T(8,128)(2,1)}, u32[]{:S(2)}) copy-start(bf16[512,512]{1,0:T(8,128)(2,1)} %refs_10_.1) | copy-start | bytes 1572868
  23.3 7.3 %collective-permute-start.7 = (f32[64,512]{1,0:T(8,128)S(1)}, f32[64,512]{1,0:T(8,128)S(1)}, u32[]{:S(2)}, u32[]{:S(2)}) collective-permute-start(f32[64,512]{1,0:T(8,128)S(1)} %add.42.refs_0_), channel_id=1, source_target_pairs={{0,8},{4,12},{8,0},{12,4},{16,24},{20,28},{24,16},{28,20},{1,9},{5... | collective-permute-start | bytes 393224 | tf_op jit(solution)/shard_map/ppermute | solution.py:207
  23.6 9.1 %collective-permute-start.9 = (f32[64,512]{1,0:T(8,128)S(1)}, f32[64,512]{1,0:T(8,128)S(1)}, u32[]{:S(2)}, u32[]{:S(2)}) collective-permute-start(f32[64,512]{1,0:T(8,128)S(1)} %add_add_fusion), channel_id=1, source_target_pairs={{0,16},{4,20},{8,24},{12,28},{16,0},{20,4},{24,8},{28,12},{1,17},{... | collective-permute-start | bytes 393224 | tf_op jit(solution)/shard_map/ppermute | solution.py:207
  30.6 9.3 %copy-start.6 = (f32[512]{0:T(512)S(1)}, f32[512]{0:T(512)}, u32[]{:S(2)}) copy-start(f32[512]{0:T(512)} %param.18) | copy-start | bytes 6148
  30.6 9.3 %collective-permute-start.8 = (f32[128,512]{1,0:T(8,128)S(1)}, f32[128,512]{1,0:T(8,128)S(1)}, u32[]{:S(2)}, u32[]{:S(2)}) collective-permute-start(f32[128,512]{1,0:T(8,128)S(1)} %pad_maximum_fusion), channel_id=1, source_target_pairs={{0,4},{4,0},{8,12},{12,8},{16,20},{20,16},{24,28},{28,24},{1,5},{5... | collective-permute-start | bytes 786440 | tf_op jit(solution)/shard_map/ppermute | solution.py:207
  32.7 6.0 %collective-permute-start.12 = (f32[64,512]{1,0:T(8,128)S(1)}, f32[64,512]{1,0:T(8,128)S(1)}, u32[]{:S(2)}, u32[]{:S(2)}) collective-permute-start(f32[64,512]{1,0:T(8,128)S(1)} %add.43.refs_3_), channel_id=1, source_target_pairs={{0,12},{4,8},{8,4},{12,0},{16,28},{20,24},{24,20},{28,16},{1,13},{... | collective-permute-start | bytes 393224 | tf_op jit(solution)/shard_map/ppermute | solution.py:207
  33.0 6.9 %collective-permute-start.11 = (f32[64,512]{1,0:T(8,128)S(1)}, f32[64,512]{1,0:T(8,128)S(1)}, u32[]{:S(2)}, u32[]{:S(2)}) collective-permute-start(f32[64,512]{1,0:T(8,128)S(1)} %add.43.refs_3_), channel_id=1, source_target_pairs={{0,4},{4,0},{8,12},{12,8},{16,20},{20,16},{24,28},{28,24},{1,5},{5... | collective-permute-start | bytes 393224 | tf_op jit(solution)/shard_map/ppermute | solution.py:207
  33.8 6.1 %collective-permute-start.10 = (f32[64,512]{1,0:T(8,128)S(1)}, f32[64,512]{1,0:T(8,128)S(1)}, u32[]{:S(2)}, u32[]{:S(2)}) collective-permute-start(f32[64,512]{1,0:T(8,128)S(1)} %add.43.refs_3_), channel_id=1, source_target_pairs={{0,8},{4,12},{8,0},{12,4},{16,24},{20,28},{24,16},{28,20},{1,9},{5... | collective-permute-start | bytes 393224 | tf_op jit(solution)/shard_map/ppermute | solution.py:207
  43.2 1.4 %collective-permute-start.13 = (f32[64,512]{1,0:T(8,128)S(1)}, f32[64,512]{1,0:T(8,128)S(1)}, u32[]{:S(2)}, u32[]{:S(2)}) collective-permute-start(f32[64,512]{1,0:T(8,128)S(1)} %get-tuple-element.47), channel_id=1, source_target_pairs={{0,1},{1,0},{2,3},{3,2},{4,5},{5,4},{6,7},{7,6},{8,9},{9,8},{10,11... | collective-permute-start | bytes 393224 | tf_op jit(solution)/shard_map/ppermute | solution.py:207
  43.3 2.9 %collective-permute-start.15 = (f32[64,512]{1,0:T(8,128)S(1)}, f32[64,512]{1,0:T(8,128)S(1)}, u32[]{:S(2)}, u32[]{:S(2)}) collective-permute-start(f32[64,512]{1,0:T(8,128)S(1)} %get-tuple-element.49), channel_id=1, source_target_pairs={{0,1},{1,0},{2,3},{3,2},{4,5},{5,4},{6,7},{7,6},{8,9},{9,8},{10,11... | collective-permute-start | bytes 393224 | tf_op jit(solution)/shard_map/ppermute | solution.py:207
  44.6 6.4 %collective-permute-start.14 = (f32[64,512]{1,0:T(8,128)S(1)}, f32[64,512]{1,0:T(8,128)S(1)}, u32[]{:S(2)}, u32[]{:S(2)}) collective-permute-start(f32[64,512]{1,0:T(8,128)S(1)} %add.44), channel_id=1, source_target_pairs={{0,2},{1,3},{2,0},{3,1},{4,6},{5,7},{6,4},{7,5},{8,10},{9,11},{10,... | collective-permute-start | bytes 393224 | tf_op jit(solution)/shard_map/ppermute | solution.py:207
  46.2 8.3 %copy-start.3 = (bf16[512,512]{1,0:T(8,128)(2,1)S(1)}, bf16[512,512]{1,0:T(8,128)(2,1)}, u32[]{:S(2)}) copy-start(bf16[512,512]{1,0:T(8,128)(2,1)} %refs_6_.1) | copy-start | bytes 1572868
  46.2 8.3 %copy-start.4 = (bf16[512,512]{1,0:T(8,128)(2,1)S(1)}, bf16[512,512]{1,0:T(8,128)(2,1)}, u32[]{:S(2)}) copy-start(bf16[512,512]{1,0:T(8,128)(2,1)} %refs_7_.1) | copy-start | bytes 1572868
  46.2 6.9 %collective-permute-start.16 = (f32[64,512]{1,0:T(8,128)S(1)}, f32[64,512]{1,0:T(8,128)S(1)}, u32[]{:S(2)}, u32[]{:S(2)}) collective-permute-start(f32[64,512]{1,0:T(8,128)S(1)} %add.46), channel_id=1, source_target_pairs={{0,2},{1,3},{2,0},{3,1},{4,6},{5,7},{6,4},{7,5},{8,10},{9,11},{10,... | collective-permute-start | bytes 393224 | tf_op jit(solution)/shard_map/ppermute | solution.py:207
  51.1 2.1 %collective-permute-start.17 = (f32[64,512]{1,0:T(8,128)S(1)}, f32[64,512]{1,0:T(8,128)S(1)}, u32[]{:S(2)}, u32[]{:S(2)}) collective-permute-start(f32[64,512]{1,0:T(8,128)S(1)} %add.45.refs_0_), channel_id=1, source_target_pairs={{0,1},{1,0},{2,3},{3,2},{4,5},{5,4},{6,7},{7,6},{8,9},{9,8},{10,11... | collective-permute-start | bytes 393224 | tf_op jit(solution)/shard_map/ppermute | solution.py:207
  53.1 1.4 %copy-start.7 = (f32[512]{0:T(512)S(1)}, f32[512]{0:T(512)}, u32[]{:S(2)}) copy-start(f32[512]{0:T(512)} %param.19) | copy-start | bytes 6148
  53.1 1.4 %collective-permute-start.18 = (f32[64,512]{1,0:T(8,128)S(1)}, f32[64,512]{1,0:T(8,128)S(1)}, u32[]{:S(2)}, u32[]{:S(2)}) collective-permute-start(f32[64,512]{1,0:T(8,128)S(1)} %add.47.refs_1_), channel_id=1, source_target_pairs={{0,1},{1,0},{2,3},{3,2},{4,5},{5,4},{6,7},{7,6},{8,9},{9,8},{10,11... | collective-permute-start | bytes 393224 | tf_op jit(solution)/shard_map/ppermute | solution.py:207

commit v3 on v2

--- a/solution.py
+++ b/solution.py
@@ -9,11 +9,12 @@
 
 ATOM_DEV = 64
 GROUP = 4
-MASKS = (0, 2, 1, 3)
+NEAR, FAR, BOTH = 1, 2, 3
 SHARES = (4, 4)
-REDUCE_STEPWISE = (False, False)
-SPREAD_STEPWISE = (True, False)
+REDUCE_STEPWISE = (False, True)
+SPREAD_STEPWISE = (False, False)
 PIECES = 2
+PARTS = 2
 LANES = 128
 HIDE_FLOPS = 8 * 10**9
 VMEM_LIMIT = 40 * 1024 * 1024
@@ -39,9 +40,16 @@
     return [atoms // (GROUP * sum(SHARES)) * share for share in SHARES]
 
 
+def partner_mask(kind, core):
+    if kind in (NEAR, FAR) and core == 0:
+        return NEAR + FAR - kind
+    return kind
+
+
 def target_place(atoms, sizes):
     device = lax.axis_index("src")
-    own = (device // 2) % 2 + (device % 2) * 2
+    low, high = device % 2, (device // 2) % 2
+    own = jnp.where(lax.axis_index("tgt") % 2 == 0, high + 2 * low, low + 2 * high)
     place = atoms
     base = 0
     for size in sizes:
@@ -68,19 +76,24 @@
     place = jnp.where(lax.broadcasted_iota(jnp.int32, (1, rows), 1) < live, place, -1)
     slot = lax.broadcasted_iota(jnp.int32, (size * GROUP, rows), 0) + sum(sizes[:wave]) * GROUP
     chosen = one_hot(place, slot)
-    states = fetch()
+    total = fetch(chosen)
     at = 0
     for chunk_ref in chunk_refs:
         count = chunk_ref.shape[0]
-        chunk_ref[...] = jnp.dot(chosen[at : at + count], states, preferred_element_type=jnp.float32)
+        chunk_ref[...] = total[at : at + count]
         at += count
 
 
 def first_sum_kernel(sizes, live_hbm, target_hbm, state_hbm, *refs):
     *chunk_refs, live_out, target_ref, state_ref, live_ref, sems = refs
+    rows = state_ref.shape[0]
+    blocks = [pl.ds(first, rows // PARTS) for first in range(0, rows, rows // PARTS)]
     copies = [
         pltpu.make_async_copy(source, place, sems.at[index])
-        for index, (source, place) in enumerate(((live_hbm, live_ref), (target_hbm, target_ref), (state_hbm, state_ref)))
+        for index, (source, place) in enumerate(
+            [(live_hbm, live_ref), (target_hbm, target_ref)]
+            + [(state_hbm.at[block], state_ref.at[block]) for block in blocks]
+        )
     ]
     for copy in copies:
         copy.start()
@@ -89,15 +102,20 @@
     live_out[...] = jnp.full(live_out.shape, live, jnp.int32)
     copies[1].wait()
 
-    def fetch():
-        copies[2].wait()
-        return state_ref[...]
+    def fetch(chosen):
+        total = None
+        for index, block in enumerate(blocks):
+            copies[2 + index].wait()
+            part = slice(index * block.size, (index + 1) * block.size)
+            term = jnp.dot(chosen[:, part], state_ref[block, :], preferred_element_type=jnp.float32)
+            total = term if total is None else total + term
+        return total
 
     store_sums(0, sizes, live, target_ref[...], fetch, chunk_refs)
 
 
 def later_sum_kernel(wave, sizes, live_ref, target_ref, state_ref, *chunk_refs):
-    store_sums(wave, sizes, live_ref[:, :1], target_ref[...], lambda: state_ref[...], chunk_refs)
+    store_sums(wave, sizes, live_ref[:, :1], target_ref[...], lambda chosen: jnp.dot(chosen, state_ref[...], preferred_element_type=jnp.float32), chunk_refs)
 
 
 def chunk_shapes(wave, size, channels):
@@ -115,7 +133,7 @@
     out = call(
         functools.partial(first_sum_kernel, sizes), chunk_shapes(0, sizes[0], channels) + handed_on, [HBM] * 3,
         2 * sizes[0] * GROUP * rows * channels,
-        [pltpu.SMEM((1, 1), jnp.int32), pltpu.SemaphoreType.DMA((3,))],
+        [pltpu.SMEM((1, 1), jnp.int32), pltpu.SemaphoreType.DMA((2 + PARTS,))],
         limit=FIRST_VMEM_LIMIT,
     )(live, targets, states)
     return out[:-3], *out[-3:]
@@ -207,6 +225,19 @@
     return lax.ppermute(value, axis, [(i, i ^ mask) for i in range(lax.axis_size(axis))])
 
 
+def swap_group(value, kind):
+    across = lax.axis_size("tgt")
+    return lax.ppermute(
+        value,
+        ("src", "tgt"),
+        [
+            (i * across + j, (i ^ partner_mask(kind, j % 2)) * across + j)
+            for i in range(lax.axis_size("src"))
+            for j in range(across)
+        ],
+    )
+
+
 def higher_masks(axis, low):
     masks = []
     while low < lax.axis_size(axis):
@@ -221,18 +252,18 @@
 
 def spread(total, stepwise):
     if not stepwise:
-        return [total] + [swap(total, "src", mask) for mask in MASKS[1:]]
-    second = swap(total, "src", MASKS[1])
-    return [total, second, swap(jnp.concatenate([total, second]), "src", MASKS[2])]
+        return [total] + [swap_group(total, kind) for kind in (NEAR, FAR, BOTH)]
+    near = swap_group(total, NEAR)
+    return [total, near, swap_group(jnp.concatenate([total, near]), FAR)]
 
 
 def reduce(chunks, stepwise, ready):
     if not stepwise:
-        parts = ready([swap(chunk, "src", mask) for chunk, mask in zip(chunks[1:], MASKS[1:])])
+        parts = ready([swap_group(chunks[kind], kind) for kind in (BOTH, NEAR, FAR)])
         return chunks[0] + parts[0] + parts[1] + parts[2]
     size = chunks[0].shape[0]
-    part = swap(chunks[2], "src", MASKS[2])
-    return chunks[0] + part[:size] + ready(swap(chunks[1] + part[size:], "src", MASKS[1]))
+    part = swap_group(chunks[2], FAR)
+    return chunks[0] + part[:size] + ready(swap_group(chunks[1] + part[size:], NEAR))
 
 
 def target_totals(waves, between):
@@ -242,7 +273,6 @@
     sums = [first, second]
     for mask in higher_masks("src", GROUP):
         parts = [swap(value, "src", mask) for value in sums]
-        parts[0] = tie(parts[0], sums[1])
         sums = [value + part for value, part in zip(sums, parts)]
     return [chunk for value, stepwise in zip(sums, SPREAD_STEPWISE) for chunk in spread(value, stepwise)], made
 

time: 57.7 us -> 56.3 us (0.976)
  starting transfers between devices: 23.7 us -> 22.7 us
  Pallas kernels: 9.93 us -> 9.09 us
    ppermute x19 -> x8, starting transfers between devices: 23.7 us -> 6.74 us  [swap(): lax.ppermute(value, axis, [(i, i ^ mask) for i in range(lax.axis_size(axi...]
    ppermute x0 -> x11, starting transfers between devices: none -> 16 us  [swap_group(): lax.ppermute(value, ('src', 'tgt'), [(i * across + j, (i ^ partner_mask(k...]
    ppermute x0 -> x11, waiting for transfers between devices: none -> 13.1 us  [swap_group(): lax.ppermute(value, ('src', 'tgt'), [(i * across + j, (i ^ partner_mask(k...]
    ppermute x19 -> x8, waiting for transfers between devices: 22.8 us -> 10.1 us  [swap(): lax.ppermute(value, axis, [(i, i ^ mask) for i in range(lax.axis_size(axi...]
  transfers between devices with their start and end apart: 19 -> 19, of which waited for: 11 -> 13; matrix products, arithmetic and copies ran while one was open for 0% -> 0% of each run, Pallas kernels for 3% -> 2%
where the time goes in v3:
time: 56.3 us; the launch traced here: 56.1 us
  waiting for transfers between devices  23.2 us (41%)
  starting transfers between devices  22.7 us (40%)
  Pallas kernels  9.09 us (16%)
  between operations  0.81 us (1%)
    ppermute x11, starting transfers between devices, swap_group(): lax.ppermute(value, ('src', 'tgt'), [(i * across + j, (i ^ partner_mask(k...  16 us
    ppermute x11, waiting for transfers between devices, swap_group(): lax.ppermute(value, ('src', 'tgt'), [(i * across + j, (i ^ partner_mask(k...  13.1 us
    ppermute x8, waiting for transfers between devices, swap(): lax.ppermute(value, axis, [(i, i ^ mask) for i in range(lax.axis_size(axi...  10.1 us
    ppermute x8, starting transfers between devices, swap(): lax.ppermute(value, axis, [(i, i ^ mask) for i in range(lax.axis_size(axi...  6.74 us
    pallas_call x1, Pallas kernels, body(): call(functools.partial(layer_one_kernel, len(totals)), [jax.ShapeDtypeStr...  3.3 us
    pallas_call x1, Pallas kernels, body(): call(functools.partial(layer_two_kernel, len(totals)), jax.ShapeDtypeStru...  3.03 us
    pallas_call x1, Pallas kernels, first_sums(): call(functools.partial(first_sum_kernel, sizes), chunk_shapes(0, sizes[0]...  1.68 us
  transfers between devices with their start and end apart: 19, of which 13 were waited for; matrix products, arithmetic and copies ran while one was open for 0% of the time, Pallas kernels for 2%

profile of v3, /device:TPU:0, one launch (start us, length us, event | category | flops | bytes accessed | tf_op | source)
XLA Modules:
  0.0 56.1 jit_solution(15110802367740438187)
XLA Ops:
  0.7 0.0 copy-done
  0.7 1.7 %shard_map.100 = (f32[64,512]{1,0:T(8,128)S(1)}, f32[64,512]{1,0:T(8,128)S(1)}, f32[64,512]{1,0:T(8,128)S(1)}, f32[64,512]{1,0:T(8,128)S(1)}, s32[1,128]{1,0:T(1...) custom-call(s32[1,1]{1,0:T(1,128)S(6)} %copy.11.live_hbm, s32[1,1024]{1,0:T(1,128)S(1)} %bitcast.6, ...), custom_call_target="tpu_custom_call" | custom-call | flops 268435456 | tf_op jit(solution)/shard_map/pallas_call | solution.py:133
  2.4 4.0 %collective-permute-start = (f32[64,512]{1,0:T(8,128)S(1)}, f32[64,512]{1,0:T(8,128)S(1)}, u32[]{:S(2)}, u32[]{:S(2)}) collective-permute-start(f32[64,512]{1,0:T(8,128)S(1)} %get-tuple-element.26), channel_id=1, source_target_pairs={{0,12},{1,13},{2,14},{3,15},{4,8},{5,9},{6,10},{7,11},{8,4},{9,5},... | collective-permute-start | bytes 393224 | tf_op jit(solution)/shard_map/ppermute | solution.py:230
  6.4 0.4 collective-permute-start.1
  6.9 0.2 collective-permute-start.2
  7.1 0.5 shard_map.101
  7.6 1.9 %collective-permute-start.7 = (f32[128,512]{1,0:T(8,128)S(1)}, f32[128,512]{1,0:T(8,128)S(1)}, u32[]{:S(2)}, u32[]{:S(2)}) collective-permute-start(f32[128,512]{1,0:T(8,128)S(1)} %get-tuple-element.32), channel_id=1, source_target_pairs={{0,4},{1,9},{2,6},{3,11},{4,0},{5,13},{6,2},{7,15},{8,12},{9,1},{1... | collective-permute-start | bytes 786440 | tf_op jit(solution)/shard_map/ppermute | solution.py:230
  9.5 0.9 %collective-permute-done = f32[64,512]{1,0:T(8,128)S(1)} collective-permute-done((f32[64,512]{1,0:T(8,128)S(1)}, f32[64,512]{1,0:T(8,128)S(1)}, u32[]{:S(2)}, u32[]{:S(2)}) %collective-permute-start) | collective-permute-done | bytes 131104 | tf_op jit(solution)/shard_map/ppermute | solution.py:230
  10.3 3.7 %collective-permute-done.1 = f32[64,512]{1,0:T(8,128)S(1)} collective-permute-done((f32[64,512]{1,0:T(8,128)S(1)}, f32[64,512]{1,0:T(8,128)S(1)}, u32[]{:S(2)}, u32[]{:S(2)}) %collective-permute-start.1) | collective-permute-done | bytes 131104 | tf_op jit(solution)/shard_map/ppermute | solution.py:230
  14.0 0.0 collective-permute-done.2
  14.1 2.7 %collective-permute-start.3 = (f32[64,512]{1,0:T(8,128)S(1)}, f32[64,512]{1,0:T(8,128)S(1)}, u32[]{:S(2)}, u32[]{:S(2)}) collective-permute-start(f32[64,512]{1,0:T(8,128)S(1)} %add_add_fusion.tie_ref), channel_id=1, source_target_pairs={{0,16},{4,20},{8,24},{12,28},{16,0},{20,4},{24,8},{28,12},{1,17},{... | collective-permute-start | bytes 393224 | tf_op jit(solution)/shard_map/ppermute | solution.py:225
  16.7 0.0 collective-permute-done.7
  16.8 1.6 %collective-permute-start.8 = (f32[64,512]{1,0:T(8,128)S(1)}, f32[64,512]{1,0:T(8,128)S(1)}, u32[]{:S(2)}, u32[]{:S(2)}) collective-permute-start(f32[64,512]{1,0:T(8,128)S(1)} %slice_add_fusion), channel_id=1, source_target_pairs={{0,8},{1,5},{2,10},{3,7},{4,12},{5,1},{6,14},{7,3},{8,0},{9,13},{1... | collective-permute-start | bytes 393224 | tf_op jit(solution)/shard_map/ppermute | solution.py:230
  18.4 0.6 %shard_map.102 = (bf16[1024,512]{1,0:T(8,128)(2,1)S(1)}, bf16[1024,256]{1,0:T(8,128)(2,1)S(1)}, bf16[256,1024]{1,0:T(8,128)(2,1)S(1)}) custom-call(s32[1,1024]{1,0:T(1,128)S(1)} %get-tuple-element.29.target_ref, s32[1,1024]{1,0:T(1,128)S(1)} %bitcast.7, f32[64,512]{1,0:T(8,128)S(1)} %add_add_fusion.tie_ref), custom_call_target="tpu_custom_call" | custom-call | flops 8000000000 | tf_op jit(solution)/shard_map/pallas_call | solution.py:311
  19.0 3.6 %collective-permute-done.8 = f32[64,512]{1,0:T(8,128)S(1)} collective-permute-done((f32[64,512]{1,0:T(8,128)S(1)}, f32[64,512]{1,0:T(8,128)S(1)}, u32[]{:S(2)}, u32[]{:S(2)}) %collective-permute-start.8) | collective-permute-done | bytes 131104 | tf_op jit(solution)/shard_map/ppermute | solution.py:230
  22.6 0.0 copy-start.1
  22.6 1.2 %collective-permute-start.9 = (f32[64,512]{1,0:T(8,128)S(1)}, f32[64,512]{1,0:T(8,128)S(1)}, u32[]{:S(2)}, u32[]{:S(2)}) collective-permute-start(f32[64,512]{1,0:T(8,128)S(1)} %fusion), channel_id=1, source_target_pairs={{0,16},{4,20},{8,24},{12,28},{16,0},{20,4},{24,8},{28,12},{1,17},{... | collective-permute-start | bytes 393224 | tf_op jit(solution)/shard_map/ppermute | solution.py:225
  23.9 0.0 collective-permute-done.3
  23.9 0.0 copy-start.6
  23.9 2.7 %collective-permute-start.6 = (f32[64,512]{1,0:T(8,128)S(1)}, f32[64,512]{1,0:T(8,128)S(1)}, u32[]{:S(2)}, u32[]{:S(2)}) collective-permute-start(f32[64,512]{1,0:T(8,128)S(1)} %add.39.refs_0_), channel_id=1, source_target_pairs={{0,12},{1,13},{2,14},{3,15},{4,8},{5,9},{6,10},{7,11},{8,4},{9,5},... | collective-permute-start | bytes 393224 | tf_op jit(solution)/shard_map/ppermute | solution.py:230
  26.6 1.3 %collective-permute-start.5 = (f32[64,512]{1,0:T(8,128)S(1)}, f32[64,512]{1,0:T(8,128)S(1)}, u32[]{:S(2)}, u32[]{:S(2)}) collective-permute-start(f32[64,512]{1,0:T(8,128)S(1)} %add.39.refs_0_), channel_id=1, source_target_pairs={{0,4},{1,9},{2,6},{3,11},{4,0},{5,13},{6,2},{7,15},{8,12},{9,1},{1... | collective-permute-start | bytes 393224 | tf_op jit(solution)/shard_map/ppermute | solution.py:230
  27.9 0.0 collective-permute-start.4
  27.9 1.8 %collective-permute-done.9 = f32[64,512]{1,0:T(8,128)S(1)} collective-permute-done((f32[64,512]{1,0:T(8,128)S(1)}, f32[64,512]{1,0:T(8,128)S(1)}, u32[]{:S(2)}, u32[]{:S(2)}) %collective-permute-start.9) | collective-permute-done | bytes 131104 | tf_op jit(solution)/shard_map/ppermute | solution.py:225
  29.7 1.2 %collective-permute-start.12 = (f32[64,512]{1,0:T(8,128)S(1)}, f32[64,512]{1,0:T(8,128)S(1)}, u32[]{:S(2)}, u32[]{:S(2)}) collective-permute-start(f32[64,512]{1,0:T(8,128)S(1)} %add.43.refs_4_), channel_id=1, source_target_pairs={{0,12},{1,13},{2,14},{3,15},{4,8},{5,9},{6,10},{7,11},{8,4},{9,5},... | collective-permute-start | bytes 393224 | tf_op jit(solution)/shard_map/ppermute | solution.py:230
  31.0 1.4 %collective-permute-start.11 = (f32[64,512]{1,0:T(8,128)S(1)}, f32[64,512]{1,0:T(8,128)S(1)}, u32[]{:S(2)}, u32[]{:S(2)}) collective-permute-start(f32[64,512]{1,0:T(8,128)S(1)} %add.43.refs_4_), channel_id=1, source_target_pairs={{0,4},{1,9},{2,6},{3,11},{4,0},{5,13},{6,2},{7,15},{8,12},{9,1},{1... | collective-permute-start | bytes 393224 | tf_op jit(solution)/shard_map/ppermute | solution.py:230
  32.3 0.3 collective-permute-done.6.refs_3_
  32.7 1.2 %collective-permute-start.10 = (f32[64,512]{1,0:T(8,128)S(1)}, f32[64,512]{1,0:T(8,128)S(1)}, u32[]{:S(2)}, u32[]{:S(2)}) collective-permute-start(f32[64,512]{1,0:T(8,128)S(1)} %add.43.refs_4_), channel_id=1, source_target_pairs={{0,8},{1,5},{2,10},{3,7},{4,12},{5,1},{6,14},{7,3},{8,0},{9,13},{1... | collective-permute-start | bytes 393224 | tf_op jit(solution)/shard_map/ppermute | solution.py:230
  33.8 1.2 %collective-permute-done.5.refs_2_ = f32[64,512]{1,0:T(8,128)S(1)} collective-permute-done((f32[64,512]{1,0:T(8,128)S(1)}, f32[64,512]{1,0:T(8,128)S(1)}, u32[]{:S(2)}, u32[]{:S(2)}) %collective-permute-start.5) | collective-permute-done | bytes 131104 | tf_op jit(solution)/shard_map/ppermute | solution.py:230
  35.1 0.0 collective-permute-done.4.refs_1_
  35.1 2.3 %collective-permute-done.12.refs_7_ = f32[64,512]{1,0:T(8,128)S(1)} collective-permute-done((f32[64,512]{1,0:T(8,128)S(1)}, f32[64,512]{1,0:T(8,128)S(1)}, u32[]{:S(2)}, u32[]{:S(2)}) %collective-permute-start.12) | collective-permute-done | bytes 131104 | tf_op jit(solution)/shard_map/ppermute | solution.py:230
  37.4 0.8 %collective-permute-done.11.refs_6_ = f32[64,512]{1,0:T(8,128)S(1)} collective-permute-done((f32[64,512]{1,0:T(8,128)S(1)}, f32[64,512]{1,0:T(8,128)S(1)}, u32[]{:S(2)}, u32[]{:S(2)}) %collective-permute-start.11) | collective-permute-done | bytes 131104 | tf_op jit(solution)/shard_map/ppermute | solution.py:230
  38.2 0.3 collective-permute-done.10.refs_5_
  38.4 0.0 copy-done.2
  38.4 3.3 %shard_map.103 = (bf16[1024,512]{1,0:T(8,128)(2,1)S(1)}, f32[64,512]{1,0:T(8,128)S(1)}, f32[64,512]{1,0:T(8,128)S(1)}, f32[64,512]{1,0:T(8,128)S(1)}, f32[64,512]{1,0:T(8,128)S(1)}) custom-call(s32[1,128]{1,0:T(1,128)S(1)} %get-tuple-element.24.live_ref, f32[64,512]{1,0:T(8,128)S(1)} %add.39.refs_0_, f32[64,512]{1,0:T(8,128)S(1)} %collective-permute-done.4.refs_1_, ...), custom_call_target="tpu_custom_call" | custom-call | flops 2952790016 | tf_op jit(solution)/shard_map/pallas_call | solution.py:322
  41.7 0.1 collective-permute-start.13
  41.8 0.5 collective-permute-start.15
  42.3 0.8 %collective-permute-done.13 = f32[64,512]{1,0:T(8,128)S(1)} collective-permute-done((f32[64,512]{1,0:T(8,128)S(1)}, f32[64,512]{1,0:T(8,128)S(1)}, u32[]{:S(2)}, u32[]{:S(2)}) %collective-permute-start.13) | collective-permute-done | bytes 131104 | tf_op jit(solution)/shard_map/ppermute | solution.py:225
  43.2 1.7 %collective-permute-start.14 = (f32[64,512]{1,0:T(8,128)S(1)}, f32[64,512]{1,0:T(8,128)S(1)}, u32[]{:S(2)}, u32[]{:S(2)}) collective-permute-start(f32[64,512]{1,0:T(8,128)S(1)} %add.44), channel_id=1, source_target_pairs={{0,2},{1,3},{2,0},{3,1},{4,6},{5,7},{6,4},{7,5},{8,10},{9,11},{10,... | collective-permute-start | bytes 393224 | tf_op jit(solution)/shard_map/ppermute | solution.py:225
  44.8 0.0 collective-permute-done.15
  44.9 0.5 collective-permute-start.16
  45.4 4.2 %collective-permute-done.14 = f32[64,512]{1,0:T(8,128)S(1)} collective-permute-done((f32[64,512]{1,0:T(8,128)S(1)}, f32[64,512]{1,0:T(8,128)S(1)}, u32[]{:S(2)}, u32[]{:S(2)}) %collective-permute-start.14) | collective-permute-done | bytes 131104 | tf_op jit(solution)/shard_map/ppermute | solution.py:225
  49.6 0.1 collective-permute-start.17
  49.7 1.9 %collective-permute-done.16 = f32[64,512]{1,0:T(8,128)S(1)} collective-permute-done((f32[64,512]{1,0:T(8,128)S(1)}, f32[64,512]{1,0:T(8,128)S(1)}, u32[]{:S(2)}, u32[]{:S(2)}) %collective-permute-start.16) | collective-permute-done | bytes 131104 | tf_op jit(solution)/shard_map/ppermute | solution.py:225
  51.6 0.0 copy-start.7
  51.6 0.1 collective-permute-start.18
  51.7 0.0 collective-permute-done.17.refs_2_
  51.7 1.3 %collective-permute-done.18.refs_3_ = f32[64,512]{1,0:T(8,128)S(1)} collective-permute-done((f32[64,512]{1,0:T(8,128)S(1)}, f32[64,512]{1,0:T(8,128)S(1)}, u32[]{:S(2)}, u32[]{:S(2)}) %collective-permute-start.18) | collective-permute-done | bytes 131104 | tf_op jit(solution)/shard_map/ppermute | solution.py:225
  53.1 3.0 %shard_map.104 = bf16[1024,512]{1,0:T(8,128)(2,1)} custom-call(s32[1,128]{1,0:T(1,128)S(1)} %get-tuple-element.24.live_ref, f32[64,512]{1,0:T(8,128)S(1)} %add.45.refs_0_, f32[64,512]{1,0:T(8,128)S(1)} %add.47.refs_1_, f32[64,512]{1,0:T(8,128)S(1)} %collective-permute-done.17.refs_2_, f32[64,512]{1,0:T(8,128)S(1)} %collective-permute-done.18.refs_3_, ...), custom_call_target="tpu_custom_call" | custom-call | flops 1879048192 | tf_op jit(solution)/shard_map/pallas_call | solution.py:331
  (20 shorter events, 0.2 us)
Async XLA Ops:
  0.0 0.7 %copy-start = (s32[1,1,1024]{2,1,0:T(1,128)S(1)}, s32[1,1,1024]{2,1,0:T(1,128)}, u32[]{:S(2)}) copy-start(s32[1,1,1024]{2,1,0:T(1,128)} %param.12) | copy-start | bytes 12292
  2.4 8.0 %collective-permute-start = (f32[64,512]{1,0:T(8,128)S(1)}, f32[64,512]{1,0:T(8,128)S(1)}, u32[]{:S(2)}, u32[]{:S(2)}) collective-permute-start(f32[64,512]{1,0:T(8,128)S(1)} %get-tuple-element.26), channel_id=1, source_target_pairs={{0,12},{1,13},{2,14},{3,15},{4,8},{5,9},{6,10},{7,11},{8,4},{9,5},... | collective-permute-start | bytes 393224 | tf_op jit(solution)/shard_map/ppermute | solution.py:230
  6.4 7.6 %collective-permute-start.1 = (f32[64,512]{1,0:T(8,128)S(1)}, f32[64,512]{1,0:T(8,128)S(1)}, u32[]{:S(2)}, u32[]{:S(2)}) collective-permute-start(f32[64,512]{1,0:T(8,128)S(1)} %get-tuple-element.27), channel_id=1, source_target_pairs={{0,8},{1,5},{2,10},{3,7},{4,12},{5,1},{6,14},{7,3},{8,0},{9,13},{1... | collective-permute-start | bytes 393224 | tf_op jit(solution)/shard_map/ppermute | solution.py:230
  6.9 7.2 %collective-permute-start.2 = (f32[64,512]{1,0:T(8,128)S(1)}, f32[64,512]{1,0:T(8,128)S(1)}, u32[]{:S(2)}, u32[]{:S(2)}) collective-permute-start(f32[64,512]{1,0:T(8,128)S(1)} %get-tuple-element.28), channel_id=1, source_target_pairs={{0,4},{1,9},{2,6},{3,11},{4,0},{5,13},{6,2},{7,15},{8,12},{9,1},{1... | collective-permute-start | bytes 393224 | tf_op jit(solution)/shard_map/ppermute | solution.py:230
  7.6 9.2 %collective-permute-start.7 = (f32[128,512]{1,0:T(8,128)S(1)}, f32[128,512]{1,0:T(8,128)S(1)}, u32[]{:S(2)}, u32[]{:S(2)}) collective-permute-start(f32[128,512]{1,0:T(8,128)S(1)} %get-tuple-element.32), channel_id=1, source_target_pairs={{0,4},{1,9},{2,6},{3,11},{4,0},{5,13},{6,2},{7,15},{8,12},{9,1},{1... | collective-permute-start | bytes 786440 | tf_op jit(solution)/shard_map/ppermute | solution.py:230
  14.1 9.8 %collective-permute-start.3 = (f32[64,512]{1,0:T(8,128)S(1)}, f32[64,512]{1,0:T(8,128)S(1)}, u32[]{:S(2)}, u32[]{:S(2)}) collective-permute-start(f32[64,512]{1,0:T(8,128)S(1)} %add_add_fusion.tie_ref), channel_id=1, source_target_pairs={{0,16},{4,20},{8,24},{12,28},{16,0},{20,4},{24,8},{28,12},{1,17},{... | collective-permute-start | bytes 393224 | tf_op jit(solution)/shard_map/ppermute | solution.py:225
  16.7 1.7 %copy-start.5 = (s32[1,1,1024]{2,1,0:T(1,128)S(1)}, s32[1,1,1024]{2,1,0:T(1,128)}, u32[]{:S(2)}) copy-start(s32[1,1,1024]{2,1,0:T(1,128)} %param.11) | copy-start | bytes 12292
  16.8 5.8 %collective-permute-start.8 = (f32[64,512]{1,0:T(8,128)S(1)}, f32[64,512]{1,0:T(8,128)S(1)}, u32[]{:S(2)}, u32[]{:S(2)}) collective-permute-start(f32[64,512]{1,0:T(8,128)S(1)} %slice_add_fusion), channel_id=1, source_target_pairs={{0,8},{1,5},{2,10},{3,7},{4,12},{5,1},{6,14},{7,3},{8,0},{9,13},{1... | collective-permute-start | bytes 393224 | tf_op jit(solution)/shard_map/ppermute | solution.py:230
  22.6 15.8 %copy-start.2 = (bf16[512,512]{1,0:T(8,128)(2,1)S(1)}, bf16[512,512]{1,0:T(8,128)(2,1)}, u32[]{:S(2)}) copy-start(bf16[512,512]{1,0:T(8,128)(2,1)} %refs_12_.1) | copy-start | bytes 1572868
  22.6 15.8 %copy-start.1 = (bf16[512,512]{1,0:T(8,128)(2,1)S(1)}, bf16[512,512]{1,0:T(8,128)(2,1)}, u32[]{:S(2)}) copy-start(bf16[512,512]{1,0:T(8,128)(2,1)} %refs_11_.1) | copy-start | bytes 1572868
  22.6 7.1 %collective-permute-start.9 = (f32[64,512]{1,0:T(8,128)S(1)}, f32[64,512]{1,0:T(8,128)S(1)}, u32[]{:S(2)}, u32[]{:S(2)}) collective-permute-start(f32[64,512]{1,0:T(8,128)S(1)} %fusion), channel_id=1, source_target_pairs={{0,16},{4,20},{8,24},{12,28},{16,0},{20,4},{24,8},{28,12},{1,17},{... | collective-permute-start | bytes 393224 | tf_op jit(solution)/shard_map/ppermute | solution.py:225
  23.9 14.5 %copy-start.6 = (f32[512]{0:T(512)S(1)}, f32[512]{0:T(512)}, u32[]{:S(2)}) copy-start(f32[512]{0:T(512)} %param.18) | copy-start | bytes 6148
  23.9 8.8 %collective-permute-start.6 = (f32[64,512]{1,0:T(8,128)S(1)}, f32[64,512]{1,0:T(8,128)S(1)}, u32[]{:S(2)}, u32[]{:S(2)}) collective-permute-start(f32[64,512]{1,0:T(8,128)S(1)} %add.39.refs_0_), channel_id=1, source_target_pairs={{0,12},{1,13},{2,14},{3,15},{4,8},{5,9},{6,10},{7,11},{8,4},{9,5},... | collective-permute-start | bytes 393224 | tf_op jit(solution)/shard_map/ppermute | solution.py:230
  26.6 8.5 %collective-permute-start.5 = (f32[64,512]{1,0:T(8,128)S(1)}, f32[64,512]{1,0:T(8,128)S(1)}, u32[]{:S(2)}, u32[]{:S(2)}) collective-permute-start(f32[64,512]{1,0:T(8,128)S(1)} %add.39.refs_0_), channel_id=1, source_target_pairs={{0,4},{1,9},{2,6},{3,11},{4,0},{5,13},{6,2},{7,15},{8,12},{9,1},{1... | collective-permute-start | bytes 393224 | tf_op jit(solution)/shard_map/ppermute | solution.py:230
  27.9 7.2 %collective-permute-start.4 = (f32[64,512]{1,0:T(8,128)S(1)}, f32[64,512]{1,0:T(8,128)S(1)}, u32[]{:S(2)}, u32[]{:S(2)}) collective-permute-start(f32[64,512]{1,0:T(8,128)S(1)} %add.39.refs_0_), channel_id=1, source_target_pairs={{0,8},{1,5},{2,10},{3,7},{4,12},{5,1},{6,14},{7,3},{8,0},{9,13},{1... | collective-permute-start | bytes 393224 | tf_op jit(solution)/shard_map/ppermute | solution.py:230
  29.7 7.6 %collective-permute-start.12 = (f32[64,512]{1,0:T(8,128)S(1)}, f32[64,512]{1,0:T(8,128)S(1)}, u32[]{:S(2)}, u32[]{:S(2)}) collective-permute-start(f32[64,512]{1,0:T(8,128)S(1)} %add.43.refs_4_), channel_id=1, source_target_pairs={{0,12},{1,13},{2,14},{3,15},{4,8},{5,9},{6,10},{7,11},{8,4},{9,5},... | collective-permute-start | bytes 393224 | tf_op jit(solution)/shard_map/ppermute | solution.py:230
  31.0 7.2 %collective-permute-start.11 = (f32[64,512]{1,0:T(8,128)S(1)}, f32[64,512]{1,0:T(8,128)S(1)}, u32[]{:S(2)}, u32[]{:S(2)}) collective-permute-start(f32[64,512]{1,0:T(8,128)S(1)} %add.43.refs_4_), channel_id=1, source_target_pairs={{0,4},{1,9},{2,6},{3,11},{4,0},{5,13},{6,2},{7,15},{8,12},{9,1},{1... | collective-permute-start | bytes 393224 | tf_op jit(solution)/shard_map/ppermute | solution.py:230
  32.7 5.8 %collective-permute-start.10 = (f32[64,512]{1,0:T(8,128)S(1)}, f32[64,512]{1,0:T(8,128)S(1)}, u32[]{:S(2)}, u32[]{:S(2)}) collective-permute-start(f32[64,512]{1,0:T(8,128)S(1)} %add.43.refs_4_), channel_id=1, source_target_pairs={{0,8},{1,5},{2,10},{3,7},{4,12},{5,1},{6,14},{7,3},{8,0},{9,13},{1... | collective-permute-start | bytes 393224 | tf_op jit(solution)/shard_map/ppermute | solution.py:230
  41.7 1.4 %collective-permute-start.13 = (f32[64,512]{1,0:T(8,128)S(1)}, f32[64,512]{1,0:T(8,128)S(1)}, u32[]{:S(2)}, u32[]{:S(2)}) collective-permute-start(f32[64,512]{1,0:T(8,128)S(1)} %get-tuple-element.39), channel_id=1, source_target_pairs={{0,1},{1,0},{2,3},{3,2},{4,5},{5,4},{6,7},{7,6},{8,9},{9,8},{10,11... | collective-permute-start | bytes 393224 | tf_op jit(solution)/shard_map/ppermute | solution.py:225
  41.8 3.0 %collective-permute-start.15 = (f32[64,512]{1,0:T(8,128)S(1)}, f32[64,512]{1,0:T(8,128)S(1)}, u32[]{:S(2)}, u32[]{:S(2)}) collective-permute-start(f32[64,512]{1,0:T(8,128)S(1)} %get-tuple-element.41), channel_id=1, source_target_pairs={{0,1},{1,0},{2,3},{3,2},{4,5},{5,4},{6,7},{7,6},{8,9},{9,8},{10,11... | collective-permute-start | bytes 393224 | tf_op jit(solution)/shard_map/ppermute | solution.py:225
  43.2 6.4 %collective-permute-start.14 = (f32[64,512]{1,0:T(8,128)S(1)}, f32[64,512]{1,0:T(8,128)S(1)}, u32[]{:S(2)}, u32[]{:S(2)}) collective-permute-start(f32[64,512]{1,0:T(8,128)S(1)} %add.44), channel_id=1, source_target_pairs={{0,2},{1,3},{2,0},{3,1},{4,6},{5,7},{6,4},{7,5},{8,10},{9,11},{10,... | collective-permute-start | bytes 393224 | tf_op jit(solution)/shard_map/ppermute | solution.py:225
  44.8 8.2 %copy-start.3 = (bf16[512,512]{1,0:T(8,128)(2,1)S(1)}, bf16[512,512]{1,0:T(8,128)(2,1)}, u32[]{:S(2)}) copy-start(bf16[512,512]{1,0:T(8,128)(2,1)} %refs_6_.1) | copy-start | bytes 1572868
  44.8 8.2 %copy-start.4 = (bf16[512,512]{1,0:T(8,128)(2,1)S(1)}, bf16[512,512]{1,0:T(8,128)(2,1)}, u32[]{:S(2)}) copy-start(bf16[512,512]{1,0:T(8,128)(2,1)} %refs_7_.1) | copy-start | bytes 1572868
  44.9 6.7 %collective-permute-start.16 = (f32[64,512]{1,0:T(8,128)S(1)}, f32[64,512]{1,0:T(8,128)S(1)}, u32[]{:S(2)}, u32[]{:S(2)}) collective-permute-start(f32[64,512]{1,0:T(8,128)S(1)} %add.46), channel_id=1, source_target_pairs={{0,2},{1,3},{2,0},{3,1},{4,6},{5,7},{6,4},{7,5},{8,10},{9,11},{10,... | collective-permute-start | bytes 393224 | tf_op jit(solution)/shard_map/ppermute | solution.py:225
  49.6 2.1 %collective-permute-start.17 = (f32[64,512]{1,0:T(8,128)S(1)}, f32[64,512]{1,0:T(8,128)S(1)}, u32[]{:S(2)}, u32[]{:S(2)}) collective-permute-start(f32[64,512]{1,0:T(8,128)S(1)} %add.45.refs_0_), channel_id=1, source_target_pairs={{0,1},{1,0},{2,3},{3,2},{4,5},{5,4},{6,7},{7,6},{8,9},{9,8},{10,11... | collective-permute-start | bytes 393224 | tf_op jit(solution)/shard_map/ppermute | solution.py:225
  51.6 1.4 %copy-start.7 = (f32[512]{0:T(512)S(1)}, f32[512]{0:T(512)}, u32[]{:S(2)}) copy-start(f32[512]{0:T(512)} %param.19) | copy-start | bytes 6148
  51.6 1.4 %collective-permute-start.18 = (f32[64,512]{1,0:T(8,128)S(1)}, f32[64,512]{1,0:T(8,128)S(1)}, u32[]{:S(2)}, u32[]{:S(2)}) collective-permute-start(f32[64,512]{1,0:T(8,128)S(1)} %add.47.refs_1_), channel_id=1, source_target_pairs={{0,1},{1,0},{2,3},{3,2},{4,5},{5,4},{6,7},{7,6},{8,9},{9,8},{10,11... | collective-permute-start | bytes 393224 | tf_op jit(solution)/shard_map/ppermute | solution.py:225

commit v4 on v3

--- a/solution.py
+++ b/solution.py
@@ -13,25 +13,25 @@
 SHARES = (4, 4)
 REDUCE_STEPWISE = (False, True)
 SPREAD_STEPWISE = (False, False)
-PIECES = 2
+PIECES = (1, 1)
 PARTS = 2
 LANES = 128
 HIDE_FLOPS = 8 * 10**9
 VMEM_LIMIT = 40 * 1024 * 1024
-FIRST_VMEM_LIMIT = 52 * 1024 * 1024
 
 VMEM = pl.BlockSpec(memory_space=pltpu.VMEM)
 HBM = pl.BlockSpec(memory_space=pltpu.HBM)
-
-
-def call(kernel, out_shape, in_specs, flops, scratch=(), out_specs=None, limit=VMEM_LIMIT):
+SMEM = pl.BlockSpec(memory_space=pltpu.SMEM)
+
+
+def call(kernel, out_shape, in_specs, flops, scratch=(), out_specs=None):
     return pl.pallas_call(
         kernel,
         out_shape=out_shape,
         in_specs=in_specs,
         out_specs=jax.tree.map(lambda _: VMEM, out_shape) if out_specs is None else out_specs,
         scratch_shapes=list(scratch),
-        compiler_params=pltpu.CompilerParams(vmem_limit_bytes=limit),
+        compiler_params=pltpu.CompilerParams(vmem_limit_bytes=VMEM_LIMIT),
         cost_estimate=pl.CostEstimate(flops=flops, bytes_accessed=0, transcendentals=0),
     )
 
@@ -61,8 +61,21 @@
     return place
 
 
+def piece_sizes(half):
+    return [half // sum(PIECES) * piece for piece in PIECES]
+
+
 def source_place(atoms, half):
-    return jnp.bitwise_xor(atoms, (lax.axis_index("tgt") % 2) * half)
+    own = (lax.axis_index("tgt") % 2) * half
+    ours = jnp.bitwise_xor(atoms, own)
+    other = (ours >= half).astype(jnp.int32)
+    inside = ours - other * half
+    place = atoms
+    base = 0
+    for size in piece_sizes(half):
+        place = jnp.where(inside >= base, 2 * base + other * size + inside - base, place)
+        base += size
+    return place
 
 
 def one_hot(place, slot):
@@ -84,28 +97,26 @@
         at += count
 
 
-def first_sum_kernel(sizes, live_hbm, target_hbm, state_hbm, *refs):
-    *chunk_refs, live_out, target_ref, state_ref, live_ref, sems = refs
+def first_sum_kernel(sizes, live_ref, target_hbm, state_hbm, *refs):
+    *chunk_refs, live_out, target_ref, state_ref, sems = refs
     rows = state_ref.shape[0]
     blocks = [pl.ds(first, rows // PARTS) for first in range(0, rows, rows // PARTS)]
     copies = [
         pltpu.make_async_copy(source, place, sems.at[index])
         for index, (source, place) in enumerate(
-            [(live_hbm, live_ref), (target_hbm, target_ref)]
-            + [(state_hbm.at[block], state_ref.at[block]) for block in blocks]
+            [(target_hbm, target_ref)] + [(state_hbm.at[block], state_ref.at[block]) for block in blocks]
         )
     ]
     for copy in copies:
         copy.start()
-    copies[0].wait()
     live = live_ref[0, 0]
     live_out[...] = jnp.full(live_out.shape, live, jnp.int32)
-    copies[1].wait()
+    copies[0].wait()
 
     def fetch(chosen):
         total = None
         for index, block in enumerate(blocks):
-            copies[2 + index].wait()
+            copies[1 + index].wait()
             part = slice(index * block.size, (index + 1) * block.size)
             term = jnp.dot(chosen[:, part], state_ref[block, :], preferred_element_type=jnp.float32)
             total = term if total is None else total + term
@@ -115,7 +126,10 @@
 
 
 def later_sum_kernel(wave, sizes, live_ref, target_ref, state_ref, *chunk_refs):
-    store_sums(wave, sizes, live_ref[:, :1], target_ref[...], lambda chosen: jnp.dot(chosen, state_ref[...], preferred_element_type=jnp.float32), chunk_refs)
+    def fetch(chosen):
+        return jnp.dot(chosen, state_ref[...], preferred_element_type=jnp.float32)
+
+    store_sums(wave, sizes, live_ref[:, :1], target_ref[...], fetch, chunk_refs)
 
 
 def chunk_shapes(wave, size, channels):
@@ -131,11 +145,10 @@
         jax.ShapeDtypeStruct(states.shape, states.dtype),
     ]
     out = call(
-        functools.partial(first_sum_kernel, sizes), chunk_shapes(0, sizes[0], channels) + handed_on, [HBM] * 3,
+        functools.partial(first_sum_kernel, sizes), chunk_shapes(0, sizes[0], channels) + handed_on, [SMEM, HBM, HBM],
         2 * sizes[0] * GROUP * rows * channels,
-        [pltpu.SMEM((1, 1), jnp.int32), pltpu.SemaphoreType.DMA((2 + PARTS,))],
-        limit=FIRST_VMEM_LIMIT,
-    )(live, targets, states)
+        [pltpu.SemaphoreType.DMA((1 + PARTS,))],
+    )(live, *(pltpu.with_memory_space_constraint(value, pltpu.HBM) for value in (targets, states)))
     return out[:-3], *out[-3:]
 
 
@@ -147,16 +160,22 @@
     )(live, targets, states)
 
 
-def choose_kernel(sizes, half, target_ref, source_ref, tie_ref, target_chosen_ref, source_chosen_ref, source_pick_ref):
+def choose_kernel(sizes, half, target_ref, source_ref, tie_ref, *refs):
     del tie_ref
     rows = target_ref.shape[1]
     sources = source_place(source_ref[...], half)
-    for values, chosen_ref in ((target_place(target_ref[...], sizes), target_chosen_ref), (sources, source_chosen_ref)):
-        place = jnp.transpose(jnp.broadcast_to(values, (LANES, rows)))
-        lane = lax.broadcasted_iota(jnp.int32, (rows, LANES), 1)
-        for first in range(0, chosen_ref.shape[1], LANES):
-            chosen_ref[:, first : first + LANES] = one_hot(place, lane + first)
-    source_pick_ref[...] = one_hot(sources, lax.broadcasted_iota(jnp.int32, source_pick_ref.shape, 0))
+    pick_ref, refs = refs[0], refs[1:]
+    for place, part_refs in ((target_place(target_ref[...], sizes), refs[: len(sizes)]), (sources, refs[len(sizes) :])):
+        place = jnp.transpose(jnp.broadcast_to(place, (LANES, rows)))
+        base = 0
+        for part_ref in part_refs:
+            count = part_ref.shape[1]
+            for first in range(0, count, LANES):
+                width = min(LANES, count - first)
+                lane = lax.broadcasted_iota(jnp.int32, (rows, width), 1) + (base + first)
+                part_ref[:, first : first + width] = one_hot(place[:, :width], lane)
+            base += count
+    pick_ref[...] = one_hot(sources, lax.broadcasted_iota(jnp.int32, pick_ref.shape, 0))
 
 
 def split_sums(sum_refs, parts_ref):
@@ -172,12 +191,33 @@
         at += size
 
 
-def normed_activated(chosen_ref, parts_ref, state_ref, inner_ref, gain_ref):
+def gather(chosen_ref, parts_ref):
     chosen = chosen_ref[...]
-    gathered = jnp.dot(
+    return jnp.dot(
         jnp.concatenate([chosen, chosen, chosen], axis=1), parts_ref[...], preferred_element_type=jnp.float32
     )
-    message = gathered - state_ref[...].astype(jnp.float32)
+
+
+def gather_kernel(n_sums, *refs):
+    sum_refs = refs[:n_sums]
+    chosen_ref, gathered_ref, parts_ref = refs[n_sums:]
+    split_sums(sum_refs, parts_ref)
+    gathered_ref[...] = gather(chosen_ref, parts_ref)
+
+
+def gather_first(sums, chosen):
+    rows, count = chosen.shape
+    channels = sums[0].shape[1]
+    return call(
+        functools.partial(gather_kernel, len(sums)),
+        jax.ShapeDtypeStruct((rows, channels), jnp.float32),
+        [VMEM] * (len(sums) + 1), 6 * rows * count * channels,
+        [pltpu.VMEM((3 * count, channels), jnp.bfloat16)],
+    )(*sums, chosen)
+
+
+def normed_activated(gathered_ref, chosen_ref, parts_ref, state_ref, inner_ref, gain_ref):
+    message = gathered_ref[...] + gather(chosen_ref, parts_ref) - state_ref[...].astype(jnp.float32)
     mean_square = jnp.mean(message * message, axis=-1, keepdims=True)
     normed = message * lax.rsqrt(mean_square + 1e-05) * gain_ref[...]
     activated = jax.nn.relu(
@@ -194,21 +234,23 @@
 
 def layer_one_kernel(n_sums, live_ref, *refs):
     sum_refs = refs[:n_sums]
-    chosen_ref, pick_ref, state_ref, inner_ref, outer_ref, gain_ref, reverse_ref, *piece_refs, parts_ref = refs[n_sums:]
+    gathered_ref, chosen_ref, pick_ref, state_ref, inner_ref, outer_ref, gain_ref, reverse_ref, *piece_refs, parts_ref = refs[n_sums:]
     split_sums(sum_refs, parts_ref)
-    normed, activated = normed_activated(chosen_ref, parts_ref, state_ref, inner_ref, gain_ref)
+    normed, activated = normed_activated(gathered_ref, chosen_ref, parts_ref, state_ref, inner_ref, gain_ref)
     reverse_ref[...] = finish(normed, activated, outer_ref, live_ref, 0)
     total = jnp.dot(pick_ref[...], reverse_ref[...], preferred_element_type=jnp.float32)
-    size = piece_refs[0].shape[0]
-    for index, piece_ref in enumerate(piece_refs):
-        piece_ref[...] = total[index * size : (index + 1) * size]
+    at = 0
+    for piece_ref in piece_refs:
+        count = piece_ref.shape[0]
+        piece_ref[...] = total[at : at + count]
+        at += count
 
 
 def layer_two_kernel(n_sums, live_ref, *refs):
     sum_refs = refs[:n_sums]
-    chosen_ref, state_ref, inner_ref, outer_ref, gain_ref, final_hbm, parts_ref, final_ref, sems = refs[n_sums:]
+    gathered_ref, chosen_ref, state_ref, inner_ref, outer_ref, gain_ref, final_hbm, parts_ref, final_ref, sems = refs[n_sums:]
     split_sums(sum_refs, parts_ref)
-    normed, activated = normed_activated(chosen_ref, parts_ref, state_ref, inner_ref, gain_ref)
+    normed, activated = normed_activated(gathered_ref, chosen_ref, parts_ref, state_ref, inner_ref, gain_ref)
     block = final_ref.shape[0] // 2
     copies = []
     for index in range(2):
@@ -274,14 +316,14 @@
     for mask in higher_masks("src", GROUP):
         parts = [swap(value, "src", mask) for value in sums]
         sums = [value + part for value, part in zip(sums, parts)]
-    return [chunk for value, stepwise in zip(sums, SPREAD_STEPWISE) for chunk in spread(value, stepwise)], made
+    return [spread(value, stepwise) for value, stepwise in zip(sums, SPREAD_STEPWISE)], made
 
 
 def source_totals(pieces):
-    own = [mine + swap(theirs, "tgt", 1) for mine, theirs in zip(pieces[:PIECES], pieces[PIECES:])]
+    own = [mine + swap(theirs, "tgt", 1) for mine, theirs in pieces]
     for mask in higher_masks("tgt", 2):
         own = [value + swap(value, "tgt", mask) for value in own]
-    return own + [swap(value, "tgt", 1) for value in own]
+    return [[value, swap(value, "tgt", 1)] for value in own]
 
 
 def body(
@@ -307,39 +349,43 @@
     first, live, targets, states = first_sums(states, targets, live_edges, sizes)
     waves = [first] + [later_sums(states, targets, live, wave, sizes) for wave in range(1, len(sizes))]
 
+    pieces = piece_sizes(half)
+    n_waves = len(sizes)
+
     def choose(first):
         return call(
             functools.partial(choose_kernel, sizes, half),
-            [
-                jax.ShapeDtypeStruct((rows, target_atoms), jnp.bfloat16),
-                jax.ShapeDtypeStruct((rows, source_atoms), jnp.bfloat16),
-                jax.ShapeDtypeStruct((source_atoms, rows), jnp.bfloat16),
-            ],
+            [jax.ShapeDtypeStruct((source_atoms, rows), jnp.bfloat16)]
+            + [jax.ShapeDtypeStruct((rows, GROUP * size), jnp.bfloat16) for size in sizes]
+            + [jax.ShapeDtypeStruct((rows, 2 * size), jnp.bfloat16) for size in pieces],
             [VMEM] * 3, HIDE_FLOPS,
         )(targets, sources, first)
 
-    totals, (target_chosen, source_chosen, source_pick) = target_totals(waves, choose)
-    reverse_state, *pieces = call(
-        functools.partial(layer_one_kernel, len(totals)),
+    totals, (source_pick, *chosen) = target_totals(waves, choose)
+    target_chosen, source_chosen = chosen[:n_waves], chosen[n_waves:]
+    gathered = gather_first(totals[0], target_chosen[0])
+    reverse_state, *sums = call(
+        functools.partial(layer_one_kernel, len(totals[1])),
         [jax.ShapeDtypeStruct((rows, channels), jnp.bfloat16)]
-        + [jax.ShapeDtypeStruct((half // PIECES, channels), jnp.float32)] * (2 * PIECES),
-        [VMEM] * (len(totals) + 7),
-        2 * rows * channels * (3 * target_atoms + 2 * channels + source_atoms),
-        [pltpu.VMEM((3 * target_atoms, channels), jnp.bfloat16)],
-    )(live, *totals, target_chosen, source_pick, states, inner_one, outer_one, gain_one.reshape(1, channels))
-    totals = source_totals(pieces)
+        + [jax.ShapeDtypeStruct((size, channels), jnp.float32) for size in pieces for _ in range(2)],
+        [VMEM] * (len(totals[1]) + 8),
+        2 * rows * channels * (3 * GROUP * sizes[1] + 2 * channels + source_atoms),
+        [pltpu.VMEM((3 * GROUP * sizes[1], channels), jnp.bfloat16)],
+    )(live, *totals[1], gathered, target_chosen[1], source_pick, states, inner_one, outer_one, gain_one.reshape(1, channels))
+    totals = source_totals(list(zip(sums[::2], sums[1::2])))
+    gathered = gather_first(totals[0], source_chosen[0])
     final_state = call(
-        functools.partial(layer_two_kernel, len(totals)),
+        functools.partial(layer_two_kernel, len(totals[1])),
         jax.ShapeDtypeStruct((rows, channels), jnp.bfloat16),
-        [VMEM] * (len(totals) + 6),
-        2 * rows * channels * (3 * source_atoms + 2 * channels),
+        [VMEM] * (len(totals[1]) + 7),
+        2 * rows * channels * (6 * pieces[1] + 2 * channels),
         [
-            pltpu.VMEM((3 * source_atoms, channels), jnp.bfloat16),
+            pltpu.VMEM((6 * pieces[1], channels), jnp.bfloat16),
             pltpu.VMEM((rows, channels), jnp.bfloat16),
             pltpu.SemaphoreType.DMA((2,)),
         ],
         HBM,
-    )(live, *totals, source_chosen, reverse_state, inner_two, outer_two, gain_two.reshape(1, channels))
+    )(live, *totals[1], gathered, source_chosen[1], reverse_state, inner_two, outer_two, gain_two.reshape(1, channels))
     return final_state.reshape(1, 1, rows, channels)
 
 

time: 56.3 us -> 55.4 us (0.984)
  waiting for transfers between devices: 23.2 us -> 21.5 us
  Pallas kernels: 9.09 us -> 9.9 us
    ppermute x11, waiting for transfers between devices: 13.1 us -> 12.1 us  [swap_group(): lax.ppermute(value, ('src', 'tgt'), [(i * across + j, (i ^ partner_mask(k...]
    pallas_call x2 -> x4, Pallas kernels: 6.33 us -> 7.16 us  [the longest x1 2.87 us: body(): call(functools.partial(layer_two_kernel, len(totals[1])), jax.ShapeDtypeS...]
    ppermute x8, waiting for transfers between devices: 10.1 us -> 9.42 us  [swap(): lax.ppermute(value, axis, [(i, i ^ mask) for i in range(lax.axis_size(axi...]
  transfers between devices with their start and end apart: 19 -> 19, of which waited for: 13 -> 13; matrix products, arithmetic and copies ran while one was open for 0% -> 0% of each run, Pallas kernels for 2% -> 5%
where the time goes in v4:
time: 55.4 us; the launch traced here: 55.2 us
  starting transfers between devices  22.7 us (41%)
  waiting for transfers between devices  21.5 us (39%)
  Pallas kernels  9.9 us (18%)
  between operations  0.82 us (1%)
    ppermute x11, starting transfers between devices, swap_group(): lax.ppermute(value, ('src', 'tgt'), [(i * across + j, (i ^ partner_mask(k...  16 us
    ppermute x11, waiting for transfers between devices, swap_group(): lax.ppermute(value, ('src', 'tgt'), [(i * across + j, (i ^ partner_mask(k...  12.1 us
    ppermute x8, waiting for transfers between devices, swap(): lax.ppermute(value, axis, [(i, i ^ mask) for i in range(lax.axis_size(axi...  9.42 us
    ppermute x8, starting transfers between devices, swap(): lax.ppermute(value, axis, [(i, i ^ mask) for i in range(lax.axis_size(axi...  6.74 us
    pallas_call x1, Pallas kernels, body(): call(functools.partial(layer_two_kernel, len(totals[1])), jax.ShapeDtypeS...  2.87 us
    pallas_call x1, Pallas kernels, body(): call(functools.partial(layer_one_kernel, len(totals[1])), [jax.ShapeDtype...  2.57 us
    pallas_call x2, Pallas kernels, gather_first(): call(functools.partial(gather_kernel, len(sums)), jax.ShapeDtypeStruct((r...  1.71 us
    pallas_call x1, Pallas kernels, first_sums(): call(functools.partial(first_sum_kernel, sizes), chunk_shapes(0, sizes[0]...  1.68 us
  transfers between devices with their start and end apart: 19, of which 13 were waited for; matrix products, arithmetic and copies ran while one was open for 0% of the time, Pallas kernels for 5%

profile of v4, /device:TPU:0, one launch (start us, length us, event | category | flops | bytes accessed | tf_op | source)
XLA Modules:
  0.0 55.2 jit_solution(11312466802803580483)
XLA Ops:
  0.7 1.7 %shard_map.100 = (f32[64,512]{1,0:T(8,128)S(1)}, f32[64,512]{1,0:T(8,128)S(1)}, f32[64,512]{1,0:T(8,128)S(1)}, f32[64,512]{1,0:T(8,128)S(1)}, s32[1,128]{1,0:T(1...) custom-call(s32[1,1]{1,0:T(1,128)S(6)} %copy.11.live_ref, s32[1,1024]{1,0:T(1,128)} %bitcast.10, ...), custom_call_target="tpu_custom_call" | custom-call | flops 268435456 | tf_op jit(solution)/shard_map/pallas_call | solution.py:147
  2.4 4.0 %collective-permute-start.2 = (f32[64,512]{1,0:T(8,128)S(1)}, f32[64,512]{1,0:T(8,128)S(1)}, u32[]{:S(2)}, u32[]{:S(2)}) collective-permute-start(f32[64,512]{1,0:T(8,128)S(1)} %get-tuple-element.33), channel_id=1, source_target_pairs={{0,12},{1,13},{2,14},{3,15},{4,8},{5,9},{6,10},{7,11},{8,4},{9,5},... | collective-permute-start | bytes 393224 | tf_op jit(solution)/shard_map/ppermute | solution.py:272
  6.4 0.4 collective-permute-start.3
  6.9 0.2 collective-permute-start.4
  7.0 0.5 shard_map.101
  7.5 1.9 %collective-permute-start = (f32[128,512]{1,0:T(8,128)S(1)}, f32[128,512]{1,0:T(8,128)S(1)}, u32[]{:S(2)}, u32[]{:S(2)}) collective-permute-start(f32[128,512]{1,0:T(8,128)S(1)} %get-tuple-element.30), channel_id=1, source_target_pairs={{0,4},{1,9},{2,6},{3,11},{4,0},{5,13},{6,2},{7,15},{8,12},{9,1},{1... | collective-permute-start | bytes 786440 | tf_op jit(solution)/shard_map/ppermute | solution.py:272
  9.4 0.9 %collective-permute-done.2 = f32[64,512]{1,0:T(8,128)S(1)} collective-permute-done((f32[64,512]{1,0:T(8,128)S(1)}, f32[64,512]{1,0:T(8,128)S(1)}, u32[]{:S(2)}, u32[]{:S(2)}) %collective-permute-start.2) | collective-permute-done | bytes 131104 | tf_op jit(solution)/shard_map/ppermute | solution.py:272
  10.3 3.7 %collective-permute-done.3 = f32[64,512]{1,0:T(8,128)S(1)} collective-permute-done((f32[64,512]{1,0:T(8,128)S(1)}, f32[64,512]{1,0:T(8,128)S(1)}, u32[]{:S(2)}, u32[]{:S(2)}) %collective-permute-start.3) | collective-permute-done | bytes 131104 | tf_op jit(solution)/shard_map/ppermute | solution.py:272
  14.0 0.0 collective-permute-done.4
  14.1 2.7 %collective-permute-start.9 = (f32[64,512]{1,0:T(8,128)S(1)}, f32[64,512]{1,0:T(8,128)S(1)}, u32[]{:S(2)}, u32[]{:S(2)}) collective-permute-start(f32[64,512]{1,0:T(8,128)S(1)} %add_add_fusion.tie_ref), channel_id=1, source_target_pairs={{0,16},{4,20},{8,24},{12,28},{16,0},{20,4},{24,8},{28,12},{1,17},{... | collective-permute-start | bytes 393224 | tf_op jit(solution)/shard_map/ppermute | solution.py:267
  16.7 0.0 collective-permute-done
  16.8 1.6 %collective-permute-start.1 = (f32[64,512]{1,0:T(8,128)S(1)}, f32[64,512]{1,0:T(8,128)S(1)}, u32[]{:S(2)}, u32[]{:S(2)}) collective-permute-start(f32[64,512]{1,0:T(8,128)S(1)} %slice_add_fusion), channel_id=1, source_target_pairs={{0,8},{1,5},{2,10},{3,7},{4,12},{5,1},{6,14},{7,3},{8,0},{9,13},{1... | collective-permute-start | bytes 393224 | tf_op jit(solution)/shard_map/ppermute | solution.py:272
  18.4 0.6 %shard_map.102 = (bf16[256,1024]{1,0:T(8,128)(2,1)S(1)}, bf16[1024,256]{1,0:T(8,128)(2,1)S(1)}, bf16[1024,256]{1,0:T(8,128)(2,1)S(1)}, bf16[1024,128]{1,0:T(8,128)(2,1)S(1)}, bf16[1024,128]{1,0:T(8,128)(2,1)S(1)}) custom-call(s32[1,1024]{1,0:T(1,128)S(1)} %get-tuple-element.27.target_ref, s32[1,1024]{1,0:T(1,128)S(1)} %bitcast.7, ...), custom_call_target="tpu_custom_call" | custom-call | flops 8000000000 | tf_op jit(solution)/shard_map/pallas_call | solution.py:356
  19.0 3.6 %collective-permute-done.1 = f32[64,512]{1,0:T(8,128)S(1)} collective-permute-done((f32[64,512]{1,0:T(8,128)S(1)}, f32[64,512]{1,0:T(8,128)S(1)}, u32[]{:S(2)}, u32[]{:S(2)}) %collective-permute-start.1) | collective-permute-done | bytes 131104 | tf_op jit(solution)/shard_map/ppermute | solution.py:272
  22.6 0.0 copy-start.3
  22.6 0.0 copy-start.4
  22.6 0.0 copy-start.6
  22.7 1.2 %collective-permute-start.5 = (f32[64,512]{1,0:T(8,128)S(1)}, f32[64,512]{1,0:T(8,128)S(1)}, u32[]{:S(2)}, u32[]{:S(2)}) collective-permute-start(f32[64,512]{1,0:T(8,128)S(1)} %fusion), channel_id=1, source_target_pairs={{0,16},{4,20},{8,24},{12,28},{16,0},{20,4},{24,8},{28,12},{1,17},{... | collective-permute-start | bytes 393224 | tf_op jit(solution)/shard_map/ppermute | solution.py:267
  23.9 0.0 collective-permute-done.9
  23.9 2.7 %collective-permute-start.12 = (f32[64,512]{1,0:T(8,128)S(1)}, f32[64,512]{1,0:T(8,128)S(1)}, u32[]{:S(2)}, u32[]{:S(2)}) collective-permute-start(f32[64,512]{1,0:T(8,128)S(1)} %add.43.refs_0_), channel_id=1, source_target_pairs={{0,12},{1,13},{2,14},{3,15},{4,8},{5,9},{6,10},{7,11},{8,4},{9,5},... | collective-permute-start | bytes 393224 | tf_op jit(solution)/shard_map/ppermute | solution.py:272
  26.6 1.3 %collective-permute-start.11 = (f32[64,512]{1,0:T(8,128)S(1)}, f32[64,512]{1,0:T(8,128)S(1)}, u32[]{:S(2)}, u32[]{:S(2)}) collective-permute-start(f32[64,512]{1,0:T(8,128)S(1)} %add.43.refs_0_), channel_id=1, source_target_pairs={{0,4},{1,9},{2,6},{3,11},{4,0},{5,13},{6,2},{7,15},{8,12},{9,1},{1... | collective-permute-start | bytes 393224 | tf_op jit(solution)/shard_map/ppermute | solution.py:272
  27.9 0.0 collective-permute-start.10
  27.9 1.8 %collective-permute-done.5 = f32[64,512]{1,0:T(8,128)S(1)} collective-permute-done((f32[64,512]{1,0:T(8,128)S(1)}, f32[64,512]{1,0:T(8,128)S(1)}, u32[]{:S(2)}, u32[]{:S(2)}) %collective-permute-start.5) | collective-permute-done | bytes 131104 | tf_op jit(solution)/shard_map/ppermute | solution.py:267
  29.7 1.2 %collective-permute-start.8 = (f32[64,512]{1,0:T(8,128)S(1)}, f32[64,512]{1,0:T(8,128)S(1)}, u32[]{:S(2)}, u32[]{:S(2)}) collective-permute-start(f32[64,512]{1,0:T(8,128)S(1)} %add.42.refs_0_), channel_id=1, source_target_pairs={{0,12},{1,13},{2,14},{3,15},{4,8},{5,9},{6,10},{7,11},{8,4},{9,5},... | collective-permute-start | bytes 393224 | tf_op jit(solution)/shard_map/ppermute | solution.py:272
  31.0 1.4 %collective-permute-start.7 = (f32[64,512]{1,0:T(8,128)S(1)}, f32[64,512]{1,0:T(8,128)S(1)}, u32[]{:S(2)}, u32[]{:S(2)}) collective-permute-start(f32[64,512]{1,0:T(8,128)S(1)} %add.42.refs_0_), channel_id=1, source_target_pairs={{0,4},{1,9},{2,6},{3,11},{4,0},{5,13},{6,2},{7,15},{8,12},{9,1},{1... | collective-permute-start | bytes 393224 | tf_op jit(solution)/shard_map/ppermute | solution.py:272
  32.4 0.3 collective-permute-done.12.refs_3_
  32.7 1.2 %collective-permute-start.6 = (f32[64,512]{1,0:T(8,128)S(1)}, f32[64,512]{1,0:T(8,128)S(1)}, u32[]{:S(2)}, u32[]{:S(2)}) collective-permute-start(f32[64,512]{1,0:T(8,128)S(1)} %add.42.refs_0_), channel_id=1, source_target_pairs={{0,8},{1,5},{2,10},{3,7},{4,12},{5,1},{6,14},{7,3},{8,0},{9,13},{1... | collective-permute-start | bytes 393224 | tf_op jit(solution)/shard_map/ppermute | solution.py:272
  33.8 1.2 %collective-permute-done.11.refs_2_ = f32[64,512]{1,0:T(8,128)S(1)} collective-permute-done((f32[64,512]{1,0:T(8,128)S(1)}, f32[64,512]{1,0:T(8,128)S(1)}, u32[]{:S(2)}, u32[]{:S(2)}) %collective-permute-start.11) | collective-permute-done | bytes 131104 | tf_op jit(solution)/shard_map/ppermute | solution.py:272
  35.1 0.0 collective-permute-done.10.refs_1_
  35.1 1.0 %shard_map.103.refs_4_ = f32[1024,512]{1,0:T(8,128)S(1)} custom-call(f32[64,512]{1,0:T(8,128)S(1)} %add.43.refs_0_, f32[64,512]{1,0:T(8,128)S(1)} %collective-permute-done.10.refs_1_, f32[64,512]{1,0:T(8,128)S(1)} %collective-permute-done.11.refs_2_, f32[64,512]{1,0:T(8,128)S(1)} %collective-permute-done.12.refs_3_, ...), custom_call_target="tpu_custom_call" | custom-call | flops 805306368 | tf_op jit(solution)/shard_map/pallas_call | solution.py:211
  36.1 1.3 %collective-permute-done.8.refs_3_ = f32[64,512]{1,0:T(8,128)S(1)} collective-permute-done((f32[64,512]{1,0:T(8,128)S(1)}, f32[64,512]{1,0:T(8,128)S(1)}, u32[]{:S(2)}, u32[]{:S(2)}) %collective-permute-start.8) | collective-permute-done | bytes 131104 | tf_op jit(solution)/shard_map/ppermute | solution.py:272
  37.4 0.8 %collective-permute-done.7.refs_2_ = f32[64,512]{1,0:T(8,128)S(1)} collective-permute-done((f32[64,512]{1,0:T(8,128)S(1)}, f32[64,512]{1,0:T(8,128)S(1)}, u32[]{:S(2)}, u32[]{:S(2)}) %collective-permute-start.7) | collective-permute-done | bytes 131104 | tf_op jit(solution)/shard_map/ppermute | solution.py:272
  38.2 0.3 collective-permute-done.6.refs_1_
  38.4 2.6 %shard_map.104 = (bf16[1024,512]{1,0:T(8,128)(2,1)S(1)}, f32[64,512]{1,0:T(8,128)S(1)}, f32[64,512]{1,0:T(8,128)S(1)}, f32[64,512]{1,0:T(8,128)S(1)}, f32[64,512]{1,0:T(8,128)S(1)}) custom-call(s32[1,128]{1,0:T(1,128)S(1)} %get-tuple-element.26.live_ref, f32[64,512]{1,0:T(8,128)S(1)} %add.42.refs_0_, f32[64,512]{1,0:T(8,128)S(1)} %collective-permute-done.6.refs_1_, ...), custom_call_target="tpu_custom_call" | custom-call | flops 2147483648 | tf_op jit(solution)/shard_map/pallas_call | solution.py:367
  41.0 0.1 collective-permute-start.16
  41.1 0.5 collective-permute-start.13
  41.6 0.8 %collective-permute-done.16 = f32[64,512]{1,0:T(8,128)S(1)} collective-permute-done((f32[64,512]{1,0:T(8,128)S(1)}, f32[64,512]{1,0:T(8,128)S(1)}, u32[]{:S(2)}, u32[]{:S(2)}) %collective-permute-start.16) | collective-permute-done | bytes 131104 | tf_op jit(solution)/shard_map/ppermute | solution.py:267
  42.5 1.6 %collective-permute-start.17 = (f32[64,512]{1,0:T(8,128)S(1)}, f32[64,512]{1,0:T(8,128)S(1)}, u32[]{:S(2)}, u32[]{:S(2)}) collective-permute-start(f32[64,512]{1,0:T(8,128)S(1)} %add.46), channel_id=1, source_target_pairs={{0,2},{1,3},{2,0},{3,1},{4,6},{5,7},{6,4},{7,5},{8,10},{9,11},{10,... | collective-permute-start | bytes 393224 | tf_op jit(solution)/shard_map/ppermute | solution.py:267
  44.0 0.0 collective-permute-done.13
  44.0 0.6 %collective-permute-start.14 = (f32[64,512]{1,0:T(8,128)S(1)}, f32[64,512]{1,0:T(8,128)S(1)}, u32[]{:S(2)}, u32[]{:S(2)}) collective-permute-start(f32[64,512]{1,0:T(8,128)S(1)} %add.44), channel_id=1, source_target_pairs={{0,2},{1,3},{2,0},{3,1},{4,6},{5,7},{6,4},{7,5},{8,10},{9,11},{10,... | collective-permute-start | bytes 393224 | tf_op jit(solution)/shard_map/ppermute | solution.py:267
  44.6 4.2 %collective-permute-done.17 = f32[64,512]{1,0:T(8,128)S(1)} collective-permute-done((f32[64,512]{1,0:T(8,128)S(1)}, f32[64,512]{1,0:T(8,128)S(1)}, u32[]{:S(2)}, u32[]{:S(2)}) %collective-permute-start.17) | collective-permute-done | bytes 131104 | tf_op jit(solution)/shard_map/ppermute | solution.py:267
  48.9 0.1 collective-permute-start.18
  49.0 1.9 %collective-permute-done.14 = f32[64,512]{1,0:T(8,128)S(1)} collective-permute-done((f32[64,512]{1,0:T(8,128)S(1)}, f32[64,512]{1,0:T(8,128)S(1)}, u32[]{:S(2)}, u32[]{:S(2)}) %collective-permute-start.14) | collective-permute-done | bytes 131104 | tf_op jit(solution)/shard_map/ppermute | solution.py:267
  50.9 0.1 collective-permute-start.15
  51.0 0.0 collective-permute-done.18.refs_1_
  51.0 0.7 %shard_map.105.refs_2_ = f32[1024,512]{1,0:T(8,128)S(1)} custom-call(f32[64,512]{1,0:T(8,128)S(1)} %add.47.refs_0_, f32[64,512]{1,0:T(8,128)S(1)} %collective-permute-done.18.refs_1_, bf16[1024,128]{1,0:T(8,128)(2,1)S(1)} %get-tuple-element.39.refs_2_), custom_call_target="tpu_custom_call" | custom-call | flops 402653184 | tf_op jit(solution)/shard_map/pallas_call | solution.py:211
  51.7 0.6 %collective-permute-done.15.refs_1_ = f32[64,512]{1,0:T(8,128)S(1)} collective-permute-done((f32[64,512]{1,0:T(8,128)S(1)}, f32[64,512]{1,0:T(8,128)S(1)}, u32[]{:S(2)}, u32[]{:S(2)}) %collective-permute-start.15) | collective-permute-done | bytes 131104 | tf_op jit(solution)/shard_map/ppermute | solution.py:267
  52.3 2.9 %shard_map.106 = bf16[1024,512]{1,0:T(8,128)(2,1)} custom-call(s32[1,128]{1,0:T(1,128)S(1)} %get-tuple-element.26.live_ref, f32[64,512]{1,0:T(8,128)S(1)} %add.45.refs_0_, f32[64,512]{1,0:T(8,128)S(1)} %collective-permute-done.15.refs_1_, f32[1024,512]{1,0:T(8,128)S(1)} %shard_map.105.refs_2_, bf16[1024,128]{1,0:T(8,128)(2,1)S(1)} %get-tuple-element.40.refs_3_, ...), custom_call_target="tpu_custom_call" | custom-call | flops 1476395008 | tf_op jit(solution)/shard_map/pallas_call | solution.py:377
  (20 shorter events, 0.2 us)
Async XLA Ops:
  0.0 18.4 %copy-start.5 = (s32[1,1,1024]{2,1,0:T(1,128)S(1)}, s32[1,1,1024]{2,1,0:T(1,128)}, u32[]{:S(2)}) copy-start(s32[1,1,1024]{2,1,0:T(1,128)} %param.11) | copy-start | bytes 12292
  2.4 8.0 %collective-permute-start.2 = (f32[64,512]{1,0:T(8,128)S(1)}, f32[64,512]{1,0:T(8,128)S(1)}, u32[]{:S(2)}, u32[]{:S(2)}) collective-permute-start(f32[64,512]{1,0:T(8,128)S(1)} %get-tuple-element.33), channel_id=1, source_target_pairs={{0,12},{1,13},{2,14},{3,15},{4,8},{5,9},{6,10},{7,11},{8,4},{9,5},... | collective-permute-start | bytes 393224 | tf_op jit(solution)/shard_map/ppermute | solution.py:272
  6.4 7.6 %collective-permute-start.3 = (f32[64,512]{1,0:T(8,128)S(1)}, f32[64,512]{1,0:T(8,128)S(1)}, u32[]{:S(2)}, u32[]{:S(2)}) collective-permute-start(f32[64,512]{1,0:T(8,128)S(1)} %get-tuple-element.34), channel_id=1, source_target_pairs={{0,8},{1,5},{2,10},{3,7},{4,12},{5,1},{6,14},{7,3},{8,0},{9,13},{1... | collective-permute-start | bytes 393224 | tf_op jit(solution)/shard_map/ppermute | solution.py:272
  6.9 7.2 %collective-permute-start.4 = (f32[64,512]{1,0:T(8,128)S(1)}, f32[64,512]{1,0:T(8,128)S(1)}, u32[]{:S(2)}, u32[]{:S(2)}) collective-permute-start(f32[64,512]{1,0:T(8,128)S(1)} %get-tuple-element.35), channel_id=1, source_target_pairs={{0,4},{1,9},{2,6},{3,11},{4,0},{5,13},{6,2},{7,15},{8,12},{9,1},{1... | collective-permute-start | bytes 393224 | tf_op jit(solution)/shard_map/ppermute | solution.py:272
  7.5 9.2 %collective-permute-start = (f32[128,512]{1,0:T(8,128)S(1)}, f32[128,512]{1,0:T(8,128)S(1)}, u32[]{:S(2)}, u32[]{:S(2)}) collective-permute-start(f32[128,512]{1,0:T(8,128)S(1)} %get-tuple-element.30), channel_id=1, source_target_pairs={{0,4},{1,9},{2,6},{3,11},{4,0},{5,13},{6,2},{7,15},{8,12},{9,1},{1... | collective-permute-start | bytes 786440 | tf_op jit(solution)/shard_map/ppermute | solution.py:272
  14.1 9.8 %collective-permute-start.9 = (f32[64,512]{1,0:T(8,128)S(1)}, f32[64,512]{1,0:T(8,128)S(1)}, u32[]{:S(2)}, u32[]{:S(2)}) collective-permute-start(f32[64,512]{1,0:T(8,128)S(1)} %add_add_fusion.tie_ref), channel_id=1, source_target_pairs={{0,16},{4,20},{8,24},{12,28},{16,0},{20,4},{24,8},{28,12},{1,17},{... | collective-permute-start | bytes 393224 | tf_op jit(solution)/shard_map/ppermute | solution.py:267
  16.8 5.8 %collective-permute-start.1 = (f32[64,512]{1,0:T(8,128)S(1)}, f32[64,512]{1,0:T(8,128)S(1)}, u32[]{:S(2)}, u32[]{:S(2)}) collective-permute-start(f32[64,512]{1,0:T(8,128)S(1)} %slice_add_fusion), channel_id=1, source_target_pairs={{0,8},{1,5},{2,10},{3,7},{4,12},{5,1},{6,14},{7,3},{8,0},{9,13},{1... | collective-permute-start | bytes 393224 | tf_op jit(solution)/shard_map/ppermute | solution.py:272
  22.6 15.8 %copy-start.3 = (bf16[512,512]{1,0:T(8,128)(2,1)S(1)}, bf16[512,512]{1,0:T(8,128)(2,1)}, u32[]{:S(2)}) copy-start(bf16[512,512]{1,0:T(8,128)(2,1)} %refs_8_.1) | copy-start | bytes 1572868
  22.6 15.8 %copy-start.4 = (bf16[512,512]{1,0:T(8,128)(2,1)S(1)}, bf16[512,512]{1,0:T(8,128)(2,1)}, u32[]{:S(2)}) copy-start(bf16[512,512]{1,0:T(8,128)(2,1)} %refs_9_.1) | copy-start | bytes 1572868
  22.6 15.8 %copy-start.6 = (f32[512]{0:T(512)S(1)}, f32[512]{0:T(512)}, u32[]{:S(2)}) copy-start(f32[512]{0:T(512)} %param.18) | copy-start | bytes 6148
  22.7 7.1 %collective-permute-start.5 = (f32[64,512]{1,0:T(8,128)S(1)}, f32[64,512]{1,0:T(8,128)S(1)}, u32[]{:S(2)}, u32[]{:S(2)}) collective-permute-start(f32[64,512]{1,0:T(8,128)S(1)} %fusion), channel_id=1, source_target_pairs={{0,16},{4,20},{8,24},{12,28},{16,0},{20,4},{24,8},{28,12},{1,17},{... | collective-permute-start | bytes 393224 | tf_op jit(solution)/shard_map/ppermute | solution.py:267
  23.9 8.8 %collective-permute-start.12 = (f32[64,512]{1,0:T(8,128)S(1)}, f32[64,512]{1,0:T(8,128)S(1)}, u32[]{:S(2)}, u32[]{:S(2)}) collective-permute-start(f32[64,512]{1,0:T(8,128)S(1)} %add.43.refs_0_), channel_id=1, source_target_pairs={{0,12},{1,13},{2,14},{3,15},{4,8},{5,9},{6,10},{7,11},{8,4},{9,5},... | collective-permute-start | bytes 393224 | tf_op jit(solution)/shard_map/ppermute | solution.py:272
  26.6 8.5 %collective-permute-start.11 = (f32[64,512]{1,0:T(8,128)S(1)}, f32[64,512]{1,0:T(8,128)S(1)}, u32[]{:S(2)}, u32[]{:S(2)}) collective-permute-start(f32[64,512]{1,0:T(8,128)S(1)} %add.43.refs_0_), channel_id=1, source_target_pairs={{0,4},{1,9},{2,6},{3,11},{4,0},{5,13},{6,2},{7,15},{8,12},{9,1},{1... | collective-permute-start | bytes 393224 | tf_op jit(solution)/shard_map/ppermute | solution.py:272
  27.9 7.2 %collective-permute-start.10 = (f32[64,512]{1,0:T(8,128)S(1)}, f32[64,512]{1,0:T(8,128)S(1)}, u32[]{:S(2)}, u32[]{:S(2)}) collective-permute-start(f32[64,512]{1,0:T(8,128)S(1)} %add.43.refs_0_), channel_id=1, source_target_pairs={{0,8},{1,5},{2,10},{3,7},{4,12},{5,1},{6,14},{7,3},{8,0},{9,13},{1... | collective-permute-start | bytes 393224 | tf_op jit(solution)/shard_map/ppermute | solution.py:272
  29.7 7.6 %collective-permute-start.8 = (f32[64,512]{1,0:T(8,128)S(1)}, f32[64,512]{1,0:T(8,128)S(1)}, u32[]{:S(2)}, u32[]{:S(2)}) collective-permute-start(f32[64,512]{1,0:T(8,128)S(1)} %add.42.refs_0_), channel_id=1, source_target_pairs={{0,12},{1,13},{2,14},{3,15},{4,8},{5,9},{6,10},{7,11},{8,4},{9,5},... | collective-permute-start | bytes 393224 | tf_op jit(solution)/shard_map/ppermute | solution.py:272
  31.0 7.2 %collective-permute-start.7 = (f32[64,512]{1,0:T(8,128)S(1)}, f32[64,512]{1,0:T(8,128)S(1)}, u32[]{:S(2)}, u32[]{:S(2)}) collective-permute-start(f32[64,512]{1,0:T(8,128)S(1)} %add.42.refs_0_), channel_id=1, source_target_pairs={{0,4},{1,9},{2,6},{3,11},{4,0},{5,13},{6,2},{7,15},{8,12},{9,1},{1... | collective-permute-start | bytes 393224 | tf_op jit(solution)/shard_map/ppermute | solution.py:272
  32.7 5.8 %collective-permute-start.6 = (f32[64,512]{1,0:T(8,128)S(1)}, f32[64,512]{1,0:T(8,128)S(1)}, u32[]{:S(2)}, u32[]{:S(2)}) collective-permute-start(f32[64,512]{1,0:T(8,128)S(1)} %add.42.refs_0_), channel_id=1, source_target_pairs={{0,8},{1,5},{2,10},{3,7},{4,12},{5,1},{6,14},{7,3},{8,0},{9,13},{1... | collective-permute-start | bytes 393224 | tf_op jit(solution)/shard_map/ppermute | solution.py:272
  41.0 1.4 %collective-permute-start.16 = (f32[64,512]{1,0:T(8,128)S(1)}, f32[64,512]{1,0:T(8,128)S(1)}, u32[]{:S(2)}, u32[]{:S(2)}) collective-permute-start(f32[64,512]{1,0:T(8,128)S(1)} %get-tuple-element.45), channel_id=1, source_target_pairs={{0,1},{1,0},{2,3},{3,2},{4,5},{5,4},{6,7},{7,6},{8,9},{9,8},{10,11... | collective-permute-start | bytes 393224 | tf_op jit(solution)/shard_map/ppermute | solution.py:267
  41.1 2.9 %collective-permute-start.13 = (f32[64,512]{1,0:T(8,128)S(1)}, f32[64,512]{1,0:T(8,128)S(1)}, u32[]{:S(2)}, u32[]{:S(2)}) collective-permute-start(f32[64,512]{1,0:T(8,128)S(1)} %get-tuple-element.43), channel_id=1, source_target_pairs={{0,1},{1,0},{2,3},{3,2},{4,5},{5,4},{6,7},{7,6},{8,9},{9,8},{10,11... | collective-permute-start | bytes 393224 | tf_op jit(solution)/shard_map/ppermute | solution.py:267
  42.4 9.9 %copy-start = (bf16[512,512]{1,0:T(8,128)(2,1)S(1)}, bf16[512,512]{1,0:T(8,128)(2,1)}, u32[]{:S(2)}) copy-start(bf16[512,512]{1,0:T(8,128)(2,1)} %refs_5_.1) | copy-start | bytes 1572868
  42.4 9.9 %copy-start.1 = (bf16[512,512]{1,0:T(8,128)(2,1)S(1)}, bf16[512,512]{1,0:T(8,128)(2,1)}, u32[]{:S(2)}) copy-start(bf16[512,512]{1,0:T(8,128)(2,1)} %refs_6_.1) | copy-start | bytes 1572868
  42.4 9.9 %copy-start.2 = (f32[512]{0:T(512)S(1)}, f32[512]{0:T(512)}, u32[]{:S(2)}) copy-start(f32[512]{0:T(512)} %param.19) | copy-start | bytes 6148
  42.5 6.4 %collective-permute-start.17 = (f32[64,512]{1,0:T(8,128)S(1)}, f32[64,512]{1,0:T(8,128)S(1)}, u32[]{:S(2)}, u32[]{:S(2)}) collective-permute-start(f32[64,512]{1,0:T(8,128)S(1)} %add.46), channel_id=1, source_target_pairs={{0,2},{1,3},{2,0},{3,1},{4,6},{5,7},{6,4},{7,5},{8,10},{9,11},{10,... | collective-permute-start | bytes 393224 | tf_op jit(solution)/shard_map/ppermute | solution.py:267
  44.0 6.8 %collective-permute-start.14 = (f32[64,512]{1,0:T(8,128)S(1)}, f32[64,512]{1,0:T(8,128)S(1)}, u32[]{:S(2)}, u32[]{:S(2)}) collective-permute-start(f32[64,512]{1,0:T(8,128)S(1)} %add.44), channel_id=1, source_target_pairs={{0,2},{1,3},{2,0},{3,1},{4,6},{5,7},{6,4},{7,5},{8,10},{9,11},{10,... | collective-permute-start | bytes 393224 | tf_op jit(solution)/shard_map/ppermute | solution.py:267
  48.9 2.1 %collective-permute-start.18 = (f32[64,512]{1,0:T(8,128)S(1)}, f32[64,512]{1,0:T(8,128)S(1)}, u32[]{:S(2)}, u32[]{:S(2)}) collective-permute-start(f32[64,512]{1,0:T(8,128)S(1)} %add.47.refs_0_), channel_id=1, source_target_pairs={{0,1},{1,0},{2,3},{3,2},{4,5},{5,4},{6,7},{7,6},{8,9},{9,8},{10,11... | collective-permute-start | bytes 393224 | tf_op jit(solution)/shard_map/ppermute | solution.py:267
  50.9 1.4 %collective-permute-start.15 = (f32[64,512]{1,0:T(8,128)S(1)}, f32[64,512]{1,0:T(8,128)S(1)}, u32[]{:S(2)}, u32[]{:S(2)}) collective-permute-start(f32[64,512]{1,0:T(8,128)S(1)} %add.45.refs_0_), channel_id=1, source_target_pairs={{0,1},{1,0},{2,3},{3,2},{4,5},{5,4},{6,7},{7,6},{8,9},{9,8},{10,11... | collective-permute-start | bytes 393224 | tf_op jit(solution)/shard_map/ppermute | solution.py:267

commit v5 on v4

--- a/solution.py
+++ b/solution.py
@@ -160,7 +160,7 @@
     )(live, targets, states)
 
 
-def choose_kernel(sizes, half, target_ref, source_ref, tie_ref, *refs):
+def choose_kernel(sizes, half, live_ref, target_ref, source_ref, tie_ref, *refs):
     del tie_ref
     rows = target_ref.shape[1]
     sources = source_place(source_ref[...], half)
@@ -175,20 +175,17 @@
                 lane = lax.broadcasted_iota(jnp.int32, (rows, width), 1) + (base + first)
                 part_ref[:, first : first + width] = one_hot(place[:, :width], lane)
             base += count
+    sources = jnp.where(lax.broadcasted_iota(jnp.int32, (1, rows), 1) < live_ref[:, :1], sources, -1)
     pick_ref[...] = one_hot(sources, lax.broadcasted_iota(jnp.int32, pick_ref.shape, 0))
 
 
 def split_sums(sum_refs, parts_ref):
     total = parts_ref.shape[0] // 3
-    at = 0
-    for sum_ref in sum_refs:
-        size = sum_ref.shape[0]
-        value = sum_ref[...]
-        for part in range(3):
-            low = value.astype(jnp.bfloat16)
-            parts_ref[part * total + at : part * total + at + size, :] = low
-            value = value - low.astype(jnp.float32)
-        at += size
+    value = jnp.concatenate([sum_ref[...] for sum_ref in sum_refs])
+    for part in range(3):
+        low = value.astype(jnp.bfloat16)
+        parts_ref[part * total : (part + 1) * total, :] = low
+        value = value - low.astype(jnp.float32)
 
 
 def gather(chosen_ref, parts_ref):
@@ -200,24 +197,24 @@
 
 def gather_kernel(n_sums, *refs):
     sum_refs = refs[:n_sums]
-    chosen_ref, gathered_ref, parts_ref = refs[n_sums:]
+    chosen_ref, state_ref, message_ref, parts_ref = refs[n_sums:]
     split_sums(sum_refs, parts_ref)
-    gathered_ref[...] = gather(chosen_ref, parts_ref)
-
-
-def gather_first(sums, chosen):
+    message_ref[...] = gather(chosen_ref, parts_ref) - state_ref[...].astype(jnp.float32)
+
+
+def gather_first(sums, chosen, states):
     rows, count = chosen.shape
     channels = sums[0].shape[1]
     return call(
         functools.partial(gather_kernel, len(sums)),
         jax.ShapeDtypeStruct((rows, channels), jnp.float32),
-        [VMEM] * (len(sums) + 1), 6 * rows * count * channels,
+        [VMEM] * (len(sums) + 2), 6 * rows * count * channels,
         [pltpu.VMEM((3 * count, channels), jnp.bfloat16)],
-    )(*sums, chosen)
-
-
-def normed_activated(gathered_ref, chosen_ref, parts_ref, state_ref, inner_ref, gain_ref):
-    message = gathered_ref[...] + gather(chosen_ref, parts_ref) - state_ref[...].astype(jnp.float32)
+    )(*sums, chosen, states)
+
+
+def normed_activated(message_ref, chosen_ref, parts_ref, inner_ref, gain_ref):
+    message = message_ref[...] + gather(chosen_ref, parts_ref)
     mean_square = jnp.mean(message * message, axis=-1, keepdims=True)
     normed = message * lax.rsqrt(mean_square + 1e-05) * gain_ref[...]
     activated = jax.nn.relu(
@@ -226,18 +223,21 @@
     return normed, activated
 
 
-def finish(normed, activated, outer_ref, live_ref, first_row):
-    result = normed + jnp.dot(activated, outer_ref[...], preferred_element_type=jnp.float32)
+def finish(normed, activated, outer_ref):
+    return normed + jnp.dot(activated, outer_ref[...], preferred_element_type=jnp.float32)
+
+
+def only_live(result, live_ref, first_row):
     row = lax.broadcasted_iota(jnp.int32, (result.shape[0], 1), 0) + first_row
     return jnp.where(row < live_ref[:, :1], result, jnp.float32(0.0)).astype(jnp.bfloat16)
 
 
-def layer_one_kernel(n_sums, live_ref, *refs):
+def layer_one_kernel(n_sums, *refs):
     sum_refs = refs[:n_sums]
-    gathered_ref, chosen_ref, pick_ref, state_ref, inner_ref, outer_ref, gain_ref, reverse_ref, *piece_refs, parts_ref = refs[n_sums:]
+    message_ref, chosen_ref, pick_ref, inner_ref, outer_ref, gain_ref, reverse_ref, *piece_refs, parts_ref = refs[n_sums:]
     split_sums(sum_refs, parts_ref)
-    normed, activated = normed_activated(gathered_ref, chosen_ref, parts_ref, state_ref, inner_ref, gain_ref)
-    reverse_ref[...] = finish(normed, activated, outer_ref, live_ref, 0)
+    normed, activated = normed_activated(message_ref, chosen_ref, parts_ref, inner_ref, gain_ref)
+    reverse_ref[...] = finish(normed, activated, outer_ref).astype(jnp.bfloat16)
     total = jnp.dot(pick_ref[...], reverse_ref[...], preferred_element_type=jnp.float32)
     at = 0
     for piece_ref in piece_refs:
@@ -248,15 +248,17 @@
 
 def layer_two_kernel(n_sums, live_ref, *refs):
     sum_refs = refs[:n_sums]
-    gathered_ref, chosen_ref, state_ref, inner_ref, outer_ref, gain_ref, final_hbm, parts_ref, final_ref, sems = refs[n_sums:]
+    message_ref, chosen_ref, inner_ref, outer_ref, gain_ref, final_hbm, parts_ref, final_ref, sems = refs[n_sums:]
     split_sums(sum_refs, parts_ref)
-    normed, activated = normed_activated(gathered_ref, chosen_ref, parts_ref, state_ref, inner_ref, gain_ref)
+    normed, activated = normed_activated(message_ref, chosen_ref, parts_ref, inner_ref, gain_ref)
     block = final_ref.shape[0] // 2
     copies = []
     for index in range(2):
         rows = pl.ds(index * block, block)
         part = slice(index * block, (index + 1) * block)
-        final_ref[rows, :] = finish(normed[part], activated[part], outer_ref, live_ref, index * block)
+        final_ref[rows, :] = only_live(
+            finish(normed[part], activated[part], outer_ref), live_ref, index * block
+        )
         copies.append(pltpu.make_async_copy(final_ref.at[rows], final_hbm.at[rows], sems.at[index]))
         copies[-1].start()
     for copy in copies:
@@ -315,7 +317,8 @@
     sums = [first, second]
     for mask in higher_masks("src", GROUP):
         parts = [swap(value, "src", mask) for value in sums]
-        sums = [value + part for value, part in zip(sums, parts)]
+        first = sums[0] + tie(parts[0], sums[1])
+        sums = [first, sums[1] + tie(parts[1], first)]
     return [spread(value, stepwise) for value, stepwise in zip(sums, SPREAD_STEPWISE)], made
 
 
@@ -358,26 +361,26 @@
             [jax.ShapeDtypeStruct((source_atoms, rows), jnp.bfloat16)]
             + [jax.ShapeDtypeStruct((rows, GROUP * size), jnp.bfloat16) for size in sizes]
             + [jax.ShapeDtypeStruct((rows, 2 * size), jnp.bfloat16) for size in pieces],
-            [VMEM] * 3, HIDE_FLOPS,
-        )(targets, sources, first)
+            [VMEM] * 4, HIDE_FLOPS,
+        )(live, targets, sources, first)
 
     totals, (source_pick, *chosen) = target_totals(waves, choose)
     target_chosen, source_chosen = chosen[:n_waves], chosen[n_waves:]
-    gathered = gather_first(totals[0], target_chosen[0])
+    message = gather_first(totals[0], target_chosen[0], states)
     reverse_state, *sums = call(
         functools.partial(layer_one_kernel, len(totals[1])),
         [jax.ShapeDtypeStruct((rows, channels), jnp.bfloat16)]
         + [jax.ShapeDtypeStruct((size, channels), jnp.float32) for size in pieces for _ in range(2)],
-        [VMEM] * (len(totals[1]) + 8),
+        [VMEM] * (len(totals[1]) + 6),
         2 * rows * channels * (3 * GROUP * sizes[1] + 2 * channels + source_atoms),
         [pltpu.VMEM((3 * GROUP * sizes[1], channels), jnp.bfloat16)],
-    )(live, *totals[1], gathered, target_chosen[1], source_pick, states, inner_one, outer_one, gain_one.reshape(1, channels))
+    )(*totals[1], message, target_chosen[1], source_pick, inner_one, outer_one, gain_one.reshape(1, channels))
     totals = source_totals(list(zip(sums[::2], sums[1::2])))
-    gathered = gather_first(totals[0], source_chosen[0])
+    message = gather_first(totals[0], source_chosen[0], reverse_state)
     final_state = call(
         functools.partial(layer_two_kernel, len(totals[1])),
         jax.ShapeDtypeStruct((rows, channels), jnp.bfloat16),
-        [VMEM] * (len(totals[1]) + 7),
+        [VMEM] * (len(totals[1]) + 6),
         2 * rows * channels * (6 * pieces[1] + 2 * channels),
         [
             pltpu.VMEM((6 * pieces[1], channels), jnp.bfloat16),
@@ -385,7 +388,7 @@
             pltpu.SemaphoreType.DMA((2,)),
         ],
         HBM,
-    )(live, *totals[1], gathered, source_chosen[1], reverse_state, inner_two, outer_two, gain_two.reshape(1, channels))
+    )(live, *totals[1], message, source_chosen[1], inner_two, outer_two, gain_two.reshape(1, channels))
     return final_state.reshape(1, 1, rows, channels)
 
 

time: 55.4 us -> 55 us (level)
  no operation moved by 1% of the time
where the time goes in v5:
time: 55 us; the launch traced here: 54.8 us
  starting transfers between devices  22.7 us (41%)
  waiting for transfers between devices  21.4 us (39%)
  Pallas kernels  9.6 us (17%)
  between operations  0.85 us (2%)
    ppermute x11, starting transfers between devices, swap_group(): lax.ppermute(value, ('src', 'tgt'), [(i * across + j, (i ^ partner_mask(k...  16 us
    ppermute x11, waiting for transfers between devices, swap_group(): lax.ppermute(value, ('src', 'tgt'), [(i * across + j, (i ^ partner_mask(k...  12 us
    ppermute x8, waiting for transfers between devices, swap(): lax.ppermute(value, axis, [(i, i ^ mask) for i in range(lax.axis_size(axi...  9.39 us
    ppermute x8, starting transfers between devices, swap(): lax.ppermute(value, axis, [(i, i ^ mask) for i in range(lax.axis_size(axi...  6.74 us
    pallas_call x1, Pallas kernels, body(): call(functools.partial(layer_two_kernel, len(totals[1])), jax.ShapeDtypeS...  2.67 us
    pallas_call x1, Pallas kernels, body(): call(functools.partial(layer_one_kernel, len(totals[1])), [jax.ShapeDtype...  2.42 us
    pallas_call x2, Pallas kernels, gather_first(): call(functools.partial(gather_kernel, len(sums)), jax.ShapeDtypeStruct((r...  1.71 us
    pallas_call x1, Pallas kernels, first_sums(): call(functools.partial(first_sum_kernel, sizes), chunk_shapes(0, sizes[0]...  1.68 us
  transfers between devices with their start and end apart: 19, of which 13 were waited for; matrix products, arithmetic and copies ran while one was open for 0% of the time, Pallas kernels for 5%

profile of v5, /device:TPU:0, one launch (start us, length us, event | category | flops | bytes accessed | tf_op | source)
XLA Modules:
  0.0 54.8 jit_solution(5014917048370097208)
XLA Ops:
  0.7 1.7 %shard_map.100 = (f32[64,512]{1,0:T(8,128)S(1)}, f32[64,512]{1,0:T(8,128)S(1)}, f32[64,512]{1,0:T(8,128)S(1)}, f32[64,512]{1,0:T(8,128)S(1)}, s32[1,128]{1,0:T(1...) custom-call(s32[1,1]{1,0:T(1,128)S(6)} %copy.11.live_ref, s32[1,1024]{1,0:T(1,128)} %bitcast.10, ...), custom_call_target="tpu_custom_call" | custom-call | flops 268435456 | tf_op jit(solution)/shard_map/pallas_call | solution.py:147
  2.4 4.0 %collective-permute-start.2 = (f32[64,512]{1,0:T(8,128)S(1)}, f32[64,512]{1,0:T(8,128)S(1)}, u32[]{:S(2)}, u32[]{:S(2)}) collective-permute-start(f32[64,512]{1,0:T(8,128)S(1)} %get-tuple-element.35), channel_id=1, source_target_pairs={{0,12},{1,13},{2,14},{3,15},{4,8},{5,9},{6,10},{7,11},{8,4},{9,5},... | collective-permute-start | bytes 393224 | tf_op jit(solution)/shard_map/ppermute | solution.py:274
  6.4 0.4 collective-permute-start.3
  6.9 0.2 collective-permute-start.4
  7.0 0.5 shard_map.101
  7.5 1.9 %collective-permute-start = (f32[128,512]{1,0:T(8,128)S(1)}, f32[128,512]{1,0:T(8,128)S(1)}, u32[]{:S(2)}, u32[]{:S(2)}) collective-permute-start(f32[128,512]{1,0:T(8,128)S(1)} %get-tuple-element.32), channel_id=1, source_target_pairs={{0,4},{1,9},{2,6},{3,11},{4,0},{5,13},{6,2},{7,15},{8,12},{9,1},{1... | collective-permute-start | bytes 786440 | tf_op jit(solution)/shard_map/ppermute | solution.py:274
  9.4 0.9 %collective-permute-done.2 = f32[64,512]{1,0:T(8,128)S(1)} collective-permute-done((f32[64,512]{1,0:T(8,128)S(1)}, f32[64,512]{1,0:T(8,128)S(1)}, u32[]{:S(2)}, u32[]{:S(2)}) %collective-permute-start.2) | collective-permute-done | bytes 131104 | tf_op jit(solution)/shard_map/ppermute | solution.py:274
  10.3 3.7 %collective-permute-done.3 = f32[64,512]{1,0:T(8,128)S(1)} collective-permute-done((f32[64,512]{1,0:T(8,128)S(1)}, f32[64,512]{1,0:T(8,128)S(1)}, u32[]{:S(2)}, u32[]{:S(2)}) %collective-permute-start.3) | collective-permute-done | bytes 131104 | tf_op jit(solution)/shard_map/ppermute | solution.py:274
  14.0 0.0 collective-permute-done.4
  14.1 2.7 %collective-permute-start.6 = (f32[64,512]{1,0:T(8,128)S(1)}, f32[64,512]{1,0:T(8,128)S(1)}, u32[]{:S(2)}, u32[]{:S(2)}) collective-permute-start(f32[64,512]{1,0:T(8,128)S(1)} %add_add_fusion.tie_ref), channel_id=1, source_target_pairs={{0,16},{4,20},{8,24},{12,28},{16,0},{20,4},{24,8},{28,12},{1,17},{... | collective-permute-start | bytes 393224 | tf_op jit(solution)/shard_map/ppermute | solution.py:269
  16.7 0.0 collective-permute-done
  16.8 1.6 %collective-permute-start.1 = (f32[64,512]{1,0:T(8,128)S(1)}, f32[64,512]{1,0:T(8,128)S(1)}, u32[]{:S(2)}, u32[]{:S(2)}) collective-permute-start(f32[64,512]{1,0:T(8,128)S(1)} %slice_add_fusion), channel_id=1, source_target_pairs={{0,8},{1,5},{2,10},{3,7},{4,12},{5,1},{6,14},{7,3},{8,0},{9,13},{1... | collective-permute-start | bytes 393224 | tf_op jit(solution)/shard_map/ppermute | solution.py:274
  18.4 0.6 %shard_map.102 = (bf16[256,1024]{1,0:T(8,128)(2,1)S(1)}, bf16[1024,256]{1,0:T(8,128)(2,1)S(1)}, bf16[1024,256]{1,0:T(8,128)(2,1)S(1)}, bf16[1024,128]{1,0:T(8,128)(2,1)S(1)}, bf16[1024,128]{1,0:T(8,128)(2,1)S(1)}) custom-call(s32[1,128]{1,0:T(1,128)S(1)} %get-tuple-element.28.live_ref, s32[1,1024]{1,0:T(1,128)S(1)} %get-tuple-element.29.target_ref, ...), custom_call_target="tpu_custom_call" | custom-call | flops 8000000000 | tf_op jit(solution)/shard_map/pallas_call | solution.py:359
  19.1 3.5 %collective-permute-done.1 = f32[64,512]{1,0:T(8,128)S(1)} collective-permute-done((f32[64,512]{1,0:T(8,128)S(1)}, f32[64,512]{1,0:T(8,128)S(1)}, u32[]{:S(2)}, u32[]{:S(2)}) %collective-permute-start.1) | collective-permute-done | bytes 131104 | tf_op jit(solution)/shard_map/ppermute | solution.py:274
  22.6 1.2 %collective-permute-start.5 = (f32[64,512]{1,0:T(8,128)S(1)}, f32[64,512]{1,0:T(8,128)S(1)}, u32[]{:S(2)}, u32[]{:S(2)}) collective-permute-start(f32[64,512]{1,0:T(8,128)S(1)} %fusion), channel_id=1, source_target_pairs={{0,16},{4,20},{8,24},{12,28},{16,0},{20,4},{24,8},{28,12},{1,17},{... | collective-permute-start | bytes 393224 | tf_op jit(solution)/shard_map/ppermute | solution.py:269
  23.9 2.7 %collective-permute-start.12 = (f32[64,512]{1,0:T(8,128)S(1)}, f32[64,512]{1,0:T(8,128)S(1)}, u32[]{:S(2)}, u32[]{:S(2)}) collective-permute-start(f32[64,512]{1,0:T(8,128)S(1)} %add.42.refs_0_), channel_id=1, source_target_pairs={{0,12},{1,13},{2,14},{3,15},{4,8},{5,9},{6,10},{7,11},{8,4},{9,5},... | collective-permute-start | bytes 393224 | tf_op jit(solution)/shard_map/ppermute | solution.py:274
  26.5 1.3 %collective-permute-start.11 = (f32[64,512]{1,0:T(8,128)S(1)}, f32[64,512]{1,0:T(8,128)S(1)}, u32[]{:S(2)}, u32[]{:S(2)}) collective-permute-start(f32[64,512]{1,0:T(8,128)S(1)} %add.42.refs_0_), channel_id=1, source_target_pairs={{0,4},{1,9},{2,6},{3,11},{4,0},{5,13},{6,2},{7,15},{8,12},{9,1},{1... | collective-permute-start | bytes 393224 | tf_op jit(solution)/shard_map/ppermute | solution.py:274
  27.8 1.8 %collective-permute-done.5 = f32[64,512]{1,0:T(8,128)S(1)} collective-permute-done((f32[64,512]{1,0:T(8,128)S(1)}, f32[64,512]{1,0:T(8,128)S(1)}, u32[]{:S(2)}, u32[]{:S(2)}) %collective-permute-start.5) | collective-permute-done | bytes 131104 | tf_op jit(solution)/shard_map/ppermute | solution.py:269
  29.7 0.0 copy-start
  29.7 0.0 copy-start.1
  29.7 0.0 copy-start.5
  29.7 1.2 %collective-permute-start.9 = (f32[64,512]{1,0:T(8,128)S(1)}, f32[64,512]{1,0:T(8,128)S(1)}, u32[]{:S(2)}, u32[]{:S(2)}) collective-permute-start(f32[64,512]{1,0:T(8,128)S(1)} %add.43.refs_0_), channel_id=1, source_target_pairs={{0,12},{1,13},{2,14},{3,15},{4,8},{5,9},{6,10},{7,11},{8,4},{9,5},... | collective-permute-start | bytes 393224 | tf_op jit(solution)/shard_map/ppermute | solution.py:274
  31.0 1.4 %collective-permute-start.8 = (f32[64,512]{1,0:T(8,128)S(1)}, f32[64,512]{1,0:T(8,128)S(1)}, u32[]{:S(2)}, u32[]{:S(2)}) collective-permute-start(f32[64,512]{1,0:T(8,128)S(1)} %add.43.refs_0_), channel_id=1, source_target_pairs={{0,4},{1,9},{2,6},{3,11},{4,0},{5,13},{6,2},{7,15},{8,12},{9,1},{1... | collective-permute-start | bytes 393224 | tf_op jit(solution)/shard_map/ppermute | solution.py:274
  32.4 0.3 collective-permute-done.12.refs_3_
  32.6 1.2 %collective-permute-start.7 = (f32[64,512]{1,0:T(8,128)S(1)}, f32[64,512]{1,0:T(8,128)S(1)}, u32[]{:S(2)}, u32[]{:S(2)}) collective-permute-start(f32[64,512]{1,0:T(8,128)S(1)} %add.43.refs_0_), channel_id=1, source_target_pairs={{0,8},{1,5},{2,10},{3,7},{4,12},{5,1},{6,14},{7,3},{8,0},{9,13},{1... | collective-permute-start | bytes 393224 | tf_op jit(solution)/shard_map/ppermute | solution.py:274
  33.8 1.2 %collective-permute-done.11.refs_2_ = f32[64,512]{1,0:T(8,128)S(1)} collective-permute-done((f32[64,512]{1,0:T(8,128)S(1)}, f32[64,512]{1,0:T(8,128)S(1)}, u32[]{:S(2)}, u32[]{:S(2)}) %collective-permute-start.11) | collective-permute-done | bytes 131104 | tf_op jit(solution)/shard_map/ppermute | solution.py:274
  35.0 1.0 %shard_map.103.refs_4_ = f32[1024,512]{1,0:T(8,128)S(1)} custom-call(f32[64,512]{1,0:T(8,128)S(1)} %add.42.refs_0_, f32[64,512]{1,0:T(8,128)S(1)} %collective-permute-done.10.refs_1_, f32[64,512]{1,0:T(8,128)S(1)} %collective-permute-done.11.refs_2_, f32[64,512]{1,0:T(8,128)S(1)} %collective-permute-done.12.refs_3_, ...), custom_call_target="tpu_custom_call" | custom-call | flops 805306368 | tf_op jit(solution)/shard_map/pallas_call | solution.py:208
  36.0 1.3 %collective-permute-done.9.refs_3_ = f32[64,512]{1,0:T(8,128)S(1)} collective-permute-done((f32[64,512]{1,0:T(8,128)S(1)}, f32[64,512]{1,0:T(8,128)S(1)}, u32[]{:S(2)}, u32[]{:S(2)}) %collective-permute-start.9) | collective-permute-done | bytes 131104 | tf_op jit(solution)/shard_map/ppermute | solution.py:274
  37.3 0.8 %collective-permute-done.8.refs_2_ = f32[64,512]{1,0:T(8,128)S(1)} collective-permute-done((f32[64,512]{1,0:T(8,128)S(1)}, f32[64,512]{1,0:T(8,128)S(1)}, u32[]{:S(2)}, u32[]{:S(2)}) %collective-permute-start.8) | collective-permute-done | bytes 131104 | tf_op jit(solution)/shard_map/ppermute | solution.py:274
  38.1 0.3 collective-permute-done.7.refs_1_
  38.4 2.4 %shard_map.104 = (bf16[1024,512]{1,0:T(8,128)(2,1)S(1)}, f32[64,512]{1,0:T(8,128)S(1)}, f32[64,512]{1,0:T(8,128)S(1)}, f32[64,512]{1,0:T(8,128)S(1)}, f32[64,512]{1,0:T(8,128)S(1)}) custom-call(f32[64,512]{1,0:T(8,128)S(1)} %add.43.refs_0_, f32[64,512]{1,0:T(8,128)S(1)} %collective-permute-done.7.refs_1_, f32[64,512]{1,0:T(8,128)S(1)} %collective-permute-done.8.refs_2_, ...), custom_call_target="tpu_custom_call" | custom-call | flops 2147483648 | tf_op jit(solution)/shard_map/pallas_call | solution.py:370
  40.8 0.1 collective-permute-start.16
  40.9 0.5 collective-permute-start.13
  41.4 0.8 %collective-permute-done.16 = f32[64,512]{1,0:T(8,128)S(1)} collective-permute-done((f32[64,512]{1,0:T(8,128)S(1)}, f32[64,512]{1,0:T(8,128)S(1)}, u32[]{:S(2)}, u32[]{:S(2)}) %collective-permute-start.16) | collective-permute-done | bytes 131104 | tf_op jit(solution)/shard_map/ppermute | solution.py:269
  42.3 1.6 %collective-permute-start.17 = (f32[64,512]{1,0:T(8,128)S(1)}, f32[64,512]{1,0:T(8,128)S(1)}, u32[]{:S(2)}, u32[]{:S(2)}) collective-permute-start(f32[64,512]{1,0:T(8,128)S(1)} %add.46), channel_id=1, source_target_pairs={{0,2},{1,3},{2,0},{3,1},{4,6},{5,7},{6,4},{7,5},{8,10},{9,11},{10,... | collective-permute-start | bytes 393224 | tf_op jit(solution)/shard_map/ppermute | solution.py:269
  43.8 0.0 collective-permute-done.13
  43.8 0.6 %collective-permute-start.14 = (f32[64,512]{1,0:T(8,128)S(1)}, f32[64,512]{1,0:T(8,128)S(1)}, u32[]{:S(2)}, u32[]{:S(2)}) collective-permute-start(f32[64,512]{1,0:T(8,128)S(1)} %add.44), channel_id=1, source_target_pairs={{0,2},{1,3},{2,0},{3,1},{4,6},{5,7},{6,4},{7,5},{8,10},{9,11},{10,... | collective-permute-start | bytes 393224 | tf_op jit(solution)/shard_map/ppermute | solution.py:269
  44.4 4.2 %collective-permute-done.17 = f32[64,512]{1,0:T(8,128)S(1)} collective-permute-done((f32[64,512]{1,0:T(8,128)S(1)}, f32[64,512]{1,0:T(8,128)S(1)}, u32[]{:S(2)}, u32[]{:S(2)}) %collective-permute-start.17) | collective-permute-done | bytes 131104 | tf_op jit(solution)/shard_map/ppermute | solution.py:269
  48.7 0.0 copy-start.2
  48.7 0.0 copy-start.3
  48.7 0.0 copy-start.6
  48.7 0.1 collective-permute-start.18
  48.8 1.9 %collective-permute-done.14 = f32[64,512]{1,0:T(8,128)S(1)} collective-permute-done((f32[64,512]{1,0:T(8,128)S(1)}, f32[64,512]{1,0:T(8,128)S(1)}, u32[]{:S(2)}, u32[]{:S(2)}) %collective-permute-start.14) | collective-permute-done | bytes 131104 | tf_op jit(solution)/shard_map/ppermute | solution.py:269
  50.7 0.1 collective-permute-start.15
  50.8 0.0 collective-permute-done.18.refs_1_
  50.8 0.7 %shard_map.105.refs_2_ = f32[1024,512]{1,0:T(8,128)S(1)} custom-call(f32[64,512]{1,0:T(8,128)S(1)} %add.47.refs_0_, f32[64,512]{1,0:T(8,128)S(1)} %collective-permute-done.18.refs_1_, bf16[1024,128]{1,0:T(8,128)(2,1)S(1)} %get-tuple-element.41.refs_2_, bf16[1024,512]{1,0:T(8,128)(2,1)S(1)} %get-tuple-element.50.refs_3_), custom_call_target="tpu_custom_call" | custom-call | flops 402653184 | tf_op jit(solution)/shard_map/pallas_call | solution.py:208
  51.5 0.6 %collective-permute-done.15.refs_1_ = f32[64,512]{1,0:T(8,128)S(1)} collective-permute-done((f32[64,512]{1,0:T(8,128)S(1)}, f32[64,512]{1,0:T(8,128)S(1)}, u32[]{:S(2)}, u32[]{:S(2)}) %collective-permute-start.15) | collective-permute-done | bytes 131104 | tf_op jit(solution)/shard_map/ppermute | solution.py:269
  52.1 2.7 %shard_map.106 = bf16[1024,512]{1,0:T(8,128)(2,1)} custom-call(s32[1,128]{1,0:T(1,128)S(1)} %get-tuple-element.28.live_ref, f32[64,512]{1,0:T(8,128)S(1)} %add.45.refs_0_, f32[64,512]{1,0:T(8,128)S(1)} %collective-permute-done.15.refs_1_, f32[1024,512]{1,0:T(8,128)S(1)} %shard_map.105.refs_2_, bf16[1024,128]{1,0:T(8,128)(2,1)S(1)} %get-tuple-element.42.refs_3_, ...), custom_call_target="tpu_custom_call" | custom-call | flops 1476395008 | tf_op jit(solution)/shard_map/pallas_call | solution.py:380
  (20 shorter events, 0.2 us)
Async XLA Ops:
  0.0 18.4 %copy-start.4 = (s32[1,1,1024]{2,1,0:T(1,128)S(1)}, s32[1,1,1024]{2,1,0:T(1,128)}, u32[]{:S(2)}) copy-start(s32[1,1,1024]{2,1,0:T(1,128)} %param.11) | copy-start | bytes 12292
  2.4 8.0 %collective-permute-start.2 = (f32[64,512]{1,0:T(8,128)S(1)}, f32[64,512]{1,0:T(8,128)S(1)}, u32[]{:S(2)}, u32[]{:S(2)}) collective-permute-start(f32[64,512]{1,0:T(8,128)S(1)} %get-tuple-element.35), channel_id=1, source_target_pairs={{0,12},{1,13},{2,14},{3,15},{4,8},{5,9},{6,10},{7,11},{8,4},{9,5},... | collective-permute-start | bytes 393224 | tf_op jit(solution)/shard_map/ppermute | solution.py:274
  6.4 7.6 %collective-permute-start.3 = (f32[64,512]{1,0:T(8,128)S(1)}, f32[64,512]{1,0:T(8,128)S(1)}, u32[]{:S(2)}, u32[]{:S(2)}) collective-permute-start(f32[64,512]{1,0:T(8,128)S(1)} %get-tuple-element.36), channel_id=1, source_target_pairs={{0,8},{1,5},{2,10},{3,7},{4,12},{5,1},{6,14},{7,3},{8,0},{9,13},{1... | collective-permute-start | bytes 393224 | tf_op jit(solution)/shard_map/ppermute | solution.py:274
  6.9 7.2 %collective-permute-start.4 = (f32[64,512]{1,0:T(8,128)S(1)}, f32[64,512]{1,0:T(8,128)S(1)}, u32[]{:S(2)}, u32[]{:S(2)}) collective-permute-start(f32[64,512]{1,0:T(8,128)S(1)} %get-tuple-element.37), channel_id=1, source_target_pairs={{0,4},{1,9},{2,6},{3,11},{4,0},{5,13},{6,2},{7,15},{8,12},{9,1},{1... | collective-permute-start | bytes 393224 | tf_op jit(solution)/shard_map/ppermute | solution.py:274
  7.5 9.2 %collective-permute-start = (f32[128,512]{1,0:T(8,128)S(1)}, f32[128,512]{1,0:T(8,128)S(1)}, u32[]{:S(2)}, u32[]{:S(2)}) collective-permute-start(f32[128,512]{1,0:T(8,128)S(1)} %get-tuple-element.32), channel_id=1, source_target_pairs={{0,4},{1,9},{2,6},{3,11},{4,0},{5,13},{6,2},{7,15},{8,12},{9,1},{1... | collective-permute-start | bytes 786440 | tf_op jit(solution)/shard_map/ppermute | solution.py:274
  14.1 9.8 %collective-permute-start.6 = (f32[64,512]{1,0:T(8,128)S(1)}, f32[64,512]{1,0:T(8,128)S(1)}, u32[]{:S(2)}, u32[]{:S(2)}) collective-permute-start(f32[64,512]{1,0:T(8,128)S(1)} %add_add_fusion.tie_ref), channel_id=1, source_target_pairs={{0,16},{4,20},{8,24},{12,28},{16,0},{20,4},{24,8},{28,12},{1,17},{... | collective-permute-start | bytes 393224 | tf_op jit(solution)/shard_map/ppermute | solution.py:269
  16.8 5.8 %collective-permute-start.1 = (f32[64,512]{1,0:T(8,128)S(1)}, f32[64,512]{1,0:T(8,128)S(1)}, u32[]{:S(2)}, u32[]{:S(2)}) collective-permute-start(f32[64,512]{1,0:T(8,128)S(1)} %slice_add_fusion), channel_id=1, source_target_pairs={{0,8},{1,5},{2,10},{3,7},{4,12},{5,1},{6,14},{7,3},{8,0},{9,13},{1... | collective-permute-start | bytes 393224 | tf_op jit(solution)/shard_map/ppermute | solution.py:274
  22.6 7.1 %collective-permute-start.5 = (f32[64,512]{1,0:T(8,128)S(1)}, f32[64,512]{1,0:T(8,128)S(1)}, u32[]{:S(2)}, u32[]{:S(2)}) collective-permute-start(f32[64,512]{1,0:T(8,128)S(1)} %fusion), channel_id=1, source_target_pairs={{0,16},{4,20},{8,24},{12,28},{16,0},{20,4},{24,8},{28,12},{1,17},{... | collective-permute-start | bytes 393224 | tf_op jit(solution)/shard_map/ppermute | solution.py:269
  23.9 8.8 %collective-permute-start.12 = (f32[64,512]{1,0:T(8,128)S(1)}, f32[64,512]{1,0:T(8,128)S(1)}, u32[]{:S(2)}, u32[]{:S(2)}) collective-permute-start(f32[64,512]{1,0:T(8,128)S(1)} %add.42.refs_0_), channel_id=1, source_target_pairs={{0,12},{1,13},{2,14},{3,15},{4,8},{5,9},{6,10},{7,11},{8,4},{9,5},... | collective-permute-start | bytes 393224 | tf_op jit(solution)/shard_map/ppermute | solution.py:274
  26.5 8.5 %collective-permute-start.11 = (f32[64,512]{1,0:T(8,128)S(1)}, f32[64,512]{1,0:T(8,128)S(1)}, u32[]{:S(2)}, u32[]{:S(2)}) collective-permute-start(f32[64,512]{1,0:T(8,128)S(1)} %add.42.refs_0_), channel_id=1, source_target_pairs={{0,4},{1,9},{2,6},{3,11},{4,0},{5,13},{6,2},{7,15},{8,12},{9,1},{1... | collective-permute-start | bytes 393224 | tf_op jit(solution)/shard_map/ppermute | solution.py:274
  27.8 7.2 %collective-permute-start.10 = (f32[64,512]{1,0:T(8,128)S(1)}, f32[64,512]{1,0:T(8,128)S(1)}, u32[]{:S(2)}, u32[]{:S(2)}) collective-permute-start(f32[64,512]{1,0:T(8,128)S(1)} %add.42.refs_0_), channel_id=1, source_target_pairs={{0,8},{1,5},{2,10},{3,7},{4,12},{5,1},{6,14},{7,3},{8,0},{9,13},{1... | collective-permute-start | bytes 393224 | tf_op jit(solution)/shard_map/ppermute | solution.py:274
  29.7 8.7 %copy-start = (bf16[512,512]{1,0:T(8,128)(2,1)S(1)}, bf16[512,512]{1,0:T(8,128)(2,1)}, u32[]{:S(2)}) copy-start(bf16[512,512]{1,0:T(8,128)(2,1)} %refs_7_.1) | copy-start | bytes 1572868
  29.7 8.7 %copy-start.1 = (bf16[512,512]{1,0:T(8,128)(2,1)S(1)}, bf16[512,512]{1,0:T(8,128)(2,1)}, u32[]{:S(2)}) copy-start(bf16[512,512]{1,0:T(8,128)(2,1)} %refs_8_.1) | copy-start | bytes 1572868
  29.7 8.7 %copy-start.5 = (f32[512]{0:T(512)S(1)}, f32[512]{0:T(512)}, u32[]{:S(2)}) copy-start(f32[512]{0:T(512)} %param.18) | copy-start | bytes 6148
  29.7 7.6 %collective-permute-start.9 = (f32[64,512]{1,0:T(8,128)S(1)}, f32[64,512]{1,0:T(8,128)S(1)}, u32[]{:S(2)}, u32[]{:S(2)}) collective-permute-start(f32[64,512]{1,0:T(8,128)S(1)} %add.43.refs_0_), channel_id=1, source_target_pairs={{0,12},{1,13},{2,14},{3,15},{4,8},{5,9},{6,10},{7,11},{8,4},{9,5},... | collective-permute-start | bytes 393224 | tf_op jit(solution)/shard_map/ppermute | solution.py:274
  31.0 7.1 %collective-permute-start.8 = (f32[64,512]{1,0:T(8,128)S(1)}, f32[64,512]{1,0:T(8,128)S(1)}, u32[]{:S(2)}, u32[]{:S(2)}) collective-permute-start(f32[64,512]{1,0:T(8,128)S(1)} %add.43.refs_0_), channel_id=1, source_target_pairs={{0,4},{1,9},{2,6},{3,11},{4,0},{5,13},{6,2},{7,15},{8,12},{9,1},{1... | collective-permute-start | bytes 393224 | tf_op jit(solution)/shard_map/ppermute | solution.py:274
  32.6 5.8 %collective-permute-start.7 = (f32[64,512]{1,0:T(8,128)S(1)}, f32[64,512]{1,0:T(8,128)S(1)}, u32[]{:S(2)}, u32[]{:S(2)}) collective-permute-start(f32[64,512]{1,0:T(8,128)S(1)} %add.43.refs_0_), channel_id=1, source_target_pairs={{0,8},{1,5},{2,10},{3,7},{4,12},{5,1},{6,14},{7,3},{8,0},{9,13},{1... | collective-permute-start | bytes 393224 | tf_op jit(solution)/shard_map/ppermute | solution.py:274
  40.8 1.4 %collective-permute-start.16 = (f32[64,512]{1,0:T(8,128)S(1)}, f32[64,512]{1,0:T(8,128)S(1)}, u32[]{:S(2)}, u32[]{:S(2)}) collective-permute-start(f32[64,512]{1,0:T(8,128)S(1)} %get-tuple-element.49), channel_id=1, source_target_pairs={{0,1},{1,0},{2,3},{3,2},{4,5},{5,4},{6,7},{7,6},{8,9},{9,8},{10,11... | collective-permute-start | bytes 393224 | tf_op jit(solution)/shard_map/ppermute | solution.py:269
  40.9 2.9 %collective-permute-start.13 = (f32[64,512]{1,0:T(8,128)S(1)}, f32[64,512]{1,0:T(8,128)S(1)}, u32[]{:S(2)}, u32[]{:S(2)}) collective-permute-start(f32[64,512]{1,0:T(8,128)S(1)} %get-tuple-element.47), channel_id=1, source_target_pairs={{0,1},{1,0},{2,3},{3,2},{4,5},{5,4},{6,7},{7,6},{8,9},{9,8},{10,11... | collective-permute-start | bytes 393224 | tf_op jit(solution)/shard_map/ppermute | solution.py:269
  42.3 6.4 %collective-permute-start.17 = (f32[64,512]{1,0:T(8,128)S(1)}, f32[64,512]{1,0:T(8,128)S(1)}, u32[]{:S(2)}, u32[]{:S(2)}) collective-permute-start(f32[64,512]{1,0:T(8,128)S(1)} %add.46), channel_id=1, source_target_pairs={{0,2},{1,3},{2,0},{3,1},{4,6},{5,7},{6,4},{7,5},{8,10},{9,11},{10,... | collective-permute-start | bytes 393224 | tf_op jit(solution)/shard_map/ppermute | solution.py:269
  43.8 6.8 %collective-permute-start.14 = (f32[64,512]{1,0:T(8,128)S(1)}, f32[64,512]{1,0:T(8,128)S(1)}, u32[]{:S(2)}, u32[]{:S(2)}) collective-permute-start(f32[64,512]{1,0:T(8,128)S(1)} %add.44), channel_id=1, source_target_pairs={{0,2},{1,3},{2,0},{3,1},{4,6},{5,7},{6,4},{7,5},{8,10},{9,11},{10,... | collective-permute-start | bytes 393224 | tf_op jit(solution)/shard_map/ppermute | solution.py:269
  48.7 3.4 %copy-start.2 = (bf16[512,512]{1,0:T(8,128)(2,1)S(1)}, bf16[512,512]{1,0:T(8,128)(2,1)}, u32[]{:S(2)}) copy-start(bf16[512,512]{1,0:T(8,128)(2,1)} %refs_4_.1) | copy-start | bytes 1572868
  48.7 3.4 %copy-start.3 = (bf16[512,512]{1,0:T(8,128)(2,1)S(1)}, bf16[512,512]{1,0:T(8,128)(2,1)}, u32[]{:S(2)}) copy-start(bf16[512,512]{1,0:T(8,128)(2,1)} %refs_5_.1) | copy-start | bytes 1572868
  48.7 3.4 %copy-start.6 = (f32[512]{0:T(512)S(1)}, f32[512]{0:T(512)}, u32[]{:S(2)}) copy-start(f32[512]{0:T(512)} %param.19) | copy-start | bytes 6148
  48.7 2.1 %collective-permute-start.18 = (f32[64,512]{1,0:T(8,128)S(1)}, f32[64,512]{1,0:T(8,128)S(1)}, u32[]{:S(2)}, u32[]{:S(2)}) collective-permute-start(f32[64,512]{1,0:T(8,128)S(1)} %add.47.refs_0_), channel_id=1, source_target_pairs={{0,1},{1,0},{2,3},{3,2},{4,5},{5,4},{6,7},{7,6},{8,9},{9,8},{10,11... | collective-permute-start | bytes 393224 | tf_op jit(solution)/shard_map/ppermute | solution.py:269
  50.7 1.4 %collective-permute-start.15 = (f32[64,512]{1,0:T(8,128)S(1)}, f32[64,512]{1,0:T(8,128)S(1)}, u32[]{:S(2)}, u32[]{:S(2)}) collective-permute-start(f32[64,512]{1,0:T(8,128)S(1)} %add.45.refs_0_), channel_id=1, source_target_pairs={{0,1},{1,0},{2,3},{3,2},{4,5},{5,4},{6,7},{7,6},{8,9},{9,8},{10,11... | collective-permute-start | bytes 393224 | tf_op jit(solution)/shard_map/ppermute | solution.py:269

commit v6 on v5

--- a/solution.py
+++ b/solution.py
@@ -160,20 +160,20 @@
     )(live, targets, states)
 
 
-def choose_kernel(sizes, half, live_ref, target_ref, source_ref, tie_ref, *refs):
+def choose_kernel(sizes, half, live_ref, target_ref, source_ref, tie_ref, pick_ref, *refs):
     del tie_ref
     rows = target_ref.shape[1]
     sources = source_place(source_ref[...], half)
-    pick_ref, refs = refs[0], refs[1:]
-    for place, part_refs in ((target_place(target_ref[...], sizes), refs[: len(sizes)]), (sources, refs[len(sizes) :])):
+    for place, part_refs in ((target_place(target_ref[...], sizes), refs[:2]), (sources, refs[2:])):
         place = jnp.transpose(jnp.broadcast_to(place, (LANES, rows)))
         base = 0
         for part_ref in part_refs:
-            count = part_ref.shape[1]
-            for first in range(0, count, LANES):
-                width = min(LANES, count - first)
-                lane = lax.broadcasted_iota(jnp.int32, (rows, width), 1) + (base + first)
-                part_ref[:, first : first + width] = one_hot(place[:, :width], lane)
+            columns = part_ref.shape[1]
+            count = columns // 3
+            for first in range(0, columns, LANES):
+                width = min(LANES, columns - first)
+                slot = (lax.broadcasted_iota(jnp.int32, (1, width), 1) + first) % count + base
+                part_ref[:, first : first + width] = one_hot(place[:, :width], slot)
             base += count
     sources = jnp.where(lax.broadcasted_iota(jnp.int32, (1, rows), 1) < live_ref[:, :1], sources, -1)
     pick_ref[...] = one_hot(sources, lax.broadcasted_iota(jnp.int32, pick_ref.shape, 0))
@@ -189,10 +189,7 @@
 
 
 def gather(chosen_ref, parts_ref):
-    chosen = chosen_ref[...]
-    return jnp.dot(
-        jnp.concatenate([chosen, chosen, chosen], axis=1), parts_ref[...], preferred_element_type=jnp.float32
-    )
+    return jnp.dot(chosen_ref[...], parts_ref[...], preferred_element_type=jnp.float32)
 
 
 def gather_kernel(n_sums, *refs):
@@ -203,13 +200,13 @@
 
 
 def gather_first(sums, chosen, states):
-    rows, count = chosen.shape
+    rows, columns = chosen.shape
     channels = sums[0].shape[1]
     return call(
         functools.partial(gather_kernel, len(sums)),
         jax.ShapeDtypeStruct((rows, channels), jnp.float32),
-        [VMEM] * (len(sums) + 2), 6 * rows * count * channels,
-        [pltpu.VMEM((3 * count, channels), jnp.bfloat16)],
+        [VMEM] * (len(sums) + 2), 2 * rows * columns * channels,
+        [pltpu.VMEM((columns, channels), jnp.bfloat16)],
     )(*sums, chosen, states)
 
 
@@ -251,9 +248,9 @@
     message_ref, chosen_ref, inner_ref, outer_ref, gain_ref, final_hbm, parts_ref, final_ref, sems = refs[n_sums:]
     split_sums(sum_refs, parts_ref)
     normed, activated = normed_activated(message_ref, chosen_ref, parts_ref, inner_ref, gain_ref)
-    block = final_ref.shape[0] // 2
+    block = final_ref.shape[0] // 4
     copies = []
-    for index in range(2):
+    for index in range(4):
         rows = pl.ds(index * block, block)
         part = slice(index * block, (index + 1) * block)
         final_ref[rows, :] = only_live(
@@ -353,42 +350,44 @@
     waves = [first] + [later_sums(states, targets, live, wave, sizes) for wave in range(1, len(sizes))]
 
     pieces = piece_sizes(half)
-    n_waves = len(sizes)
+    parts = (
+        GROUP * sizes[0] + sizes[1], (GROUP - 1) * sizes[1], 2 * pieces[0] + pieces[1], pieces[1]
+    )
 
     def choose(first):
         return call(
             functools.partial(choose_kernel, sizes, half),
             [jax.ShapeDtypeStruct((source_atoms, rows), jnp.bfloat16)]
-            + [jax.ShapeDtypeStruct((rows, GROUP * size), jnp.bfloat16) for size in sizes]
-            + [jax.ShapeDtypeStruct((rows, 2 * size), jnp.bfloat16) for size in pieces],
+            + [jax.ShapeDtypeStruct((rows, 3 * count), jnp.bfloat16) for count in parts],
             [VMEM] * 4, HIDE_FLOPS,
         )(live, targets, sources, first)
 
     totals, (source_pick, *chosen) = target_totals(waves, choose)
-    target_chosen, source_chosen = chosen[:n_waves], chosen[n_waves:]
-    message = gather_first(totals[0], target_chosen[0], states)
+    early, late = totals[0] + totals[1][:1], totals[1][1:]
+    message = gather_first(early, chosen[0], states)
     reverse_state, *sums = call(
-        functools.partial(layer_one_kernel, len(totals[1])),
+        functools.partial(layer_one_kernel, len(late)),
         [jax.ShapeDtypeStruct((rows, channels), jnp.bfloat16)]
         + [jax.ShapeDtypeStruct((size, channels), jnp.float32) for size in pieces for _ in range(2)],
-        [VMEM] * (len(totals[1]) + 6),
-        2 * rows * channels * (3 * GROUP * sizes[1] + 2 * channels + source_atoms),
-        [pltpu.VMEM((3 * GROUP * sizes[1], channels), jnp.bfloat16)],
-    )(*totals[1], message, target_chosen[1], source_pick, inner_one, outer_one, gain_one.reshape(1, channels))
+        [VMEM] * (len(late) + 6),
+        2 * rows * channels * (3 * parts[1] + 2 * channels + source_atoms),
+        [pltpu.VMEM((3 * parts[1], channels), jnp.bfloat16)],
+    )(*late, message, chosen[1], source_pick, inner_one, outer_one, gain_one.reshape(1, channels))
     totals = source_totals(list(zip(sums[::2], sums[1::2])))
-    message = gather_first(totals[0], source_chosen[0], reverse_state)
+    early, late = totals[0] + totals[1][:1], totals[1][1:]
+    message = gather_first(early, chosen[2], reverse_state)
     final_state = call(
-        functools.partial(layer_two_kernel, len(totals[1])),
+        functools.partial(layer_two_kernel, len(late)),
         jax.ShapeDtypeStruct((rows, channels), jnp.bfloat16),
-        [VMEM] * (len(totals[1]) + 6),
-        2 * rows * channels * (6 * pieces[1] + 2 * channels),
+        [VMEM] * (len(late) + 6),
+        2 * rows * channels * (3 * parts[3] + 2 * channels),
         [
-            pltpu.VMEM((6 * pieces[1], channels), jnp.bfloat16),
+            pltpu.VMEM((3 * parts[3], channels), jnp.bfloat16),
             pltpu.VMEM((rows, channels), jnp.bfloat16),
-            pltpu.SemaphoreType.DMA((2,)),
+            pltpu.SemaphoreType.DMA((4,)),
         ],
         HBM,
-    )(live, *totals[1], message, source_chosen[1], inner_two, outer_two, gain_two.reshape(1, channels))
+    )(live, *late, message, chosen[3], inner_two, outer_two, gain_two.reshape(1, channels))
     return final_state.reshape(1, 1, rows, channels)
 
 

time: 55 us -> 54.7 us (level)
  waiting for transfers between devices: 21.4 us -> 20.1 us
  Pallas kernels: 9.6 us -> 10.5 us
    ppermute x11, waiting for transfers between devices: 12 us -> 11 us  [swap_group(): lax.ppermute(value, ('src', 'tgt'), [(i * across + j, (i ^ partner_mask(k...]
    pallas_call x1, Pallas kernels: 0.64 us -> 1.31 us  [choose(): call(functools.partial(choose_kernel, sizes, half), [jax.ShapeDtypeStruct...]
  transfers between devices with their start and end apart: 19 -> 19, of which waited for: 13 -> 13; matrix products, arithmetic and copies ran while one was open for 0% -> 0% of each run, Pallas kernels for 5% -> 7%
where the time goes in v6:
time: 54.7 us; the launch traced here: 54.5 us
  starting transfers between devices  22.7 us (41%)
  waiting for transfers between devices  20.1 us (37%)
  Pallas kernels  10.5 us (19%)
  between operations  0.85 us (2%)
    ppermute x11, starting transfers between devices, swap_group(): lax.ppermute(value, ('src', 'tgt'), [(i * across + j, (i ^ partner_mask(k...  16 us
    ppermute x11, waiting for transfers between devices, swap_group(): lax.ppermute(value, ('src', 'tgt'), [(i * across + j, (i ^ partner_mask(k...  11 us
    ppermute x8, waiting for transfers between devices, swap(): lax.ppermute(value, axis, [(i, i ^ mask) for i in range(lax.axis_size(axi...  9.09 us
    ppermute x8, starting transfers between devices, swap(): lax.ppermute(value, axis, [(i, i ^ mask) for i in range(lax.axis_size(axi...  6.74 us
    pallas_call x1, Pallas kernels, body(): call(functools.partial(layer_two_kernel, len(late)), jax.ShapeDtypeStruct...  2.41 us
    pallas_call x1, Pallas kernels, body(): call(functools.partial(layer_one_kernel, len(late)), [jax.ShapeDtypeStruc...  2.4 us
    pallas_call x2, Pallas kernels, gather_first(): call(functools.partial(gather_kernel, len(sums)), jax.ShapeDtypeStruct((r...  2.25 us
    pallas_call x1, Pallas kernels, first_sums(): call(functools.partial(first_sum_kernel, sizes), chunk_shapes(0, sizes[0]...  1.68 us
  transfers between devices with their start and end apart: 19, of which 13 were waited for; matrix products, arithmetic and copies ran while one was open for 0% of the time, Pallas kernels for 7%

profile of v6, /device:TPU:0, one launch (start us, length us, event | category | flops | bytes accessed | tf_op | source)
XLA Modules:
  0.0 54.5 jit_solution(1766117366942866231)
XLA Ops:
  0.7 1.7 %shard_map.100 = (f32[64,512]{1,0:T(8,128)S(1)}, f32[64,512]{1,0:T(8,128)S(1)}, f32[64,512]{1,0:T(8,128)S(1)}, f32[64,512]{1,0:T(8,128)S(1)}, s32[1,128]{1,0:T(1...) custom-call(s32[1,1]{1,0:T(1,128)S(6)} %copy.11.live_ref, s32[1,1024]{1,0:T(1,128)} %bitcast.10, ...), custom_call_target="tpu_custom_call" | custom-call | flops 268435456 | tf_op jit(solution)/shard_map/pallas_call | solution.py:147
  2.4 4.0 %collective-permute-start.2 = (f32[64,512]{1,0:T(8,128)S(1)}, f32[64,512]{1,0:T(8,128)S(1)}, u32[]{:S(2)}, u32[]{:S(2)}) collective-permute-start(f32[64,512]{1,0:T(8,128)S(1)} %get-tuple-element.35), channel_id=1, source_target_pairs={{0,12},{1,13},{2,14},{3,15},{4,8},{5,9},{6,10},{7,11},{8,4},{9,5},... | collective-permute-start | bytes 393224 | tf_op jit(solution)/shard_map/ppermute | solution.py:271
  6.4 0.4 collective-permute-start.3
  6.9 0.2 collective-permute-start.4
  7.0 0.5 shard_map.101
  7.5 1.9 %collective-permute-start = (f32[128,512]{1,0:T(8,128)S(1)}, f32[128,512]{1,0:T(8,128)S(1)}, u32[]{:S(2)}, u32[]{:S(2)}) collective-permute-start(f32[128,512]{1,0:T(8,128)S(1)} %get-tuple-element.32), channel_id=1, source_target_pairs={{0,4},{1,9},{2,6},{3,11},{4,0},{5,13},{6,2},{7,15},{8,12},{9,1},{1... | collective-permute-start | bytes 786440 | tf_op jit(solution)/shard_map/ppermute | solution.py:271
  9.4 0.9 %collective-permute-done.2 = f32[64,512]{1,0:T(8,128)S(1)} collective-permute-done((f32[64,512]{1,0:T(8,128)S(1)}, f32[64,512]{1,0:T(8,128)S(1)}, u32[]{:S(2)}, u32[]{:S(2)}) %collective-permute-start.2) | collective-permute-done | bytes 131104 | tf_op jit(solution)/shard_map/ppermute | solution.py:271
  10.3 3.7 %collective-permute-done.3 = f32[64,512]{1,0:T(8,128)S(1)} collective-permute-done((f32[64,512]{1,0:T(8,128)S(1)}, f32[64,512]{1,0:T(8,128)S(1)}, u32[]{:S(2)}, u32[]{:S(2)}) %collective-permute-start.3) | collective-permute-done | bytes 131104 | tf_op jit(solution)/shard_map/ppermute | solution.py:271
  14.0 0.0 collective-permute-done.4
  14.1 2.7 %collective-permute-start.6 = (f32[64,512]{1,0:T(8,128)S(1)}, f32[64,512]{1,0:T(8,128)S(1)}, u32[]{:S(2)}, u32[]{:S(2)}) collective-permute-start(f32[64,512]{1,0:T(8,128)S(1)} %add_add_fusion.tie_ref), channel_id=1, source_target_pairs={{0,16},{4,20},{8,24},{12,28},{16,0},{20,4},{24,8},{28,12},{1,17},{... | collective-permute-start | bytes 393224 | tf_op jit(solution)/shard_map/ppermute | solution.py:266
  16.7 0.0 collective-permute-done
  16.7 1.6 %collective-permute-start.1 = (f32[64,512]{1,0:T(8,128)S(1)}, f32[64,512]{1,0:T(8,128)S(1)}, u32[]{:S(2)}, u32[]{:S(2)}) collective-permute-start(f32[64,512]{1,0:T(8,128)S(1)} %slice_add_fusion), channel_id=1, source_target_pairs={{0,8},{1,5},{2,10},{3,7},{4,12},{5,1},{6,14},{7,3},{8,0},{9,13},{1... | collective-permute-start | bytes 393224 | tf_op jit(solution)/shard_map/ppermute | solution.py:271
  18.4 1.3 %shard_map.102 = (bf16[256,1024]{1,0:T(8,128)(2,1)S(1)}, bf16[1024,960]{1,0:T(8,128)(2,1)S(1)}, bf16[1024,576]{1,0:T(8,128)(2,1)S(1)}, bf16[1024,576]{1,0:T(8,128)(2,1)S(1)}, bf16[1024,192]{1,0:T(8,128)(2,1)S(1)}) custom-call(s32[1,128]{1,0:T(1,128)S(1)} %get-tuple-element.28.live_ref, s32[1,1024]{1,0:T(1,128)S(1)} %get-tuple-element.29.target_ref, ...), custom_call_target="tpu_custom_call" | custom-call | flops 8000000000 | tf_op jit(solution)/shard_map/pallas_call | solution.py:358
  19.7 2.9 %collective-permute-done.1 = f32[64,512]{1,0:T(8,128)S(1)} collective-permute-done((f32[64,512]{1,0:T(8,128)S(1)}, f32[64,512]{1,0:T(8,128)S(1)}, u32[]{:S(2)}, u32[]{:S(2)}) %collective-permute-start.1) | collective-permute-done | bytes 131104 | tf_op jit(solution)/shard_map/ppermute | solution.py:271
  22.6 1.2 %collective-permute-start.5 = (f32[64,512]{1,0:T(8,128)S(1)}, f32[64,512]{1,0:T(8,128)S(1)}, u32[]{:S(2)}, u32[]{:S(2)}) collective-permute-start(f32[64,512]{1,0:T(8,128)S(1)} %fusion), channel_id=1, source_target_pairs={{0,16},{4,20},{8,24},{12,28},{16,0},{20,4},{24,8},{28,12},{1,17},{... | collective-permute-start | bytes 393224 | tf_op jit(solution)/shard_map/ppermute | solution.py:266
  23.9 2.7 %collective-permute-start.12 = (f32[64,512]{1,0:T(8,128)S(1)}, f32[64,512]{1,0:T(8,128)S(1)}, u32[]{:S(2)}, u32[]{:S(2)}) collective-permute-start(f32[64,512]{1,0:T(8,128)S(1)} %add.42.refs_0_), channel_id=1, source_target_pairs={{0,12},{1,13},{2,14},{3,15},{4,8},{5,9},{6,10},{7,11},{8,4},{9,5},... | collective-permute-start | bytes 393224 | tf_op jit(solution)/shard_map/ppermute | solution.py:271
  26.5 1.3 %collective-permute-start.11 = (f32[64,512]{1,0:T(8,128)S(1)}, f32[64,512]{1,0:T(8,128)S(1)}, u32[]{:S(2)}, u32[]{:S(2)}) collective-permute-start(f32[64,512]{1,0:T(8,128)S(1)} %add.42.refs_0_), channel_id=1, source_target_pairs={{0,4},{1,9},{2,6},{3,11},{4,0},{5,13},{6,2},{7,15},{8,12},{9,1},{1... | collective-permute-start | bytes 393224 | tf_op jit(solution)/shard_map/ppermute | solution.py:271
  27.8 1.8 %collective-permute-done.5 = f32[64,512]{1,0:T(8,128)S(1)} collective-permute-done((f32[64,512]{1,0:T(8,128)S(1)}, f32[64,512]{1,0:T(8,128)S(1)}, u32[]{:S(2)}, u32[]{:S(2)}) %collective-permute-start.5) | collective-permute-done | bytes 131104 | tf_op jit(solution)/shard_map/ppermute | solution.py:266
  29.7 0.0 copy-start.3
  29.7 0.0 copy-start.4
  29.7 0.0 copy-start.6
  29.7 1.3 %collective-permute-start.9 = (f32[64,512]{1,0:T(8,128)S(1)}, f32[64,512]{1,0:T(8,128)S(1)}, u32[]{:S(2)}, u32[]{:S(2)}) collective-permute-start(f32[64,512]{1,0:T(8,128)S(1)} %add.43.refs_4_), channel_id=1, source_target_pairs={{0,12},{1,13},{2,14},{3,15},{4,8},{5,9},{6,10},{7,11},{8,4},{9,5},... | collective-permute-start | bytes 393224 | tf_op jit(solution)/shard_map/ppermute | solution.py:271
  31.0 1.4 %collective-permute-start.8 = (f32[64,512]{1,0:T(8,128)S(1)}, f32[64,512]{1,0:T(8,128)S(1)}, u32[]{:S(2)}, u32[]{:S(2)}) collective-permute-start(f32[64,512]{1,0:T(8,128)S(1)} %add.43.refs_4_), channel_id=1, source_target_pairs={{0,4},{1,9},{2,6},{3,11},{4,0},{5,13},{6,2},{7,15},{8,12},{9,1},{1... | collective-permute-start | bytes 393224 | tf_op jit(solution)/shard_map/ppermute | solution.py:271
  32.4 0.3 collective-permute-done.12.refs_3_
  32.6 1.2 %collective-permute-start.7 = (f32[64,512]{1,0:T(8,128)S(1)}, f32[64,512]{1,0:T(8,128)S(1)}, u32[]{:S(2)}, u32[]{:S(2)}) collective-permute-start(f32[64,512]{1,0:T(8,128)S(1)} %add.43.refs_4_), channel_id=1, source_target_pairs={{0,8},{1,5},{2,10},{3,7},{4,12},{5,1},{6,14},{7,3},{8,0},{9,13},{1... | collective-permute-start | bytes 393224 | tf_op jit(solution)/shard_map/ppermute | solution.py:271
  33.8 1.2 %collective-permute-done.11.refs_2_ = f32[64,512]{1,0:T(8,128)S(1)} collective-permute-done((f32[64,512]{1,0:T(8,128)S(1)}, f32[64,512]{1,0:T(8,128)S(1)}, u32[]{:S(2)}, u32[]{:S(2)}) %collective-permute-start.11) | collective-permute-done | bytes 131104 | tf_op jit(solution)/shard_map/ppermute | solution.py:271
  35.0 1.3 %shard_map.103.refs_3_ = f32[1024,512]{1,0:T(8,128)S(1)} custom-call(f32[64,512]{1,0:T(8,128)S(1)} %add.42.refs_0_, f32[64,512]{1,0:T(8,128)S(1)} %collective-permute-done.10.refs_1_, f32[64,512]{1,0:T(8,128)S(1)} %collective-permute-done.11.refs_2_, f32[64,512]{1,0:T(8,128)S(1)} %collective-permute-done.12.refs_3_, f32[64,512]{1,0:T(8,128)S(1)} %add.43.refs_4_, ...), custom_call_target="tpu_custom_call" | custom-call | flops 1006632960 | tf_op jit(solution)/shard_map/pallas_call | solution.py:205
  36.3 1.0 %collective-permute-done.9.refs_2_ = f32[64,512]{1,0:T(8,128)S(1)} collective-permute-done((f32[64,512]{1,0:T(8,128)S(1)}, f32[64,512]{1,0:T(8,128)S(1)}, u32[]{:S(2)}, u32[]{:S(2)}) %collective-permute-start.9) | collective-permute-done | bytes 131104 | tf_op jit(solution)/shard_map/ppermute | solution.py:271
  37.3 0.8 %collective-permute-done.8.refs_1_ = f32[64,512]{1,0:T(8,128)S(1)} collective-permute-done((f32[64,512]{1,0:T(8,128)S(1)}, f32[64,512]{1,0:T(8,128)S(1)}, u32[]{:S(2)}, u32[]{:S(2)}) %collective-permute-start.8) | collective-permute-done | bytes 131104 | tf_op jit(solution)/shard_map/ppermute | solution.py:271
  38.1 0.3 collective-permute-done.7.refs_0_
  38.4 2.4 %shard_map.104 = (bf16[1024,512]{1,0:T(8,128)(2,1)S(1)}, f32[64,512]{1,0:T(8,128)S(1)}, f32[64,512]{1,0:T(8,128)S(1)}, f32[64,512]{1,0:T(8,128)S(1)}, f32[64,512]{1,0:T(8,128)S(1)}) custom-call(f32[64,512]{1,0:T(8,128)S(1)} %collective-permute-done.7.refs_0_, f32[64,512]{1,0:T(8,128)S(1)} %collective-permute-done.8.refs_1_, ...), custom_call_target="tpu_custom_call" | custom-call | flops 1946157056 | tf_op jit(solution)/shard_map/pallas_call | solution.py:368
  40.8 0.1 collective-permute-start.16
  40.9 0.5 collective-permute-start.13
  41.4 0.8 %collective-permute-done.16 = f32[64,512]{1,0:T(8,128)S(1)} collective-permute-done((f32[64,512]{1,0:T(8,128)S(1)}, f32[64,512]{1,0:T(8,128)S(1)}, u32[]{:S(2)}, u32[]{:S(2)}) %collective-permute-start.16) | collective-permute-done | bytes 131104 | tf_op jit(solution)/shard_map/ppermute | solution.py:266
  42.2 1.6 %collective-permute-start.17 = (f32[64,512]{1,0:T(8,128)S(1)}, f32[64,512]{1,0:T(8,128)S(1)}, u32[]{:S(2)}, u32[]{:S(2)}) collective-permute-start(f32[64,512]{1,0:T(8,128)S(1)} %add.46), channel_id=1, source_target_pairs={{0,2},{1,3},{2,0},{3,1},{4,6},{5,7},{6,4},{7,5},{8,10},{9,11},{10,... | collective-permute-start | bytes 393224 | tf_op jit(solution)/shard_map/ppermute | solution.py:266
  43.8 0.0 collective-permute-done.13
  43.8 0.6 %collective-permute-start.14 = (f32[64,512]{1,0:T(8,128)S(1)}, f32[64,512]{1,0:T(8,128)S(1)}, u32[]{:S(2)}, u32[]{:S(2)}) collective-permute-start(f32[64,512]{1,0:T(8,128)S(1)} %add.44), channel_id=1, source_target_pairs={{0,2},{1,3},{2,0},{3,1},{4,6},{5,7},{6,4},{7,5},{8,10},{9,11},{10,... | collective-permute-start | bytes 393224 | tf_op jit(solution)/shard_map/ppermute | solution.py:266
  44.4 4.2 %collective-permute-done.17 = f32[64,512]{1,0:T(8,128)S(1)} collective-permute-done((f32[64,512]{1,0:T(8,128)S(1)}, f32[64,512]{1,0:T(8,128)S(1)}, u32[]{:S(2)}, u32[]{:S(2)}) %collective-permute-start.17) | collective-permute-done | bytes 131104 | tf_op jit(solution)/shard_map/ppermute | solution.py:266
  48.7 0.1 collective-permute-start.18
  48.7 1.9 %collective-permute-done.14 = f32[64,512]{1,0:T(8,128)S(1)} collective-permute-done((f32[64,512]{1,0:T(8,128)S(1)}, f32[64,512]{1,0:T(8,128)S(1)}, u32[]{:S(2)}, u32[]{:S(2)}) %collective-permute-start.14) | collective-permute-done | bytes 131104 | tf_op jit(solution)/shard_map/ppermute | solution.py:266
  50.7 0.1 collective-permute-start.15
  50.8 0.0 collective-permute-done.18.refs_1_
  50.8 0.0 copy-start
  50.8 0.0 copy-start.1
  50.8 0.0 copy-start.2
  50.8 1.0 %shard_map.105.refs_1_ = f32[1024,512]{1,0:T(8,128)S(1)} custom-call(f32[64,512]{1,0:T(8,128)S(1)} %add.47.refs_0_, f32[64,512]{1,0:T(8,128)S(1)} %collective-permute-done.18.refs_1_, f32[64,512]{1,0:T(8,128)S(1)} %add.45.refs_2_, bf16[1024,576]{1,0:T(8,128)(2,1)S(1)} %get-tuple-element.41.refs_3_, bf16[1024,512]{1,0:T(8,128)(2,1)S(1)} %get-tuple-element.50.refs_4_), custom_call_target="tpu_custom_call" | custom-call | flops 603979776 | tf_op jit(solution)/shard_map/pallas_call | solution.py:205
  51.8 0.3 collective-permute-done.15.refs_0_
  52.1 2.4 %shard_map.106 = bf16[1024,512]{1,0:T(8,128)(2,1)} custom-call(s32[1,128]{1,0:T(1,128)S(1)} %get-tuple-element.28.live_ref, f32[64,512]{1,0:T(8,128)S(1)} %collective-permute-done.15.refs_0_, f32[1024,512]{1,0:T(8,128)S(1)} %shard_map.105.refs_1_, bf16[1024,192]{1,0:T(8,128)(2,1)S(1)} %get-tuple-element.42.refs_2_, bf16[512,512]{1,0:T(8,128)(2,1)S(1)} %copy-done, ...), custom_call_target="tpu_custom_call" | custom-call | flops 1275068416 | tf_op jit(solution)/shard_map/pallas_call | solution.py:379
  (20 shorter events, 0.2 us)
Async XLA Ops:
  0.0 18.4 %copy-start.5 = (s32[1,1,1024]{2,1,0:T(1,128)S(1)}, s32[1,1,1024]{2,1,0:T(1,128)}, u32[]{:S(2)}) copy-start(s32[1,1,1024]{2,1,0:T(1,128)} %param.11) | copy-start | bytes 12292
  2.4 7.9 %collective-permute-start.2 = (f32[64,512]{1,0:T(8,128)S(1)}, f32[64,512]{1,0:T(8,128)S(1)}, u32[]{:S(2)}, u32[]{:S(2)}) collective-permute-start(f32[64,512]{1,0:T(8,128)S(1)} %get-tuple-element.35), channel_id=1, source_target_pairs={{0,12},{1,13},{2,14},{3,15},{4,8},{5,9},{6,10},{7,11},{8,4},{9,5},... | collective-permute-start | bytes 393224 | tf_op jit(solution)/shard_map/ppermute | solution.py:271
  6.4 7.6 %collective-permute-start.3 = (f32[64,512]{1,0:T(8,128)S(1)}, f32[64,512]{1,0:T(8,128)S(1)}, u32[]{:S(2)}, u32[]{:S(2)}) collective-permute-start(f32[64,512]{1,0:T(8,128)S(1)} %get-tuple-element.36), channel_id=1, source_target_pairs={{0,8},{1,5},{2,10},{3,7},{4,12},{5,1},{6,14},{7,3},{8,0},{9,13},{1... | collective-permute-start | bytes 393224 | tf_op jit(solution)/shard_map/ppermute | solution.py:271
  6.9 7.2 %collective-permute-start.4 = (f32[64,512]{1,0:T(8,128)S(1)}, f32[64,512]{1,0:T(8,128)S(1)}, u32[]{:S(2)}, u32[]{:S(2)}) collective-permute-start(f32[64,512]{1,0:T(8,128)S(1)} %get-tuple-element.37), channel_id=1, source_target_pairs={{0,4},{1,9},{2,6},{3,11},{4,0},{5,13},{6,2},{7,15},{8,12},{9,1},{1... | collective-permute-start | bytes 393224 | tf_op jit(solution)/shard_map/ppermute | solution.py:271
  7.5 9.2 %collective-permute-start = (f32[128,512]{1,0:T(8,128)S(1)}, f32[128,512]{1,0:T(8,128)S(1)}, u32[]{:S(2)}, u32[]{:S(2)}) collective-permute-start(f32[128,512]{1,0:T(8,128)S(1)} %get-tuple-element.32), channel_id=1, source_target_pairs={{0,4},{1,9},{2,6},{3,11},{4,0},{5,13},{6,2},{7,15},{8,12},{9,1},{1... | collective-permute-start | bytes 786440 | tf_op jit(solution)/shard_map/ppermute | solution.py:271
  14.1 9.8 %collective-permute-start.6 = (f32[64,512]{1,0:T(8,128)S(1)}, f32[64,512]{1,0:T(8,128)S(1)}, u32[]{:S(2)}, u32[]{:S(2)}) collective-permute-start(f32[64,512]{1,0:T(8,128)S(1)} %add_add_fusion.tie_ref), channel_id=1, source_target_pairs={{0,16},{4,20},{8,24},{12,28},{16,0},{20,4},{24,8},{28,12},{1,17},{... | collective-permute-start | bytes 393224 | tf_op jit(solution)/shard_map/ppermute | solution.py:266
  16.7 5.8 %collective-permute-start.1 = (f32[64,512]{1,0:T(8,128)S(1)}, f32[64,512]{1,0:T(8,128)S(1)}, u32[]{:S(2)}, u32[]{:S(2)}) collective-permute-start(f32[64,512]{1,0:T(8,128)S(1)} %slice_add_fusion), channel_id=1, source_target_pairs={{0,8},{1,5},{2,10},{3,7},{4,12},{5,1},{6,14},{7,3},{8,0},{9,13},{1... | collective-permute-start | bytes 393224 | tf_op jit(solution)/shard_map/ppermute | solution.py:271
  22.6 7.0 %collective-permute-start.5 = (f32[64,512]{1,0:T(8,128)S(1)}, f32[64,512]{1,0:T(8,128)S(1)}, u32[]{:S(2)}, u32[]{:S(2)}) collective-permute-start(f32[64,512]{1,0:T(8,128)S(1)} %fusion), channel_id=1, source_target_pairs={{0,16},{4,20},{8,24},{12,28},{16,0},{20,4},{24,8},{28,12},{1,17},{... | collective-permute-start | bytes 393224 | tf_op jit(solution)/shard_map/ppermute | solution.py:266
  23.9 8.8 %collective-permute-start.12 = (f32[64,512]{1,0:T(8,128)S(1)}, f32[64,512]{1,0:T(8,128)S(1)}, u32[]{:S(2)}, u32[]{:S(2)}) collective-permute-start(f32[64,512]{1,0:T(8,128)S(1)} %add.42.refs_0_), channel_id=1, source_target_pairs={{0,12},{1,13},{2,14},{3,15},{4,8},{5,9},{6,10},{7,11},{8,4},{9,5},... | collective-permute-start | bytes 393224 | tf_op jit(solution)/shard_map/ppermute | solution.py:271
  26.5 8.5 %collective-permute-start.11 = (f32[64,512]{1,0:T(8,128)S(1)}, f32[64,512]{1,0:T(8,128)S(1)}, u32[]{:S(2)}, u32[]{:S(2)}) collective-permute-start(f32[64,512]{1,0:T(8,128)S(1)} %add.42.refs_0_), channel_id=1, source_target_pairs={{0,4},{1,9},{2,6},{3,11},{4,0},{5,13},{6,2},{7,15},{8,12},{9,1},{1... | collective-permute-start | bytes 393224 | tf_op jit(solution)/shard_map/ppermute | solution.py:271
  27.8 7.2 %collective-permute-start.10 = (f32[64,512]{1,0:T(8,128)S(1)}, f32[64,512]{1,0:T(8,128)S(1)}, u32[]{:S(2)}, u32[]{:S(2)}) collective-permute-start(f32[64,512]{1,0:T(8,128)S(1)} %add.42.refs_0_), channel_id=1, source_target_pairs={{0,8},{1,5},{2,10},{3,7},{4,12},{5,1},{6,14},{7,3},{8,0},{9,13},{1... | collective-permute-start | bytes 393224 | tf_op jit(solution)/shard_map/ppermute | solution.py:271
  29.7 8.7 %copy-start.3 = (bf16[512,512]{1,0:T(8,128)(2,1)S(1)}, bf16[512,512]{1,0:T(8,128)(2,1)}, u32[]{:S(2)}) copy-start(bf16[512,512]{1,0:T(8,128)(2,1)} %refs_6_.1) | copy-start | bytes 1572868
  29.7 8.7 %copy-start.4 = (bf16[512,512]{1,0:T(8,128)(2,1)S(1)}, bf16[512,512]{1,0:T(8,128)(2,1)}, u32[]{:S(2)}) copy-start(bf16[512,512]{1,0:T(8,128)(2,1)} %refs_7_.1) | copy-start | bytes 1572868
  29.7 8.7 %copy-start.6 = (f32[512]{0:T(512)S(1)}, f32[512]{0:T(512)}, u32[]{:S(2)}) copy-start(f32[512]{0:T(512)} %param.18) | copy-start | bytes 6148
  29.7 7.6 %collective-permute-start.9 = (f32[64,512]{1,0:T(8,128)S(1)}, f32[64,512]{1,0:T(8,128)S(1)}, u32[]{:S(2)}, u32[]{:S(2)}) collective-permute-start(f32[64,512]{1,0:T(8,128)S(1)} %add.43.refs_4_), channel_id=1, source_target_pairs={{0,12},{1,13},{2,14},{3,15},{4,8},{5,9},{6,10},{7,11},{8,4},{9,5},... | collective-permute-start | bytes 393224 | tf_op jit(solution)/shard_map/ppermute | solution.py:271
  31.0 7.1 %collective-permute-start.8 = (f32[64,512]{1,0:T(8,128)S(1)}, f32[64,512]{1,0:T(8,128)S(1)}, u32[]{:S(2)}, u32[]{:S(2)}) collective-permute-start(f32[64,512]{1,0:T(8,128)S(1)} %add.43.refs_4_), channel_id=1, source_target_pairs={{0,4},{1,9},{2,6},{3,11},{4,0},{5,13},{6,2},{7,15},{8,12},{9,1},{1... | collective-permute-start | bytes 393224 | tf_op jit(solution)/shard_map/ppermute | solution.py:271
  32.6 5.7 %collective-permute-start.7 = (f32[64,512]{1,0:T(8,128)S(1)}, f32[64,512]{1,0:T(8,128)S(1)}, u32[]{:S(2)}, u32[]{:S(2)}) collective-permute-start(f32[64,512]{1,0:T(8,128)S(1)} %add.43.refs_4_), channel_id=1, source_target_pairs={{0,8},{1,5},{2,10},{3,7},{4,12},{5,1},{6,14},{7,3},{8,0},{9,13},{1... | collective-permute-start | bytes 393224 | tf_op jit(solution)/shard_map/ppermute | solution.py:271
  40.8 1.4 %collective-permute-start.16 = (f32[64,512]{1,0:T(8,128)S(1)}, f32[64,512]{1,0:T(8,128)S(1)}, u32[]{:S(2)}, u32[]{:S(2)}) collective-permute-start(f32[64,512]{1,0:T(8,128)S(1)} %get-tuple-element.49), channel_id=1, source_target_pairs={{0,1},{1,0},{2,3},{3,2},{4,5},{5,4},{6,7},{7,6},{8,9},{9,8},{10,11... | collective-permute-start | bytes 393224 | tf_op jit(solution)/shard_map/ppermute | solution.py:266
  40.9 2.9 %collective-permute-start.13 = (f32[64,512]{1,0:T(8,128)S(1)}, f32[64,512]{1,0:T(8,128)S(1)}, u32[]{:S(2)}, u32[]{:S(2)}) collective-permute-start(f32[64,512]{1,0:T(8,128)S(1)} %get-tuple-element.47), channel_id=1, source_target_pairs={{0,1},{1,0},{2,3},{3,2},{4,5},{5,4},{6,7},{7,6},{8,9},{9,8},{10,11... | collective-permute-start | bytes 393224 | tf_op jit(solution)/shard_map/ppermute | solution.py:266
  42.2 6.4 %collective-permute-start.17 = (f32[64,512]{1,0:T(8,128)S(1)}, f32[64,512]{1,0:T(8,128)S(1)}, u32[]{:S(2)}, u32[]{:S(2)}) collective-permute-start(f32[64,512]{1,0:T(8,128)S(1)} %add.46), channel_id=1, source_target_pairs={{0,2},{1,3},{2,0},{3,1},{4,6},{5,7},{6,4},{7,5},{8,10},{9,11},{10,... | collective-permute-start | bytes 393224 | tf_op jit(solution)/shard_map/ppermute | solution.py:266
  43.8 6.8 %collective-permute-start.14 = (f32[64,512]{1,0:T(8,128)S(1)}, f32[64,512]{1,0:T(8,128)S(1)}, u32[]{:S(2)}, u32[]{:S(2)}) collective-permute-start(f32[64,512]{1,0:T(8,128)S(1)} %add.44), channel_id=1, source_target_pairs={{0,2},{1,3},{2,0},{3,1},{4,6},{5,7},{6,4},{7,5},{8,10},{9,11},{10,... | collective-permute-start | bytes 393224 | tf_op jit(solution)/shard_map/ppermute | solution.py:266
  48.7 2.1 %collective-permute-start.18 = (f32[64,512]{1,0:T(8,128)S(1)}, f32[64,512]{1,0:T(8,128)S(1)}, u32[]{:S(2)}, u32[]{:S(2)}) collective-permute-start(f32[64,512]{1,0:T(8,128)S(1)} %add.47.refs_0_), channel_id=1, source_target_pairs={{0,1},{1,0},{2,3},{3,2},{4,5},{5,4},{6,7},{7,6},{8,9},{9,8},{10,11... | collective-permute-start | bytes 393224 | tf_op jit(solution)/shard_map/ppermute | solution.py:266
  50.7 1.4 %collective-permute-start.15 = (f32[64,512]{1,0:T(8,128)S(1)}, f32[64,512]{1,0:T(8,128)S(1)}, u32[]{:S(2)}, u32[]{:S(2)}) collective-permute-start(f32[64,512]{1,0:T(8,128)S(1)} %add.45.refs_2_), channel_id=1, source_target_pairs={{0,1},{1,0},{2,3},{3,2},{4,5},{5,4},{6,7},{7,6},{8,9},{9,8},{10,11... | collective-permute-start | bytes 393224 | tf_op jit(solution)/shard_map/ppermute | solution.py:266
  50.8 1.3 %copy-start = (bf16[512,512]{1,0:T(8,128)(2,1)S(1)}, bf16[512,512]{1,0:T(8,128)(2,1)}, u32[]{:S(2)}) copy-start(bf16[512,512]{1,0:T(8,128)(2,1)} %refs_3_.1) | copy-start | bytes 1572868
  50.8 1.3 %copy-start.1 = (bf16[512,512]{1,0:T(8,128)(2,1)S(1)}, bf16[512,512]{1,0:T(8,128)(2,1)}, u32[]{:S(2)}) copy-start(bf16[512,512]{1,0:T(8,128)(2,1)} %refs_4_.1) | copy-start | bytes 1572868
  50.8 1.3 %copy-start.2 = (f32[512]{0:T(512)S(1)}, f32[512]{0:T(512)}, u32[]{:S(2)}) copy-start(f32[512]{0:T(512)} %param.19) | copy-start | bytes 6148

commit v7 on v6

--- a/solution.py
+++ b/solution.py
@@ -14,7 +14,7 @@
 REDUCE_STEPWISE = (False, True)
 SPREAD_STEPWISE = (False, False)
 PIECES = (1, 1)
-PARTS = 2
+PARTS = 4
 LANES = 128
 HIDE_FLOPS = 8 * 10**9
 VMEM_LIMIT = 40 * 1024 * 1024

time: 54.7 us -> 54.6 us (level)
  no operation moved by 1% of the time
where the time goes in v7:
time: 54.6 us; the launch traced here: 54.4 us
  starting transfers between devices  22.7 us (42%)
  waiting for transfers between devices  20.1 us (37%)
  Pallas kernels  10.5 us (19%)
  between operations  0.85 us (2%)
    ppermute x11, starting transfers between devices, swap_group(): lax.ppermute(value, ('src', 'tgt'), [(i * across + j, (i ^ partner_mask(k...  16 us
    ppermute x11, waiting for transfers between devices, swap_group(): lax.ppermute(value, ('src', 'tgt'), [(i * across + j, (i ^ partner_mask(k...  11 us
    ppermute x8, waiting for transfers between devices, swap(): lax.ppermute(value, axis, [(i, i ^ mask) for i in range(lax.axis_size(axi...  9.09 us
    ppermute x8, starting transfers between devices, swap(): lax.ppermute(value, axis, [(i, i ^ mask) for i in range(lax.axis_size(axi...  6.73 us
    pallas_call x1, Pallas kernels, body(): call(functools.partial(layer_two_kernel, len(late)), jax.ShapeDtypeStruct...  2.4 us
    pallas_call x1, Pallas kernels, body(): call(functools.partial(layer_one_kernel, len(late)), [jax.ShapeDtypeStruc...  2.39 us
    pallas_call x2, Pallas kernels, gather_first(): call(functools.partial(gather_kernel, len(sums)), jax.ShapeDtypeStruct((r...  2.27 us
    pallas_call x1, Pallas kernels, first_sums(): call(functools.partial(first_sum_kernel, sizes), chunk_shapes(0, sizes[0]...  1.64 us
  transfers between devices with their start and end apart: 19, of which 13 were waited for; matrix products, arithmetic and copies ran while one was open for 0% of the time, Pallas kernels for 7%

profile of v7, /device:TPU:0, one launch (start us, length us, event | category | flops | bytes accessed | tf_op | source)
XLA Modules:
  0.0 54.4 jit_solution(9824954286161585556)
XLA Ops:
  0.7 1.6 %shard_map.100 = (f32[64,512]{1,0:T(8,128)S(1)}, f32[64,512]{1,0:T(8,128)S(1)}, f32[64,512]{1,0:T(8,128)S(1)}, f32[64,512]{1,0:T(8,128)S(1)}, s32[1,128]{1,0:T(1...) custom-call(s32[1,1]{1,0:T(1,128)S(6)} %copy.11.live_ref, s32[1,1024]{1,0:T(1,128)} %bitcast.10, ...), custom_call_target="tpu_custom_call" | custom-call | flops 268435456 | tf_op jit(solution)/shard_map/pallas_call | solution.py:147
  2.3 4.0 %collective-permute-start.2 = (f32[64,512]{1,0:T(8,128)S(1)}, f32[64,512]{1,0:T(8,128)S(1)}, u32[]{:S(2)}, u32[]{:S(2)}) collective-permute-start(f32[64,512]{1,0:T(8,128)S(1)} %get-tuple-element.35), channel_id=1, source_target_pairs={{0,12},{1,13},{2,14},{3,15},{4,8},{5,9},{6,10},{7,11},{8,4},{9,5},... | collective-permute-start | bytes 393224 | tf_op jit(solution)/shard_map/ppermute | solution.py:271
  6.4 0.5 collective-permute-start.3
  6.8 0.2 collective-permute-start.4
  7.0 0.5 shard_map.101
  7.5 1.9 %collective-permute-start = (f32[128,512]{1,0:T(8,128)S(1)}, f32[128,512]{1,0:T(8,128)S(1)}, u32[]{:S(2)}, u32[]{:S(2)}) collective-permute-start(f32[128,512]{1,0:T(8,128)S(1)} %get-tuple-element.32), channel_id=1, source_target_pairs={{0,4},{1,9},{2,6},{3,11},{4,0},{5,13},{6,2},{7,15},{8,12},{9,1},{1... | collective-permute-start | bytes 786440 | tf_op jit(solution)/shard_map/ppermute | solution.py:271
  9.4 0.9 %collective-permute-done.2 = f32[64,512]{1,0:T(8,128)S(1)} collective-permute-done((f32[64,512]{1,0:T(8,128)S(1)}, f32[64,512]{1,0:T(8,128)S(1)}, u32[]{:S(2)}, u32[]{:S(2)}) %collective-permute-start.2) | collective-permute-done | bytes 131104 | tf_op jit(solution)/shard_map/ppermute | solution.py:271
  10.3 3.7 %collective-permute-done.3 = f32[64,512]{1,0:T(8,128)S(1)} collective-permute-done((f32[64,512]{1,0:T(8,128)S(1)}, f32[64,512]{1,0:T(8,128)S(1)}, u32[]{:S(2)}, u32[]{:S(2)}) %collective-permute-start.3) | collective-permute-done | bytes 131104 | tf_op jit(solution)/shard_map/ppermute | solution.py:271
  14.0 0.0 collective-permute-done.4
  14.0 2.6 %collective-permute-start.6 = (f32[64,512]{1,0:T(8,128)S(1)}, f32[64,512]{1,0:T(8,128)S(1)}, u32[]{:S(2)}, u32[]{:S(2)}) collective-permute-start(f32[64,512]{1,0:T(8,128)S(1)} %add_add_fusion.tie_ref), channel_id=1, source_target_pairs={{0,16},{4,20},{8,24},{12,28},{16,0},{20,4},{24,8},{28,12},{1,17},{... | collective-permute-start | bytes 393224 | tf_op jit(solution)/shard_map/ppermute | solution.py:266
  16.7 0.0 collective-permute-done
  16.7 1.6 %collective-permute-start.1 = (f32[64,512]{1,0:T(8,128)S(1)}, f32[64,512]{1,0:T(8,128)S(1)}, u32[]{:S(2)}, u32[]{:S(2)}) collective-permute-start(f32[64,512]{1,0:T(8,128)S(1)} %slice_add_fusion), channel_id=1, source_target_pairs={{0,8},{1,5},{2,10},{3,7},{4,12},{5,1},{6,14},{7,3},{8,0},{9,13},{1... | collective-permute-start | bytes 393224 | tf_op jit(solution)/shard_map/ppermute | solution.py:271
  18.3 1.3 %shard_map.102 = (bf16[256,1024]{1,0:T(8,128)(2,1)S(1)}, bf16[1024,960]{1,0:T(8,128)(2,1)S(1)}, bf16[1024,576]{1,0:T(8,128)(2,1)S(1)}, bf16[1024,576]{1,0:T(8,128)(2,1)S(1)}, bf16[1024,192]{1,0:T(8,128)(2,1)S(1)}) custom-call(s32[1,128]{1,0:T(1,128)S(1)} %get-tuple-element.28.live_ref, s32[1,1024]{1,0:T(1,128)S(1)} %get-tuple-element.29.target_ref, ...), custom_call_target="tpu_custom_call" | custom-call | flops 8000000000 | tf_op jit(solution)/shard_map/pallas_call | solution.py:358
  19.7 2.9 %collective-permute-done.1 = f32[64,512]{1,0:T(8,128)S(1)} collective-permute-done((f32[64,512]{1,0:T(8,128)S(1)}, f32[64,512]{1,0:T(8,128)S(1)}, u32[]{:S(2)}, u32[]{:S(2)}) %collective-permute-start.1) | collective-permute-done | bytes 131104 | tf_op jit(solution)/shard_map/ppermute | solution.py:271
  22.5 1.2 %collective-permute-start.5 = (f32[64,512]{1,0:T(8,128)S(1)}, f32[64,512]{1,0:T(8,128)S(1)}, u32[]{:S(2)}, u32[]{:S(2)}) collective-permute-start(f32[64,512]{1,0:T(8,128)S(1)} %fusion), channel_id=1, source_target_pairs={{0,16},{4,20},{8,24},{12,28},{16,0},{20,4},{24,8},{28,12},{1,17},{... | collective-permute-start | bytes 393224 | tf_op jit(solution)/shard_map/ppermute | solution.py:266
  23.8 2.7 %collective-permute-start.12 = (f32[64,512]{1,0:T(8,128)S(1)}, f32[64,512]{1,0:T(8,128)S(1)}, u32[]{:S(2)}, u32[]{:S(2)}) collective-permute-start(f32[64,512]{1,0:T(8,128)S(1)} %add.42.refs_0_), channel_id=1, source_target_pairs={{0,12},{1,13},{2,14},{3,15},{4,8},{5,9},{6,10},{7,11},{8,4},{9,5},... | collective-permute-start | bytes 393224 | tf_op jit(solution)/shard_map/ppermute | solution.py:271
  26.5 1.3 %collective-permute-start.11 = (f32[64,512]{1,0:T(8,128)S(1)}, f32[64,512]{1,0:T(8,128)S(1)}, u32[]{:S(2)}, u32[]{:S(2)}) collective-permute-start(f32[64,512]{1,0:T(8,128)S(1)} %add.42.refs_0_), channel_id=1, source_target_pairs={{0,4},{1,9},{2,6},{3,11},{4,0},{5,13},{6,2},{7,15},{8,12},{9,1},{1... | collective-permute-start | bytes 393224 | tf_op jit(solution)/shard_map/ppermute | solution.py:271
  27.8 0.0 collective-permute-start.10
  27.8 1.8 %collective-permute-done.5 = f32[64,512]{1,0:T(8,128)S(1)} collective-permute-done((f32[64,512]{1,0:T(8,128)S(1)}, f32[64,512]{1,0:T(8,128)S(1)}, u32[]{:S(2)}, u32[]{:S(2)}) %collective-permute-start.5) | collective-permute-done | bytes 131104 | tf_op jit(solution)/shard_map/ppermute | solution.py:266
  29.6 0.0 copy-start.3
  29.6 0.0 copy-start.4
  29.6 0.0 copy-start.6
  29.7 1.2 %collective-permute-start.9 = (f32[64,512]{1,0:T(8,128)S(1)}, f32[64,512]{1,0:T(8,128)S(1)}, u32[]{:S(2)}, u32[]{:S(2)}) collective-permute-start(f32[64,512]{1,0:T(8,128)S(1)} %add.43.refs_4_), channel_id=1, source_target_pairs={{0,12},{1,13},{2,14},{3,15},{4,8},{5,9},{6,10},{7,11},{8,4},{9,5},... | collective-permute-start | bytes 393224 | tf_op jit(solution)/shard_map/ppermute | solution.py:271
  30.9 1.4 %collective-permute-start.8 = (f32[64,512]{1,0:T(8,128)S(1)}, f32[64,512]{1,0:T(8,128)S(1)}, u32[]{:S(2)}, u32[]{:S(2)}) collective-permute-start(f32[64,512]{1,0:T(8,128)S(1)} %add.43.refs_4_), channel_id=1, source_target_pairs={{0,4},{1,9},{2,6},{3,11},{4,0},{5,13},{6,2},{7,15},{8,12},{9,1},{1... | collective-permute-start | bytes 393224 | tf_op jit(solution)/shard_map/ppermute | solution.py:271
  32.3 0.3 collective-permute-done.12.refs_3_
  32.6 1.2 %collective-permute-start.7 = (f32[64,512]{1,0:T(8,128)S(1)}, f32[64,512]{1,0:T(8,128)S(1)}, u32[]{:S(2)}, u32[]{:S(2)}) collective-permute-start(f32[64,512]{1,0:T(8,128)S(1)} %add.43.refs_4_), channel_id=1, source_target_pairs={{0,8},{1,5},{2,10},{3,7},{4,12},{5,1},{6,14},{7,3},{8,0},{9,13},{1... | collective-permute-start | bytes 393224 | tf_op jit(solution)/shard_map/ppermute | solution.py:271
  33.7 1.2 %collective-permute-done.11.refs_2_ = f32[64,512]{1,0:T(8,128)S(1)} collective-permute-done((f32[64,512]{1,0:T(8,128)S(1)}, f32[64,512]{1,0:T(8,128)S(1)}, u32[]{:S(2)}, u32[]{:S(2)}) %collective-permute-start.11) | collective-permute-done | bytes 131104 | tf_op jit(solution)/shard_map/ppermute | solution.py:271
  35.0 1.3 %shard_map.103.refs_3_ = f32[1024,512]{1,0:T(8,128)S(1)} custom-call(f32[64,512]{1,0:T(8,128)S(1)} %add.42.refs_0_, f32[64,512]{1,0:T(8,128)S(1)} %collective-permute-done.10.refs_1_, f32[64,512]{1,0:T(8,128)S(1)} %collective-permute-done.11.refs_2_, f32[64,512]{1,0:T(8,128)S(1)} %collective-permute-done.12.refs_3_, f32[64,512]{1,0:T(8,128)S(1)} %add.43.refs_4_, ...), custom_call_target="tpu_custom_call" | custom-call | flops 1006632960 | tf_op jit(solution)/shard_map/pallas_call | solution.py:205
  36.3 1.0 %collective-permute-done.9.refs_2_ = f32[64,512]{1,0:T(8,128)S(1)} collective-permute-done((f32[64,512]{1,0:T(8,128)S(1)}, f32[64,512]{1,0:T(8,128)S(1)}, u32[]{:S(2)}, u32[]{:S(2)}) %collective-permute-start.9) | collective-permute-done | bytes 131104 | tf_op jit(solution)/shard_map/ppermute | solution.py:271
  37.3 0.8 %collective-permute-done.8.refs_1_ = f32[64,512]{1,0:T(8,128)S(1)} collective-permute-done((f32[64,512]{1,0:T(8,128)S(1)}, f32[64,512]{1,0:T(8,128)S(1)}, u32[]{:S(2)}, u32[]{:S(2)}) %collective-permute-start.8) | collective-permute-done | bytes 131104 | tf_op jit(solution)/shard_map/ppermute | solution.py:271
  38.1 0.3 collective-permute-done.7.refs_0_
  38.3 2.4 %shard_map.104 = (bf16[1024,512]{1,0:T(8,128)(2,1)S(1)}, f32[64,512]{1,0:T(8,128)S(1)}, f32[64,512]{1,0:T(8,128)S(1)}, f32[64,512]{1,0:T(8,128)S(1)}, f32[64,512]{1,0:T(8,128)S(1)}) custom-call(f32[64,512]{1,0:T(8,128)S(1)} %collective-permute-done.7.refs_0_, f32[64,512]{1,0:T(8,128)S(1)} %collective-permute-done.8.refs_1_, ...), custom_call_target="tpu_custom_call" | custom-call | flops 1946157056 | tf_op jit(solution)/shard_map/pallas_call | solution.py:368
  40.7 0.1 collective-permute-start.16
  40.8 0.5 collective-permute-start.13
  41.3 0.8 %collective-permute-done.16 = f32[64,512]{1,0:T(8,128)S(1)} collective-permute-done((f32[64,512]{1,0:T(8,128)S(1)}, f32[64,512]{1,0:T(8,128)S(1)}, u32[]{:S(2)}, u32[]{:S(2)}) %collective-permute-start.16) | collective-permute-done | bytes 131104 | tf_op jit(solution)/shard_map/ppermute | solution.py:266
  42.2 1.7 %collective-permute-start.17 = (f32[64,512]{1,0:T(8,128)S(1)}, f32[64,512]{1,0:T(8,128)S(1)}, u32[]{:S(2)}, u32[]{:S(2)}) collective-permute-start(f32[64,512]{1,0:T(8,128)S(1)} %add.46), channel_id=1, source_target_pairs={{0,2},{1,3},{2,0},{3,1},{4,6},{5,7},{6,4},{7,5},{8,10},{9,11},{10,... | collective-permute-start | bytes 393224 | tf_op jit(solution)/shard_map/ppermute | solution.py:266
  43.9 0.0 collective-permute-done.13
  43.9 0.5 collective-permute-start.14
  44.4 4.2 %collective-permute-done.17 = f32[64,512]{1,0:T(8,128)S(1)} collective-permute-done((f32[64,512]{1,0:T(8,128)S(1)}, f32[64,512]{1,0:T(8,128)S(1)}, u32[]{:S(2)}, u32[]{:S(2)}) %collective-permute-start.17) | collective-permute-done | bytes 131104 | tf_op jit(solution)/shard_map/ppermute | solution.py:266
  48.6 0.1 collective-permute-start.18
  48.7 1.9 %collective-permute-done.14 = f32[64,512]{1,0:T(8,128)S(1)} collective-permute-done((f32[64,512]{1,0:T(8,128)S(1)}, f32[64,512]{1,0:T(8,128)S(1)}, u32[]{:S(2)}, u32[]{:S(2)}) %collective-permute-start.14) | collective-permute-done | bytes 131104 | tf_op jit(solution)/shard_map/ppermute | solution.py:266
  50.6 0.1 collective-permute-start.15
  50.7 0.0 copy-start
  50.7 0.0 copy-start.1
  50.7 0.0 copy-start.2
  50.7 1.0 %shard_map.105.refs_1_ = f32[1024,512]{1,0:T(8,128)S(1)} custom-call(f32[64,512]{1,0:T(8,128)S(1)} %add.47.refs_0_, f32[64,512]{1,0:T(8,128)S(1)} %collective-permute-done.18.refs_1_, f32[64,512]{1,0:T(8,128)S(1)} %add.45.refs_2_, bf16[1024,576]{1,0:T(8,128)(2,1)S(1)} %get-tuple-element.41.refs_3_, bf16[1024,512]{1,0:T(8,128)(2,1)S(1)} %get-tuple-element.50.refs_4_), custom_call_target="tpu_custom_call" | custom-call | flops 603979776 | tf_op jit(solution)/shard_map/pallas_call | solution.py:205
  51.7 0.3 collective-permute-done.15.refs_0_
  52.0 2.4 %shard_map.106 = bf16[1024,512]{1,0:T(8,128)(2,1)} custom-call(s32[1,128]{1,0:T(1,128)S(1)} %get-tuple-element.28.live_ref, f32[64,512]{1,0:T(8,128)S(1)} %collective-permute-done.15.refs_0_, f32[1024,512]{1,0:T(8,128)S(1)} %shard_map.105.refs_1_, bf16[1024,192]{1,0:T(8,128)(2,1)S(1)} %get-tuple-element.42.refs_2_, bf16[512,512]{1,0:T(8,128)(2,1)S(1)} %copy-done, ...), custom_call_target="tpu_custom_call" | custom-call | flops 1275068416 | tf_op jit(solution)/shard_map/pallas_call | solution.py:379
  (20 shorter events, 0.2 us)
Async XLA Ops:
  0.0 18.3 %copy-start.5 = (s32[1,1,1024]{2,1,0:T(1,128)S(1)}, s32[1,1,1024]{2,1,0:T(1,128)}, u32[]{:S(2)}) copy-start(s32[1,1,1024]{2,1,0:T(1,128)} %param.11) | copy-start | bytes 12292
  2.3 7.9 %collective-permute-start.2 = (f32[64,512]{1,0:T(8,128)S(1)}, f32[64,512]{1,0:T(8,128)S(1)}, u32[]{:S(2)}, u32[]{:S(2)}) collective-permute-start(f32[64,512]{1,0:T(8,128)S(1)} %get-tuple-element.35), channel_id=1, source_target_pairs={{0,12},{1,13},{2,14},{3,15},{4,8},{5,9},{6,10},{7,11},{8,4},{9,5},... | collective-permute-start | bytes 393224 | tf_op jit(solution)/shard_map/ppermute | solution.py:271
  6.4 7.6 %collective-permute-start.3 = (f32[64,512]{1,0:T(8,128)S(1)}, f32[64,512]{1,0:T(8,128)S(1)}, u32[]{:S(2)}, u32[]{:S(2)}) collective-permute-start(f32[64,512]{1,0:T(8,128)S(1)} %get-tuple-element.36), channel_id=1, source_target_pairs={{0,8},{1,5},{2,10},{3,7},{4,12},{5,1},{6,14},{7,3},{8,0},{9,13},{1... | collective-permute-start | bytes 393224 | tf_op jit(solution)/shard_map/ppermute | solution.py:271
  6.8 7.2 %collective-permute-start.4 = (f32[64,512]{1,0:T(8,128)S(1)}, f32[64,512]{1,0:T(8,128)S(1)}, u32[]{:S(2)}, u32[]{:S(2)}) collective-permute-start(f32[64,512]{1,0:T(8,128)S(1)} %get-tuple-element.37), channel_id=1, source_target_pairs={{0,4},{1,9},{2,6},{3,11},{4,0},{5,13},{6,2},{7,15},{8,12},{9,1},{1... | collective-permute-start | bytes 393224 | tf_op jit(solution)/shard_map/ppermute | solution.py:271
  7.5 9.2 %collective-permute-start = (f32[128,512]{1,0:T(8,128)S(1)}, f32[128,512]{1,0:T(8,128)S(1)}, u32[]{:S(2)}, u32[]{:S(2)}) collective-permute-start(f32[128,512]{1,0:T(8,128)S(1)} %get-tuple-element.32), channel_id=1, source_target_pairs={{0,4},{1,9},{2,6},{3,11},{4,0},{5,13},{6,2},{7,15},{8,12},{9,1},{1... | collective-permute-start | bytes 786440 | tf_op jit(solution)/shard_map/ppermute | solution.py:271
  14.0 9.7 %collective-permute-start.6 = (f32[64,512]{1,0:T(8,128)S(1)}, f32[64,512]{1,0:T(8,128)S(1)}, u32[]{:S(2)}, u32[]{:S(2)}) collective-permute-start(f32[64,512]{1,0:T(8,128)S(1)} %add_add_fusion.tie_ref), channel_id=1, source_target_pairs={{0,16},{4,20},{8,24},{12,28},{16,0},{20,4},{24,8},{28,12},{1,17},{... | collective-permute-start | bytes 393224 | tf_op jit(solution)/shard_map/ppermute | solution.py:266
  16.7 5.8 %collective-permute-start.1 = (f32[64,512]{1,0:T(8,128)S(1)}, f32[64,512]{1,0:T(8,128)S(1)}, u32[]{:S(2)}, u32[]{:S(2)}) collective-permute-start(f32[64,512]{1,0:T(8,128)S(1)} %slice_add_fusion), channel_id=1, source_target_pairs={{0,8},{1,5},{2,10},{3,7},{4,12},{5,1},{6,14},{7,3},{8,0},{9,13},{1... | collective-permute-start | bytes 393224 | tf_op jit(solution)/shard_map/ppermute | solution.py:271
  22.5 7.0 %collective-permute-start.5 = (f32[64,512]{1,0:T(8,128)S(1)}, f32[64,512]{1,0:T(8,128)S(1)}, u32[]{:S(2)}, u32[]{:S(2)}) collective-permute-start(f32[64,512]{1,0:T(8,128)S(1)} %fusion), channel_id=1, source_target_pairs={{0,16},{4,20},{8,24},{12,28},{16,0},{20,4},{24,8},{28,12},{1,17},{... | collective-permute-start | bytes 393224 | tf_op jit(solution)/shard_map/ppermute | solution.py:266
  23.8 8.8 %collective-permute-start.12 = (f32[64,512]{1,0:T(8,128)S(1)}, f32[64,512]{1,0:T(8,128)S(1)}, u32[]{:S(2)}, u32[]{:S(2)}) collective-permute-start(f32[64,512]{1,0:T(8,128)S(1)} %add.42.refs_0_), channel_id=1, source_target_pairs={{0,12},{1,13},{2,14},{3,15},{4,8},{5,9},{6,10},{7,11},{8,4},{9,5},... | collective-permute-start | bytes 393224 | tf_op jit(solution)/shard_map/ppermute | solution.py:271
  26.5 8.5 %collective-permute-start.11 = (f32[64,512]{1,0:T(8,128)S(1)}, f32[64,512]{1,0:T(8,128)S(1)}, u32[]{:S(2)}, u32[]{:S(2)}) collective-permute-start(f32[64,512]{1,0:T(8,128)S(1)} %add.42.refs_0_), channel_id=1, source_target_pairs={{0,4},{1,9},{2,6},{3,11},{4,0},{5,13},{6,2},{7,15},{8,12},{9,1},{1... | collective-permute-start | bytes 393224 | tf_op jit(solution)/shard_map/ppermute | solution.py:271
  27.8 7.2 %collective-permute-start.10 = (f32[64,512]{1,0:T(8,128)S(1)}, f32[64,512]{1,0:T(8,128)S(1)}, u32[]{:S(2)}, u32[]{:S(2)}) collective-permute-start(f32[64,512]{1,0:T(8,128)S(1)} %add.42.refs_0_), channel_id=1, source_target_pairs={{0,8},{1,5},{2,10},{3,7},{4,12},{5,1},{6,14},{7,3},{8,0},{9,13},{1... | collective-permute-start | bytes 393224 | tf_op jit(solution)/shard_map/ppermute | solution.py:271
  29.6 8.7 %copy-start.3 = (bf16[512,512]{1,0:T(8,128)(2,1)S(1)}, bf16[512,512]{1,0:T(8,128)(2,1)}, u32[]{:S(2)}) copy-start(bf16[512,512]{1,0:T(8,128)(2,1)} %refs_6_.1) | copy-start | bytes 1572868
  29.6 8.7 %copy-start.4 = (bf16[512,512]{1,0:T(8,128)(2,1)S(1)}, bf16[512,512]{1,0:T(8,128)(2,1)}, u32[]{:S(2)}) copy-start(bf16[512,512]{1,0:T(8,128)(2,1)} %refs_7_.1) | copy-start | bytes 1572868
  29.6 8.7 %copy-start.6 = (f32[512]{0:T(512)S(1)}, f32[512]{0:T(512)}, u32[]{:S(2)}) copy-start(f32[512]{0:T(512)} %param.18) | copy-start | bytes 6148
  29.7 7.6 %collective-permute-start.9 = (f32[64,512]{1,0:T(8,128)S(1)}, f32[64,512]{1,0:T(8,128)S(1)}, u32[]{:S(2)}, u32[]{:S(2)}) collective-permute-start(f32[64,512]{1,0:T(8,128)S(1)} %add.43.refs_4_), channel_id=1, source_target_pairs={{0,12},{1,13},{2,14},{3,15},{4,8},{5,9},{6,10},{7,11},{8,4},{9,5},... | collective-permute-start | bytes 393224 | tf_op jit(solution)/shard_map/ppermute | solution.py:271
  30.9 7.2 %collective-permute-start.8 = (f32[64,512]{1,0:T(8,128)S(1)}, f32[64,512]{1,0:T(8,128)S(1)}, u32[]{:S(2)}, u32[]{:S(2)}) collective-permute-start(f32[64,512]{1,0:T(8,128)S(1)} %add.43.refs_4_), channel_id=1, source_target_pairs={{0,4},{1,9},{2,6},{3,11},{4,0},{5,13},{6,2},{7,15},{8,12},{9,1},{1... | collective-permute-start | bytes 393224 | tf_op jit(solution)/shard_map/ppermute | solution.py:271
  32.6 5.7 %collective-permute-start.7 = (f32[64,512]{1,0:T(8,128)S(1)}, f32[64,512]{1,0:T(8,128)S(1)}, u32[]{:S(2)}, u32[]{:S(2)}) collective-permute-start(f32[64,512]{1,0:T(8,128)S(1)} %add.43.refs_4_), channel_id=1, source_target_pairs={{0,8},{1,5},{2,10},{3,7},{4,12},{5,1},{6,14},{7,3},{8,0},{9,13},{1... | collective-permute-start | bytes 393224 | tf_op jit(solution)/shard_map/ppermute | solution.py:271
  40.7 1.4 %collective-permute-start.16 = (f32[64,512]{1,0:T(8,128)S(1)}, f32[64,512]{1,0:T(8,128)S(1)}, u32[]{:S(2)}, u32[]{:S(2)}) collective-permute-start(f32[64,512]{1,0:T(8,128)S(1)} %get-tuple-element.49), channel_id=1, source_target_pairs={{0,1},{1,0},{2,3},{3,2},{4,5},{5,4},{6,7},{7,6},{8,9},{9,8},{10,11... | collective-permute-start | bytes 393224 | tf_op jit(solution)/shard_map/ppermute | solution.py:266
  40.8 3.0 %collective-permute-start.13 = (f32[64,512]{1,0:T(8,128)S(1)}, f32[64,512]{1,0:T(8,128)S(1)}, u32[]{:S(2)}, u32[]{:S(2)}) collective-permute-start(f32[64,512]{1,0:T(8,128)S(1)} %get-tuple-element.47), channel_id=1, source_target_pairs={{0,1},{1,0},{2,3},{3,2},{4,5},{5,4},{6,7},{7,6},{8,9},{9,8},{10,11... | collective-permute-start | bytes 393224 | tf_op jit(solution)/shard_map/ppermute | solution.py:266
  42.2 6.4 %collective-permute-start.17 = (f32[64,512]{1,0:T(8,128)S(1)}, f32[64,512]{1,0:T(8,128)S(1)}, u32[]{:S(2)}, u32[]{:S(2)}) collective-permute-start(f32[64,512]{1,0:T(8,128)S(1)} %add.46), channel_id=1, source_target_pairs={{0,2},{1,3},{2,0},{3,1},{4,6},{5,7},{6,4},{7,5},{8,10},{9,11},{10,... | collective-permute-start | bytes 393224 | tf_op jit(solution)/shard_map/ppermute | solution.py:266
  43.9 6.7 %collective-permute-start.14 = (f32[64,512]{1,0:T(8,128)S(1)}, f32[64,512]{1,0:T(8,128)S(1)}, u32[]{:S(2)}, u32[]{:S(2)}) collective-permute-start(f32[64,512]{1,0:T(8,128)S(1)} %add.44), channel_id=1, source_target_pairs={{0,2},{1,3},{2,0},{3,1},{4,6},{5,7},{6,4},{7,5},{8,10},{9,11},{10,... | collective-permute-start | bytes 393224 | tf_op jit(solution)/shard_map/ppermute | solution.py:266
  48.6 2.1 %collective-permute-start.18 = (f32[64,512]{1,0:T(8,128)S(1)}, f32[64,512]{1,0:T(8,128)S(1)}, u32[]{:S(2)}, u32[]{:S(2)}) collective-permute-start(f32[64,512]{1,0:T(8,128)S(1)} %add.47.refs_0_), channel_id=1, source_target_pairs={{0,1},{1,0},{2,3},{3,2},{4,5},{5,4},{6,7},{7,6},{8,9},{9,8},{10,11... | collective-permute-start | bytes 393224 | tf_op jit(solution)/shard_map/ppermute | solution.py:266
  50.6 1.4 %collective-permute-start.15 = (f32[64,512]{1,0:T(8,128)S(1)}, f32[64,512]{1,0:T(8,128)S(1)}, u32[]{:S(2)}, u32[]{:S(2)}) collective-permute-start(f32[64,512]{1,0:T(8,128)S(1)} %add.45.refs_2_), channel_id=1, source_target_pairs={{0,1},{1,0},{2,3},{3,2},{4,5},{5,4},{6,7},{7,6},{8,9},{9,8},{10,11... | collective-permute-start | bytes 393224 | tf_op jit(solution)/shard_map/ppermute | solution.py:266
  50.7 1.3 %copy-start = (bf16[512,512]{1,0:T(8,128)(2,1)S(1)}, bf16[512,512]{1,0:T(8,128)(2,1)}, u32[]{:S(2)}) copy-start(bf16[512,512]{1,0:T(8,128)(2,1)} %refs_3_.1) | copy-start | bytes 1572868
  50.7 1.3 %copy-start.1 = (bf16[512,512]{1,0:T(8,128)(2,1)S(1)}, bf16[512,512]{1,0:T(8,128)(2,1)}, u32[]{:S(2)}) copy-start(bf16[512,512]{1,0:T(8,128)(2,1)} %refs_4_.1) | copy-start | bytes 1572868
  50.7 1.3 %copy-start.2 = (f32[512]{0:T(512)S(1)}, f32[512]{0:T(512)}, u32[]{:S(2)}) copy-start(f32[512]{0:T(512)} %param.19) | copy-start | bytes 6148

commit v8 on v7

--- a/solution.py
+++ b/solution.py
@@ -315,7 +315,7 @@
     for mask in higher_masks("src", GROUP):
         parts = [swap(value, "src", mask) for value in sums]
         first = sums[0] + tie(parts[0], sums[1])
-        sums = [first, sums[1] + tie(parts[1], first)]
+        sums = [first, sums[1] + parts[1]]
     return [spread(value, stepwise) for value, stepwise in zip(sums, SPREAD_STEPWISE)], made
 
 

time: 54.6 us -> 54.6 us (level)
  no operation moved by 1% of the time
where the time goes in v8:
time: 54.6 us; the launch traced here: 54.4 us
  starting transfers between devices  22.7 us (42%)
  waiting for transfers between devices  20.1 us (37%)
  Pallas kernels  10.5 us (19%)
  between operations  0.85 us (2%)
    ppermute x11, starting transfers between devices, swap_group(): lax.ppermute(value, ('src', 'tgt'), [(i * across + j, (i ^ partner_mask(k...  16 us
    ppermute x11, waiting for transfers between devices, swap_group(): lax.ppermute(value, ('src', 'tgt'), [(i * across + j, (i ^ partner_mask(k...  11 us
    ppermute x8, waiting for transfers between devices, swap(): lax.ppermute(value, axis, [(i, i ^ mask) for i in range(lax.axis_size(axi...  9.09 us
    ppermute x8, starting transfers between devices, swap(): lax.ppermute(value, axis, [(i, i ^ mask) for i in range(lax.axis_size(axi...  6.73 us
    pallas_call x1, Pallas kernels, body(): call(functools.partial(layer_two_kernel, len(late)), jax.ShapeDtypeStruct...  2.4 us
    pallas_call x1, Pallas kernels, body(): call(functools.partial(layer_one_kernel, len(late)), [jax.ShapeDtypeStruc...  2.39 us
    pallas_call x2, Pallas kernels, gather_first(): call(functools.partial(gather_kernel, len(sums)), jax.ShapeDtypeStruct((r...  2.27 us
    pallas_call x1, Pallas kernels, first_sums(): call(functools.partial(first_sum_kernel, sizes), chunk_shapes(0, sizes[0]...  1.64 us
  transfers between devices with their start and end apart: 19, of which 13 were waited for; matrix products, arithmetic and copies ran while one was open for 0% of the time, Pallas kernels for 7%

profile of v8, /device:TPU:0, one launch (start us, length us, event | category | flops | bytes accessed | tf_op | source)
XLA Modules:
  0.0 54.4 jit_solution(9824954286161585556)
XLA Ops:
  0.7 1.6 %shard_map.100 = (f32[64,512]{1,0:T(8,128)S(1)}, f32[64,512]{1,0:T(8,128)S(1)}, f32[64,512]{1,0:T(8,128)S(1)}, f32[64,512]{1,0:T(8,128)S(1)}, s32[1,128]{1,0:T(1...) custom-call(s32[1,1]{1,0:T(1,128)S(6)} %copy.11.live_ref, s32[1,1024]{1,0:T(1,128)} %bitcast.10, ...), custom_call_target="tpu_custom_call" | custom-call | flops 268435456 | tf_op jit(solution)/shard_map/pallas_call | solution.py:147
  2.3 4.0 %collective-permute-start.2 = (f32[64,512]{1,0:T(8,128)S(1)}, f32[64,512]{1,0:T(8,128)S(1)}, u32[]{:S(2)}, u32[]{:S(2)}) collective-permute-start(f32[64,512]{1,0:T(8,128)S(1)} %get-tuple-element.34), channel_id=1, source_target_pairs={{0,12},{1,13},{2,14},{3,15},{4,8},{5,9},{6,10},{7,11},{8,4},{9,5},... | collective-permute-start | bytes 393224 | tf_op jit(solution)/shard_map/ppermute | solution.py:271
  6.4 0.5 collective-permute-start.3
  6.8 0.2 collective-permute-start.4
  7.0 0.5 shard_map.101
  7.5 1.9 %collective-permute-start = (f32[128,512]{1,0:T(8,128)S(1)}, f32[128,512]{1,0:T(8,128)S(1)}, u32[]{:S(2)}, u32[]{:S(2)}) collective-permute-start(f32[128,512]{1,0:T(8,128)S(1)} %get-tuple-element.31), channel_id=1, source_target_pairs={{0,4},{1,9},{2,6},{3,11},{4,0},{5,13},{6,2},{7,15},{8,12},{9,1},{1... | collective-permute-start | bytes 786440 | tf_op jit(solution)/shard_map/ppermute | solution.py:271
  9.4 0.9 %collective-permute-done.2 = f32[64,512]{1,0:T(8,128)S(1)} collective-permute-done((f32[64,512]{1,0:T(8,128)S(1)}, f32[64,512]{1,0:T(8,128)S(1)}, u32[]{:S(2)}, u32[]{:S(2)}) %collective-permute-start.2) | collective-permute-done | bytes 131104 | tf_op jit(solution)/shard_map/ppermute | solution.py:271
  10.3 3.7 %collective-permute-done.3 = f32[64,512]{1,0:T(8,128)S(1)} collective-permute-done((f32[64,512]{1,0:T(8,128)S(1)}, f32[64,512]{1,0:T(8,128)S(1)}, u32[]{:S(2)}, u32[]{:S(2)}) %collective-permute-start.3) | collective-permute-done | bytes 131104 | tf_op jit(solution)/shard_map/ppermute | solution.py:271
  14.0 0.0 collective-permute-done.4
  14.0 2.6 %collective-permute-start.9 = (f32[64,512]{1,0:T(8,128)S(1)}, f32[64,512]{1,0:T(8,128)S(1)}, u32[]{:S(2)}, u32[]{:S(2)}) collective-permute-start(f32[64,512]{1,0:T(8,128)S(1)} %add_add_fusion.tie_ref), channel_id=1, source_target_pairs={{0,16},{4,20},{8,24},{12,28},{16,0},{20,4},{24,8},{28,12},{1,17},{... | collective-permute-start | bytes 393224 | tf_op jit(solution)/shard_map/ppermute | solution.py:266
  16.7 0.0 collective-permute-done
  16.7 1.6 %collective-permute-start.1 = (f32[64,512]{1,0:T(8,128)S(1)}, f32[64,512]{1,0:T(8,128)S(1)}, u32[]{:S(2)}, u32[]{:S(2)}) collective-permute-start(f32[64,512]{1,0:T(8,128)S(1)} %slice_add_fusion), channel_id=1, source_target_pairs={{0,8},{1,5},{2,10},{3,7},{4,12},{5,1},{6,14},{7,3},{8,0},{9,13},{1... | collective-permute-start | bytes 393224 | tf_op jit(solution)/shard_map/ppermute | solution.py:271
  18.3 1.3 %shard_map.102 = (bf16[256,1024]{1,0:T(8,128)(2,1)S(1)}, bf16[1024,960]{1,0:T(8,128)(2,1)S(1)}, bf16[1024,576]{1,0:T(8,128)(2,1)S(1)}, bf16[1024,576]{1,0:T(8,128)(2,1)S(1)}, bf16[1024,192]{1,0:T(8,128)(2,1)S(1)}) custom-call(s32[1,128]{1,0:T(1,128)S(1)} %get-tuple-element.27.live_ref, s32[1,1024]{1,0:T(1,128)S(1)} %get-tuple-element.28.target_ref, ...), custom_call_target="tpu_custom_call" | custom-call | flops 8000000000 | tf_op jit(solution)/shard_map/pallas_call | solution.py:358
  19.7 2.9 %collective-permute-done.1 = f32[64,512]{1,0:T(8,128)S(1)} collective-permute-done((f32[64,512]{1,0:T(8,128)S(1)}, f32[64,512]{1,0:T(8,128)S(1)}, u32[]{:S(2)}, u32[]{:S(2)}) %collective-permute-start.1) | collective-permute-done | bytes 131104 | tf_op jit(solution)/shard_map/ppermute | solution.py:271
  22.5 1.2 %collective-permute-start.5 = (f32[64,512]{1,0:T(8,128)S(1)}, f32[64,512]{1,0:T(8,128)S(1)}, u32[]{:S(2)}, u32[]{:S(2)}) collective-permute-start(f32[64,512]{1,0:T(8,128)S(1)} %fusion), channel_id=1, source_target_pairs={{0,16},{4,20},{8,24},{12,28},{16,0},{20,4},{24,8},{28,12},{1,17},{... | collective-permute-start | bytes 393224 | tf_op jit(solution)/shard_map/ppermute | solution.py:266
  23.8 2.7 %collective-permute-start.12 = (f32[64,512]{1,0:T(8,128)S(1)}, f32[64,512]{1,0:T(8,128)S(1)}, u32[]{:S(2)}, u32[]{:S(2)}) collective-permute-start(f32[64,512]{1,0:T(8,128)S(1)} %add.43.refs_0_), channel_id=1, source_target_pairs={{0,12},{1,13},{2,14},{3,15},{4,8},{5,9},{6,10},{7,11},{8,4},{9,5},... | collective-permute-start | bytes 393224 | tf_op jit(solution)/shard_map/ppermute | solution.py:271
  26.5 1.3 %collective-permute-start.11 = (f32[64,512]{1,0:T(8,128)S(1)}, f32[64,512]{1,0:T(8,128)S(1)}, u32[]{:S(2)}, u32[]{:S(2)}) collective-permute-start(f32[64,512]{1,0:T(8,128)S(1)} %add.43.refs_0_), channel_id=1, source_target_pairs={{0,4},{1,9},{2,6},{3,11},{4,0},{5,13},{6,2},{7,15},{8,12},{9,1},{1... | collective-permute-start | bytes 393224 | tf_op jit(solution)/shard_map/ppermute | solution.py:271
  27.8 0.0 collective-permute-start.10
  27.8 1.8 %collective-permute-done.5 = f32[64,512]{1,0:T(8,128)S(1)} collective-permute-done((f32[64,512]{1,0:T(8,128)S(1)}, f32[64,512]{1,0:T(8,128)S(1)}, u32[]{:S(2)}, u32[]{:S(2)}) %collective-permute-start.5) | collective-permute-done | bytes 131104 | tf_op jit(solution)/shard_map/ppermute | solution.py:266
  29.6 0.0 copy-start.3
  29.6 0.0 copy-start.4
  29.6 0.0 copy-start.6
  29.7 1.2 %collective-permute-start.8 = (f32[64,512]{1,0:T(8,128)S(1)}, f32[64,512]{1,0:T(8,128)S(1)}, u32[]{:S(2)}, u32[]{:S(2)}) collective-permute-start(f32[64,512]{1,0:T(8,128)S(1)} %add.42.refs_4_), channel_id=1, source_target_pairs={{0,12},{1,13},{2,14},{3,15},{4,8},{5,9},{6,10},{7,11},{8,4},{9,5},... | collective-permute-start | bytes 393224 | tf_op jit(solution)/shard_map/ppermute | solution.py:271
  30.9 1.4 %collective-permute-start.7 = (f32[64,512]{1,0:T(8,128)S(1)}, f32[64,512]{1,0:T(8,128)S(1)}, u32[]{:S(2)}, u32[]{:S(2)}) collective-permute-start(f32[64,512]{1,0:T(8,128)S(1)} %add.42.refs_4_), channel_id=1, source_target_pairs={{0,4},{1,9},{2,6},{3,11},{4,0},{5,13},{6,2},{7,15},{8,12},{9,1},{1... | collective-permute-start | bytes 393224 | tf_op jit(solution)/shard_map/ppermute | solution.py:271
  32.3 0.3 collective-permute-done.12.refs_3_
  32.6 1.2 %collective-permute-start.6 = (f32[64,512]{1,0:T(8,128)S(1)}, f32[64,512]{1,0:T(8,128)S(1)}, u32[]{:S(2)}, u32[]{:S(2)}) collective-permute-start(f32[64,512]{1,0:T(8,128)S(1)} %add.42.refs_4_), channel_id=1, source_target_pairs={{0,8},{1,5},{2,10},{3,7},{4,12},{5,1},{6,14},{7,3},{8,0},{9,13},{1... | collective-permute-start | bytes 393224 | tf_op jit(solution)/shard_map/ppermute | solution.py:271
  33.7 1.2 %collective-permute-done.11.refs_2_ = f32[64,512]{1,0:T(8,128)S(1)} collective-permute-done((f32[64,512]{1,0:T(8,128)S(1)}, f32[64,512]{1,0:T(8,128)S(1)}, u32[]{:S(2)}, u32[]{:S(2)}) %collective-permute-start.11) | collective-permute-done | bytes 131104 | tf_op jit(solution)/shard_map/ppermute | solution.py:271
  35.0 1.3 %shard_map.103.refs_3_ = f32[1024,512]{1,0:T(8,128)S(1)} custom-call(f32[64,512]{1,0:T(8,128)S(1)} %add.43.refs_0_, f32[64,512]{1,0:T(8,128)S(1)} %collective-permute-done.10.refs_1_, f32[64,512]{1,0:T(8,128)S(1)} %collective-permute-done.11.refs_2_, f32[64,512]{1,0:T(8,128)S(1)} %collective-permute-done.12.refs_3_, f32[64,512]{1,0:T(8,128)S(1)} %add.42.refs_4_, ...), custom_call_target="tpu_custom_call" | custom-call | flops 1006632960 | tf_op jit(solution)/shard_map/pallas_call | solution.py:205
  36.3 1.0 %collective-permute-done.8.refs_2_ = f32[64,512]{1,0:T(8,128)S(1)} collective-permute-done((f32[64,512]{1,0:T(8,128)S(1)}, f32[64,512]{1,0:T(8,128)S(1)}, u32[]{:S(2)}, u32[]{:S(2)}) %collective-permute-start.8) | collective-permute-done | bytes 131104 | tf_op jit(solution)/shard_map/ppermute | solution.py:271
  37.3 0.8 %collective-permute-done.7.refs_1_ = f32[64,512]{1,0:T(8,128)S(1)} collective-permute-done((f32[64,512]{1,0:T(8,128)S(1)}, f32[64,512]{1,0:T(8,128)S(1)}, u32[]{:S(2)}, u32[]{:S(2)}) %collective-permute-start.7) | collective-permute-done | bytes 131104 | tf_op jit(solution)/shard_map/ppermute | solution.py:271
  38.1 0.3 collective-permute-done.6.refs_0_
  38.3 2.4 %shard_map.104 = (bf16[1024,512]{1,0:T(8,128)(2,1)S(1)}, f32[64,512]{1,0:T(8,128)S(1)}, f32[64,512]{1,0:T(8,128)S(1)}, f32[64,512]{1,0:T(8,128)S(1)}, f32[64,512]{1,0:T(8,128)S(1)}) custom-call(f32[64,512]{1,0:T(8,128)S(1)} %collective-permute-done.6.refs_0_, f32[64,512]{1,0:T(8,128)S(1)} %collective-permute-done.7.refs_1_, ...), custom_call_target="tpu_custom_call" | custom-call | flops 1946157056 | tf_op jit(solution)/shard_map/pallas_call | solution.py:368
  40.7 0.1 collective-permute-start.16
  40.8 0.5 collective-permute-start.13
  41.3 0.8 %collective-permute-done.16 = f32[64,512]{1,0:T(8,128)S(1)} collective-permute-done((f32[64,512]{1,0:T(8,128)S(1)}, f32[64,512]{1,0:T(8,128)S(1)}, u32[]{:S(2)}, u32[]{:S(2)}) %collective-permute-start.16) | collective-permute-done | bytes 131104 | tf_op jit(solution)/shard_map/ppermute | solution.py:266
  42.2 1.7 %collective-permute-start.17 = (f32[64,512]{1,0:T(8,128)S(1)}, f32[64,512]{1,0:T(8,128)S(1)}, u32[]{:S(2)}, u32[]{:S(2)}) collective-permute-start(f32[64,512]{1,0:T(8,128)S(1)} %add.46), channel_id=1, source_target_pairs={{0,2},{1,3},{2,0},{3,1},{4,6},{5,7},{6,4},{7,5},{8,10},{9,11},{10,... | collective-permute-start | bytes 393224 | tf_op jit(solution)/shard_map/ppermute | solution.py:266
  43.9 0.0 collective-permute-done.13
  43.9 0.5 collective-permute-start.14
  44.4 4.2 %collective-permute-done.17 = f32[64,512]{1,0:T(8,128)S(1)} collective-permute-done((f32[64,512]{1,0:T(8,128)S(1)}, f32[64,512]{1,0:T(8,128)S(1)}, u32[]{:S(2)}, u32[]{:S(2)}) %collective-permute-start.17) | collective-permute-done | bytes 131104 | tf_op jit(solution)/shard_map/ppermute | solution.py:266
  48.6 0.1 collective-permute-start.18
  48.7 1.9 %collective-permute-done.14 = f32[64,512]{1,0:T(8,128)S(1)} collective-permute-done((f32[64,512]{1,0:T(8,128)S(1)}, f32[64,512]{1,0:T(8,128)S(1)}, u32[]{:S(2)}, u32[]{:S(2)}) %collective-permute-start.14) | collective-permute-done | bytes 131104 | tf_op jit(solution)/shard_map/ppermute | solution.py:266
  50.6 0.1 collective-permute-start.15
  50.7 0.0 copy-start
  50.7 0.0 copy-start.1
  50.7 0.0 copy-start.2
  50.7 1.0 %shard_map.105.refs_1_ = f32[1024,512]{1,0:T(8,128)S(1)} custom-call(f32[64,512]{1,0:T(8,128)S(1)} %add.47.refs_0_, f32[64,512]{1,0:T(8,128)S(1)} %collective-permute-done.18.refs_1_, f32[64,512]{1,0:T(8,128)S(1)} %add.45.refs_2_, bf16[1024,576]{1,0:T(8,128)(2,1)S(1)} %get-tuple-element.40.refs_3_, bf16[1024,512]{1,0:T(8,128)(2,1)S(1)} %get-tuple-element.48.refs_4_), custom_call_target="tpu_custom_call" | custom-call | flops 603979776 | tf_op jit(solution)/shard_map/pallas_call | solution.py:205
  51.7 0.3 collective-permute-done.15.refs_0_
  52.0 2.4 %shard_map.106 = bf16[1024,512]{1,0:T(8,128)(2,1)} custom-call(s32[1,128]{1,0:T(1,128)S(1)} %get-tuple-element.27.live_ref, f32[64,512]{1,0:T(8,128)S(1)} %collective-permute-done.15.refs_0_, f32[1024,512]{1,0:T(8,128)S(1)} %shard_map.105.refs_1_, bf16[1024,192]{1,0:T(8,128)(2,1)S(1)} %get-tuple-element.41.refs_2_, bf16[512,512]{1,0:T(8,128)(2,1)S(1)} %copy-done, ...), custom_call_target="tpu_custom_call" | custom-call | flops 1275068416 | tf_op jit(solution)/shard_map/pallas_call | solution.py:379
  (20 shorter events, 0.2 us)
Async XLA Ops:
  0.0 18.3 %copy-start.5 = (s32[1,1,1024]{2,1,0:T(1,128)S(1)}, s32[1,1,1024]{2,1,0:T(1,128)}, u32[]{:S(2)}) copy-start(s32[1,1,1024]{2,1,0:T(1,128)} %param.11) | copy-start | bytes 12292
  2.3 7.9 %collective-permute-start.2 = (f32[64,512]{1,0:T(8,128)S(1)}, f32[64,512]{1,0:T(8,128)S(1)}, u32[]{:S(2)}, u32[]{:S(2)}) collective-permute-start(f32[64,512]{1,0:T(8,128)S(1)} %get-tuple-element.34), channel_id=1, source_target_pairs={{0,12},{1,13},{2,14},{3,15},{4,8},{5,9},{6,10},{7,11},{8,4},{9,5},... | collective-permute-start | bytes 393224 | tf_op jit(solution)/shard_map/ppermute | solution.py:271
  6.4 7.6 %collective-permute-start.3 = (f32[64,512]{1,0:T(8,128)S(1)}, f32[64,512]{1,0:T(8,128)S(1)}, u32[]{:S(2)}, u32[]{:S(2)}) collective-permute-start(f32[64,512]{1,0:T(8,128)S(1)} %get-tuple-element.35), channel_id=1, source_target_pairs={{0,8},{1,5},{2,10},{3,7},{4,12},{5,1},{6,14},{7,3},{8,0},{9,13},{1... | collective-permute-start | bytes 393224 | tf_op jit(solution)/shard_map/ppermute | solution.py:271
  6.8 7.2 %collective-permute-start.4 = (f32[64,512]{1,0:T(8,128)S(1)}, f32[64,512]{1,0:T(8,128)S(1)}, u32[]{:S(2)}, u32[]{:S(2)}) collective-permute-start(f32[64,512]{1,0:T(8,128)S(1)} %get-tuple-element.36), channel_id=1, source_target_pairs={{0,4},{1,9},{2,6},{3,11},{4,0},{5,13},{6,2},{7,15},{8,12},{9,1},{1... | collective-permute-start | bytes 393224 | tf_op jit(solution)/shard_map/ppermute | solution.py:271
  7.5 9.2 %collective-permute-start = (f32[128,512]{1,0:T(8,128)S(1)}, f32[128,512]{1,0:T(8,128)S(1)}, u32[]{:S(2)}, u32[]{:S(2)}) collective-permute-start(f32[128,512]{1,0:T(8,128)S(1)} %get-tuple-element.31), channel_id=1, source_target_pairs={{0,4},{1,9},{2,6},{3,11},{4,0},{5,13},{6,2},{7,15},{8,12},{9,1},{1... | collective-permute-start | bytes 786440 | tf_op jit(solution)/shard_map/ppermute | solution.py:271
  14.0 9.7 %collective-permute-start.9 = (f32[64,512]{1,0:T(8,128)S(1)}, f32[64,512]{1,0:T(8,128)S(1)}, u32[]{:S(2)}, u32[]{:S(2)}) collective-permute-start(f32[64,512]{1,0:T(8,128)S(1)} %add_add_fusion.tie_ref), channel_id=1, source_target_pairs={{0,16},{4,20},{8,24},{12,28},{16,0},{20,4},{24,8},{28,12},{1,17},{... | collective-permute-start | bytes 393224 | tf_op jit(solution)/shard_map/ppermute | solution.py:266
  16.7 5.8 %collective-permute-start.1 = (f32[64,512]{1,0:T(8,128)S(1)}, f32[64,512]{1,0:T(8,128)S(1)}, u32[]{:S(2)}, u32[]{:S(2)}) collective-permute-start(f32[64,512]{1,0:T(8,128)S(1)} %slice_add_fusion), channel_id=1, source_target_pairs={{0,8},{1,5},{2,10},{3,7},{4,12},{5,1},{6,14},{7,3},{8,0},{9,13},{1... | collective-permute-start | bytes 393224 | tf_op jit(solution)/shard_map/ppermute | solution.py:271
  22.5 7.0 %collective-permute-start.5 = (f32[64,512]{1,0:T(8,128)S(1)}, f32[64,512]{1,0:T(8,128)S(1)}, u32[]{:S(2)}, u32[]{:S(2)}) collective-permute-start(f32[64,512]{1,0:T(8,128)S(1)} %fusion), channel_id=1, source_target_pairs={{0,16},{4,20},{8,24},{12,28},{16,0},{20,4},{24,8},{28,12},{1,17},{... | collective-permute-start | bytes 393224 | tf_op jit(solution)/shard_map/ppermute | solution.py:266
  23.8 8.8 %collective-permute-start.12 = (f32[64,512]{1,0:T(8,128)S(1)}, f32[64,512]{1,0:T(8,128)S(1)}, u32[]{:S(2)}, u32[]{:S(2)}) collective-permute-start(f32[64,512]{1,0:T(8,128)S(1)} %add.43.refs_0_), channel_id=1, source_target_pairs={{0,12},{1,13},{2,14},{3,15},{4,8},{5,9},{6,10},{7,11},{8,4},{9,5},... | collective-permute-start | bytes 393224 | tf_op jit(solution)/shard_map/ppermute | solution.py:271
  26.5 8.5 %collective-permute-start.11 = (f32[64,512]{1,0:T(8,128)S(1)}, f32[64,512]{1,0:T(8,128)S(1)}, u32[]{:S(2)}, u32[]{:S(2)}) collective-permute-start(f32[64,512]{1,0:T(8,128)S(1)} %add.43.refs_0_), channel_id=1, source_target_pairs={{0,4},{1,9},{2,6},{3,11},{4,0},{5,13},{6,2},{7,15},{8,12},{9,1},{1... | collective-permute-start | bytes 393224 | tf_op jit(solution)/shard_map/ppermute | solution.py:271
  27.8 7.2 %collective-permute-start.10 = (f32[64,512]{1,0:T(8,128)S(1)}, f32[64,512]{1,0:T(8,128)S(1)}, u32[]{:S(2)}, u32[]{:S(2)}) collective-permute-start(f32[64,512]{1,0:T(8,128)S(1)} %add.43.refs_0_), channel_id=1, source_target_pairs={{0,8},{1,5},{2,10},{3,7},{4,12},{5,1},{6,14},{7,3},{8,0},{9,13},{1... | collective-permute-start | bytes 393224 | tf_op jit(solution)/shard_map/ppermute | solution.py:271
  29.6 8.7 %copy-start.3 = (bf16[512,512]{1,0:T(8,128)(2,1)S(1)}, bf16[512,512]{1,0:T(8,128)(2,1)}, u32[]{:S(2)}) copy-start(bf16[512,512]{1,0:T(8,128)(2,1)} %refs_6_.1) | copy-start | bytes 1572868
  29.6 8.7 %copy-start.4 = (bf16[512,512]{1,0:T(8,128)(2,1)S(1)}, bf16[512,512]{1,0:T(8,128)(2,1)}, u32[]{:S(2)}) copy-start(bf16[512,512]{1,0:T(8,128)(2,1)} %refs_7_.1) | copy-start | bytes 1572868
  29.6 8.7 %copy-start.6 = (f32[512]{0:T(512)S(1)}, f32[512]{0:T(512)}, u32[]{:S(2)}) copy-start(f32[512]{0:T(512)} %param.18) | copy-start | bytes 6148
  29.7 7.6 %collective-permute-start.8 = (f32[64,512]{1,0:T(8,128)S(1)}, f32[64,512]{1,0:T(8,128)S(1)}, u32[]{:S(2)}, u32[]{:S(2)}) collective-permute-start(f32[64,512]{1,0:T(8,128)S(1)} %add.42.refs_4_), channel_id=1, source_target_pairs={{0,12},{1,13},{2,14},{3,15},{4,8},{5,9},{6,10},{7,11},{8,4},{9,5},... | collective-permute-start | bytes 393224 | tf_op jit(solution)/shard_map/ppermute | solution.py:271
  30.9 7.2 %collective-permute-start.7 = (f32[64,512]{1,0:T(8,128)S(1)}, f32[64,512]{1,0:T(8,128)S(1)}, u32[]{:S(2)}, u32[]{:S(2)}) collective-permute-start(f32[64,512]{1,0:T(8,128)S(1)} %add.42.refs_4_), channel_id=1, source_target_pairs={{0,4},{1,9},{2,6},{3,11},{4,0},{5,13},{6,2},{7,15},{8,12},{9,1},{1... | collective-permute-start | bytes 393224 | tf_op jit(solution)/shard_map/ppermute | solution.py:271
  32.6 5.7 %collective-permute-start.6 = (f32[64,512]{1,0:T(8,128)S(1)}, f32[64,512]{1,0:T(8,128)S(1)}, u32[]{:S(2)}, u32[]{:S(2)}) collective-permute-start(f32[64,512]{1,0:T(8,128)S(1)} %add.42.refs_4_), channel_id=1, source_target_pairs={{0,8},{1,5},{2,10},{3,7},{4,12},{5,1},{6,14},{7,3},{8,0},{9,13},{1... | collective-permute-start | bytes 393224 | tf_op jit(solution)/shard_map/ppermute | solution.py:271
  40.7 1.4 %collective-permute-start.16 = (f32[64,512]{1,0:T(8,128)S(1)}, f32[64,512]{1,0:T(8,128)S(1)}, u32[]{:S(2)}, u32[]{:S(2)}) collective-permute-start(f32[64,512]{1,0:T(8,128)S(1)} %get-tuple-element.47), channel_id=1, source_target_pairs={{0,1},{1,0},{2,3},{3,2},{4,5},{5,4},{6,7},{7,6},{8,9},{9,8},{10,11... | collective-permute-start | bytes 393224 | tf_op jit(solution)/shard_map/ppermute | solution.py:266
  40.8 3.0 %collective-permute-start.13 = (f32[64,512]{1,0:T(8,128)S(1)}, f32[64,512]{1,0:T(8,128)S(1)}, u32[]{:S(2)}, u32[]{:S(2)}) collective-permute-start(f32[64,512]{1,0:T(8,128)S(1)} %get-tuple-element.45), channel_id=1, source_target_pairs={{0,1},{1,0},{2,3},{3,2},{4,5},{5,4},{6,7},{7,6},{8,9},{9,8},{10,11... | collective-permute-start | bytes 393224 | tf_op jit(solution)/shard_map/ppermute | solution.py:266
  42.2 6.4 %collective-permute-start.17 = (f32[64,512]{1,0:T(8,128)S(1)}, f32[64,512]{1,0:T(8,128)S(1)}, u32[]{:S(2)}, u32[]{:S(2)}) collective-permute-start(f32[64,512]{1,0:T(8,128)S(1)} %add.46), channel_id=1, source_target_pairs={{0,2},{1,3},{2,0},{3,1},{4,6},{5,7},{6,4},{7,5},{8,10},{9,11},{10,... | collective-permute-start | bytes 393224 | tf_op jit(solution)/shard_map/ppermute | solution.py:266
  43.9 6.7 %collective-permute-start.14 = (f32[64,512]{1,0:T(8,128)S(1)}, f32[64,512]{1,0:T(8,128)S(1)}, u32[]{:S(2)}, u32[]{:S(2)}) collective-permute-start(f32[64,512]{1,0:T(8,128)S(1)} %add.44), channel_id=1, source_target_pairs={{0,2},{1,3},{2,0},{3,1},{4,6},{5,7},{6,4},{7,5},{8,10},{9,11},{10,... | collective-permute-start | bytes 393224 | tf_op jit(solution)/shard_map/ppermute | solution.py:266
  48.6 2.1 %collective-permute-start.18 = (f32[64,512]{1,0:T(8,128)S(1)}, f32[64,512]{1,0:T(8,128)S(1)}, u32[]{:S(2)}, u32[]{:S(2)}) collective-permute-start(f32[64,512]{1,0:T(8,128)S(1)} %add.47.refs_0_), channel_id=1, source_target_pairs={{0,1},{1,0},{2,3},{3,2},{4,5},{5,4},{6,7},{7,6},{8,9},{9,8},{10,11... | collective-permute-start | bytes 393224 | tf_op jit(solution)/shard_map/ppermute | solution.py:266
  50.6 1.4 %collective-permute-start.15 = (f32[64,512]{1,0:T(8,128)S(1)}, f32[64,512]{1,0:T(8,128)S(1)}, u32[]{:S(2)}, u32[]{:S(2)}) collective-permute-start(f32[64,512]{1,0:T(8,128)S(1)} %add.45.refs_2_), channel_id=1, source_target_pairs={{0,1},{1,0},{2,3},{3,2},{4,5},{5,4},{6,7},{7,6},{8,9},{9,8},{10,11... | collective-permute-start | bytes 393224 | tf_op jit(solution)/shard_map/ppermute | solution.py:266
  50.7 1.3 %copy-start = (bf16[512,512]{1,0:T(8,128)(2,1)S(1)}, bf16[512,512]{1,0:T(8,128)(2,1)}, u32[]{:S(2)}) copy-start(bf16[512,512]{1,0:T(8,128)(2,1)} %refs_3_.1) | copy-start | bytes 1572868
  50.7 1.3 %copy-start.1 = (bf16[512,512]{1,0:T(8,128)(2,1)S(1)}, bf16[512,512]{1,0:T(8,128)(2,1)}, u32[]{:S(2)}) copy-start(bf16[512,512]{1,0:T(8,128)(2,1)} %refs_4_.1) | copy-start | bytes 1572868
  50.7 1.3 %copy-start.2 = (f32[512]{0:T(512)S(1)}, f32[512]{0:T(512)}, u32[]{:S(2)}) copy-start(f32[512]{0:T(512)} %param.19) | copy-start | bytes 6148

commit v9 on v7

--- a/solution.py
+++ b/solution.py
@@ -82,12 +82,14 @@
     return jnp.where(place == slot, jnp.float32(1.0), jnp.float32(0.0)).astype(jnp.bfloat16)
 
 
-def store_sums(wave, sizes, live, targets, fetch, chunk_refs):
+def store_sums(wave, sizes, live, targets, fetch, chunk_refs, first_chunk=0):
     rows = targets.shape[1]
     size = sizes[wave]
     place = target_place(targets, sizes)
     place = jnp.where(lax.broadcasted_iota(jnp.int32, (1, rows), 1) < live, place, -1)
-    slot = lax.broadcasted_iota(jnp.int32, (size * GROUP, rows), 0) + sum(sizes[:wave]) * GROUP
+    count = sum(chunk_ref.shape[0] for chunk_ref in chunk_refs)
+    base = sum(sizes[:wave]) * GROUP + first_chunk * size
+    slot = lax.broadcasted_iota(jnp.int32, (count, rows), 0) + base
     chosen = one_hot(place, slot)
     total = fetch(chosen)
     at = 0
@@ -122,7 +124,7 @@
             total = term if total is None else total + term
         return total
 
-    store_sums(0, sizes, live, target_ref[...], fetch, chunk_refs)
+    store_sums(0, sizes, live, target_ref[...], fetch, chunk_refs, BOTH)
 
 
 def later_sum_kernel(wave, sizes, live_ref, target_ref, state_ref, *chunk_refs):
@@ -145,18 +147,16 @@
         jax.ShapeDtypeStruct(states.shape, states.dtype),
     ]
     out = call(
-        functools.partial(first_sum_kernel, sizes), chunk_shapes(0, sizes[0], channels) + handed_on, [SMEM, HBM, HBM],
-        2 * sizes[0] * GROUP * rows * channels,
+        functools.partial(first_sum_kernel, sizes), chunk_shapes(0, sizes[0], channels)[BOTH:] + handed_on, [SMEM, HBM, HBM],
+        2 * sizes[0] * rows * channels,
         [pltpu.SemaphoreType.DMA((1 + PARTS,))],
     )(live, *(pltpu.with_memory_space_constraint(value, pltpu.HBM) for value in (targets, states)))
     return out[:-3], *out[-3:]
 
 
-def later_sums(states, targets, live, wave, sizes):
-    rows, channels = states.shape
+def later_sums(states, targets, live, wave, sizes, shapes, flops):
     return call(
-        functools.partial(later_sum_kernel, wave, sizes), chunk_shapes(wave, sizes[wave], channels), [VMEM] * 3,
-        2 * sizes[wave] * GROUP * rows * channels,
+        functools.partial(later_sum_kernel, wave, sizes), shapes, [VMEM] * 3, flops,
     )(live, targets, states)
 
 
@@ -347,7 +347,9 @@
     sizes = wave_sizes(target_atoms)
     half = source_atoms // 2
     first, live, targets, states = first_sums(states, targets, live_edges, sizes)
-    waves = [first] + [later_sums(states, targets, live, wave, sizes) for wave in range(1, len(sizes))]
+    shapes = [chunk_shapes(wave, size, channels) for wave, size in enumerate(sizes)]
+    rest = later_sums(states, targets, live, 0, sizes, shapes[0][:BOTH], 2 * BOTH * sizes[0] * rows * channels)
+    waves = [rest + first, later_sums(states, targets, live, 1, sizes, shapes[1], 2 * GROUP * sizes[1] * rows * channels)]
 
     pieces = piece_sizes(half)
     parts = (

time: 54.6 us -> 54.8 us (level)
  starting transfers between devices: 22.7 us -> 25 us
  waiting for transfers between devices: 20.1 us -> 17.8 us
    ppermute x11, starting transfers between devices: 16 us -> 17.8 us  [swap_group(): lax.ppermute(value, ('src', 'tgt'), [(i * across + j, (i ^ partner_mask(k...]
    ppermute x8, waiting for transfers between devices: 9.09 us -> 7.51 us  [swap(): lax.ppermute(value, axis, [(i, i ^ mask) for i in range(lax.axis_size(axi...]
    ppermute x11, waiting for transfers between devices: 11 us -> 10.3 us  [swap_group(): lax.ppermute(value, ('src', 'tgt'), [(i * across + j, (i ^ partner_mask(k...]
  transfers between devices with their start and end apart: 19 -> 19, of which waited for: 13 -> 12; matrix products, arithmetic and copies ran while one was open for 0% -> 0% of each run, Pallas kernels for 7% -> 8%
where the time goes in v9:
time: 54.8 us; the launch traced here: 54.7 us
  starting transfers between devices  25 us (46%)
  waiting for transfers between devices  17.8 us (32%)
  Pallas kernels  10.8 us (20%)
  between operations  0.85 us (2%)
    ppermute x11, starting transfers between devices, swap_group(): lax.ppermute(value, ('src', 'tgt'), [(i * across + j, (i ^ partner_mask(k...  17.8 us
    ppermute x11, waiting for transfers between devices, swap_group(): lax.ppermute(value, ('src', 'tgt'), [(i * across + j, (i ^ partner_mask(k...  10.3 us
    ppermute x8, waiting for transfers between devices, swap(): lax.ppermute(value, axis, [(i, i ^ mask) for i in range(lax.axis_size(axi...  7.51 us
    ppermute x8, starting transfers between devices, swap(): lax.ppermute(value, axis, [(i, i ^ mask) for i in range(lax.axis_size(axi...  7.19 us
    pallas_call x1, Pallas kernels, body(): call(functools.partial(layer_two_kernel, len(late)), jax.ShapeDtypeStruct...  2.41 us
    pallas_call x1, Pallas kernels, body(): call(functools.partial(layer_one_kernel, len(late)), [jax.ShapeDtypeStruc...  2.41 us
    pallas_call x2, Pallas kernels, gather_first(): call(functools.partial(gather_kernel, len(sums)), jax.ShapeDtypeStruct((r...  2.25 us
    pallas_call x1, Pallas kernels, first_sums(): call(functools.partial(first_sum_kernel, sizes), chunk_shapes(0, sizes[0]...  1.44 us
  transfers between devices with their start and end apart: 19, of which 12 were waited for; matrix products, arithmetic and copies ran while one was open for 0% of the time, Pallas kernels for 8%

profile of v9, /device:TPU:0, one launch (start us, length us, event | category | flops | bytes accessed | tf_op | source)
XLA Modules:
  0.0 54.7 jit_solution(180641508939685586)
XLA Ops:
  0.7 1.4 %shard_map.100 = (f32[64,512]{1,0:T(8,128)S(1)}, s32[1,128]{1,0:T(1,128)S(1)}, s32[1,1024]{1,0:T(1,128)S(1)}, bf16[1024,512]{1,0:T(8,128)(2,1)S(1)}) custom-call(s32[1,1]{1,0:T(1,128)S(6)} %copy.11.live_ref, s32[1,1024]{1,0:T(1,128)} %bitcast.10, bf16[1024,512]{1,0:T(8,128)(2,1)} %bitcast.9), custom_call_target="tpu_custom_call" | custom-call | flops 67108864 | tf_op jit(solution)/shard_map/pallas_call | solution.py:149
  2.1 4.0 %collective-permute-start.2 = (f32[64,512]{1,0:T(8,128)S(1)}, f32[64,512]{1,0:T(8,128)S(1)}, u32[]{:S(2)}, u32[]{:S(2)}) collective-permute-start(f32[64,512]{1,0:T(8,128)S(1)} %get-tuple-element.35), channel_id=1, source_target_pairs={{0,12},{1,13},{2,14},{3,15},{4,8},{5,9},{6,10},{7,11},{8,4},{9,5},... | collective-permute-start | bytes 393224 | tf_op jit(solution)/shard_map/ppermute | solution.py:271
  6.2 0.5 shard_map.102
  6.6 0.5 collective-permute-start.3
  7.1 0.1 collective-permute-start.4
  7.3 0.5 shard_map.101
  7.8 2.0 %collective-permute-start = (f32[128,512]{1,0:T(8,128)S(1)}, f32[128,512]{1,0:T(8,128)S(1)}, u32[]{:S(2)}, u32[]{:S(2)}) collective-permute-start(f32[128,512]{1,0:T(8,128)S(1)} %get-tuple-element.32), channel_id=1, source_target_pairs={{0,4},{1,9},{2,6},{3,11},{4,0},{5,13},{6,2},{7,15},{8,12},{9,1},{1... | collective-permute-start | bytes 786440 | tf_op jit(solution)/shard_map/ppermute | solution.py:271
  9.7 0.3 collective-permute-done.2
  10.1 3.3 %collective-permute-done.3 = f32[64,512]{1,0:T(8,128)S(1)} collective-permute-done((f32[64,512]{1,0:T(8,128)S(1)}, f32[64,512]{1,0:T(8,128)S(1)}, u32[]{:S(2)}, u32[]{:S(2)}) %collective-permute-start.3) | collective-permute-done | bytes 131104 | tf_op jit(solution)/shard_map/ppermute | solution.py:271
  13.4 0.0 collective-permute-done.4
  13.4 2.7 %collective-permute-start.6 = (f32[64,512]{1,0:T(8,128)S(1)}, f32[64,512]{1,0:T(8,128)S(1)}, u32[]{:S(2)}, u32[]{:S(2)}) collective-permute-start(f32[64,512]{1,0:T(8,128)S(1)} %add_add_fusion.tie_ref), channel_id=1, source_target_pairs={{0,16},{4,20},{8,24},{12,28},{16,0},{20,4},{24,8},{28,12},{1,17},{... | collective-permute-start | bytes 393224 | tf_op jit(solution)/shard_map/ppermute | solution.py:266
  16.1 2.0 %collective-permute-start.1 = (f32[64,512]{1,0:T(8,128)S(1)}, f32[64,512]{1,0:T(8,128)S(1)}, u32[]{:S(2)}, u32[]{:S(2)}) collective-permute-start(f32[64,512]{1,0:T(8,128)S(1)} %slice_add_fusion), channel_id=1, source_target_pairs={{0,8},{1,5},{2,10},{3,7},{4,12},{5,1},{6,14},{7,3},{8,0},{9,13},{1... | collective-permute-start | bytes 393224 | tf_op jit(solution)/shard_map/ppermute | solution.py:271
  18.1 1.3 %shard_map.103 = (bf16[256,1024]{1,0:T(8,128)(2,1)S(1)}, bf16[1024,960]{1,0:T(8,128)(2,1)S(1)}, bf16[1024,576]{1,0:T(8,128)(2,1)S(1)}, bf16[1024,576]{1,0:T(8,128)(2,1)S(1)}, bf16[1024,192]{1,0:T(8,128)(2,1)S(1)}) custom-call(s32[1,128]{1,0:T(1,128)S(1)} %get-tuple-element.28.live_ref, s32[1,1024]{1,0:T(1,128)S(1)} %get-tuple-element.29.target_ref, ...), custom_call_target="tpu_custom_call" | custom-call | flops 8000000000 | tf_op jit(solution)/shard_map/pallas_call | solution.py:360
  19.5 2.6 %collective-permute-done.1 = f32[64,512]{1,0:T(8,128)S(1)} collective-permute-done((f32[64,512]{1,0:T(8,128)S(1)}, f32[64,512]{1,0:T(8,128)S(1)}, u32[]{:S(2)}, u32[]{:S(2)}) %collective-permute-start.1) | collective-permute-done | bytes 131104 | tf_op jit(solution)/shard_map/ppermute | solution.py:271
  22.1 1.7 %collective-permute-start.5 = (f32[64,512]{1,0:T(8,128)S(1)}, f32[64,512]{1,0:T(8,128)S(1)}, u32[]{:S(2)}, u32[]{:S(2)}) collective-permute-start(f32[64,512]{1,0:T(8,128)S(1)} %fusion), channel_id=1, source_target_pairs={{0,16},{4,20},{8,24},{12,28},{16,0},{20,4},{24,8},{28,12},{1,17},{... | collective-permute-start | bytes 393224 | tf_op jit(solution)/shard_map/ppermute | solution.py:266
  23.8 4.1 %collective-permute-start.12 = (f32[64,512]{1,0:T(8,128)S(1)}, f32[64,512]{1,0:T(8,128)S(1)}, u32[]{:S(2)}, u32[]{:S(2)}) collective-permute-start(f32[64,512]{1,0:T(8,128)S(1)} %add.42.refs_0_), channel_id=1, source_target_pairs={{0,12},{1,13},{2,14},{3,15},{4,8},{5,9},{6,10},{7,11},{8,4},{9,5},... | collective-permute-start | bytes 393224 | tf_op jit(solution)/shard_map/ppermute | solution.py:271
  27.9 0.0 collective-permute-start.11
  27.9 0.6 %collective-permute-start.10 = (f32[64,512]{1,0:T(8,128)S(1)}, f32[64,512]{1,0:T(8,128)S(1)}, u32[]{:S(2)}, u32[]{:S(2)}) collective-permute-start(f32[64,512]{1,0:T(8,128)S(1)} %add.42.refs_0_), channel_id=1, source_target_pairs={{0,8},{1,5},{2,10},{3,7},{4,12},{5,1},{6,14},{7,3},{8,0},{9,13},{1... | collective-permute-start | bytes 393224 | tf_op jit(solution)/shard_map/ppermute | solution.py:271
  28.5 0.2 collective-permute-done.5
  28.8 0.0 copy-start.3
  28.8 0.0 copy-start.4
  28.8 0.0 copy-start.6
  28.8 2.7 %collective-permute-start.9 = (f32[64,512]{1,0:T(8,128)S(1)}, f32[64,512]{1,0:T(8,128)S(1)}, u32[]{:S(2)}, u32[]{:S(2)}) collective-permute-start(f32[64,512]{1,0:T(8,128)S(1)} %add.43.refs_4_), channel_id=1, source_target_pairs={{0,12},{1,13},{2,14},{3,15},{4,8},{5,9},{6,10},{7,11},{8,4},{9,5},... | collective-permute-start | bytes 393224 | tf_op jit(solution)/shard_map/ppermute | solution.py:271
  31.5 0.9 %collective-permute-start.8 = (f32[64,512]{1,0:T(8,128)S(1)}, f32[64,512]{1,0:T(8,128)S(1)}, u32[]{:S(2)}, u32[]{:S(2)}) collective-permute-start(f32[64,512]{1,0:T(8,128)S(1)} %add.43.refs_4_), channel_id=1, source_target_pairs={{0,4},{1,9},{2,6},{3,11},{4,0},{5,13},{6,2},{7,15},{8,12},{9,1},{1... | collective-permute-start | bytes 393224 | tf_op jit(solution)/shard_map/ppermute | solution.py:271
  32.4 1.1 %collective-permute-done.12.refs_3_ = f32[64,512]{1,0:T(8,128)S(1)} collective-permute-done((f32[64,512]{1,0:T(8,128)S(1)}, f32[64,512]{1,0:T(8,128)S(1)}, u32[]{:S(2)}, u32[]{:S(2)}) %collective-permute-start.12) | collective-permute-done | bytes 131104 | tf_op jit(solution)/shard_map/ppermute | solution.py:271
  33.5 0.7 %collective-permute-start.7 = (f32[64,512]{1,0:T(8,128)S(1)}, f32[64,512]{1,0:T(8,128)S(1)}, u32[]{:S(2)}, u32[]{:S(2)}) collective-permute-start(f32[64,512]{1,0:T(8,128)S(1)} %add.43.refs_4_), channel_id=1, source_target_pairs={{0,8},{1,5},{2,10},{3,7},{4,12},{5,1},{6,14},{7,3},{8,0},{9,13},{1... | collective-permute-start | bytes 393224 | tf_op jit(solution)/shard_map/ppermute | solution.py:271
  34.3 0.8 %collective-permute-done.11.refs_2_ = f32[64,512]{1,0:T(8,128)S(1)} collective-permute-done((f32[64,512]{1,0:T(8,128)S(1)}, f32[64,512]{1,0:T(8,128)S(1)}, u32[]{:S(2)}, u32[]{:S(2)}) %collective-permute-start.11) | collective-permute-done | bytes 131104 | tf_op jit(solution)/shard_map/ppermute | solution.py:271
  35.1 0.0 collective-permute-done.10.refs_1_
  35.1 1.3 %shard_map.104.refs_3_ = f32[1024,512]{1,0:T(8,128)S(1)} custom-call(f32[64,512]{1,0:T(8,128)S(1)} %add.42.refs_0_, f32[64,512]{1,0:T(8,128)S(1)} %collective-permute-done.10.refs_1_, f32[64,512]{1,0:T(8,128)S(1)} %collective-permute-done.11.refs_2_, f32[64,512]{1,0:T(8,128)S(1)} %collective-permute-done.12.refs_3_, f32[64,512]{1,0:T(8,128)S(1)} %add.43.refs_4_, ...), custom_call_target="tpu_custom_call" | custom-call | flops 1006632960 | tf_op jit(solution)/shard_map/pallas_call | solution.py:205
  36.4 1.5 %collective-permute-done.9.refs_2_ = f32[64,512]{1,0:T(8,128)S(1)} collective-permute-done((f32[64,512]{1,0:T(8,128)S(1)}, f32[64,512]{1,0:T(8,128)S(1)}, u32[]{:S(2)}, u32[]{:S(2)}) %collective-permute-start.9) | collective-permute-done | bytes 131104 | tf_op jit(solution)/shard_map/ppermute | solution.py:271
  37.9 0.6 %collective-permute-done.7.refs_0_ = f32[64,512]{1,0:T(8,128)S(1)} collective-permute-done((f32[64,512]{1,0:T(8,128)S(1)}, f32[64,512]{1,0:T(8,128)S(1)}, u32[]{:S(2)}, u32[]{:S(2)}) %collective-permute-start.7) | collective-permute-done | bytes 131104 | tf_op jit(solution)/shard_map/ppermute | solution.py:271
  38.5 2.4 %shard_map.105 = (bf16[1024,512]{1,0:T(8,128)(2,1)S(1)}, f32[64,512]{1,0:T(8,128)S(1)}, f32[64,512]{1,0:T(8,128)S(1)}, f32[64,512]{1,0:T(8,128)S(1)}, f32[64,512]{1,0:T(8,128)S(1)}) custom-call(f32[64,512]{1,0:T(8,128)S(1)} %collective-permute-done.7.refs_0_, f32[64,512]{1,0:T(8,128)S(1)} %collective-permute-done.8.refs_1_, ...), custom_call_target="tpu_custom_call" | custom-call | flops 1946157056 | tf_op jit(solution)/shard_map/pallas_call | solution.py:370
  40.9 0.1 collective-permute-start.16
  41.0 0.5 collective-permute-start.13
  41.5 0.8 %collective-permute-done.16 = f32[64,512]{1,0:T(8,128)S(1)} collective-permute-done((f32[64,512]{1,0:T(8,128)S(1)}, f32[64,512]{1,0:T(8,128)S(1)}, u32[]{:S(2)}, u32[]{:S(2)}) %collective-permute-start.16) | collective-permute-done | bytes 131104 | tf_op jit(solution)/shard_map/ppermute | solution.py:266
  42.4 1.3 %collective-permute-start.17 = (f32[64,512]{1,0:T(8,128)S(1)}, f32[64,512]{1,0:T(8,128)S(1)}, u32[]{:S(2)}, u32[]{:S(2)}) collective-permute-start(f32[64,512]{1,0:T(8,128)S(1)} %add.46), channel_id=1, source_target_pairs={{0,2},{1,3},{2,0},{3,1},{4,6},{5,7},{6,4},{7,5},{8,10},{9,11},{10,... | collective-permute-start | bytes 393224 | tf_op jit(solution)/shard_map/ppermute | solution.py:266
  43.7 0.0 collective-permute-done.13
  43.8 0.8 %collective-permute-start.14 = (f32[64,512]{1,0:T(8,128)S(1)}, f32[64,512]{1,0:T(8,128)S(1)}, u32[]{:S(2)}, u32[]{:S(2)}) collective-permute-start(f32[64,512]{1,0:T(8,128)S(1)} %add.44), channel_id=1, source_target_pairs={{0,2},{1,3},{2,0},{3,1},{4,6},{5,7},{6,4},{7,5},{8,10},{9,11},{10,... | collective-permute-start | bytes 393224 | tf_op jit(solution)/shard_map/ppermute | solution.py:266
  44.6 4.2 %collective-permute-done.17 = f32[64,512]{1,0:T(8,128)S(1)} collective-permute-done((f32[64,512]{1,0:T(8,128)S(1)}, f32[64,512]{1,0:T(8,128)S(1)}, u32[]{:S(2)}, u32[]{:S(2)}) %collective-permute-start.17) | collective-permute-done | bytes 131104 | tf_op jit(solution)/shard_map/ppermute | solution.py:266
  48.8 0.1 collective-permute-start.18
  48.9 1.9 %collective-permute-done.14 = f32[64,512]{1,0:T(8,128)S(1)} collective-permute-done((f32[64,512]{1,0:T(8,128)S(1)}, f32[64,512]{1,0:T(8,128)S(1)}, u32[]{:S(2)}, u32[]{:S(2)}) %collective-permute-start.14) | collective-permute-done | bytes 131104 | tf_op jit(solution)/shard_map/ppermute | solution.py:266
  50.8 0.1 collective-permute-start.15
  50.9 0.0 copy-start
  50.9 0.0 copy-start.1
  50.9 0.0 copy-start.2
  51.0 1.0 %shard_map.106.refs_1_ = f32[1024,512]{1,0:T(8,128)S(1)} custom-call(f32[64,512]{1,0:T(8,128)S(1)} %add.47.refs_0_, f32[64,512]{1,0:T(8,128)S(1)} %collective-permute-done.18.refs_1_, f32[64,512]{1,0:T(8,128)S(1)} %add.45.refs_2_, bf16[1024,576]{1,0:T(8,128)(2,1)S(1)} %get-tuple-element.41.refs_3_, bf16[1024,512]{1,0:T(8,128)(2,1)S(1)} %get-tuple-element.50.refs_4_), custom_call_target="tpu_custom_call" | custom-call | flops 603979776 | tf_op jit(solution)/shard_map/pallas_call | solution.py:205
  52.0 0.3 collective-permute-done.15.refs_0_
  52.3 2.4 %shard_map.107 = bf16[1024,512]{1,0:T(8,128)(2,1)} custom-call(s32[1,128]{1,0:T(1,128)S(1)} %get-tuple-element.28.live_ref, f32[64,512]{1,0:T(8,128)S(1)} %collective-permute-done.15.refs_0_, f32[1024,512]{1,0:T(8,128)S(1)} %shard_map.106.refs_1_, bf16[1024,192]{1,0:T(8,128)(2,1)S(1)} %get-tuple-element.42.refs_2_, bf16[512,512]{1,0:T(8,128)(2,1)S(1)} %copy-done, ...), custom_call_target="tpu_custom_call" | custom-call | flops 1275068416 | tf_op jit(solution)/shard_map/pallas_call | solution.py:381
  (21 shorter events, 0.2 us)
Async XLA Ops:
  0.7 17.5 %copy-start.5 = (s32[1,1,1024]{2,1,0:T(1,128)S(1)}, s32[1,1,1024]{2,1,0:T(1,128)}, u32[]{:S(2)}) copy-start(s32[1,1,1024]{2,1,0:T(1,128)} %param.11) | copy-start | bytes 12292
  2.1 8.0 %collective-permute-start.2 = (f32[64,512]{1,0:T(8,128)S(1)}, f32[64,512]{1,0:T(8,128)S(1)}, u32[]{:S(2)}, u32[]{:S(2)}) collective-permute-start(f32[64,512]{1,0:T(8,128)S(1)} %get-tuple-element.35), channel_id=1, source_target_pairs={{0,12},{1,13},{2,14},{3,15},{4,8},{5,9},{6,10},{7,11},{8,4},{9,5},... | collective-permute-start | bytes 393224 | tf_op jit(solution)/shard_map/ppermute | solution.py:271
  6.6 6.8 %collective-permute-start.3 = (f32[64,512]{1,0:T(8,128)S(1)}, f32[64,512]{1,0:T(8,128)S(1)}, u32[]{:S(2)}, u32[]{:S(2)}) collective-permute-start(f32[64,512]{1,0:T(8,128)S(1)} %get-tuple-element.36), channel_id=1, source_target_pairs={{0,8},{1,5},{2,10},{3,7},{4,12},{5,1},{6,14},{7,3},{8,0},{9,13},{1... | collective-permute-start | bytes 393224 | tf_op jit(solution)/shard_map/ppermute | solution.py:271
  7.1 6.3 %collective-permute-start.4 = (f32[64,512]{1,0:T(8,128)S(1)}, f32[64,512]{1,0:T(8,128)S(1)}, u32[]{:S(2)}, u32[]{:S(2)}) collective-permute-start(f32[64,512]{1,0:T(8,128)S(1)} %get-tuple-element.37), channel_id=1, source_target_pairs={{0,4},{1,9},{2,6},{3,11},{4,0},{5,13},{6,2},{7,15},{8,12},{9,1},{1... | collective-permute-start | bytes 393224 | tf_op jit(solution)/shard_map/ppermute | solution.py:271
  7.8 8.3 %collective-permute-start = (f32[128,512]{1,0:T(8,128)S(1)}, f32[128,512]{1,0:T(8,128)S(1)}, u32[]{:S(2)}, u32[]{:S(2)}) collective-permute-start(f32[128,512]{1,0:T(8,128)S(1)} %get-tuple-element.32), channel_id=1, source_target_pairs={{0,4},{1,9},{2,6},{3,11},{4,0},{5,13},{6,2},{7,15},{8,12},{9,1},{1... | collective-permute-start | bytes 786440 | tf_op jit(solution)/shard_map/ppermute | solution.py:271
  13.4 10.3 %collective-permute-start.6 = (f32[64,512]{1,0:T(8,128)S(1)}, f32[64,512]{1,0:T(8,128)S(1)}, u32[]{:S(2)}, u32[]{:S(2)}) collective-permute-start(f32[64,512]{1,0:T(8,128)S(1)} %add_add_fusion.tie_ref), channel_id=1, source_target_pairs={{0,16},{4,20},{8,24},{12,28},{16,0},{20,4},{24,8},{28,12},{1,17},{... | collective-permute-start | bytes 393224 | tf_op jit(solution)/shard_map/ppermute | solution.py:266
  16.1 5.9 %collective-permute-start.1 = (f32[64,512]{1,0:T(8,128)S(1)}, f32[64,512]{1,0:T(8,128)S(1)}, u32[]{:S(2)}, u32[]{:S(2)}) collective-permute-start(f32[64,512]{1,0:T(8,128)S(1)} %slice_add_fusion), channel_id=1, source_target_pairs={{0,8},{1,5},{2,10},{3,7},{4,12},{5,1},{6,14},{7,3},{8,0},{9,13},{1... | collective-permute-start | bytes 393224 | tf_op jit(solution)/shard_map/ppermute | solution.py:271
  22.1 6.7 %collective-permute-start.5 = (f32[64,512]{1,0:T(8,128)S(1)}, f32[64,512]{1,0:T(8,128)S(1)}, u32[]{:S(2)}, u32[]{:S(2)}) collective-permute-start(f32[64,512]{1,0:T(8,128)S(1)} %fusion), channel_id=1, source_target_pairs={{0,16},{4,20},{8,24},{12,28},{16,0},{20,4},{24,8},{28,12},{1,17},{... | collective-permute-start | bytes 393224 | tf_op jit(solution)/shard_map/ppermute | solution.py:266
  23.8 9.8 %collective-permute-start.12 = (f32[64,512]{1,0:T(8,128)S(1)}, f32[64,512]{1,0:T(8,128)S(1)}, u32[]{:S(2)}, u32[]{:S(2)}) collective-permute-start(f32[64,512]{1,0:T(8,128)S(1)} %add.42.refs_0_), channel_id=1, source_target_pairs={{0,12},{1,13},{2,14},{3,15},{4,8},{5,9},{6,10},{7,11},{8,4},{9,5},... | collective-permute-start | bytes 393224 | tf_op jit(solution)/shard_map/ppermute | solution.py:271
  27.9 7.2 %collective-permute-start.11 = (f32[64,512]{1,0:T(8,128)S(1)}, f32[64,512]{1,0:T(8,128)S(1)}, u32[]{:S(2)}, u32[]{:S(2)}) collective-permute-start(f32[64,512]{1,0:T(8,128)S(1)} %add.42.refs_0_), channel_id=1, source_target_pairs={{0,4},{1,9},{2,6},{3,11},{4,0},{5,13},{6,2},{7,15},{8,12},{9,1},{1... | collective-permute-start | bytes 393224 | tf_op jit(solution)/shard_map/ppermute | solution.py:271
  27.9 7.2 %collective-permute-start.10 = (f32[64,512]{1,0:T(8,128)S(1)}, f32[64,512]{1,0:T(8,128)S(1)}, u32[]{:S(2)}, u32[]{:S(2)}) collective-permute-start(f32[64,512]{1,0:T(8,128)S(1)} %add.42.refs_0_), channel_id=1, source_target_pairs={{0,8},{1,5},{2,10},{3,7},{4,12},{5,1},{6,14},{7,3},{8,0},{9,13},{1... | collective-permute-start | bytes 393224 | tf_op jit(solution)/shard_map/ppermute | solution.py:271
  28.8 9.7 %copy-start.3 = (bf16[512,512]{1,0:T(8,128)(2,1)S(1)}, bf16[512,512]{1,0:T(8,128)(2,1)}, u32[]{:S(2)}) copy-start(bf16[512,512]{1,0:T(8,128)(2,1)} %refs_6_.1) | copy-start | bytes 1572868
  28.8 9.7 %copy-start.4 = (bf16[512,512]{1,0:T(8,128)(2,1)S(1)}, bf16[512,512]{1,0:T(8,128)(2,1)}, u32[]{:S(2)}) copy-start(bf16[512,512]{1,0:T(8,128)(2,1)} %refs_7_.1) | copy-start | bytes 1572868
  28.8 9.7 %copy-start.6 = (f32[512]{0:T(512)S(1)}, f32[512]{0:T(512)}, u32[]{:S(2)}) copy-start(f32[512]{0:T(512)} %param.18) | copy-start | bytes 6148
  28.8 9.1 %collective-permute-start.9 = (f32[64,512]{1,0:T(8,128)S(1)}, f32[64,512]{1,0:T(8,128)S(1)}, u32[]{:S(2)}, u32[]{:S(2)}) collective-permute-start(f32[64,512]{1,0:T(8,128)S(1)} %add.43.refs_4_), channel_id=1, source_target_pairs={{0,12},{1,13},{2,14},{3,15},{4,8},{5,9},{6,10},{7,11},{8,4},{9,5},... | collective-permute-start | bytes 393224 | tf_op jit(solution)/shard_map/ppermute | solution.py:271
  31.5 6.4 %collective-permute-start.8 = (f32[64,512]{1,0:T(8,128)S(1)}, f32[64,512]{1,0:T(8,128)S(1)}, u32[]{:S(2)}, u32[]{:S(2)}) collective-permute-start(f32[64,512]{1,0:T(8,128)S(1)} %add.43.refs_4_), channel_id=1, source_target_pairs={{0,4},{1,9},{2,6},{3,11},{4,0},{5,13},{6,2},{7,15},{8,12},{9,1},{1... | collective-permute-start | bytes 393224 | tf_op jit(solution)/shard_map/ppermute | solution.py:271
  33.5 5.0 %collective-permute-start.7 = (f32[64,512]{1,0:T(8,128)S(1)}, f32[64,512]{1,0:T(8,128)S(1)}, u32[]{:S(2)}, u32[]{:S(2)}) collective-permute-start(f32[64,512]{1,0:T(8,128)S(1)} %add.43.refs_4_), channel_id=1, source_target_pairs={{0,8},{1,5},{2,10},{3,7},{4,12},{5,1},{6,14},{7,3},{8,0},{9,13},{1... | collective-permute-start | bytes 393224 | tf_op jit(solution)/shard_map/ppermute | solution.py:271
  40.9 1.4 %collective-permute-start.16 = (f32[64,512]{1,0:T(8,128)S(1)}, f32[64,512]{1,0:T(8,128)S(1)}, u32[]{:S(2)}, u32[]{:S(2)}) collective-permute-start(f32[64,512]{1,0:T(8,128)S(1)} %get-tuple-element.49), channel_id=1, source_target_pairs={{0,1},{1,0},{2,3},{3,2},{4,5},{5,4},{6,7},{7,6},{8,9},{9,8},{10,11... | collective-permute-start | bytes 393224 | tf_op jit(solution)/shard_map/ppermute | solution.py:266
  41.0 2.7 %collective-permute-start.13 = (f32[64,512]{1,0:T(8,128)S(1)}, f32[64,512]{1,0:T(8,128)S(1)}, u32[]{:S(2)}, u32[]{:S(2)}) collective-permute-start(f32[64,512]{1,0:T(8,128)S(1)} %get-tuple-element.47), channel_id=1, source_target_pairs={{0,1},{1,0},{2,3},{3,2},{4,5},{5,4},{6,7},{7,6},{8,9},{9,8},{10,11... | collective-permute-start | bytes 393224 | tf_op jit(solution)/shard_map/ppermute | solution.py:266
  42.4 6.4 %collective-permute-start.17 = (f32[64,512]{1,0:T(8,128)S(1)}, f32[64,512]{1,0:T(8,128)S(1)}, u32[]{:S(2)}, u32[]{:S(2)}) collective-permute-start(f32[64,512]{1,0:T(8,128)S(1)} %add.46), channel_id=1, source_target_pairs={{0,2},{1,3},{2,0},{3,1},{4,6},{5,7},{6,4},{7,5},{8,10},{9,11},{10,... | collective-permute-start | bytes 393224 | tf_op jit(solution)/shard_map/ppermute | solution.py:266
  43.8 7.1 %collective-permute-start.14 = (f32[64,512]{1,0:T(8,128)S(1)}, f32[64,512]{1,0:T(8,128)S(1)}, u32[]{:S(2)}, u32[]{:S(2)}) collective-permute-start(f32[64,512]{1,0:T(8,128)S(1)} %add.44), channel_id=1, source_target_pairs={{0,2},{1,3},{2,0},{3,1},{4,6},{5,7},{6,4},{7,5},{8,10},{9,11},{10,... | collective-permute-start | bytes 393224 | tf_op jit(solution)/shard_map/ppermute | solution.py:266
  48.8 2.1 %collective-permute-start.18 = (f32[64,512]{1,0:T(8,128)S(1)}, f32[64,512]{1,0:T(8,128)S(1)}, u32[]{:S(2)}, u32[]{:S(2)}) collective-permute-start(f32[64,512]{1,0:T(8,128)S(1)} %add.47.refs_0_), channel_id=1, source_target_pairs={{0,1},{1,0},{2,3},{3,2},{4,5},{5,4},{6,7},{7,6},{8,9},{9,8},{10,11... | collective-permute-start | bytes 393224 | tf_op jit(solution)/shard_map/ppermute | solution.py:266
  50.8 1.4 %collective-permute-start.15 = (f32[64,512]{1,0:T(8,128)S(1)}, f32[64,512]{1,0:T(8,128)S(1)}, u32[]{:S(2)}, u32[]{:S(2)}) collective-permute-start(f32[64,512]{1,0:T(8,128)S(1)} %add.45.refs_2_), channel_id=1, source_target_pairs={{0,1},{1,0},{2,3},{3,2},{4,5},{5,4},{6,7},{7,6},{8,9},{9,8},{10,11... | collective-permute-start | bytes 393224 | tf_op jit(solution)/shard_map/ppermute | solution.py:266
  50.9 1.3 %copy-start = (bf16[512,512]{1,0:T(8,128)(2,1)S(1)}, bf16[512,512]{1,0:T(8,128)(2,1)}, u32[]{:S(2)}) copy-start(bf16[512,512]{1,0:T(8,128)(2,1)} %refs_3_.1) | copy-start | bytes 1572868
  50.9 1.3 %copy-start.1 = (bf16[512,512]{1,0:T(8,128)(2,1)S(1)}, bf16[512,512]{1,0:T(8,128)(2,1)}, u32[]{:S(2)}) copy-start(bf16[512,512]{1,0:T(8,128)(2,1)} %refs_4_.1) | copy-start | bytes 1572868
  50.9 1.3 %copy-start.2 = (f32[512]{0:T(512)S(1)}, f32[512]{0:T(512)}, u32[]{:S(2)}) copy-start(f32[512]{0:T(512)} %param.19) | copy-start | bytes 6148

commit v10 on v7

--- a/solution.py
+++ b/solution.py
@@ -82,12 +82,13 @@
     return jnp.where(place == slot, jnp.float32(1.0), jnp.float32(0.0)).astype(jnp.bfloat16)
 
 
-def store_sums(wave, sizes, live, targets, fetch, chunk_refs):
+def store_sums(wave, sizes, live, targets, fetch, chunk_refs, first_chunk=0):
     rows = targets.shape[1]
     size = sizes[wave]
     place = target_place(targets, sizes)
     place = jnp.where(lax.broadcasted_iota(jnp.int32, (1, rows), 1) < live, place, -1)
-    slot = lax.broadcasted_iota(jnp.int32, (size * GROUP, rows), 0) + sum(sizes[:wave]) * GROUP
+    count = sum(chunk_ref.shape[0] for chunk_ref in chunk_refs)
+    slot = lax.broadcasted_iota(jnp.int32, (count, rows), 0) + sum(sizes[:wave]) * GROUP + first_chunk * size
     chosen = one_hot(place, slot)
     total = fetch(chosen)
     at = 0
@@ -125,11 +126,11 @@
     store_sums(0, sizes, live, target_ref[...], fetch, chunk_refs)
 
 
-def later_sum_kernel(wave, sizes, live_ref, target_ref, state_ref, *chunk_refs):
+def later_sum_kernel(wave, sizes, first_chunk, live_ref, target_ref, state_ref, *chunk_refs):
     def fetch(chosen):
         return jnp.dot(chosen, state_ref[...], preferred_element_type=jnp.float32)
 
-    store_sums(wave, sizes, live_ref[:, :1], target_ref[...], fetch, chunk_refs)
+    store_sums(wave, sizes, live_ref[:, :1], target_ref[...], fetch, chunk_refs, first_chunk)
 
 
 def chunk_shapes(wave, size, channels):
@@ -154,10 +155,16 @@
 
 def later_sums(states, targets, live, wave, sizes):
     rows, channels = states.shape
-    return call(
-        functools.partial(later_sum_kernel, wave, sizes), chunk_shapes(wave, sizes[wave], channels), [VMEM] * 3,
-        2 * sizes[wave] * GROUP * rows * channels,
-    )(live, targets, states)
+    shapes = chunk_shapes(wave, sizes[wave], channels)
+
+    def some(first_chunk, chosen_shapes):
+        return call(
+            functools.partial(later_sum_kernel, wave, sizes, first_chunk), chosen_shapes, [VMEM] * 3,
+            sizes[wave] * GROUP * rows * channels,
+        )(live, targets, states)
+
+    sent = some(2, shapes[2:])
+    return some(0, shapes[:2]) + sent
 
 
 def choose_kernel(sizes, half, live_ref, target_ref, source_ref, tie_ref, pick_ref, *refs):

time: 54.6 us -> 54.7 us (level)
  transfers between devices with their start and end apart: 19 -> 19, of which waited for: 13 -> 13; matrix products, arithmetic and copies ran while one was open for 0% -> 0% of each run, Pallas kernels for 7% -> 8%
where the time goes in v10:
time: 54.7 us; the launch traced here: 54.6 us
  starting transfers between devices  22.5 us (41%)
  waiting for transfers between devices  20.3 us (37%)
  Pallas kernels  10.7 us (20%)
  between operations  0.85 us (2%)
    ppermute x11, starting transfers between devices, swap_group(): lax.ppermute(value, ('src', 'tgt'), [(i * across + j, (i ^ partner_mask(k...  15.8 us
    ppermute x11, waiting for transfers between devices, swap_group(): lax.ppermute(value, ('src', 'tgt'), [(i * across + j, (i ^ partner_mask(k...  11 us
    ppermute x8, waiting for transfers between devices, swap(): lax.ppermute(value, axis, [(i, i ^ mask) for i in range(lax.axis_size(axi...  9.27 us
    ppermute x8, starting transfers between devices, swap(): lax.ppermute(value, axis, [(i, i ^ mask) for i in range(lax.axis_size(axi...  6.66 us
    pallas_call x1, Pallas kernels, body(): call(functools.partial(layer_one_kernel, len(late)), [jax.ShapeDtypeStruc...  2.4 us
    pallas_call x1, Pallas kernels, body(): call(functools.partial(layer_two_kernel, len(late)), jax.ShapeDtypeStruct...  2.4 us
    pallas_call x2, Pallas kernels, gather_first(): call(functools.partial(gather_kernel, len(sums)), jax.ShapeDtypeStruct((r...  2.25 us
    pallas_call x1, Pallas kernels, first_sums(): call(functools.partial(first_sum_kernel, sizes), chunk_shapes(0, sizes[0]...  1.63 us
  transfers between devices with their start and end apart: 19, of which 13 were waited for; matrix products, arithmetic and copies ran while one was open for 0% of the time, Pallas kernels for 8%

profile of v10, /device:TPU:0, one launch (start us, length us, event | category | flops | bytes accessed | tf_op | source)
XLA Modules:
  0.0 54.6 jit_solution(17468402348233539006)
XLA Ops:
  0.7 1.6 %shard_map.100 = (f32[64,512]{1,0:T(8,128)S(1)}, f32[64,512]{1,0:T(8,128)S(1)}, f32[64,512]{1,0:T(8,128)S(1)}, f32[64,512]{1,0:T(8,128)S(1)}, s32[1,128]{1,0:T(1...) custom-call(s32[1,1]{1,0:T(1,128)S(6)} %copy.11.live_ref, s32[1,1024]{1,0:T(1,128)} %bitcast.10, ...), custom_call_target="tpu_custom_call" | custom-call | flops 268435456 | tf_op jit(solution)/shard_map/pallas_call | solution.py:148
  2.3 4.0 %collective-permute-start.2 = (f32[64,512]{1,0:T(8,128)S(1)}, f32[64,512]{1,0:T(8,128)S(1)}, u32[]{:S(2)}, u32[]{:S(2)}) collective-permute-start(f32[64,512]{1,0:T(8,128)S(1)} %get-tuple-element.33), channel_id=1, source_target_pairs={{0,12},{1,13},{2,14},{3,15},{4,8},{5,9},{6,10},{7,11},{8,4},{9,5},... | collective-permute-start | bytes 393224 | tf_op jit(solution)/shard_map/ppermute | solution.py:278
  6.3 0.5 collective-permute-start.3
  6.8 0.2 collective-permute-start.4
  7.0 0.4 shard_map.102
  7.4 1.9 %collective-permute-start = (f32[128,512]{1,0:T(8,128)S(1)}, f32[128,512]{1,0:T(8,128)S(1)}, u32[]{:S(2)}, u32[]{:S(2)}) collective-permute-start(f32[128,512]{1,0:T(8,128)S(1)} %shard_map.102), channel_id=1, source_target_pairs={{0,4},{1,9},{2,6},{3,11},{4,0},{5,13},{6,2},{7,15},{8,12},{9,1},{1... | collective-permute-start | bytes 786440 | tf_op jit(solution)/shard_map/ppermute | solution.py:278
  9.3 0.3 shard_map.101
  9.6 0.6 %collective-permute-done.2 = f32[64,512]{1,0:T(8,128)S(1)} collective-permute-done((f32[64,512]{1,0:T(8,128)S(1)}, f32[64,512]{1,0:T(8,128)S(1)}, u32[]{:S(2)}, u32[]{:S(2)}) %collective-permute-start.2) | collective-permute-done | bytes 131104 | tf_op jit(solution)/shard_map/ppermute | solution.py:278
  10.2 3.7 %collective-permute-done.3 = f32[64,512]{1,0:T(8,128)S(1)} collective-permute-done((f32[64,512]{1,0:T(8,128)S(1)}, f32[64,512]{1,0:T(8,128)S(1)}, u32[]{:S(2)}, u32[]{:S(2)}) %collective-permute-start.3) | collective-permute-done | bytes 131104 | tf_op jit(solution)/shard_map/ppermute | solution.py:278
  14.0 0.0 collective-permute-done.4
  14.0 2.6 %collective-permute-start.6 = (f32[64,512]{1,0:T(8,128)S(1)}, f32[64,512]{1,0:T(8,128)S(1)}, u32[]{:S(2)}, u32[]{:S(2)}) collective-permute-start(f32[64,512]{1,0:T(8,128)S(1)} %add_add_fusion.tie_ref), channel_id=1, source_target_pairs={{0,16},{4,20},{8,24},{12,28},{16,0},{20,4},{24,8},{28,12},{1,17},{... | collective-permute-start | bytes 393224 | tf_op jit(solution)/shard_map/ppermute | solution.py:273
  16.7 0.0 collective-permute-done
  16.7 1.6 %collective-permute-start.1 = (f32[64,512]{1,0:T(8,128)S(1)}, f32[64,512]{1,0:T(8,128)S(1)}, u32[]{:S(2)}, u32[]{:S(2)}) collective-permute-start(f32[64,512]{1,0:T(8,128)S(1)} %slice_add_fusion), channel_id=1, source_target_pairs={{0,8},{1,5},{2,10},{3,7},{4,12},{5,1},{6,14},{7,3},{8,0},{9,13},{1... | collective-permute-start | bytes 393224 | tf_op jit(solution)/shard_map/ppermute | solution.py:278
  18.3 1.3 %shard_map.103 = (bf16[256,1024]{1,0:T(8,128)(2,1)S(1)}, bf16[1024,960]{1,0:T(8,128)(2,1)S(1)}, bf16[1024,576]{1,0:T(8,128)(2,1)S(1)}, bf16[1024,576]{1,0:T(8,128)(2,1)S(1)}, bf16[1024,192]{1,0:T(8,128)(2,1)S(1)}) custom-call(s32[1,128]{1,0:T(1,128)S(1)} %get-tuple-element.27.live_ref, s32[1,1024]{1,0:T(1,128)S(1)} %get-tuple-element.28.target_ref, ...), custom_call_target="tpu_custom_call" | custom-call | flops 8000000000 | tf_op jit(solution)/shard_map/pallas_call | solution.py:365
  19.7 3.0 %collective-permute-done.1 = f32[64,512]{1,0:T(8,128)S(1)} collective-permute-done((f32[64,512]{1,0:T(8,128)S(1)}, f32[64,512]{1,0:T(8,128)S(1)}, u32[]{:S(2)}, u32[]{:S(2)}) %collective-permute-start.1) | collective-permute-done | bytes 131104 | tf_op jit(solution)/shard_map/ppermute | solution.py:278
  22.7 1.1 %collective-permute-start.5 = (f32[64,512]{1,0:T(8,128)S(1)}, f32[64,512]{1,0:T(8,128)S(1)}, u32[]{:S(2)}, u32[]{:S(2)}) collective-permute-start(f32[64,512]{1,0:T(8,128)S(1)} %fusion), channel_id=1, source_target_pairs={{0,16},{4,20},{8,24},{12,28},{16,0},{20,4},{24,8},{28,12},{1,17},{... | collective-permute-start | bytes 393224 | tf_op jit(solution)/shard_map/ppermute | solution.py:273
  23.8 0.0 collective-permute-done.6
  23.8 2.6 %collective-permute-start.12 = (f32[64,512]{1,0:T(8,128)S(1)}, f32[64,512]{1,0:T(8,128)S(1)}, u32[]{:S(2)}, u32[]{:S(2)}) collective-permute-start(f32[64,512]{1,0:T(8,128)S(1)} %add.42.refs_0_), channel_id=1, source_target_pairs={{0,12},{1,13},{2,14},{3,15},{4,8},{5,9},{6,10},{7,11},{8,4},{9,5},... | collective-permute-start | bytes 393224 | tf_op jit(solution)/shard_map/ppermute | solution.py:278
  26.5 1.3 %collective-permute-start.11 = (f32[64,512]{1,0:T(8,128)S(1)}, f32[64,512]{1,0:T(8,128)S(1)}, u32[]{:S(2)}, u32[]{:S(2)}) collective-permute-start(f32[64,512]{1,0:T(8,128)S(1)} %add.42.refs_0_), channel_id=1, source_target_pairs={{0,4},{1,9},{2,6},{3,11},{4,0},{5,13},{6,2},{7,15},{8,12},{9,1},{1... | collective-permute-start | bytes 393224 | tf_op jit(solution)/shard_map/ppermute | solution.py:278
  27.8 2.0 %collective-permute-done.5 = f32[64,512]{1,0:T(8,128)S(1)} collective-permute-done((f32[64,512]{1,0:T(8,128)S(1)}, f32[64,512]{1,0:T(8,128)S(1)}, u32[]{:S(2)}, u32[]{:S(2)}) %collective-permute-start.5) | collective-permute-done | bytes 131104 | tf_op jit(solution)/shard_map/ppermute | solution.py:273
  29.8 0.0 copy-start.3
  29.9 0.0 copy-start.4
  29.9 0.0 copy-start.6
  29.9 1.0 %collective-permute-start.9 = (f32[64,512]{1,0:T(8,128)S(1)}, f32[64,512]{1,0:T(8,128)S(1)}, u32[]{:S(2)}, u32[]{:S(2)}) collective-permute-start(f32[64,512]{1,0:T(8,128)S(1)} %add.43.refs_4_), channel_id=1, source_target_pairs={{0,12},{1,13},{2,14},{3,15},{4,8},{5,9},{6,10},{7,11},{8,4},{9,5},... | collective-permute-start | bytes 393224 | tf_op jit(solution)/shard_map/ppermute | solution.py:278
  30.9 1.4 %collective-permute-start.8 = (f32[64,512]{1,0:T(8,128)S(1)}, f32[64,512]{1,0:T(8,128)S(1)}, u32[]{:S(2)}, u32[]{:S(2)}) collective-permute-start(f32[64,512]{1,0:T(8,128)S(1)} %add.43.refs_4_), channel_id=1, source_target_pairs={{0,4},{1,9},{2,6},{3,11},{4,0},{5,13},{6,2},{7,15},{8,12},{9,1},{1... | collective-permute-start | bytes 393224 | tf_op jit(solution)/shard_map/ppermute | solution.py:278
  32.3 0.3 collective-permute-done.12.refs_3_
  32.6 1.2 %collective-permute-start.7 = (f32[64,512]{1,0:T(8,128)S(1)}, f32[64,512]{1,0:T(8,128)S(1)}, u32[]{:S(2)}, u32[]{:S(2)}) collective-permute-start(f32[64,512]{1,0:T(8,128)S(1)} %add.43.refs_4_), channel_id=1, source_target_pairs={{0,8},{1,5},{2,10},{3,7},{4,12},{5,1},{6,14},{7,3},{8,0},{9,13},{1... | collective-permute-start | bytes 393224 | tf_op jit(solution)/shard_map/ppermute | solution.py:278
  33.8 1.2 %collective-permute-done.11.refs_2_ = f32[64,512]{1,0:T(8,128)S(1)} collective-permute-done((f32[64,512]{1,0:T(8,128)S(1)}, f32[64,512]{1,0:T(8,128)S(1)}, u32[]{:S(2)}, u32[]{:S(2)}) %collective-permute-start.11) | collective-permute-done | bytes 131104 | tf_op jit(solution)/shard_map/ppermute | solution.py:278
  35.0 1.3 %shard_map.104.refs_3_ = f32[1024,512]{1,0:T(8,128)S(1)} custom-call(f32[64,512]{1,0:T(8,128)S(1)} %add.42.refs_0_, f32[64,512]{1,0:T(8,128)S(1)} %collective-permute-done.10.refs_1_, f32[64,512]{1,0:T(8,128)S(1)} %collective-permute-done.11.refs_2_, f32[64,512]{1,0:T(8,128)S(1)} %collective-permute-done.12.refs_3_, f32[64,512]{1,0:T(8,128)S(1)} %add.43.refs_4_, ...), custom_call_target="tpu_custom_call" | custom-call | flops 1006632960 | tf_op jit(solution)/shard_map/pallas_call | solution.py:212
  36.3 1.0 %collective-permute-done.9.refs_2_ = f32[64,512]{1,0:T(8,128)S(1)} collective-permute-done((f32[64,512]{1,0:T(8,128)S(1)}, f32[64,512]{1,0:T(8,128)S(1)}, u32[]{:S(2)}, u32[]{:S(2)}) %collective-permute-start.9) | collective-permute-done | bytes 131104 | tf_op jit(solution)/shard_map/ppermute | solution.py:278
  37.3 0.8 %collective-permute-done.8.refs_1_ = f32[64,512]{1,0:T(8,128)S(1)} collective-permute-done((f32[64,512]{1,0:T(8,128)S(1)}, f32[64,512]{1,0:T(8,128)S(1)}, u32[]{:S(2)}, u32[]{:S(2)}) %collective-permute-start.8) | collective-permute-done | bytes 131104 | tf_op jit(solution)/shard_map/ppermute | solution.py:278
  38.1 0.4 collective-permute-done.7.refs_0_
  38.5 2.4 %shard_map.105 = (bf16[1024,512]{1,0:T(8,128)(2,1)S(1)}, f32[64,512]{1,0:T(8,128)S(1)}, f32[64,512]{1,0:T(8,128)S(1)}, f32[64,512]{1,0:T(8,128)S(1)}, f32[64,512]{1,0:T(8,128)S(1)}) custom-call(f32[64,512]{1,0:T(8,128)S(1)} %collective-permute-done.7.refs_0_, f32[64,512]{1,0:T(8,128)S(1)} %collective-permute-done.8.refs_1_, ...), custom_call_target="tpu_custom_call" | custom-call | flops 1946157056 | tf_op jit(solution)/shard_map/pallas_call | solution.py:375
  40.9 0.1 collective-permute-start.16
  40.9 0.5 collective-permute-start.13
  41.4 0.8 %collective-permute-done.16 = f32[64,512]{1,0:T(8,128)S(1)} collective-permute-done((f32[64,512]{1,0:T(8,128)S(1)}, f32[64,512]{1,0:T(8,128)S(1)}, u32[]{:S(2)}, u32[]{:S(2)}) %collective-permute-start.16) | collective-permute-done | bytes 131104 | tf_op jit(solution)/shard_map/ppermute | solution.py:273
  42.3 1.4 %collective-permute-start.17 = (f32[64,512]{1,0:T(8,128)S(1)}, f32[64,512]{1,0:T(8,128)S(1)}, u32[]{:S(2)}, u32[]{:S(2)}) collective-permute-start(f32[64,512]{1,0:T(8,128)S(1)} %add.46), channel_id=1, source_target_pairs={{0,2},{1,3},{2,0},{3,1},{4,6},{5,7},{6,4},{7,5},{8,10},{9,11},{10,... | collective-permute-start | bytes 393224 | tf_op jit(solution)/shard_map/ppermute | solution.py:273
  43.8 0.7 %collective-permute-start.14 = (f32[64,512]{1,0:T(8,128)S(1)}, f32[64,512]{1,0:T(8,128)S(1)}, u32[]{:S(2)}, u32[]{:S(2)}) collective-permute-start(f32[64,512]{1,0:T(8,128)S(1)} %add.44), channel_id=1, source_target_pairs={{0,2},{1,3},{2,0},{3,1},{4,6},{5,7},{6,4},{7,5},{8,10},{9,11},{10,... | collective-permute-start | bytes 393224 | tf_op jit(solution)/shard_map/ppermute | solution.py:273
  44.5 4.2 %collective-permute-done.17 = f32[64,512]{1,0:T(8,128)S(1)} collective-permute-done((f32[64,512]{1,0:T(8,128)S(1)}, f32[64,512]{1,0:T(8,128)S(1)}, u32[]{:S(2)}, u32[]{:S(2)}) %collective-permute-start.17) | collective-permute-done | bytes 131104 | tf_op jit(solution)/shard_map/ppermute | solution.py:273
  48.7 0.1 collective-permute-start.18
  48.8 1.9 %collective-permute-done.14 = f32[64,512]{1,0:T(8,128)S(1)} collective-permute-done((f32[64,512]{1,0:T(8,128)S(1)}, f32[64,512]{1,0:T(8,128)S(1)}, u32[]{:S(2)}, u32[]{:S(2)}) %collective-permute-start.14) | collective-permute-done | bytes 131104 | tf_op jit(solution)/shard_map/ppermute | solution.py:273
  50.8 0.1 collective-permute-start.15
  50.8 0.0 copy-start
  50.9 0.0 copy-start.1
  50.9 0.0 copy-start.2
  50.9 1.0 %shard_map.106.refs_1_ = f32[1024,512]{1,0:T(8,128)S(1)} custom-call(f32[64,512]{1,0:T(8,128)S(1)} %add.47.refs_0_, f32[64,512]{1,0:T(8,128)S(1)} %collective-permute-done.18.refs_1_, f32[64,512]{1,0:T(8,128)S(1)} %add.45.refs_2_, bf16[1024,576]{1,0:T(8,128)(2,1)S(1)} %get-tuple-element.39.refs_3_, bf16[1024,512]{1,0:T(8,128)(2,1)S(1)} %get-tuple-element.48.refs_4_), custom_call_target="tpu_custom_call" | custom-call | flops 603979776 | tf_op jit(solution)/shard_map/pallas_call | solution.py:212
  51.9 0.3 collective-permute-done.15.refs_0_
  52.2 2.4 %shard_map.107 = bf16[1024,512]{1,0:T(8,128)(2,1)} custom-call(s32[1,128]{1,0:T(1,128)S(1)} %get-tuple-element.27.live_ref, f32[64,512]{1,0:T(8,128)S(1)} %collective-permute-done.15.refs_0_, f32[1024,512]{1,0:T(8,128)S(1)} %shard_map.106.refs_1_, bf16[1024,192]{1,0:T(8,128)(2,1)S(1)} %get-tuple-element.40.refs_2_, bf16[512,512]{1,0:T(8,128)(2,1)S(1)} %copy-done, ...), custom_call_target="tpu_custom_call" | custom-call | flops 1275068416 | tf_op jit(solution)/shard_map/pallas_call | solution.py:386
  (21 shorter events, 0.2 us)
Async XLA Ops:
  0.7 17.7 %copy-start.5 = (s32[1,1,1024]{2,1,0:T(1,128)S(1)}, s32[1,1,1024]{2,1,0:T(1,128)}, u32[]{:S(2)}) copy-start(s32[1,1,1024]{2,1,0:T(1,128)} %param.11) | copy-start | bytes 12292
  2.3 7.9 %collective-permute-start.2 = (f32[64,512]{1,0:T(8,128)S(1)}, f32[64,512]{1,0:T(8,128)S(1)}, u32[]{:S(2)}, u32[]{:S(2)}) collective-permute-start(f32[64,512]{1,0:T(8,128)S(1)} %get-tuple-element.33), channel_id=1, source_target_pairs={{0,12},{1,13},{2,14},{3,15},{4,8},{5,9},{6,10},{7,11},{8,4},{9,5},... | collective-permute-start | bytes 393224 | tf_op jit(solution)/shard_map/ppermute | solution.py:278
  6.3 7.6 %collective-permute-start.3 = (f32[64,512]{1,0:T(8,128)S(1)}, f32[64,512]{1,0:T(8,128)S(1)}, u32[]{:S(2)}, u32[]{:S(2)}) collective-permute-start(f32[64,512]{1,0:T(8,128)S(1)} %get-tuple-element.34), channel_id=1, source_target_pairs={{0,8},{1,5},{2,10},{3,7},{4,12},{5,1},{6,14},{7,3},{8,0},{9,13},{1... | collective-permute-start | bytes 393224 | tf_op jit(solution)/shard_map/ppermute | solution.py:278
  6.8 7.2 %collective-permute-start.4 = (f32[64,512]{1,0:T(8,128)S(1)}, f32[64,512]{1,0:T(8,128)S(1)}, u32[]{:S(2)}, u32[]{:S(2)}) collective-permute-start(f32[64,512]{1,0:T(8,128)S(1)} %get-tuple-element.35), channel_id=1, source_target_pairs={{0,4},{1,9},{2,6},{3,11},{4,0},{5,13},{6,2},{7,15},{8,12},{9,1},{1... | collective-permute-start | bytes 393224 | tf_op jit(solution)/shard_map/ppermute | solution.py:278
  7.4 9.3 %collective-permute-start = (f32[128,512]{1,0:T(8,128)S(1)}, f32[128,512]{1,0:T(8,128)S(1)}, u32[]{:S(2)}, u32[]{:S(2)}) collective-permute-start(f32[128,512]{1,0:T(8,128)S(1)} %shard_map.102), channel_id=1, source_target_pairs={{0,4},{1,9},{2,6},{3,11},{4,0},{5,13},{6,2},{7,15},{8,12},{9,1},{1... | collective-permute-start | bytes 786440 | tf_op jit(solution)/shard_map/ppermute | solution.py:278
  14.0 9.8 %collective-permute-start.6 = (f32[64,512]{1,0:T(8,128)S(1)}, f32[64,512]{1,0:T(8,128)S(1)}, u32[]{:S(2)}, u32[]{:S(2)}) collective-permute-start(f32[64,512]{1,0:T(8,128)S(1)} %add_add_fusion.tie_ref), channel_id=1, source_target_pairs={{0,16},{4,20},{8,24},{12,28},{16,0},{20,4},{24,8},{28,12},{1,17},{... | collective-permute-start | bytes 393224 | tf_op jit(solution)/shard_map/ppermute | solution.py:273
  16.7 5.9 %collective-permute-start.1 = (f32[64,512]{1,0:T(8,128)S(1)}, f32[64,512]{1,0:T(8,128)S(1)}, u32[]{:S(2)}, u32[]{:S(2)}) collective-permute-start(f32[64,512]{1,0:T(8,128)S(1)} %slice_add_fusion), channel_id=1, source_target_pairs={{0,8},{1,5},{2,10},{3,7},{4,12},{5,1},{6,14},{7,3},{8,0},{9,13},{1... | collective-permute-start | bytes 393224 | tf_op jit(solution)/shard_map/ppermute | solution.py:278
  22.7 7.2 %collective-permute-start.5 = (f32[64,512]{1,0:T(8,128)S(1)}, f32[64,512]{1,0:T(8,128)S(1)}, u32[]{:S(2)}, u32[]{:S(2)}) collective-permute-start(f32[64,512]{1,0:T(8,128)S(1)} %fusion), channel_id=1, source_target_pairs={{0,16},{4,20},{8,24},{12,28},{16,0},{20,4},{24,8},{28,12},{1,17},{... | collective-permute-start | bytes 393224 | tf_op jit(solution)/shard_map/ppermute | solution.py:273
  23.8 8.8 %collective-permute-start.12 = (f32[64,512]{1,0:T(8,128)S(1)}, f32[64,512]{1,0:T(8,128)S(1)}, u32[]{:S(2)}, u32[]{:S(2)}) collective-permute-start(f32[64,512]{1,0:T(8,128)S(1)} %add.42.refs_0_), channel_id=1, source_target_pairs={{0,12},{1,13},{2,14},{3,15},{4,8},{5,9},{6,10},{7,11},{8,4},{9,5},... | collective-permute-start | bytes 393224 | tf_op jit(solution)/shard_map/ppermute | solution.py:278
  26.5 8.6 %collective-permute-start.11 = (f32[64,512]{1,0:T(8,128)S(1)}, f32[64,512]{1,0:T(8,128)S(1)}, u32[]{:S(2)}, u32[]{:S(2)}) collective-permute-start(f32[64,512]{1,0:T(8,128)S(1)} %add.42.refs_0_), channel_id=1, source_target_pairs={{0,4},{1,9},{2,6},{3,11},{4,0},{5,13},{6,2},{7,15},{8,12},{9,1},{1... | collective-permute-start | bytes 393224 | tf_op jit(solution)/shard_map/ppermute | solution.py:278
  27.8 7.2 %collective-permute-start.10 = (f32[64,512]{1,0:T(8,128)S(1)}, f32[64,512]{1,0:T(8,128)S(1)}, u32[]{:S(2)}, u32[]{:S(2)}) collective-permute-start(f32[64,512]{1,0:T(8,128)S(1)} %add.42.refs_0_), channel_id=1, source_target_pairs={{0,8},{1,5},{2,10},{3,7},{4,12},{5,1},{6,14},{7,3},{8,0},{9,13},{1... | collective-permute-start | bytes 393224 | tf_op jit(solution)/shard_map/ppermute | solution.py:278
  29.8 8.6 %copy-start.3 = (bf16[512,512]{1,0:T(8,128)(2,1)S(1)}, bf16[512,512]{1,0:T(8,128)(2,1)}, u32[]{:S(2)}) copy-start(bf16[512,512]{1,0:T(8,128)(2,1)} %refs_6_.1) | copy-start | bytes 1572868
  29.9 8.6 %copy-start.4 = (bf16[512,512]{1,0:T(8,128)(2,1)S(1)}, bf16[512,512]{1,0:T(8,128)(2,1)}, u32[]{:S(2)}) copy-start(bf16[512,512]{1,0:T(8,128)(2,1)} %refs_7_.1) | copy-start | bytes 1572868
  29.9 8.6 %copy-start.6 = (f32[512]{0:T(512)S(1)}, f32[512]{0:T(512)}, u32[]{:S(2)}) copy-start(f32[512]{0:T(512)} %param.18) | copy-start | bytes 6148
  29.9 7.4 %collective-permute-start.9 = (f32[64,512]{1,0:T(8,128)S(1)}, f32[64,512]{1,0:T(8,128)S(1)}, u32[]{:S(2)}, u32[]{:S(2)}) collective-permute-start(f32[64,512]{1,0:T(8,128)S(1)} %add.43.refs_4_), channel_id=1, source_target_pairs={{0,12},{1,13},{2,14},{3,15},{4,8},{5,9},{6,10},{7,11},{8,4},{9,5},... | collective-permute-start | bytes 393224 | tf_op jit(solution)/shard_map/ppermute | solution.py:278
  30.9 7.2 %collective-permute-start.8 = (f32[64,512]{1,0:T(8,128)S(1)}, f32[64,512]{1,0:T(8,128)S(1)}, u32[]{:S(2)}, u32[]{:S(2)}) collective-permute-start(f32[64,512]{1,0:T(8,128)S(1)} %add.43.refs_4_), channel_id=1, source_target_pairs={{0,4},{1,9},{2,6},{3,11},{4,0},{5,13},{6,2},{7,15},{8,12},{9,1},{1... | collective-permute-start | bytes 393224 | tf_op jit(solution)/shard_map/ppermute | solution.py:278
  32.6 5.8 %collective-permute-start.7 = (f32[64,512]{1,0:T(8,128)S(1)}, f32[64,512]{1,0:T(8,128)S(1)}, u32[]{:S(2)}, u32[]{:S(2)}) collective-permute-start(f32[64,512]{1,0:T(8,128)S(1)} %add.43.refs_4_), channel_id=1, source_target_pairs={{0,8},{1,5},{2,10},{3,7},{4,12},{5,1},{6,14},{7,3},{8,0},{9,13},{1... | collective-permute-start | bytes 393224 | tf_op jit(solution)/shard_map/ppermute | solution.py:278
  40.9 1.4 %collective-permute-start.16 = (f32[64,512]{1,0:T(8,128)S(1)}, f32[64,512]{1,0:T(8,128)S(1)}, u32[]{:S(2)}, u32[]{:S(2)}) collective-permute-start(f32[64,512]{1,0:T(8,128)S(1)} %get-tuple-element.47), channel_id=1, source_target_pairs={{0,1},{1,0},{2,3},{3,2},{4,5},{5,4},{6,7},{7,6},{8,9},{9,8},{10,11... | collective-permute-start | bytes 393224 | tf_op jit(solution)/shard_map/ppermute | solution.py:273
  40.9 2.8 %collective-permute-start.13 = (f32[64,512]{1,0:T(8,128)S(1)}, f32[64,512]{1,0:T(8,128)S(1)}, u32[]{:S(2)}, u32[]{:S(2)}) collective-permute-start(f32[64,512]{1,0:T(8,128)S(1)} %get-tuple-element.45), channel_id=1, source_target_pairs={{0,1},{1,0},{2,3},{3,2},{4,5},{5,4},{6,7},{7,6},{8,9},{9,8},{10,11... | collective-permute-start | bytes 393224 | tf_op jit(solution)/shard_map/ppermute | solution.py:273
  42.3 6.4 %collective-permute-start.17 = (f32[64,512]{1,0:T(8,128)S(1)}, f32[64,512]{1,0:T(8,128)S(1)}, u32[]{:S(2)}, u32[]{:S(2)}) collective-permute-start(f32[64,512]{1,0:T(8,128)S(1)} %add.46), channel_id=1, source_target_pairs={{0,2},{1,3},{2,0},{3,1},{4,6},{5,7},{6,4},{7,5},{8,10},{9,11},{10,... | collective-permute-start | bytes 393224 | tf_op jit(solution)/shard_map/ppermute | solution.py:273
  43.8 7.0 %collective-permute-start.14 = (f32[64,512]{1,0:T(8,128)S(1)}, f32[64,512]{1,0:T(8,128)S(1)}, u32[]{:S(2)}, u32[]{:S(2)}) collective-permute-start(f32[64,512]{1,0:T(8,128)S(1)} %add.44), channel_id=1, source_target_pairs={{0,2},{1,3},{2,0},{3,1},{4,6},{5,7},{6,4},{7,5},{8,10},{9,11},{10,... | collective-permute-start | bytes 393224 | tf_op jit(solution)/shard_map/ppermute | solution.py:273
  48.7 2.1 %collective-permute-start.18 = (f32[64,512]{1,0:T(8,128)S(1)}, f32[64,512]{1,0:T(8,128)S(1)}, u32[]{:S(2)}, u32[]{:S(2)}) collective-permute-start(f32[64,512]{1,0:T(8,128)S(1)} %add.47.refs_0_), channel_id=1, source_target_pairs={{0,1},{1,0},{2,3},{3,2},{4,5},{5,4},{6,7},{7,6},{8,9},{9,8},{10,11... | collective-permute-start | bytes 393224 | tf_op jit(solution)/shard_map/ppermute | solution.py:273
  50.8 1.4 %collective-permute-start.15 = (f32[64,512]{1,0:T(8,128)S(1)}, f32[64,512]{1,0:T(8,128)S(1)}, u32[]{:S(2)}, u32[]{:S(2)}) collective-permute-start(f32[64,512]{1,0:T(8,128)S(1)} %add.45.refs_2_), channel_id=1, source_target_pairs={{0,1},{1,0},{2,3},{3,2},{4,5},{5,4},{6,7},{7,6},{8,9},{9,8},{10,11... | collective-permute-start | bytes 393224 | tf_op jit(solution)/shard_map/ppermute | solution.py:273
  50.8 1.3 %copy-start = (bf16[512,512]{1,0:T(8,128)(2,1)S(1)}, bf16[512,512]{1,0:T(8,128)(2,1)}, u32[]{:S(2)}) copy-start(bf16[512,512]{1,0:T(8,128)(2,1)} %refs_3_.1) | copy-start | bytes 1572868
  50.9 1.3 %copy-start.1 = (bf16[512,512]{1,0:T(8,128)(2,1)S(1)}, bf16[512,512]{1,0:T(8,128)(2,1)}, u32[]{:S(2)}) copy-start(bf16[512,512]{1,0:T(8,128)(2,1)} %refs_4_.1) | copy-start | bytes 1572868
  50.9 1.3 %copy-start.2 = (f32[512]{0:T(512)S(1)}, f32[512]{0:T(512)}, u32[]{:S(2)}) copy-start(f32[512]{0:T(512)} %param.19) | copy-start | bytes 6148
